TPU v7x, 32 devices: a whole 2x2x4 slice. The times are simulated.
32 devices in a mesh: ctx: 8 (over y, x, core), dp: 4 (over z).
Axes of the slice: x: 2, y: 2, z: 4, core: 2. Of those that a mesh axis runs over, the one named last changes fastest.
Arguments:
- q_proj: bfloat16 [4, 1024, 2048], P('dp', 'ctx'), may hold values from -6 to 6
- k_proj: bfloat16 [4, 1024, 2048], P('dp', 'ctx'), may hold values from -6 to 6
- v_proj: bfloat16 [4, 1024, 2048], P('dp', 'ctx'), may hold values from -6 to 6
- out_grad: bfloat16 [4, 1024, 2048], P('dp', 'ctx'), may hold values from -6 to 6
- contig_starts: int32 [4, 1024], P('dp', 'ctx'), may hold values 0 or 1
- filters: bfloat16 [128, 128], replicated, may hold values from -0.5 to 0.5
Outputs:
- mixed_out: bfloat16 [4, 1024, 2048], P('dp', 'ctx')
- grad_q: bfloat16 [4, 1024, 2048], P('dp', 'ctx')
- grad_k: bfloat16 [4, 1024, 2048], P('dp', 'ctx')
- grad_v: bfloat16 [4, 1024, 2048], P('dp', 'ctx')
- filter_grad: float32 [128, 128], replicated
Inputs may be any that keep to these rules, and one draw needn't show every extreme that they name: `contig_starts`: a contig runs from a 1 to the token before the next 1 or to the end of its pack.
All inputs are finite; a program needn't handle non-finite values. No bound on the sum of `contig_starts` on one device may be relied on, other than what follows from the above.
Results may differ from a plain program's by a relative error of at most 0.0053.
Values may be sent and summed in bfloat16 or wider, within the bound.
No kernel may reach another device: no remote copies, remote signals or barrier semaphores. Data moves between devices by JAX's collectives and lax.ppermute only.
A program may use at most 64 MiB of HBM per device.

v0:
```python
import math

import jax
import jax.numpy as jnp
from jax import lax
from jax.sharding import PartitionSpec as P

FILT = 128
GSIZE = 16


def passed_along(block, axis, distance):
    devices = range(lax.axis_size(axis))
    route = [(i - distance, i) for i in devices if i - distance in devices]
    return lax.ppermute(block, axis, route)


def skew_rows(row_table):
    count = row_table.shape[0]
    tiled = jnp.tile(row_table, (1, FILT))[:, : FILT * (2 * FILT - 1)]
    return tiled.reshape(count, FILT, 2 * FILT - 1)


def diagonal_sums(products):
    lead = products.shape[:-2]
    flat = products.reshape(lead + (FILT * (2 * FILT - 1),))
    flat = jnp.concatenate([flat, jnp.zeros(lead + (FILT,), flat.dtype)], axis=-1)
    return jnp.sum(flat.reshape(lead + (FILT, 2 * FILT))[..., :FILT], axis=-2)


def windows(extended):
    nblocks = extended.shape[0] // FILT - 1
    blocks = extended.reshape((nblocks + 1, FILT) + extended.shape[1:])
    return jnp.concatenate([blocks[:-1], blocks[1:, : FILT - 1]], axis=1)


def per_device(q_proj, k_proj, v_proj, out_grad, contig_starts, filters):
    queries = q_proj[0]
    keys_in = k_proj[0]
    values_in = v_proj[0]
    upstream = out_grad[0]
    rows = queries.shape[0]
    width = queries.shape[1]
    groups = filters.shape[0]
    nblocks = rows // FILT
    span = 2 * FILT - 1
    tail = FILT - 1
    per_step = math.gcd(groups, 8)
    chans = per_step * GSIZE
    segment_ids = jnp.cumsum(contig_starts[0])
    last_id = segment_ids[rows - 1]
    prod_kv = (keys_in.astype(jnp.float32) * values_in.astype(jnp.float32)).astype(jnp.bfloat16)
    cotangent = (upstream.astype(jnp.float32) * queries.astype(jnp.float32)).astype(jnp.bfloat16)
    tail_keep = segment_ids[rows - tail :] == last_id
    outgoing = prod_kv[rows - tail :] * tail_keep[:, None].astype(jnp.bfloat16)
    incoming = passed_along(outgoing, "ctx", 1)
    kv_ext = jnp.concatenate([incoming, prod_kv, jnp.zeros((1, width), jnp.bfloat16)], 0)
    seg_ext = jnp.concatenate(
        [jnp.zeros((tail,), jnp.int32), segment_ids, jnp.full((1,), -1, jnp.int32)], 0
    )
    kv_win = windows(kv_ext)
    seg_win = windows(seg_ext)
    seg_own = segment_ids.reshape(nblocks, FILT)
    fwd_mask = (seg_win[:, None, :] == seg_own[:, :, None]).astype(jnp.bfloat16)
    head_keep = segment_ids[:tail] == 0
    head = passed_along(cotangent[:tail] * head_keep[:, None].astype(jnp.bfloat16), "ctx", -1)
    cot_ext = jnp.concatenate([cotangent, head, jnp.zeros((1, width), jnp.bfloat16)], 0)
    segc_ext = jnp.concatenate(
        [segment_ids, jnp.zeros((tail,), jnp.int32) + last_id, jnp.full((1,), -1, jnp.int32)], 0
    )
    cot_win = windows(cot_ext)
    back_mask = (windows(segc_ext)[:, None, :] == seg_own[:, :, None]).astype(jnp.bfloat16)

    def group_block(index, carry):
        mixed, grad_q, grad_kv, partial_sum, filter_local = carry
        start = index * chans
        taps = lax.dynamic_slice_in_dim(filters, index * per_step, per_step, 0)
        fwd_table = skew_rows(jnp.concatenate([taps[:, ::-1], jnp.zeros_like(taps)], axis=1))
        fwd_masked = fwd_table[None] * fwd_mask[:, None]
        kv_block = lax.dynamic_slice_in_dim(kv_win, start, chans, 2).reshape(
            nblocks, span, per_step, GSIZE
        )
        conv = jnp.einsum(
            "bgts,bsgc->btgc", fwd_masked, kv_block, preferred_element_type=jnp.float32
        ).reshape(rows, chans)
        q_block = lax.dynamic_slice_in_dim(queries, start, chans, 1)
        up_block = lax.dynamic_slice_in_dim(upstream, start, chans, 1)
        cot_block = lax.dynamic_slice_in_dim(cotangent, start, chans, 1).reshape(
            nblocks, FILT, per_step, GSIZE
        )
        mixed = lax.dynamic_update_slice_in_dim(
            mixed, (q_block.astype(jnp.float32) * conv).astype(jnp.bfloat16), start, 1
        )
        grad_q = lax.dynamic_update_slice_in_dim(
            grad_q, (up_block.astype(jnp.float32) * conv).astype(jnp.bfloat16), start, 1
        )
        products = jnp.einsum(
            "btgc,bsgc->bgts", cot_block, kv_block, preferred_element_type=jnp.float32
        )
        products = products * fwd_mask[:, None].astype(jnp.float32)
        diag = jnp.sum(diagonal_sums(products), axis=0)[:, ::-1]
        filter_local = lax.dynamic_update_slice_in_dim(filter_local, diag, index * per_step, 0)
        back_table = skew_rows(jnp.concatenate([taps, jnp.zeros_like(taps)], axis=1))
        back_masked = back_table[None] * back_mask[:, None]
        cw_block = lax.dynamic_slice_in_dim(cot_win, start, chans, 2).reshape(
            nblocks, span, per_step, GSIZE
        )
        local = jnp.einsum(
            "bgsw,bwgc->bsgc", back_masked, cw_block, preferred_element_type=jnp.float32
        )
        grad_kv = lax.dynamic_update_slice_in_dim(grad_kv, local.reshape(rows, chans), start, 1)
        return (mixed, grad_q, grad_kv, partial_sum, filter_local)

    initial = (
        jnp.zeros((rows, width), jnp.bfloat16),
        jnp.zeros((rows, width), jnp.bfloat16),
        jnp.zeros((rows, width), jnp.float32),
        jnp.zeros((tail, width), jnp.float32),
        jnp.zeros((groups, FILT), jnp.float32),
    )
    mixed, grad_q, grad_kv, partial_sum, filter_local = lax.fori_loop(
        0, groups // per_step, group_block, initial
    )
    grad_k = (grad_kv * values_in.astype(jnp.float32)).astype(jnp.bfloat16)
    grad_v = (grad_kv * keys_in.astype(jnp.float32)).astype(jnp.bfloat16)
    share = lax.psum_scatter(filter_local, "dp", scatter_dimension=0, tiled=True)
    share = lax.psum(share, "ctx")
    filter_sum = lax.all_gather(share, "dp", axis=0, tiled=True)
    scale = 1.0 / math.sqrt(rows * lax.axis_size("ctx") * lax.axis_size("dp") * GSIZE)
    filter_grad = filter_sum * scale
    return (mixed[None], grad_q[None], grad_k[None], grad_v[None], filter_grad)


def solution(mesh):
    placed = (
        P("dp", "ctx", None),
        P("dp", "ctx", None),
        P("dp", "ctx", None),
        P("dp", "ctx", None),
        P("dp", "ctx"),
        P(),
    )
    return jax.shard_map(
        per_device,
        mesh=mesh,
        in_specs=placed,
        out_specs=(
            P("dp", "ctx", None),
            P("dp", "ctx", None),
            P("dp", "ctx", None),
            P("dp", "ctx", None),
            P(),
        ),
        check_vma=False,
    )
```

profile of v0, /device:TPU:0, one launch (start us, length us, event | category | flops | bytes accessed | tf_op | source)
XLA Modules:
  0.0 249.2 jit_solution(15631582921125908809)
XLA Ops:
  7.2 1.4 copy.23
  11.4 1.3 collective-permute-start.1
  12.9 1.0 slice_multiply_fusion.1
  13.9 3.1 %collective-permute-start = (bf16[127,2048]{1,0:T(8,128)(2,1)}, bf16[127,2048]{1,0:T(8,128)(2,1)S(1)}, u32[]{:S(2)}, u32[]{:S(2)}) collective-permute-start(bf16[127,2048]{1,0:T(8,128)(2,1)} %slice_multiply_fusion.1), channel_id=1, source_target_pairs={{0,4},{4,8},{8,12},{12,16},{16,20},{20,24},{24,28},{1,5},{5,9},{9,... | collective-permute-start | bytes 1560584 | tf_op jit(solution)/shard_map/ppermute | solution.py:15
  18.9 2.3 maximum_maximum_fusion.1
  21.2 2.2 reshape.302
  23.4 2.2 slice.103
  26.1 1.0 copy-done.4
  27.0 1.2 pad_maximum_fusion.1
  28.3 1.1 pad_maximum_fusion
  29.4 1.1 broadcast_in_dim.29.clone
  32.2 145.8 %while.21 = (s32[]{:T(128)}, bf16[128,2048]{1,0:T(8,128)(2,1)}, bf16[128,2048]{1,0:T(8,128)(2,1)}, f32[128,2048]{1,0:T(8,128)}, f32[128,128]{1,0:T(8,128)S(1)}, ...) while((s32[]{:T(128)}, bf16[128,2048]{1,0:T(8,128)(2,1)}, ...), condition=%wide.region_3.4_spmd.clone.clone, body=%wide.region_1.3_spmd.clone.clone.sunk | while | flops 26242440 | bytes 18328176 | solution.py:121
  34.1 1.4 reshape.335
  39.0 1.4 reshape.336
  43.3 1.4 reshape.335
  48.1 1.4 reshape.336
  52.4 1.4 reshape.335
  57.2 1.4 reshape.336
  61.5 1.4 reshape.335
  66.3 1.4 reshape.336
  70.6 1.4 reshape.335
  75.5 1.4 reshape.336
  79.7 1.4 reshape.335
  84.6 1.4 reshape.336
  88.9 1.4 reshape.335
  93.7 1.4 reshape.336
  98.0 1.4 reshape.335
  102.8 1.4 reshape.336
  107.1 1.4 reshape.335
  111.9 1.4 reshape.336
  116.2 1.4 reshape.335
  121.0 1.4 reshape.336
  125.3 1.4 reshape.335
  130.1 1.4 reshape.336
  134.4 1.4 reshape.335
  139.2 1.4 reshape.336
  143.5 1.4 reshape.335
  148.4 1.4 reshape.336
  152.6 1.4 reshape.335
  157.4 1.4 reshape.336
  161.7 1.4 reshape.335
  166.5 1.4 reshape.336
  170.8 1.4 reshape.335
  175.6 1.4 reshape.336
  178.7 2.8 %fusion.18 = (bf16[1,128,2048]{2,1,0:T(8,128)(2,1)}, bf16[1,128,2048]{2,1,0:T(8,128)(2,1)}) fusion(f32[128,2048]{1,0:T(8,128)} %get-tuple-element.224, bf16[1,128,2048]{2,1,0:T(8,128)(2,1)} %param.9, bf16[1,128,2048]{2,1,0:T(8,128)(2,1)} %param.10), kind=kLoop, calls=%fused_computation.39 | loop fusion | flops 1572864 | bytes 3145728 | tf_op jit(solution)/shard_map/broadcast_in_dim | solution.py:131
  181.4 24.3 %reduce-scatter.2.cloned.1.call-done = f32[32,128]{1,0:T(8,128)} async-done(((f32[128,128]{1,0:T(8,128)}), f32[32,128]{1,0:T(8,128)}) %reduce-scatter.2.cloned.1.call-update) | async-done | bytes 16400 | tf_op jit(solution)/shard_map/reduce_scatter | solution.py:126
  205.7 22.9 %psum.7 = f32[32,128]{1,0:T(8,128)S(1)} all-reduce(f32[32,128]{1,0:T(8,128)} %reduce-scatter.2.cloned.1.call-done), channel_id=1, replica_groups=mesh['ctx'=8,'dp'=4] {'ctx'}, use_global_device_ids=true, to_apply=%region_5.6 | all-reduce | flops 4096 | bytes 32768 | tf_op jit(solution)/shard_map/psum | solution.py:127
  228.6 13.1 %all_gather.3 = f32[128,128]{1,0:T(8,128)S(1)} all-gather(f32[32,128]{1,0:T(8,128)S(1)} %psum.7), channel_id=1, replica_groups=mesh['ctx'=8,'dp'=4] {'dp'}, dimensions={0}, use_global_device_ids=true | all-gather | bytes 81920 | tf_op jit(solution)/shard_map/all_gather | solution.py:128
  (538 shorter events, 108.5 us)
Async XLA Ops:
  7.2 1.4 copy-start.5
  7.2 1.7 copy-start.7
  7.2 198.5 %reduce-scatter.2.cloned.1.call-start = ((), (), s32[]{:S(2)}) async-start(), calls=%async_computation.1 | async-start | bytes 81920 | tf_op jit(solution)/shard_map/reduce_scatter | solution.py:126
  10.4 2.3 copy-start.2
  10.5 2.3 copy-start.3
  11.4 7.5 %collective-permute-start.1 = (bf16[127,2048]{0,1:T(8,128)(2,1)}, bf16[127,2048]{0,1:T(8,128)(2,1)}, u32[]{:S(2)}, u32[]{:S(2)}) collective-permute-start(bf16[127,2048]{0,1:T(8,128)(2,1)} %slice_multiply_fusion), channel_id=1, source_target_pairs={{4,0},{8,4},{12,8},{16,12},{20,16},{24,20},{28,24},{5,1},{9,5},{13... | collective-permute-start | bytes 1560584 | tf_op jit(solution)/shard_map/ppermute | solution.py:15
  13.9 11.8 %collective-permute-start = (bf16[127,2048]{1,0:T(8,128)(2,1)}, bf16[127,2048]{1,0:T(8,128)(2,1)S(1)}, u32[]{:S(2)}, u32[]{:S(2)}) collective-permute-start(bf16[127,2048]{1,0:T(8,128)(2,1)} %slice_multiply_fusion.1), channel_id=1, source_target_pairs={{0,4},{4,8},{8,12},{12,16},{16,20},{20,24},{24,28},{1,5},{5,9},{9,... | collective-permute-start | bytes 1560584 | tf_op jit(solution)/shard_map/ppermute | solution.py:15
  26.0 1.0 copy-start.4
  32.2 4.6 %copy-start = (bf16[128,2048]{0,1:T(8,128)(2,1)}, bf16[128,2048]{0,1:T(8,128)(2,1)S(1)}, u32[]{:S(2)}) copy-start(bf16[128,2048]{0,1:T(8,128)(2,1)S(1)} %get-tuple-element.516) | copy-start | bytes 1572868 | tf_op jit(solution)/shard_map/while
  39.0 2.4 copy-start.1
  41.4 4.5 %copy-start = (bf16[128,2048]{0,1:T(8,128)(2,1)}, bf16[128,2048]{0,1:T(8,128)(2,1)S(1)}, u32[]{:S(2)}) copy-start(bf16[128,2048]{0,1:T(8,128)(2,1)S(1)} %get-tuple-element.516) | copy-start | bytes 1572868 | tf_op jit(solution)/shard_map/while
  48.1 2.4 copy-start.1
  50.5 4.5 %copy-start = (bf16[128,2048]{0,1:T(8,128)(2,1)}, bf16[128,2048]{0,1:T(8,128)(2,1)S(1)}, u32[]{:S(2)}) copy-start(bf16[128,2048]{0,1:T(8,128)(2,1)S(1)} %get-tuple-element.516) | copy-start | bytes 1572868 | tf_op jit(solution)/shard_map/while
  57.2 2.4 copy-start.1
  59.6 4.5 %copy-start = (bf16[128,2048]{0,1:T(8,128)(2,1)}, bf16[128,2048]{0,1:T(8,128)(2,1)S(1)}, u32[]{:S(2)}) copy-start(bf16[128,2048]{0,1:T(8,128)(2,1)S(1)} %get-tuple-element.516) | copy-start | bytes 1572868 | tf_op jit(solution)/shard_map/while
  66.3 2.4 copy-start.1
  68.8 4.5 %copy-start = (bf16[128,2048]{0,1:T(8,128)(2,1)}, bf16[128,2048]{0,1:T(8,128)(2,1)S(1)}, u32[]{:S(2)}) copy-start(bf16[128,2048]{0,1:T(8,128)(2,1)S(1)} %get-tuple-element.516) | copy-start | bytes 1572868 | tf_op jit(solution)/shard_map/while
  75.5 2.4 copy-start.1
  77.9 4.5 %copy-start = (bf16[128,2048]{0,1:T(8,128)(2,1)}, bf16[128,2048]{0,1:T(8,128)(2,1)S(1)}, u32[]{:S(2)}) copy-start(bf16[128,2048]{0,1:T(8,128)(2,1)S(1)} %get-tuple-element.516) | copy-start | bytes 1572868 | tf_op jit(solution)/shard_map/while
  84.6 2.4 copy-start.1
  87.0 4.5 %copy-start = (bf16[128,2048]{0,1:T(8,128)(2,1)}, bf16[128,2048]{0,1:T(8,128)(2,1)S(1)}, u32[]{:S(2)}) copy-start(bf16[128,2048]{0,1:T(8,128)(2,1)S(1)} %get-tuple-element.516) | copy-start | bytes 1572868 | tf_op jit(solution)/shard_map/while
  93.7 2.4 copy-start.1
  96.1 4.5 %copy-start = (bf16[128,2048]{0,1:T(8,128)(2,1)}, bf16[128,2048]{0,1:T(8,128)(2,1)S(1)}, u32[]{:S(2)}) copy-start(bf16[128,2048]{0,1:T(8,128)(2,1)S(1)} %get-tuple-element.516) | copy-start | bytes 1572868 | tf_op jit(solution)/shard_map/while
  102.8 2.4 copy-start.1
  105.2 4.5 %copy-start = (bf16[128,2048]{0,1:T(8,128)(2,1)}, bf16[128,2048]{0,1:T(8,128)(2,1)S(1)}, u32[]{:S(2)}) copy-start(bf16[128,2048]{0,1:T(8,128)(2,1)S(1)} %get-tuple-element.516) | copy-start | bytes 1572868 | tf_op jit(solution)/shard_map/while
  111.9 2.4 copy-start.1
  114.3 4.5 %copy-start = (bf16[128,2048]{0,1:T(8,128)(2,1)}, bf16[128,2048]{0,1:T(8,128)(2,1)S(1)}, u32[]{:S(2)}) copy-start(bf16[128,2048]{0,1:T(8,128)(2,1)S(1)} %get-tuple-element.516) | copy-start | bytes 1572868 | tf_op jit(solution)/shard_map/while
  121.0 2.4 copy-start.1
  123.4 4.5 %copy-start = (bf16[128,2048]{0,1:T(8,128)(2,1)}, bf16[128,2048]{0,1:T(8,128)(2,1)S(1)}, u32[]{:S(2)}) copy-start(bf16[128,2048]{0,1:T(8,128)(2,1)S(1)} %get-tuple-element.516) | copy-start | bytes 1572868 | tf_op jit(solution)/shard_map/while
  130.1 2.4 copy-start.1
  132.5 4.5 %copy-start = (bf16[128,2048]{0,1:T(8,128)(2,1)}, bf16[128,2048]{0,1:T(8,128)(2,1)S(1)}, u32[]{:S(2)}) copy-start(bf16[128,2048]{0,1:T(8,128)(2,1)S(1)} %get-tuple-element.516) | copy-start | bytes 1572868 | tf_op jit(solution)/shard_map/while
  139.2 2.4 copy-start.1
  141.6 4.5 %copy-start = (bf16[128,2048]{0,1:T(8,128)(2,1)}, bf16[128,2048]{0,1:T(8,128)(2,1)S(1)}, u32[]{:S(2)}) copy-start(bf16[128,2048]{0,1:T(8,128)(2,1)S(1)} %get-tuple-element.516) | copy-start | bytes 1572868 | tf_op jit(solution)/shard_map/while
  148.3 2.4 copy-start.1
  150.7 4.5 %copy-start = (bf16[128,2048]{0,1:T(8,128)(2,1)}, bf16[128,2048]{0,1:T(8,128)(2,1)S(1)}, u32[]{:S(2)}) copy-start(bf16[128,2048]{0,1:T(8,128)(2,1)S(1)} %get-tuple-element.516) | copy-start | bytes 1572868 | tf_op jit(solution)/shard_map/while
  157.4 2.4 copy-start.1
  159.8 4.5 %copy-start = (bf16[128,2048]{0,1:T(8,128)(2,1)}, bf16[128,2048]{0,1:T(8,128)(2,1)S(1)}, u32[]{:S(2)}) copy-start(bf16[128,2048]{0,1:T(8,128)(2,1)S(1)} %get-tuple-element.516) | copy-start | bytes 1572868 | tf_op jit(solution)/shard_map/while
  166.5 2.4 copy-start.1
  168.9 4.5 %copy-start = (bf16[128,2048]{0,1:T(8,128)(2,1)}, bf16[128,2048]{0,1:T(8,128)(2,1)S(1)}, u32[]{:S(2)}) copy-start(bf16[128,2048]{0,1:T(8,128)(2,1)S(1)} %get-tuple-element.516) | copy-start | bytes 1572868 | tf_op jit(solution)/shard_map/while
  175.6 2.4 copy-start.1
  178.0 0.6 copy-start.6
Sparse Core Ops, SparseCore 0:
  178.8 26.8 reduce-scatter.1
where the time goes:
time: 252 us; the launch traced here: 249 us
  local copies, waits for them, and re-layouts  138 us (55%)
  blocking collectives  36 us (14%)
  waiting for transfers between devices  24.3 us (10%)
  other arithmetic  16.6 us (7%)
  between operations  14.2 us (6%)
  matrix products  13.3 us (5%)
  starting transfers between devices  4.37 us (2%)
    reduce_scatter x1, waiting for transfers between devices, per_device(): lax.psum_scatter(filter_local, 'dp', scatter_dimension=0, tiled=True)  24.3 us
    psum x1, blocking collectives, per_device(): share = lax.psum(share, 'ctx')  22.9 us
    reshape x16, local copies, waits for them, and re-layouts, group_block(): fwd_masked = fwd_table[None] * fwd_mask[:, None]  21.8 us
    reshape x16, local copies, waits for them, and re-layouts, group_block(): back_masked = back_table[None] * back_mask[:, None]  21.8 us
    dynamic_slice x32, local copies, waits for them, and re-layouts, group_block(): lax.dynamic_slice_in_dim(kv_win, start, chans, 2)  16 us
    dynamic_slice x16, local copies, waits for them, and re-layouts, group_block(): lax.dynamic_slice_in_dim(cot_win, start, chans, 2)  13.5 us
    all_gather x1, blocking collectives, per_device(): filter_sum = lax.all_gather(share, 'dp', axis=0, tiled=True)  13.1 us
    dynamic_update_slice x32, local copies, waits for them, and re-layouts, group_block(): lax.dynamic_update_slice_in_dim(grad_kv, local.reshape(rows, chans), star...  12.1 us
  transfers between devices with their start and end apart: 3, of which 1 were waited for; matrix products, arithmetic and copies ran while one was open for 5% of the time, Pallas kernels for 0%

commit v1 on v0

v1 whole, which is shorter than its diff:
```python
import functools
import math

import jax
import jax.numpy as jnp
from jax import lax
from jax.experimental import pallas as pl
from jax.experimental.pallas import tpu as pltpu
from jax.sharding import PartitionSpec as P

GSIZE = 16
LANES = 128
BLOCK = 512


def product(a, b):
    return (a.astype(jnp.float32) * b.astype(jnp.float32)).astype(jnp.bfloat16)


def contig_masks(starts_ref):
    rows = starts_ref.shape[1]
    starts = jnp.broadcast_to(starts_ref[...], (rows, rows)) > 0
    t = lax.broadcasted_iota(jnp.int32, (rows, rows), 0)
    s = lax.broadcasted_iota(jnp.int32, (rows, rows), 1)
    began = jnp.max(jnp.where(starts & (s <= t), s, 0), axis=1, keepdims=True)
    own = (s <= t) & (s >= began)
    first = jnp.min(jnp.where(starts, s, rows), axis=1, keepdims=True)
    previous = (s > t) & (t < first)
    last = jnp.max(jnp.where(starts, s, 0), axis=1, keepdims=True)
    following = (s < t) & (t >= last)
    as_f32 = lambda mask: jnp.where(mask, 1.0, 0.0).astype(jnp.float32)
    return as_f32(own), as_f32(previous), as_f32(following)


def reversed_taps(rows_of_taps):
    taps = rows_of_taps.shape[1]
    i = lax.broadcasted_iota(jnp.int32, (taps, taps), 0)
    j = lax.broadcasted_iota(jnp.int32, (taps, taps), 1)
    flip = jnp.where((i + j == 0) | (i + j == taps), 1.0, 0.0).astype(jnp.float32)
    return jnp.dot(
        rows_of_taps.astype(jnp.float32), flip,
        preferred_element_type=jnp.float32, precision=lax.Precision.HIGHEST,
    )


def lane_groups():
    return lax.broadcasted_iota(jnp.int32, (1, LANES), 1) // GSIZE


def filter_kernel(q_ref, k_ref, v_ref, dy_ref, kv_prev_ref, starts_ref, out_ref, own_ref, prev_ref, sums_ref):
    rows = q_ref.shape[0]
    per_tile = LANES // GSIZE

    @pl.when(pl.program_id(0) == 0)
    def _():
        own, previous, _ = contig_masks(starts_ref)
        own_ref[...] = own
        prev_ref[...] = previous

    group = lane_groups()

    def tile(index, carry):
        lanes = pl.ds(pl.multiple_of(index * LANES, LANES), LANES)
        cot = product(dy_ref[:, lanes], q_ref[:, lanes])
        kv = jnp.concatenate([product(k_ref[:, lanes], v_ref[:, lanes]), kv_prev_ref[:, lanes]], axis=0)
        for g in range(per_tile):
            picked = jnp.where(group == g, cot, jnp.zeros_like(cot))
            pairs = lax.dot_general(
                picked, kv, (((1,), (1,)), ((), ())), preferred_element_type=jnp.float32
            )
            linked = pairs[:, :rows] * own_ref[...] + pairs[:, rows:] * prev_ref[...]
            total = linked[:8]
            for i in range(1, rows // 8):
                total = total + pltpu.roll(linked[8 * i : 8 * i + 8], rows - 8 * i, 1)
            at = pl.multiple_of((index * per_tile + g) * 8, 8)
            sums_ref[pl.ds(at, 8), :] = total
        return carry

    lax.fori_loop(0, q_ref.shape[1] // LANES, tile, 0)
    groups = out_ref.shape[0]
    diagonal = sums_ref[pl.ds(0, groups, stride=8), :]
    for r in range(1, 8):
        diagonal = diagonal + pltpu.roll(sums_ref[pl.ds(r, groups, stride=8), :], rows - r, 1)
    out_ref[...] = reversed_taps(diagonal)


def conv_kernel(
    q_ref, k_ref, v_ref, dy_ref, kv_prev_ref, cot_next_ref, starts_ref, taps_ref,
    mixed_ref, grad_q_ref, grad_k_ref, grad_v_ref,
    fwd_mask_ref, back_mask_ref, taps_scr, flipped_scr,
):
    rows = q_ref.shape[0]
    per_tile = LANES // GSIZE

    @pl.when(pl.program_id(0) == 0)
    def _():
        own, previous, following = contig_masks(starts_ref)
        fwd_mask_ref[:, :rows] = own.astype(jnp.bfloat16)
        fwd_mask_ref[:, rows:] = previous.astype(jnp.bfloat16)
        back_mask_ref[:, :rows] = own.T.astype(jnp.bfloat16)
        back_mask_ref[:, rows:] = following.astype(jnp.bfloat16)

    taps_scr[...] = taps_ref[...].astype(jnp.float32)
    flipped_scr[...] = reversed_taps(taps_ref[...])
    group = lane_groups()

    def circulant(row):
        wide = pltpu.roll(jnp.broadcast_to(row, (rows, rows)), 0, 1, stride=1, stride_axis=0)
        return wide.astype(jnp.bfloat16)

    def tile(index, carry):
        lanes = pl.ds(pl.multiple_of(index * LANES, LANES), LANES)
        q, k, v, dy = (ref[:, lanes] for ref in (q_ref, k_ref, v_ref, dy_ref))
        kv = jnp.concatenate([product(k, v), kv_prev_ref[:, lanes]], axis=0)
        cot = jnp.concatenate([product(dy, q), cot_next_ref[:, lanes]], axis=0)
        at = pl.ds(pl.multiple_of(index * per_tile, per_tile), per_tile)
        taps = taps_scr[at, :]
        flipped = flipped_scr[at, :]
        conv = jnp.zeros((rows, LANES), jnp.float32)
        grad_kv = jnp.zeros((rows, LANES), jnp.float32)
        for g in range(per_tile):
            c = circulant(flipped[g : g + 1])
            table = jnp.concatenate([c, c], axis=1) * fwd_mask_ref[...]
            conv = jnp.where(group == g, jnp.dot(table, kv, preferred_element_type=jnp.float32), conv)
            c = circulant(taps[g : g + 1])
            table = jnp.concatenate([c, c], axis=1) * back_mask_ref[...]
            grad_kv = jnp.where(group == g, jnp.dot(table, cot, preferred_element_type=jnp.float32), grad_kv)
        mixed_ref[:, lanes] = (q.astype(jnp.float32) * conv).astype(jnp.bfloat16)
        grad_q_ref[:, lanes] = (dy.astype(jnp.float32) * conv).astype(jnp.bfloat16)
        grad_k_ref[:, lanes] = (grad_kv * v.astype(jnp.float32)).astype(jnp.bfloat16)
        grad_v_ref[:, lanes] = (grad_kv * k.astype(jnp.float32)).astype(jnp.bfloat16)
        return carry

    lax.fori_loop(0, q_ref.shape[1] // LANES, tile, 0)


def filter_share(q, k, v, dy, kv_prev, starts, groups):
    rows, width = q.shape
    block = math.gcd(width, BLOCK)
    wide = pl.BlockSpec((rows, block), lambda i: (0, i))
    return pl.pallas_call(
        filter_kernel,
        grid=(width // block,),
        out_shape=jax.ShapeDtypeStruct((groups, rows), jnp.float32),
        in_specs=[wide] * 5 + [pl.BlockSpec((1, rows), lambda i: (0, 0))],
        out_specs=pl.BlockSpec((block // GSIZE, rows), lambda i: (i, 0)),
        scratch_shapes=[
            pltpu.VMEM((rows, rows), jnp.float32),
            pltpu.VMEM((rows, rows), jnp.float32),
            pltpu.VMEM((block // GSIZE * 8, rows), jnp.float32),
        ],
        cost_estimate=pl.CostEstimate(
            flops=2 * rows * 2 * rows * width, bytes_accessed=10 * rows * width, transcendentals=0
        ),
        compiler_params=pltpu.CompilerParams(vmem_limit_bytes=24 << 20),
        name="filter_share",
    )(q, k, v, dy, kv_prev, starts)


def convolutions(q, k, v, dy, kv_prev, cot_next, starts, filters):
    rows, width = q.shape
    block = math.gcd(width, BLOCK)
    wide = pl.BlockSpec((rows, block), lambda i: (0, i))
    few = pl.BlockSpec((block // GSIZE, rows), lambda i: (i, 0))
    return pl.pallas_call(
        conv_kernel,
        grid=(width // block,),
        out_shape=[jax.ShapeDtypeStruct((rows, width), jnp.bfloat16)] * 4,
        in_specs=[wide] * 6 + [pl.BlockSpec((1, rows), lambda i: (0, 0)), few],
        out_specs=[wide] * 4,
        scratch_shapes=[
            pltpu.VMEM((rows, 2 * rows), jnp.bfloat16),
            pltpu.VMEM((rows, 2 * rows), jnp.bfloat16),
            pltpu.VMEM((block // GSIZE, rows), jnp.float32),
            pltpu.VMEM((block // GSIZE, rows), jnp.float32),
        ],
        cost_estimate=pl.CostEstimate(
            flops=4 * rows * 2 * rows * width, bytes_accessed=20 * rows * width, transcendentals=0
        ),
        compiler_params=pltpu.CompilerParams(vmem_limit_bytes=24 << 20),
        name="convolutions",
    )(q, k, v, dy, kv_prev, cot_next, starts, filters)


def passed_along(block, axis, distance):
    devices = range(lax.axis_size(axis))
    route = [(i - distance, i) for i in devices if i - distance in devices]
    return lax.ppermute(block, axis, route)


def summed_everywhere(share):
    axes = ("dp", "ctx")
    count = lax.axis_size("dp") * lax.axis_size("ctx")
    if share.shape[0] % count:
        return lax.psum(share, axes)
    part = share.shape[0] // count
    pieces = lax.all_to_all(share.reshape(count, part, -1), axes, 0, 0, tiled=True)
    mine = jnp.sum(pieces, axis=0)
    spread = jnp.broadcast_to(mine[None], pieces.shape)
    return lax.all_to_all(spread, axes, 0, 0, tiled=True).reshape(share.shape)


def per_device(q_proj, k_proj, v_proj, out_grad, contig_starts, filters):
    q, k, v, dy = q_proj[0], k_proj[0], v_proj[0], out_grad[0]
    rows = q.shape[0]
    groups, taps = filters.shape
    assert rows == taps == LANES
    token = lax.broadcasted_iota(jnp.int32, (rows,), 0)
    last = jnp.max(jnp.where(contig_starts[0] > 0, token, 0))
    first = jnp.min(jnp.where(contig_starts[0] > 0, token, rows))
    kv_out = jnp.where((token >= last)[:, None], product(k, v), 0)
    cot_out = jnp.where((token < first)[:, None], product(dy, q), 0)
    kv_prev = passed_along(kv_out, "ctx", 1)
    cot_next = passed_along(cot_out, "ctx", -1)
    share = filter_share(q, k, v, dy, kv_prev, contig_starts, groups)
    scale = 1.0 / math.sqrt(rows * lax.axis_size("ctx") * lax.axis_size("dp") * GSIZE)
    filter_grad = summed_everywhere(share) * scale
    outs = convolutions(q, k, v, dy, kv_prev, cot_next, contig_starts, filters)
    return tuple(out[None] for out in outs) + (filter_grad,)


def solution(mesh):
    wide = P("dp", "ctx", None)
    return jax.shard_map(
        per_device,
        mesh=mesh,
        in_specs=(wide,) * 4 + (P("dp", "ctx"), P()),
        out_specs=(wide,) * 4 + (P(),),
        check_vma=False,
    )
```

time: 252 us -> 52.6 us (0.21)
  local copies, waits for them, and re-layouts: 138 us -> 1.3 us
  waiting for transfers between devices: 24.3 us -> 0.01 us
  Pallas kernels: 0 us -> 17.6 us
  blocking collectives: 36 us -> 20.6 us
  between operations: 14.2 us -> 0.77 us
  matrix products: 13.3 us -> 0 us
  other arithmetic: 16.6 us -> 5.68 us
    reshape x49 -> x0, local copies, waits for them, and re-layouts: 55.6 us -> none  [the longest x16 21.8 us: group_block(): fwd_masked = fwd_table[None] * fwd_mask[:, None]]
    dynamic_slice x80 -> x0, local copies, waits for them, and re-layouts: 40.6 us -> none  [the longest x32 16 us: group_block(): lax.dynamic_slice_in_dim(kv_win, start, chans, 2)]
    dynamic_update_slice x96 -> x0, local copies, waits for them, and re-layouts: 26.1 us -> none  [the longest x32 12.1 us: group_block(): lax.dynamic_update_slice_in_dim(grad_kv, local.reshape(rows, chans), star...]
    reduce_scatter x1 -> x0, waiting for transfers between devices: 24.3 us -> none  [per_device(): lax.psum_scatter(filter_local, 'dp', scatter_dimension=0, tiled=True)]
    psum x1 -> x0, blocking collectives: 22.9 us -> none  [per_device(): share = lax.psum(share, 'ctx')]
    all_to_all x0 -> x1, blocking collectives: none -> 20.6 us  [summed_everywhere(): lax.all_to_all(share.reshape(count, part, -1), axes, 0, 0, tiled=True)]
    pallas_call x0 -> x2, Pallas kernels: none -> 17.6 us  [the longest x1 10.1 us: convolutions(): pl.pallas_call(conv_kernel, grid=(width // block,), out_shape=[jax.ShapeD...]
    dot_general x48 -> x0, matrix products: 13.3 us -> none  [the longest x16 5.49 us: group_block(): jnp.einsum('btgc,bsgc->bgts', cot_block, kv_block, preferred_element_type...]
  transfers between devices with their start and end apart: 3 -> 3, of which waited for: 1 -> 0; matrix products, arithmetic and copies ran while one was open for 5% -> 4% of each run, Pallas kernels for 0% -> 34%
where the time goes in v1:
time: 52.6 us; the launch traced here: 52.3 us
  blocking collectives  20.6 us (39%)
  Pallas kernels  17.6 us (33%)
  starting transfers between devices  6.37 us (12%)
  other arithmetic  5.68 us (11%)
  local copies, waits for them, and re-layouts  1.3 us (2%)
  between operations  0.77 us (1%)
    all_to_all x1, blocking collectives, summed_everywhere(): lax.all_to_all(share.reshape(count, part, -1), axes, 0, 0, tiled=True)  20.6 us
    pallas_call x1, Pallas kernels, convolutions(): pl.pallas_call(conv_kernel, grid=(width // block,), out_shape=[jax.ShapeD...  10.1 us
    pallas_call x1, Pallas kernels, filter_share(): pl.pallas_call(filter_kernel, grid=(width // block,), out_shape=jax.Shape...  7.46 us
    ppermute x2, starting transfers between devices, passed_along(): return lax.ppermute(block, axis, route)  3.67 us
    all_to_all x1, starting transfers between devices, summed_everywhere(): return lax.all_to_all(spread, axes, 0, 0, tiled=True).reshape(share.shape)  2.7 us
    select_n x1, other arithmetic, per_device(): kv_out = jnp.where((token >= last)[:, None], product(k, v), 0)  1.44 us
    reduce_min x1, other arithmetic, per_device(): first = jnp.min(jnp.where(contig_starts[0] > 0, token, rows))  1.3 us
  transfers between devices with their start and end apart: 3, of which 0 were waited for; matrix products, arithmetic and copies ran while one was open for 4% of the time, Pallas kernels for 34%

profile of v1, /device:TPU:0, one launch (start us, length us, event | category | flops | bytes accessed | tf_op | source)
XLA Modules:
  0.0 52.3 jit_solution(1267906486344616694)
XLA Ops:
  0.6 1.3 %fusion.3 = (s32[]{:T(128)}, s32[]{:T(128)}) fusion(s32[1,128]{1,0:T(1,128)} %starts_ref.3), kind=kLoop, calls=%fused_computation.8 | loop fusion | flops 638 | bytes 520 | tf_op jit(solution)/shard_map/reduce_min | solution.py:210
  1.9 0.6 %iota_compare_fusion.1 = pred[128]{0:T(512)(128)(4,1)S(1)} fusion(s32[]{:T(128)} %get-tuple-element.14), kind=kLoop, calls=%fused_computation.10 | loop fusion | flops 128 | bytes 132 | tf_op jit(solution)/shard_map/ge | solution.py:211
  2.6 0.0 copy-start
  2.6 0.0 copy-start.3
  2.6 1.4 %fusion = bf16[128,2048]{1,0:T(8,128)(2,1)S(1)} fusion(pred[128]{0:T(512)(128)(4,1)S(1)} %iota_compare_fusion.1, bf16[1,128,2048]{2,1,0:T(8,128)(2,1)} %param.8, bf16[1,128,2048]{2,1,0:T(8,128)(2,1)} %param.7), kind=kLoop, calls=%fused_computation.2 | loop fusion | flops 1310720 | bytes 1572992 | tf_op jit(solution)/shard_map/jit(_where)/select_n | solution.py:211
  4.1 2.4 %collective-permute-start = (bf16[128,2048]{1,0:T(8,128)(2,1)S(1)}, bf16[128,2048]{1,0:T(8,128)(2,1)S(1)}, u32[]{:S(2)}, u32[]{:S(2)}) collective-permute-start(bf16[128,2048]{1,0:T(8,128)(2,1)S(1)} %fusion), channel_id=1, source_target_pairs={{0,4},{4,8},{8,12},{12,16},{16,20},{20,24},{24,28},{1,5},{5,9},{9,... | collective-permute-start | bytes 1572872 | tf_op jit(solution)/shard_map/ppermute | solution.py:188
  6.5 0.7 %iota_compare_fusion = pred[128]{0:T(512)(128)(4,1)S(1)} fusion(s32[]{:T(128)} %get-tuple-element.13), kind=kLoop, calls=%fused_computation.9 | loop fusion | flops 128 | bytes 132 | tf_op jit(solution)/shard_map/lt | solution.py:212
  7.1 0.0 copy-done
  7.1 0.0 copy-done.3
  7.1 0.0 copy-start.1
  7.1 0.0 copy-start.2
  7.2 1.0 %fusion.1 = bf16[128,2048]{1,0:T(8,128)(2,1)} fusion(pred[128]{0:T(512)(128)(4,1)S(1)} %iota_compare_fusion, bf16[1,128,2048]{2,1,0:T(8,128)(2,1)S(1)} %copy-done.3, bf16[1,128,2048]{2,1,0:T(8,128)(2,1)S(1)} %copy-done), kind=kLoop, calls=%fused_computation.3 | loop fusion | flops 1310720 | bytes 1572992 | tf_op jit(solution)/shard_map/jit(_where)/select_n | solution.py:212
  8.1 1.3 %collective-permute-start.1 = (bf16[128,2048]{1,0:T(8,128)(2,1)}, bf16[128,2048]{1,0:T(8,128)(2,1)S(1)}, u32[]{:S(2)}, u32[]{:S(2)}) collective-permute-start(bf16[128,2048]{1,0:T(8,128)(2,1)} %fusion.1), channel_id=1, source_target_pairs={{4,0},{8,4},{12,8},{16,12},{20,16},{24,20},{28,24},{5,1},{9,5},{13... | collective-permute-start | bytes 1572872 | tf_op jit(solution)/shard_map/ppermute | solution.py:188
  9.4 0.0 collective-permute-done.kv_prev_ref
  9.4 0.0 copy-start.5
  9.4 0.0 copy-done.1
  9.4 0.0 copy-done.2
  9.4 0.6 %copy-done.5 = s32[1,128]{1,0:T(1,128)S(1)} copy-done((s32[1,128]{1,0:T(1,128)S(1)}, s32[1,128]{1,0:T(1,128)}, u32[]{:S(2)}) %copy-start.5) | copy-done | bytes 536
  10.1 7.5 %filter_share.1 = f32[128,128]{1,0:T(8,128)S(1)} custom-call(bf16[128,2048]{1,0:T(8,128)(2,1)S(1)} %bitcast.21, bf16[128,2048]{1,0:T(8,128)(2,1)S(1)} %bitcast.23, bf16[128,2048]{1,0:T(8,128)(2,1)S(1)} %bitcast.25, bf16[128,2048]{1,0:T(8,128)(2,1)S(1)} %bitcast.27, bf16[128,2048]{1,0:T(8,128)(2,1)S(1)} %collective-permute-done.kv_prev_ref, ...), custom_call_target="tpu_custom_call" | custom-call | flops 134217728 | bytes 2621440 | tf_op jit(solution)/shard_map/filter_share/pallas_call | solution.py:141
  17.5 20.6 %all_to_all.10 = f32[32,4,128]{2,1,0:T(4,128)S(1)} all-to-all(f32[32,4,128]{2,1,0:T(4,128)S(1)} %bitcast.29), channel_id=1, replica_groups=mesh['ctx'=8,'dp'=4] {'dp','ctx'}, dimensions={0} | all-to-all | bytes 131072 | tf_op jit(solution)/shard_map/all_to_all | solution.py:197
  38.2 0.6 %broadcast_in_dim.51 = f32[32,4,128]{2,1,0:T(4,128)} broadcast(f32[4,128]{1,0:T(4,128)S(1)} %reduce_sum.9), dimensions={1,2} | broadcast | bytes 67584 | tf_op jit(solution)/shard_map/broadcast_in_dim | solution.py:199
  38.8 0.0 copy-start.4
  38.8 2.7 %all-to-all-start.1 = ((f32[32,4,128]{2,1,0:T(4,128)}), f32[32,4,128]{2,1,0:T(4,128)S(1)}, u32[]{:S(2)}, u32[]{:S(2)}) async-start(f32[32,4,128]{2,1,0:T(4,128)} %broadcast_in_dim.51), calls=%async_computation.1 | async-start | bytes 131072 | tf_op jit(solution)/shard_map/all_to_all | solution.py:200
  41.5 0.0 collective-permute-done.1.cot_next_ref
  41.5 0.0 copy-done.4
  41.5 10.1 %convolutions.1 = (bf16[128,2048]{1,0:T(8,128)(2,1)}, bf16[128,2048]{1,0:T(8,128)(2,1)}, bf16[128,2048]{1,0:T(8,128)(2,1)}, bf16[128,2048]{1,0:T(8,128)(2,1)}) custom-call(bf16[128,2048]{1,0:T(8,128)(2,1)S(1)} %bitcast.22, bf16[128,2048]{1,0:T(8,128)(2,1)S(1)} %bitcast.24, bf16[128,2048]{1,0:T(8,128)(2,1)S(1)} %bitcast.26, bf16[128,2048]{1,0:T(8,128)(2,1)S(1)} %bitcast.28, ...), custom_call_target="tpu_custom_call" | custom-call | flops 268435456 | bytes 5242880 | tf_op jit(solution)/shard_map/convolutions/pallas_call | solution.py:165
  51.6 0.0 all-to-all-done.1
  51.6 0.6 %broadcast_multiply_fusion = f32[32,4,128]{2,1,0:T(4,128)} fusion(f32[32,4,128]{2,1,0:T(4,128)S(1)} %all-to-all-done.1), kind=kLoop, calls=%fused_computation.4 | loop fusion | flops 16384 | bytes 131072 | tf_op jit(solution)/shard_map/mul | solution.py:217
  (1 shorter events, 0.0 us)
Async XLA Ops:
  2.6 4.5 %copy-start = (bf16[1,128,2048]{2,1,0:T(8,128)(2,1)S(1)}, bf16[1,128,2048]{2,1,0:T(8,128)(2,1)}, u32[]{:S(2)}) copy-start(bf16[1,128,2048]{2,1,0:T(8,128)(2,1)} %param.6) | copy-start | bytes 1572868
  2.6 4.5 %copy-start.3 = (bf16[1,128,2048]{2,1,0:T(8,128)(2,1)S(1)}, bf16[1,128,2048]{2,1,0:T(8,128)(2,1)}, u32[]{:S(2)}) copy-start(bf16[1,128,2048]{2,1,0:T(8,128)(2,1)} %param.9) | copy-start | bytes 1572868
  4.1 5.3 %collective-permute-start = (bf16[128,2048]{1,0:T(8,128)(2,1)S(1)}, bf16[128,2048]{1,0:T(8,128)(2,1)S(1)}, u32[]{:S(2)}, u32[]{:S(2)}) collective-permute-start(bf16[128,2048]{1,0:T(8,128)(2,1)S(1)} %fusion), channel_id=1, source_target_pairs={{0,4},{4,8},{8,12},{12,16},{16,20},{20,24},{24,28},{1,5},{5,9},{9,... | collective-permute-start | bytes 1572872 | tf_op jit(solution)/shard_map/ppermute | solution.py:188
  7.1 2.3 %copy-start.1 = (bf16[1,128,2048]{2,1,0:T(8,128)(2,1)S(1)}, bf16[1,128,2048]{2,1,0:T(8,128)(2,1)}, u32[]{:S(2)}) copy-start(bf16[1,128,2048]{2,1,0:T(8,128)(2,1)} %param.7) | copy-start | bytes 1572868
  7.1 2.3 %copy-start.2 = (bf16[1,128,2048]{2,1,0:T(8,128)(2,1)S(1)}, bf16[1,128,2048]{2,1,0:T(8,128)(2,1)}, u32[]{:S(2)}) copy-start(bf16[1,128,2048]{2,1,0:T(8,128)(2,1)} %param.8) | copy-start | bytes 1572868
  8.1 33.4 %collective-permute-start.1 = (bf16[128,2048]{1,0:T(8,128)(2,1)}, bf16[128,2048]{1,0:T(8,128)(2,1)S(1)}, u32[]{:S(2)}, u32[]{:S(2)}) collective-permute-start(bf16[128,2048]{1,0:T(8,128)(2,1)} %fusion.1), channel_id=1, source_target_pairs={{4,0},{8,4},{12,8},{16,12},{20,16},{24,20},{28,24},{5,1},{9,5},{13... | collective-permute-start | bytes 1572872 | tf_op jit(solution)/shard_map/ppermute | solution.py:188
  9.4 0.7 %copy-start.5 = (s32[1,128]{1,0:T(1,128)S(1)}, s32[1,128]{1,0:T(1,128)}, u32[]{:S(2)}) copy-start(s32[1,128]{1,0:T(1,128)} %starts_ref.3) | copy-start | bytes 1540
  38.8 2.7 %copy-start.4 = (bf16[128,128]{1,0:T(8,128)(2,1)S(1)}, bf16[128,128]{1,0:T(8,128)(2,1)}, u32[]{:S(2)}) copy-start(bf16[128,128]{1,0:T(8,128)(2,1)} %taps_ref.1) | copy-start | bytes 98308
  38.8 12.8 %all-to-all-start.1 = ((f32[32,4,128]{2,1,0:T(4,128)}), f32[32,4,128]{2,1,0:T(4,128)S(1)}, u32[]{:S(2)}, u32[]{:S(2)}) async-start(f32[32,4,128]{2,1,0:T(4,128)} %broadcast_in_dim.51), calls=%async_computation.1 | async-start | bytes 131072 | tf_op jit(solution)/shard_map/all_to_all | solution.py:200

commit v2 on v1

v2 whole, which is shorter than its diff:
```python
import functools
import math

import jax
import jax.numpy as jnp
from jax import lax
from jax.experimental import pallas as pl
from jax.experimental.pallas import tpu as pltpu
from jax.sharding import PartitionSpec as P

GSIZE = 16
LANES = 128
BLOCK = 512


def product(a, b):
    return (a.astype(jnp.float32) * b.astype(jnp.float32)).astype(jnp.bfloat16)


def contig_masks(starts_ref):
    rows = starts_ref.shape[1]
    starts = jnp.broadcast_to(starts_ref[...], (rows, rows)) > 0
    t = lax.broadcasted_iota(jnp.int32, (rows, rows), 0)
    s = lax.broadcasted_iota(jnp.int32, (rows, rows), 1)
    began = jnp.max(jnp.where(starts & (s <= t), s, 0), axis=1, keepdims=True)
    own = (s <= t) & (s >= began)
    first = jnp.min(jnp.where(starts, s, rows), axis=1, keepdims=True)
    previous = (s > t) & (t < first)
    last = jnp.max(jnp.where(starts, s, 0), axis=1, keepdims=True)
    following = (s < t) & (t >= last)
    as_f32 = lambda mask: jnp.where(mask, 1.0, 0.0).astype(jnp.float32)
    return as_f32(own), as_f32(previous), as_f32(following)


def reversed_taps(rows_of_taps):
    taps = rows_of_taps.shape[1]
    i = lax.broadcasted_iota(jnp.int32, (taps, taps), 0)
    j = lax.broadcasted_iota(jnp.int32, (taps, taps), 1)
    flip = jnp.where((i + j == 0) | (i + j == taps), 1.0, 0.0).astype(jnp.float32)
    return jnp.dot(
        rows_of_taps.astype(jnp.float32), flip,
        preferred_element_type=jnp.float32, precision=lax.Precision.HIGHEST,
    )


def lane_groups():
    return lax.broadcasted_iota(jnp.int32, (1, LANES), 1) // GSIZE


def send_kernel(a_ref, b_ref, starts_ref, out_ref, *, tail):
    rows = a_ref.shape[0]
    starts = starts_ref[...] > 0
    lane = lax.broadcasted_iota(jnp.int32, starts.shape, 1)
    token = lax.broadcasted_iota(jnp.int32, (rows, 1), 0)
    if tail:
        keep = token >= jnp.max(jnp.where(starts, lane, 0), axis=1, keepdims=True)
    else:
        keep = token < jnp.min(jnp.where(starts, lane, rows), axis=1, keepdims=True)
    out = a_ref[...].astype(jnp.float32) * b_ref[...].astype(jnp.float32)
    out_ref[...] = jnp.where(keep, out, 0.0).astype(jnp.bfloat16)


def filter_kernel(
    q_ref, k_ref, v_ref, dy_ref, kv_prev_ref, starts_ref, out_ref, own_ref, prev_ref, sums_ref, *, scale
):
    rows = q_ref.shape[0]
    per_tile = LANES // GSIZE

    @pl.when(pl.program_id(0) == 0)
    def _():
        own, previous, _ = contig_masks(starts_ref)
        own_ref[...] = own
        prev_ref[...] = previous

    group = lane_groups()

    def tile(index, carry):
        lanes = pl.ds(pl.multiple_of(index * LANES, LANES), LANES)
        cot = product(dy_ref[:, lanes], q_ref[:, lanes])
        kv = jnp.concatenate([product(k_ref[:, lanes], v_ref[:, lanes]), kv_prev_ref[:, lanes]], axis=0)
        picked = jnp.concatenate(
            [jnp.where(group == g, cot, jnp.zeros_like(cot)) for g in range(per_tile)], axis=0
        )
        pairs = lax.dot_general(
            picked, kv, (((1,), (1,)), ((), ())), preferred_element_type=jnp.float32
        )
        for g in range(per_tile):
            total = None
            for i in range(rows // 8):
                at = g * rows + 8 * i
                piece = (
                    pairs[at : at + 8, :rows] * own_ref[8 * i : 8 * i + 8, :]
                    + pairs[at : at + 8, rows:] * prev_ref[8 * i : 8 * i + 8, :]
                )
                total = piece if i == 0 else total + pltpu.roll(piece, rows - 8 * i, 1)
            at = pl.multiple_of((index * per_tile + g) * 8, 8)
            sums_ref[pl.ds(at, 8), :] = total
        return carry

    lax.fori_loop(0, q_ref.shape[1] // LANES, tile, 0)
    groups = out_ref.shape[0]
    diagonal = sums_ref[pl.ds(0, groups, stride=8), :]
    for r in range(1, 8):
        diagonal = diagonal + pltpu.roll(sums_ref[pl.ds(r, groups, stride=8), :], rows - r, 1)
    out_ref[...] = reversed_taps(diagonal) * scale


def conv_kernel(a_ref, b_ref, other_ref, c_ref, d_ref, starts_ref, taps_ref, out_c_ref, out_d_ref, mask_ref, taps_scr, *, backward):
    rows = a_ref.shape[0]
    per_tile = LANES // GSIZE

    @pl.when(pl.program_id(0) == 0)
    def _():
        own, previous, following = contig_masks(starts_ref)
        mask_ref[:, :rows] = (own.T if backward else own).astype(jnp.bfloat16)
        mask_ref[:, rows:] = (following if backward else previous).astype(jnp.bfloat16)

    taps_scr[...] = taps_ref[...].astype(jnp.float32) if backward else reversed_taps(taps_ref[...])
    group = lane_groups()

    def table(row):
        wide = pltpu.roll(jnp.broadcast_to(row, (rows, rows)), 0, 1, stride=1, stride_axis=0)
        wide = wide.astype(jnp.bfloat16)
        return jnp.concatenate([wide, wide], axis=1) * mask_ref[...]

    def tile(index, carry):
        lanes = pl.ds(pl.multiple_of(index * LANES, LANES), LANES)
        x = jnp.concatenate([product(a_ref[:, lanes], b_ref[:, lanes]), other_ref[:, lanes]], axis=0)
        taps = taps_scr[pl.ds(pl.multiple_of(index * per_tile, per_tile), per_tile), :]
        tables = jnp.concatenate([table(taps[g : g + 1]) for g in range(per_tile)], axis=0)
        every = jnp.dot(tables, x, preferred_element_type=jnp.float32)
        y = every[:rows]
        for g in range(1, per_tile):
            y = jnp.where(group == g, every[g * rows : (g + 1) * rows], y)
        out_c_ref[:, lanes] = (c_ref[:, lanes].astype(jnp.float32) * y).astype(jnp.bfloat16)
        out_d_ref[:, lanes] = (d_ref[:, lanes].astype(jnp.float32) * y).astype(jnp.bfloat16)
        return carry

    lax.fori_loop(0, a_ref.shape[1] // LANES, tile, 0)


def masked_product(a, b, starts, tail):
    rows, width = a.shape
    block = math.gcd(width, BLOCK)
    wide = pl.BlockSpec((rows, block), lambda i: (0, i))
    return pl.pallas_call(
        functools.partial(send_kernel, tail=tail),
        grid=(width // block,),
        out_shape=jax.ShapeDtypeStruct((rows, width), jnp.bfloat16),
        in_specs=[wide] * 2 + [pl.BlockSpec((1, rows), lambda i: (0, 0))],
        out_specs=wide,
        cost_estimate=pl.CostEstimate(flops=2 * rows * width, bytes_accessed=6 * rows * width, transcendentals=0),
        name="sent_kv" if tail else "sent_cot",
    )(a, b, starts)


def filter_share(q, k, v, dy, kv_prev, starts, groups, scale):
    rows, width = q.shape
    block = math.gcd(width, BLOCK)
    wide = pl.BlockSpec((rows, block), lambda i: (0, i))
    return pl.pallas_call(
        functools.partial(filter_kernel, scale=scale),
        grid=(width // block,),
        out_shape=jax.ShapeDtypeStruct((groups, rows), jnp.float32),
        in_specs=[wide] * 5 + [pl.BlockSpec((1, rows), lambda i: (0, 0))],
        out_specs=pl.BlockSpec((block // GSIZE, rows), lambda i: (i, 0)),
        scratch_shapes=[
            pltpu.VMEM((rows, rows), jnp.float32),
            pltpu.VMEM((rows, rows), jnp.float32),
            pltpu.VMEM((block // GSIZE * 8, rows), jnp.float32),
        ],
        cost_estimate=pl.CostEstimate(
            flops=2 * rows * 2 * rows * width, bytes_accessed=10 * rows * width, transcendentals=0
        ),
        compiler_params=pltpu.CompilerParams(vmem_limit_bytes=24 << 20),
        name="filter_share",
    )(q, k, v, dy, kv_prev, starts)


def convolution(a, b, other, c, d, starts, filters, backward):
    rows, width = a.shape
    block = math.gcd(width, BLOCK)
    wide = pl.BlockSpec((rows, block), lambda i: (0, i))
    few = pl.BlockSpec((block // GSIZE, rows), lambda i: (i, 0))
    return pl.pallas_call(
        functools.partial(conv_kernel, backward=backward),
        grid=(width // block,),
        out_shape=[jax.ShapeDtypeStruct((rows, width), jnp.bfloat16)] * 2,
        in_specs=[wide] * 5 + [pl.BlockSpec((1, rows), lambda i: (0, 0)), few],
        out_specs=[wide] * 2,
        scratch_shapes=[
            pltpu.VMEM((rows, 2 * rows), jnp.bfloat16),
            pltpu.VMEM((block // GSIZE, rows), jnp.float32),
        ],
        cost_estimate=pl.CostEstimate(
            flops=2 * rows * 2 * rows * width, bytes_accessed=14 * rows * width, transcendentals=0
        ),
        compiler_params=pltpu.CompilerParams(vmem_limit_bytes=24 << 20),
        name="backward" if backward else "forward",
    )(a, b, other, c, d, starts, filters)


def passed_along(block, axis, distance):
    devices = range(lax.axis_size(axis))
    route = [(i - distance, i) for i in devices if i - distance in devices]
    return lax.ppermute(block, axis, route)


def summed_everywhere(share):
    axes = ("dp", "ctx")
    count = lax.axis_size("dp") * lax.axis_size("ctx")
    if share.shape[0] % count:
        return lax.psum(share, axes)
    part = share.shape[0] // count
    pieces = lax.all_to_all(share.reshape(count, part, -1), axes, 0, 0, tiled=True)
    mine = jnp.sum(pieces, axis=0)
    spread = jnp.broadcast_to(mine[None], pieces.shape)
    return lax.all_to_all(spread, axes, 0, 0, tiled=True).reshape(share.shape)


def per_device(q_proj, k_proj, v_proj, out_grad, contig_starts, filters):
    q, k, v, dy = q_proj[0], k_proj[0], v_proj[0], out_grad[0]
    rows = q.shape[0]
    groups, taps = filters.shape
    assert rows == taps == LANES
    scale = 1.0 / math.sqrt(rows * lax.axis_size("ctx") * lax.axis_size("dp") * GSIZE)
    kv_prev = passed_along(masked_product(k, v, contig_starts, True), "ctx", 1)
    cot_next = passed_along(masked_product(dy, q, contig_starts, False), "ctx", -1)
    share = filter_share(q, k, v, dy, kv_prev, contig_starts, groups, scale)
    filter_grad = summed_everywhere(share)
    mixed, grad_q = convolution(k, v, kv_prev, q, dy, contig_starts, filters, False)
    grad_k, grad_v = convolution(dy, q, cot_next, v, k, contig_starts, filters, True)
    return (mixed[None], grad_q[None], grad_k[None], grad_v[None], filter_grad)


def solution(mesh):
    wide = P("dp", "ctx", None)
    return jax.shard_map(
        per_device,
        mesh=mesh,
        in_specs=(wide,) * 4 + (P("dp", "ctx"), P()),
        out_specs=(wide,) * 4 + (P(),),
        check_vma=False,
    )
```

time: 52.6 us -> 56.4 us (1.072)
  Pallas kernels: 17.6 us -> 29.8 us
  other arithmetic: 5.68 us -> 0.04 us
  blocking collectives: 20.6 us -> 17.7 us
    pallas_call x2 -> x5, Pallas kernels: 17.6 us -> 29.8 us  [the longest x2 14.9 us: convolution(): pl.pallas_call(functools.partial(conv_kernel, backward=backward), grid=(w...]
    all_to_all x1, blocking collectives: 20.6 us -> 17.7 us  [summed_everywhere(): lax.all_to_all(share.reshape(count, part, -1), axes, 0, 0, tiled=True)]
    select_n x2 -> x0, other arithmetic: 2.4 us -> none  [the longest x1 1.44 us: per_device(): kv_out = jnp.where((token >= last)[:, None], product(k, v), 0)]
    reduce_min x1 -> x0, other arithmetic: 1.3 us -> none  [per_device(): first = jnp.min(jnp.where(contig_starts[0] > 0, token, rows))]
    lt x1 -> x0, other arithmetic: 0.65 us -> none  [per_device(): cot_out = jnp.where((token < first)[:, None], product(dy, q), 0)]
    ge x1 -> x0, other arithmetic: 0.65 us -> none  [per_device(): kv_out = jnp.where((token >= last)[:, None], product(k, v), 0)]
    mul x1 -> x0, other arithmetic: 0.64 us -> none  [per_device(): filter_grad = summed_everywhere(share) * scale]
  transfers between devices with their start and end apart: 3 -> 3, of which waited for: 0 -> 0; matrix products, arithmetic and copies ran while one was open for 4% -> 1% of each run, Pallas kernels for 34% -> 47%
where the time goes in v2:
time: 56.4 us; the launch traced here: 56 us
  Pallas kernels  29.8 us (53%)
  blocking collectives  17.7 us (31%)
  starting transfers between devices  6.36 us (11%)
  local copies, waits for them, and re-layouts  1.31 us (2%)
  between operations  0.75 us (1%)
    all_to_all x1, blocking collectives, summed_everywhere(): lax.all_to_all(share.reshape(count, part, -1), axes, 0, 0, tiled=True)  17.7 us
    pallas_call x2, Pallas kernels, convolution(): pl.pallas_call(functools.partial(conv_kernel, backward=backward), grid=(w...  14.9 us
    pallas_call x2, Pallas kernels, masked_product(): pl.pallas_call(functools.partial(send_kernel, tail=tail), grid=(width //...  7.5 us
    pallas_call x1, Pallas kernels, filter_share(): pl.pallas_call(functools.partial(filter_kernel, scale=scale), grid=(width...  7.43 us
    ppermute x2, starting transfers between devices, passed_along(): return lax.ppermute(block, axis, route)  3.66 us
    all_to_all x1, starting transfers between devices, summed_everywhere(): return lax.all_to_all(spread, axes, 0, 0, tiled=True).reshape(share.shape)  2.7 us
  transfers between devices with their start and end apart: 3, of which 0 were waited for; matrix products, arithmetic and copies ran while one was open for 1% of the time, Pallas kernels for 47%

profile of v2, /device:TPU:0, one launch (start us, length us, event | category | flops | bytes accessed | tf_op | source)
XLA Modules:
  0.0 56.0 jit_solution(2005578231268444109)
XLA Ops:
  0.6 0.0 copy-start.3
  0.6 3.7 %sent_kv.1 = bf16[128,2048]{1,0:T(8,128)(2,1)} custom-call(bf16[128,2048]{1,0:T(8,128)(2,1)} %bitcast.10, bf16[128,2048]{1,0:T(8,128)(2,1)} %bitcast.14, s32[1,128]{1,0:T(1,128)} %starts_ref.9), custom_call_target="tpu_custom_call" | custom-call | flops 524288 | bytes 1572864 | tf_op jit(solution)/shard_map/sent_kv/pallas_call | solution.py:146
  4.4 2.4 %collective-permute-start = (bf16[128,2048]{1,0:T(8,128)(2,1)}, bf16[128,2048]{1,0:T(8,128)(2,1)S(1)}, u32[]{:S(2)}, u32[]{:S(2)}) collective-permute-start(bf16[128,2048]{1,0:T(8,128)(2,1)} %sent_kv.1), channel_id=1, source_target_pairs={{0,4},{4,8},{8,12},{12,16},{16,20},{20,24},{24,28},{1,5},{5,9},{9,... | collective-permute-start | bytes 1572872 | tf_op jit(solution)/shard_map/ppermute | solution.py:206
  6.8 0.0 copy-start
  6.8 0.0 copy-start.1
  6.8 0.0 copy-start.2
  6.8 0.0 copy-start.5
  6.8 3.8 %sent_cot.1 = bf16[128,2048]{1,0:T(8,128)(2,1)} custom-call(bf16[128,2048]{1,0:T(8,128)(2,1)} %bitcast.22, bf16[128,2048]{1,0:T(8,128)(2,1)} %bitcast.18, s32[1,128]{1,0:T(1,128)} %starts_ref.9), custom_call_target="tpu_custom_call" | custom-call | flops 524288 | bytes 1572864 | tf_op jit(solution)/shard_map/sent_cot/pallas_call | solution.py:146
  10.6 1.3 %collective-permute-start.1 = (bf16[128,2048]{1,0:T(8,128)(2,1)}, bf16[128,2048]{1,0:T(8,128)(2,1)S(1)}, u32[]{:S(2)}, u32[]{:S(2)}) collective-permute-start(bf16[128,2048]{1,0:T(8,128)(2,1)} %sent_cot.1), channel_id=1, source_target_pairs={{4,0},{8,4},{12,8},{16,12},{20,16},{24,20},{28,24},{5,1},{9,5},{13... | collective-permute-start | bytes 1572872 | tf_op jit(solution)/shard_map/ppermute | solution.py:206
  11.9 0.0 collective-permute-done.other_ref.kv_prev_ref
  11.9 0.0 copy-done.3
  11.9 0.0 copy-done
  11.9 0.0 copy-done.1
  11.9 0.0 copy-done.2
  11.9 0.0 copy-done.5
  11.9 7.4 %filter_share.1 = f32[128,128]{1,0:T(8,128)S(1)} custom-call(bf16[128,2048]{1,0:T(8,128)(2,1)S(1)} %bitcast.19, bf16[128,2048]{1,0:T(8,128)(2,1)S(1)} %bitcast.11, bf16[128,2048]{1,0:T(8,128)(2,1)S(1)} %bitcast.15, bf16[128,2048]{1,0:T(8,128)(2,1)S(1)} %bitcast.23, bf16[128,2048]{1,0:T(8,128)(2,1)S(1)} %collective-permute-done.other_ref.kv_prev_ref, ...), custom_call_target="tpu_custom_call" | custom-call | flops 134217728 | bytes 2621440 | tf_op jit(solution)/shard_map/filter_share/pallas_call | solution.py:161
  19.4 17.7 %all_to_all.10 = f32[32,4,128]{2,1,0:T(4,128)S(1)} all-to-all(f32[32,4,128]{2,1,0:T(4,128)S(1)} %bitcast.26), channel_id=1, replica_groups=mesh['ctx'=8,'dp'=4] {'dp','ctx'}, dimensions={0} | all-to-all | bytes 131072 | tf_op jit(solution)/shard_map/all_to_all | solution.py:215
  37.1 0.6 %broadcast_in_dim.22 = f32[32,4,128]{2,1,0:T(4,128)} broadcast(f32[4,128]{1,0:T(4,128)S(1)} %reduce_sum.9), dimensions={1,2} | broadcast | bytes 67584 | tf_op jit(solution)/shard_map/broadcast_in_dim | solution.py:217
  37.7 0.0 copy-start.4
  37.7 2.7 %all-to-all-start.1 = ((f32[32,4,128]{2,1,0:T(4,128)}), f32[32,4,128]{2,1,0:T(4,128)S(1)}, u32[]{:S(2)}, u32[]{:S(2)}) async-start(f32[32,4,128]{2,1,0:T(4,128)} %broadcast_in_dim.22), calls=%async_computation.1 | async-start | bytes 131072 | tf_op jit(solution)/shard_map/all_to_all | solution.py:218
  40.4 0.0 copy-done.4
  40.5 7.8 %forward.1 = (bf16[128,2048]{1,0:T(8,128)(2,1)}, bf16[128,2048]{1,0:T(8,128)(2,1)}) custom-call(bf16[128,2048]{1,0:T(8,128)(2,1)S(1)} %bitcast.12, bf16[128,2048]{1,0:T(8,128)(2,1)S(1)} %bitcast.16, bf16[128,2048]{1,0:T(8,128)(2,1)S(1)} %collective-permute-done.other_ref.kv_prev_ref, bf16[128,2048]{1,0:T(8,128)(2,1)S(1)} %bitcast.20, ...), custom_call_target="tpu_custom_call" | custom-call | flops 134217728 | bytes 3670016 | tf_op jit(solution)/shard_map/forward/pallas_call | solution.py:185
  48.2 0.0 collective-permute-done.1.other_ref
  48.2 7.1 %backward.1 = (bf16[128,2048]{1,0:T(8,128)(2,1)}, bf16[128,2048]{1,0:T(8,128)(2,1)}) custom-call(bf16[128,2048]{1,0:T(8,128)(2,1)S(1)} %bitcast.25, bf16[128,2048]{1,0:T(8,128)(2,1)S(1)} %bitcast.21, bf16[128,2048]{1,0:T(8,128)(2,1)S(1)} %collective-permute-done.1.other_ref, bf16[128,2048]{1,0:T(8,128)(2,1)S(1)} %bitcast.17, bf16[128,2048]{1,0:T(8,128)(2,1)S(1)} %bitcast.13, ...), custom_call_target="tpu_custom_call" | custom-call | flops 134217728 | bytes 3670016 | tf_op jit(solution)/shard_map/backward/pallas_call | solution.py:185
  55.4 0.0 all-to-all-done.1
  55.4 0.6 %copy.12 = f32[128,128]{1,0:T(8,128)} copy(f32[128,128]{1,0:T(8,128)S(1)} %bitcast.27) | data formatting | bytes 131072
  (1 shorter events, 0.0 us)
Async XLA Ops:
  0.6 11.2 %copy-start.3 = (bf16[1,128,2048]{2,1,0:T(8,128)(2,1)S(1)}, bf16[1,128,2048]{2,1,0:T(8,128)(2,1)}, u32[]{:S(2)}) copy-start(bf16[1,128,2048]{2,1,0:T(8,128)(2,1)} %param.9) | copy-start | bytes 1572868
  4.4 7.5 %collective-permute-start = (bf16[128,2048]{1,0:T(8,128)(2,1)}, bf16[128,2048]{1,0:T(8,128)(2,1)S(1)}, u32[]{:S(2)}, u32[]{:S(2)}) collective-permute-start(bf16[128,2048]{1,0:T(8,128)(2,1)} %sent_kv.1), channel_id=1, source_target_pairs={{0,4},{4,8},{8,12},{12,16},{16,20},{20,24},{24,28},{1,5},{5,9},{9,... | collective-permute-start | bytes 1572872 | tf_op jit(solution)/shard_map/ppermute | solution.py:206
  6.8 5.1 %copy-start = (bf16[1,128,2048]{2,1,0:T(8,128)(2,1)S(1)}, bf16[1,128,2048]{2,1,0:T(8,128)(2,1)}, u32[]{:S(2)}) copy-start(bf16[1,128,2048]{2,1,0:T(8,128)(2,1)} %param.7) | copy-start | bytes 1572868
  6.8 5.1 %copy-start.1 = (bf16[1,128,2048]{2,1,0:T(8,128)(2,1)S(1)}, bf16[1,128,2048]{2,1,0:T(8,128)(2,1)}, u32[]{:S(2)}) copy-start(bf16[1,128,2048]{2,1,0:T(8,128)(2,1)} %param.8) | copy-start | bytes 1572868
  6.8 5.1 %copy-start.2 = (bf16[1,128,2048]{2,1,0:T(8,128)(2,1)S(1)}, bf16[1,128,2048]{2,1,0:T(8,128)(2,1)}, u32[]{:S(2)}) copy-start(bf16[1,128,2048]{2,1,0:T(8,128)(2,1)} %param.6) | copy-start | bytes 1572868
  6.8 5.1 %copy-start.5 = (s32[1,128]{1,0:T(1,128)S(1)}, s32[1,128]{1,0:T(1,128)}, u32[]{:S(2)}) copy-start(s32[1,128]{1,0:T(1,128)} %starts_ref.9) | copy-start | bytes 1540
  10.6 37.6 %collective-permute-start.1 = (bf16[128,2048]{1,0:T(8,128)(2,1)}, bf16[128,2048]{1,0:T(8,128)(2,1)S(1)}, u32[]{:S(2)}, u32[]{:S(2)}) collective-permute-start(bf16[128,2048]{1,0:T(8,128)(2,1)} %sent_cot.1), channel_id=1, source_target_pairs={{4,0},{8,4},{12,8},{16,12},{20,16},{24,20},{28,24},{5,1},{9,5},{13... | collective-permute-start | bytes 1572872 | tf_op jit(solution)/shard_map/ppermute | solution.py:206
  37.7 2.7 %copy-start.4 = (bf16[128,128]{1,0:T(8,128)(2,1)S(1)}, bf16[128,128]{1,0:T(8,128)(2,1)}, u32[]{:S(2)}) copy-start(bf16[128,128]{1,0:T(8,128)(2,1)} %taps_ref.3) | copy-start | bytes 98308
  37.7 17.6 %all-to-all-start.1 = ((f32[32,4,128]{2,1,0:T(4,128)}), f32[32,4,128]{2,1,0:T(4,128)S(1)}, u32[]{:S(2)}, u32[]{:S(2)}) async-start(f32[32,4,128]{2,1,0:T(4,128)} %broadcast_in_dim.22), calls=%async_computation.1 | async-start | bytes 131072 | tf_op jit(solution)/shard_map/all_to_all | solution.py:218

commit v3 on v2

--- a/solution.py
+++ b/solution.py
@@ -10,7 +10,6 @@
 
 GSIZE = 16
 LANES = 128
-BLOCK = 512
 
 
 def product(a, b):
@@ -66,11 +65,7 @@
     rows = q_ref.shape[0]
     per_tile = LANES // GSIZE
 
-    @pl.when(pl.program_id(0) == 0)
-    def _():
-        own, previous, _ = contig_masks(starts_ref)
-        own_ref[...] = own
-        prev_ref[...] = previous
+    own_ref[...], prev_ref[...], _ = contig_masks(starts_ref)
 
     group = lane_groups()
 
@@ -109,12 +104,9 @@
     rows = a_ref.shape[0]
     per_tile = LANES // GSIZE
 
-    @pl.when(pl.program_id(0) == 0)
-    def _():
-        own, previous, following = contig_masks(starts_ref)
-        mask_ref[:, :rows] = (own.T if backward else own).astype(jnp.bfloat16)
-        mask_ref[:, rows:] = (following if backward else previous).astype(jnp.bfloat16)
-
+    own, previous, following = contig_masks(starts_ref)
+    mask_ref[:, :rows] = (own.T if backward else own).astype(jnp.bfloat16)
+    mask_ref[:, rows:] = (following if backward else previous).astype(jnp.bfloat16)
     taps_scr[...] = taps_ref[...].astype(jnp.float32) if backward else reversed_taps(taps_ref[...])
     group = lane_groups()
 
@@ -139,65 +131,55 @@
     lax.fori_loop(0, a_ref.shape[1] // LANES, tile, 0)
 
 
+VMEM = pl.BlockSpec(memory_space=pltpu.VMEM)
+
+
+def local_call(kernel, name, out_shape, scratch_shapes, flops, operands):
+    outs = out_shape if isinstance(out_shape, list) else [out_shape]
+    moved = sum(math.prod(x.shape) * x.dtype.itemsize for x in [*operands, *outs])
+    return pl.pallas_call(
+        kernel,
+        out_shape=out_shape,
+        in_specs=[VMEM] * len(operands),
+        out_specs=[VMEM] * len(outs) if isinstance(out_shape, list) else VMEM,
+        scratch_shapes=scratch_shapes,
+        cost_estimate=pl.CostEstimate(flops=flops, bytes_accessed=moved, transcendentals=0),
+        compiler_params=pltpu.CompilerParams(vmem_limit_bytes=24 << 20),
+        name=name,
+    )(*operands)
+
+
 def masked_product(a, b, starts, tail):
-    rows, width = a.shape
-    block = math.gcd(width, BLOCK)
-    wide = pl.BlockSpec((rows, block), lambda i: (0, i))
-    return pl.pallas_call(
+    return local_call(
         functools.partial(send_kernel, tail=tail),
-        grid=(width // block,),
-        out_shape=jax.ShapeDtypeStruct((rows, width), jnp.bfloat16),
-        in_specs=[wide] * 2 + [pl.BlockSpec((1, rows), lambda i: (0, 0))],
-        out_specs=wide,
-        cost_estimate=pl.CostEstimate(flops=2 * rows * width, bytes_accessed=6 * rows * width, transcendentals=0),
-        name="sent_kv" if tail else "sent_cot",
-    )(a, b, starts)
+        "sent_kv" if tail else "sent_cot",
+        jax.ShapeDtypeStruct(a.shape, jnp.bfloat16), [], 2 * a.size, (a, b, starts),
+    )
 
 
 def filter_share(q, k, v, dy, kv_prev, starts, groups, scale):
     rows, width = q.shape
-    block = math.gcd(width, BLOCK)
-    wide = pl.BlockSpec((rows, block), lambda i: (0, i))
-    return pl.pallas_call(
+    table = pltpu.VMEM((rows, rows), jnp.float32)
+    return local_call(
         functools.partial(filter_kernel, scale=scale),
-        grid=(width // block,),
-        out_shape=jax.ShapeDtypeStruct((groups, rows), jnp.float32),
-        in_specs=[wide] * 5 + [pl.BlockSpec((1, rows), lambda i: (0, 0))],
-        out_specs=pl.BlockSpec((block // GSIZE, rows), lambda i: (i, 0)),
-        scratch_shapes=[
-            pltpu.VMEM((rows, rows), jnp.float32),
-            pltpu.VMEM((rows, rows), jnp.float32),
-            pltpu.VMEM((block // GSIZE * 8, rows), jnp.float32),
-        ],
-        cost_estimate=pl.CostEstimate(
-            flops=2 * rows * 2 * rows * width, bytes_accessed=10 * rows * width, transcendentals=0
-        ),
-        compiler_params=pltpu.CompilerParams(vmem_limit_bytes=24 << 20),
-        name="filter_share",
-    )(q, k, v, dy, kv_prev, starts)
+        "filter_share",
+        jax.ShapeDtypeStruct((groups, rows), jnp.float32),
+        [table, table, pltpu.VMEM((groups * 8, rows), jnp.float32)],
+        32 * rows * rows * width,
+        (q, k, v, dy, kv_prev, starts),
+    )
 
 
 def convolution(a, b, other, c, d, starts, filters, backward):
     rows, width = a.shape
-    block = math.gcd(width, BLOCK)
-    wide = pl.BlockSpec((rows, block), lambda i: (0, i))
-    few = pl.BlockSpec((block // GSIZE, rows), lambda i: (i, 0))
-    return pl.pallas_call(
+    return local_call(
         functools.partial(conv_kernel, backward=backward),
-        grid=(width // block,),
-        out_shape=[jax.ShapeDtypeStruct((rows, width), jnp.bfloat16)] * 2,
-        in_specs=[wide] * 5 + [pl.BlockSpec((1, rows), lambda i: (0, 0)), few],
-        out_specs=[wide] * 2,
-        scratch_shapes=[
-            pltpu.VMEM((rows, 2 * rows), jnp.bfloat16),
-            pltpu.VMEM((block // GSIZE, rows), jnp.float32),
-        ],
-        cost_estimate=pl.CostEstimate(
-            flops=2 * rows * 2 * rows * width, bytes_accessed=14 * rows * width, transcendentals=0
-        ),
-        compiler_params=pltpu.CompilerParams(vmem_limit_bytes=24 << 20),
-        name="backward" if backward else "forward",
-    )(a, b, other, c, d, starts, filters)
+        "backward" if backward else "forward",
+        [jax.ShapeDtypeStruct((rows, width), jnp.bfloat16)] * 2,
+        [pltpu.VMEM((rows, 2 * rows), jnp.bfloat16), pltpu.VMEM(filters.shape, jnp.float32)],
+        32 * rows * rows * width,
+        (a, b, other, c, d, starts, filters),
+    )
 
 
 def passed_along(block, axis, distance):
@@ -207,15 +189,16 @@
 
 
 def summed_everywhere(share):
-    axes = ("dp", "ctx")
-    count = lax.axis_size("dp") * lax.axis_size("ctx")
-    if share.shape[0] % count:
-        return lax.psum(share, axes)
-    part = share.shape[0] // count
-    pieces = lax.all_to_all(share.reshape(count, part, -1), axes, 0, 0, tiled=True)
-    mine = jnp.sum(pieces, axis=0)
-    spread = jnp.broadcast_to(mine[None], pieces.shape)
-    return lax.all_to_all(spread, axes, 0, 0, tiled=True).reshape(share.shape)
+    groups, taps = share.shape
+    ctx, dp = lax.axis_size("ctx"), lax.axis_size("dp")
+    part = -(-groups // ctx)
+    padded = jnp.pad(share, ((0, part * ctx - groups), (0, 0))).reshape(ctx, part, taps)
+    mine = jnp.sum(lax.all_to_all(padded, "ctx", 0, 0, tiled=True), axis=0)
+    spread = jnp.broadcast_to(mine[None], (dp, part, taps))
+    mine = jnp.sum(lax.all_to_all(spread, "dp", 0, 0, tiled=True), axis=0)
+    spread = jnp.broadcast_to(mine[None], (ctx, part, taps))
+    every = lax.all_to_all(spread, "ctx", 0, 0, tiled=True)
+    return every.reshape(ctx * part, taps)[:groups]
 
 
 def per_device(q_proj, k_proj, v_proj, out_grad, contig_starts, filters):

time: 56.4 us -> 59.2 us (1.050)
  Pallas kernels: 29.8 us -> 21.4 us
  starting transfers between devices: 6.36 us -> 12 us
  local copies, waits for them, and re-layouts: 1.31 us -> 5.69 us
  blocking collectives: 17.7 us -> 18.7 us
    pallas_call x5, Pallas kernels: 29.8 us -> 21.4 us  [local_call(): pl.pallas_call(kernel, out_shape=out_shape, in_specs=[VMEM] * len(operand...]
    all_to_all x1 -> x2, starting transfers between devices: 2.7 us -> 8.33 us  [the longest x1 4.98 us: summed_everywhere(): mine = jnp.sum(lax.all_to_all(spread, 'dp', 0, 0, tiled=True), axis=0)]
    unnamed x13 -> x21, local copies, waits for them, and re-layouts: 0.67 us -> 4.43 us
    all_to_all x1, blocking collectives: 17.7 us -> 18.7 us  [summed_everywhere(): mine = jnp.sum(lax.all_to_all(padded, 'ctx', 0, 0, tiled=True), axis=0)]
    broadcast_in_dim x1 -> x2, local copies, waits for them, and re-layouts: 0.64 us -> 1.25 us  [the longest x1 0.64 us: summed_everywhere(): spread = jnp.broadcast_to(mine[None], (ctx, part, taps))]
  transfers between devices with their start and end apart: 3 -> 4, of which waited for: 0 -> 0; matrix products, arithmetic and copies ran while one was open for 1% -> 2% of each run, Pallas kernels for 47% -> 36%
where the time goes in v3:
time: 59.2 us; the launch traced here: 58.6 us
  Pallas kernels  21.4 us (36%)
  blocking collectives  18.7 us (32%)
  starting transfers between devices  12 us (20%)
  local copies, waits for them, and re-layouts  5.69 us (10%)
  between operations  0.77 us (1%)
    pallas_call x5, Pallas kernels, local_call(): pl.pallas_call(kernel, out_shape=out_shape, in_specs=[VMEM] * len(operand...  21.4 us
    all_to_all x1, blocking collectives, summed_everywhere(): mine = jnp.sum(lax.all_to_all(padded, 'ctx', 0, 0, tiled=True), axis=0)  18.7 us
    all_to_all x1, starting transfers between devices, summed_everywhere(): mine = jnp.sum(lax.all_to_all(spread, 'dp', 0, 0, tiled=True), axis=0)  4.98 us
    unnamed x21, local copies, waits for them, and re-layouts  4.43 us
    ppermute x2, starting transfers between devices, passed_along(): return lax.ppermute(block, axis, route)  3.68 us
    all_to_all x1, starting transfers between devices, summed_everywhere(): every = lax.all_to_all(spread, 'ctx', 0, 0, tiled=True)  3.35 us
  transfers between devices with their start and end apart: 4, of which 0 were waited for; matrix products, arithmetic and copies ran while one was open for 2% of the time, Pallas kernels for 36%

profile of v3, /device:TPU:0, one launch (start us, length us, event | category | flops | bytes accessed | tf_op | source)
XLA Modules:
  0.0 58.6 jit_solution(6809104279576653706)
XLA Ops:
  0.6 0.0 copy-start.6
  0.6 0.6 %copy-done.6 = s32[1,128]{1,0:T(1,128)S(1)} copy-done((s32[1,128]{1,0:T(1,128)S(1)}, s32[1,128]{1,0:T(1,128)}, u32[]{:S(2)}) %copy-start.6) | copy-done | bytes 536
  1.3 0.0 copy-start
  1.3 1.0 %copy-done = bf16[1,128,2048]{2,1,0:T(8,128)(2,1)S(1)} copy-done((bf16[1,128,2048]{2,1,0:T(8,128)(2,1)S(1)}, bf16[1,128,2048]{2,1,0:T(8,128)(2,1)}, u32[]{:S(2)}) %copy-start) | copy-done | bytes 524312
  2.3 0.0 copy-start.2
  2.3 1.0 %copy-done.2 = bf16[1,128,2048]{2,1,0:T(8,128)(2,1)S(1)} copy-done((bf16[1,128,2048]{2,1,0:T(8,128)(2,1)S(1)}, bf16[1,128,2048]{2,1,0:T(8,128)(2,1)}, u32[]{:S(2)}) %copy-start.2) | copy-done | bytes 524312
  3.4 0.0 copy-start.4
  3.4 0.0 copy-start.5
  3.4 0.4 sent_kv.1
  3.7 2.4 %collective-permute-start = (bf16[128,2048]{1,0:T(8,128)(2,1)S(1)}, bf16[128,2048]{1,0:T(8,128)(2,1)S(1)}, u32[]{:S(2)}, u32[]{:S(2)}) collective-permute-start(bf16[128,2048]{1,0:T(8,128)(2,1)S(1)} %sent_kv.1), channel_id=1, source_target_pairs={{0,4},{4,8},{8,12},{12,16},{16,20},{20,24},{24,28},{1,5},{5,9},{9,... | collective-permute-start | bytes 1572872 | tf_op jit(solution)/shard_map/ppermute | solution.py:188
  6.1 0.0 copy-done.4
  6.2 0.0 copy-done.5
  6.2 0.0 copy-start.1
  6.2 0.0 copy-start.3
  6.2 0.4 sent_cot.1
  6.6 1.3 %collective-permute-start.1 = (bf16[128,2048]{1,0:T(8,128)(2,1)S(1)}, bf16[128,2048]{1,0:T(8,128)(2,1)S(1)}, u32[]{:S(2)}, u32[]{:S(2)}) collective-permute-start(bf16[128,2048]{1,0:T(8,128)(2,1)S(1)} %sent_cot.1), channel_id=1, source_target_pairs={{4,0},{8,4},{12,8},{16,12},{20,16},{24,20},{28,24},{5,1},{9,5},{13... | collective-permute-start | bytes 1572872 | tf_op jit(solution)/shard_map/ppermute | solution.py:188
  7.9 0.0 collective-permute-done.other_ref.kv_prev_ref
  7.9 0.0 copy-done.1
  7.9 0.0 copy-done.3
  7.9 0.0 copy-start.7
  7.9 6.6 %filter_share.1 = f32[128,128]{1,0:T(8,128)S(1)} custom-call(bf16[128,2048]{1,0:T(8,128)(2,1)S(1)} %bitcast.19, bf16[128,2048]{1,0:T(8,128)(2,1)S(1)} %bitcast.11, bf16[128,2048]{1,0:T(8,128)(2,1)S(1)} %bitcast.15, bf16[128,2048]{1,0:T(8,128)(2,1)S(1)} %bitcast.23, bf16[128,2048]{1,0:T(8,128)(2,1)S(1)} %collective-permute-done.other_ref.kv_prev_ref, ...), custom_call_target="tpu_custom_call" | custom-call | flops 1073741824 | bytes 2687488 | tf_op jit(solution)/shard_map/filter_share/pallas_call | solution.py:140
  14.5 0.0 copy-done.7
  14.6 18.7 %all_to_all.15 = f32[8,16,128]{2,1,0:T(8,128)S(1)} all-to-all(f32[8,16,128]{2,1,0:T(8,128)S(1)} %bitcast.26), channel_id=1, replica_groups=mesh['ctx'=8,'dp'=4] {'ctx'}, dimensions={0} | all-to-all | bytes 131072 | tf_op jit(solution)/shard_map/all_to_all | solution.py:196
  33.3 0.6 %broadcast_in_dim.28 = f32[4,16,128]{2,1,0:T(8,128)} broadcast(f32[16,128]{1,0:T(8,128)S(1)} %reduce_sum.18), dimensions={1,2} | broadcast | bytes 40960 | tf_op jit(solution)/shard_map/broadcast_in_dim | solution.py:197
  33.9 0.0 copy-start.9
  33.9 5.0 %all-to-all-start.1 = ((f32[4,16,128]{2,1,0:T(8,128)}), f32[4,16,128]{2,1,0:T(8,128)S(1)}, u32[]{:S(2)}, u32[]{:S(2)}) async-start(f32[4,16,128]{2,1,0:T(8,128)} %broadcast_in_dim.28), calls=%async_computation.1 | async-start | bytes 65536 | tf_op jit(solution)/shard_map/all_to_all | solution.py:198
  38.9 0.0 copy-done.9
  38.9 0.0 copy-start.8
  38.9 1.0 %copy-done.8 = bf16[128,2048]{1,0:T(8,128)(2,1)S(1)} copy-done((bf16[128,2048]{1,0:T(8,128)(2,1)S(1)}, bf16[128,2048]{1,0:T(8,128)(2,1)}, u32[]{:S(2)}) %copy-start.8) | copy-done | bytes 524312
  39.9 7.0 %forward.1 = (bf16[128,2048]{1,0:T(8,128)(2,1)}, bf16[128,2048]{1,0:T(8,128)(2,1)}) custom-call(bf16[128,2048]{1,0:T(8,128)(2,1)S(1)} %bitcast.12, bf16[128,2048]{1,0:T(8,128)(2,1)S(1)} %bitcast.16, bf16[128,2048]{1,0:T(8,128)(2,1)S(1)} %copy-done.8, bf16[128,2048]{1,0:T(8,128)(2,1)S(1)} %bitcast.20, bf16[128,2048]{1,0:T(8,128)(2,1)S(1)} %bitcast.24, ...), custom_call_target="tpu_custom_call" | custom-call | flops 1073741824 | bytes 3703296 | tf_op jit(solution)/shard_map/forward/pallas_call | solution.py:140
  46.9 0.0 all-to-all-done.1
  46.9 0.6 %broadcast_in_dim.29 = f32[8,16,128]{2,1,0:T(8,128)} broadcast(f32[16,128]{1,0:T(8,128)S(1)} %reduce_sum.19), dimensions={1,2} | broadcast | bytes 73728 | tf_op jit(solution)/shard_map/broadcast_in_dim | solution.py:199
  47.6 3.4 %all-to-all-start.2 = ((f32[8,16,128]{2,1,0:T(8,128)}), f32[8,16,128]{2,1,0:T(8,128)S(1)}, u32[]{:S(2)}, u32[]{:S(2)}) async-start(f32[8,16,128]{2,1,0:T(8,128)} %broadcast_in_dim.29), calls=%async_computation.2 | async-start | bytes 131072 | tf_op jit(solution)/shard_map/all_to_all | solution.py:200
  50.9 0.0 collective-permute-done.1.other_ref
  50.9 7.0 %backward.1 = (bf16[128,2048]{1,0:T(8,128)(2,1)}, bf16[128,2048]{1,0:T(8,128)(2,1)}) custom-call(bf16[128,2048]{1,0:T(8,128)(2,1)S(1)} %bitcast.25, bf16[128,2048]{1,0:T(8,128)(2,1)S(1)} %bitcast.21, bf16[128,2048]{1,0:T(8,128)(2,1)S(1)} %collective-permute-done.1.other_ref, bf16[128,2048]{1,0:T(8,128)(2,1)S(1)} %bitcast.17, bf16[128,2048]{1,0:T(8,128)(2,1)S(1)} %bitcast.13, ...), custom_call_target="tpu_custom_call" | custom-call | flops 1073741824 | bytes 3703296 | tf_op jit(solution)/shard_map/backward/pallas_call | solution.py:140
  58.0 0.0 all-to-all-done.2
  58.0 0.6 %copy.12 = f32[128,128]{1,0:T(8,128)} copy(f32[128,128]{1,0:T(8,128)S(1)} %bitcast.27) | data formatting | bytes 131072
  (2 shorter events, 0.0 us)
Async XLA Ops:
  0.6 0.7 %copy-start.6 = (s32[1,128]{1,0:T(1,128)S(1)}, s32[1,128]{1,0:T(1,128)}, u32[]{:S(2)}) copy-start(s32[1,128]{1,0:T(1,128)} %starts_ref.9) | copy-start | bytes 1540
  1.3 1.0 %copy-start = (bf16[1,128,2048]{2,1,0:T(8,128)(2,1)S(1)}, bf16[1,128,2048]{2,1,0:T(8,128)(2,1)}, u32[]{:S(2)}) copy-start(bf16[1,128,2048]{2,1,0:T(8,128)(2,1)} %param.7) | copy-start | bytes 1572868
  2.3 1.0 %copy-start.2 = (bf16[1,128,2048]{2,1,0:T(8,128)(2,1)S(1)}, bf16[1,128,2048]{2,1,0:T(8,128)(2,1)}, u32[]{:S(2)}) copy-start(bf16[1,128,2048]{2,1,0:T(8,128)(2,1)} %param.8) | copy-start | bytes 1572868
  3.4 2.8 %copy-start.4 = (bf16[1,128,2048]{2,1,0:T(8,128)(2,1)S(1)}, bf16[1,128,2048]{2,1,0:T(8,128)(2,1)}, u32[]{:S(2)}) copy-start(bf16[1,128,2048]{2,1,0:T(8,128)(2,1)} %param.6) | copy-start | bytes 1572868
  3.4 2.8 %copy-start.5 = (bf16[1,128,2048]{2,1,0:T(8,128)(2,1)S(1)}, bf16[1,128,2048]{2,1,0:T(8,128)(2,1)}, u32[]{:S(2)}) copy-start(bf16[1,128,2048]{2,1,0:T(8,128)(2,1)} %param.9) | copy-start | bytes 1572868
  3.7 4.1 %collective-permute-start = (bf16[128,2048]{1,0:T(8,128)(2,1)S(1)}, bf16[128,2048]{1,0:T(8,128)(2,1)S(1)}, u32[]{:S(2)}, u32[]{:S(2)}) collective-permute-start(bf16[128,2048]{1,0:T(8,128)(2,1)S(1)} %sent_kv.1), channel_id=1, source_target_pairs={{0,4},{4,8},{8,12},{12,16},{16,20},{20,24},{24,28},{1,5},{5,9},{9,... | collective-permute-start | bytes 1572872 | tf_op jit(solution)/shard_map/ppermute | solution.py:188
  6.2 1.7 %copy-start.1 = (bf16[1,128,2048]{2,1,0:T(8,128)(2,1)S(1)}, bf16[1,128,2048]{2,1,0:T(8,128)(2,1)}, u32[]{:S(2)}) copy-start(bf16[1,128,2048]{2,1,0:T(8,128)(2,1)} %param.7) | copy-start | bytes 1572868
  6.2 1.7 %copy-start.3 = (bf16[1,128,2048]{2,1,0:T(8,128)(2,1)S(1)}, bf16[1,128,2048]{2,1,0:T(8,128)(2,1)}, u32[]{:S(2)}) copy-start(bf16[1,128,2048]{2,1,0:T(8,128)(2,1)} %param.8) | copy-start | bytes 1572868
  6.6 44.4 %collective-permute-start.1 = (bf16[128,2048]{1,0:T(8,128)(2,1)S(1)}, bf16[128,2048]{1,0:T(8,128)(2,1)S(1)}, u32[]{:S(2)}, u32[]{:S(2)}) collective-permute-start(bf16[128,2048]{1,0:T(8,128)(2,1)S(1)} %sent_cot.1), channel_id=1, source_target_pairs={{4,0},{8,4},{12,8},{16,12},{20,16},{24,20},{28,24},{5,1},{9,5},{13... | collective-permute-start | bytes 1572872 | tf_op jit(solution)/shard_map/ppermute | solution.py:188
  7.9 6.7 %copy-start.7 = (bf16[128,2048]{1,0:T(8,128)(2,1)}, bf16[128,2048]{1,0:T(8,128)(2,1)S(1)}, u32[]{:S(2)}) copy-start(bf16[128,2048]{1,0:T(8,128)(2,1)S(1)} %collective-permute-done.other_ref.kv_prev_ref) | copy-start | bytes 1572868
  33.9 5.0 %copy-start.9 = (bf16[128,128]{1,0:T(8,128)(2,1)S(1)}, bf16[128,128]{1,0:T(8,128)(2,1)}, u32[]{:S(2)}) copy-start(bf16[128,128]{1,0:T(8,128)(2,1)} %taps_ref.3) | copy-start | bytes 98308
  33.9 13.0 %all-to-all-start.1 = ((f32[4,16,128]{2,1,0:T(8,128)}), f32[4,16,128]{2,1,0:T(8,128)S(1)}, u32[]{:S(2)}, u32[]{:S(2)}) async-start(f32[4,16,128]{2,1,0:T(8,128)} %broadcast_in_dim.28), calls=%async_computation.1 | async-start | bytes 65536 | tf_op jit(solution)/shard_map/all_to_all | solution.py:198
  38.9 1.0 %copy-start.8 = (bf16[128,2048]{1,0:T(8,128)(2,1)S(1)}, bf16[128,2048]{1,0:T(8,128)(2,1)}, u32[]{:S(2)}) copy-start(bf16[128,2048]{1,0:T(8,128)(2,1)} %copy-done.7) | copy-start | bytes 1572868
  47.6 10.4 %all-to-all-start.2 = ((f32[8,16,128]{2,1,0:T(8,128)}), f32[8,16,128]{2,1,0:T(8,128)S(1)}, u32[]{:S(2)}, u32[]{:S(2)}) async-start(f32[8,16,128]{2,1,0:T(8,128)} %broadcast_in_dim.29), calls=%async_computation.2 | async-start | bytes 131072 | tf_op jit(solution)/shard_map/all_to_all | solution.py:200

commit v4 on v3

--- a/solution.py
+++ b/solution.py
@@ -46,17 +46,53 @@
     return lax.broadcasted_iota(jnp.int32, (1, LANES), 1) // GSIZE
 
 
-def send_kernel(a_ref, b_ref, starts_ref, out_ref, *, tail):
-    rows = a_ref.shape[0]
+def each_tile(tile, width):
+    count = width // LANES
+    step = math.gcd(count, 4)
+
+    def body(i, carry):
+        for j in range(step):
+            tile(i * step + j)
+        return carry
+
+    lax.fori_loop(0, count // step, body, 0)
+
+
+def kept_rows(starts_ref, rows, tail):
     starts = starts_ref[...] > 0
     lane = lax.broadcasted_iota(jnp.int32, starts.shape, 1)
     token = lax.broadcasted_iota(jnp.int32, (rows, 1), 0)
     if tail:
-        keep = token >= jnp.max(jnp.where(starts, lane, 0), axis=1, keepdims=True)
-    else:
-        keep = token < jnp.min(jnp.where(starts, lane, rows), axis=1, keepdims=True)
-    out = a_ref[...].astype(jnp.float32) * b_ref[...].astype(jnp.float32)
-    out_ref[...] = jnp.where(keep, out, 0.0).astype(jnp.bfloat16)
+        return token >= jnp.max(jnp.where(starts, lane, 0), axis=1, keepdims=True)
+    return token < jnp.min(jnp.where(starts, lane, rows), axis=1, keepdims=True)
+
+
+def sent_product(a, b, keep):
+    out = a.astype(jnp.float32) * b.astype(jnp.float32)
+    return jnp.where(keep, out, 0.0).astype(jnp.bfloat16)
+
+
+def sent_cot_kernel(a_ref, b_ref, starts_ref, out_ref):
+    out_ref[...] = sent_product(a_ref[...], b_ref[...], kept_rows(starts_ref, a_ref.shape[0], False))
+
+
+def sent_kv_kernel(a_hbm, b_hbm, starts_hbm, out_ref, a_ref, b_ref, starts_ref, sems):
+    rows = a_ref.shape[0]
+    half = rows // 2
+    copies = [pltpu.make_async_copy(starts_hbm, starts_ref, sems.at[0])]
+    for h in range(2):
+        part = pl.ds(h * half, half)
+        copies.append(pltpu.make_async_copy(a_hbm.at[part], a_ref.at[part], sems.at[2 * h + 1]))
+        copies.append(pltpu.make_async_copy(b_hbm.at[part], b_ref.at[part], sems.at[2 * h + 2]))
+    for copy in copies:
+        copy.start()
+    copies[0].wait()
+    keep = kept_rows(starts_ref, rows, True)
+    for h in range(2):
+        copies[2 * h + 1].wait()
+        copies[2 * h + 2].wait()
+        at = slice(h * half, (h + 1) * half)
+        out_ref[at, :] = sent_product(a_ref[at, :], b_ref[at, :], keep[at])
 
 
 def filter_kernel(
@@ -69,30 +105,23 @@
 
     group = lane_groups()
 
-    def tile(index, carry):
+    def tile(index):
         lanes = pl.ds(pl.multiple_of(index * LANES, LANES), LANES)
         cot = product(dy_ref[:, lanes], q_ref[:, lanes])
         kv = jnp.concatenate([product(k_ref[:, lanes], v_ref[:, lanes]), kv_prev_ref[:, lanes]], axis=0)
-        picked = jnp.concatenate(
-            [jnp.where(group == g, cot, jnp.zeros_like(cot)) for g in range(per_tile)], axis=0
-        )
-        pairs = lax.dot_general(
-            picked, kv, (((1,), (1,)), ((), ())), preferred_element_type=jnp.float32
-        )
         for g in range(per_tile):
-            total = None
-            for i in range(rows // 8):
-                at = g * rows + 8 * i
-                piece = (
-                    pairs[at : at + 8, :rows] * own_ref[8 * i : 8 * i + 8, :]
-                    + pairs[at : at + 8, rows:] * prev_ref[8 * i : 8 * i + 8, :]
-                )
-                total = piece if i == 0 else total + pltpu.roll(piece, rows - 8 * i, 1)
+            picked = jnp.where(group == g, cot, jnp.zeros_like(cot))
+            pairs = lax.dot_general(
+                picked, kv, (((1,), (1,)), ((), ())), preferred_element_type=jnp.float32
+            )
+            linked = pairs[:, :rows] * own_ref[...] + pairs[:, rows:] * prev_ref[...]
+            total = linked[:8]
+            for i in range(1, rows // 8):
+                total = total + pltpu.roll(linked[8 * i : 8 * i + 8], rows - 8 * i, 1)
             at = pl.multiple_of((index * per_tile + g) * 8, 8)
             sums_ref[pl.ds(at, 8), :] = total
-        return carry
-
-    lax.fori_loop(0, q_ref.shape[1] // LANES, tile, 0)
+
+    each_tile(tile, q_ref.shape[1])
     groups = out_ref.shape[0]
     diagonal = sums_ref[pl.ds(0, groups, stride=8), :]
     for r in range(1, 8):
@@ -115,32 +144,29 @@
         wide = wide.astype(jnp.bfloat16)
         return jnp.concatenate([wide, wide], axis=1) * mask_ref[...]
 
-    def tile(index, carry):
+    def tile(index):
         lanes = pl.ds(pl.multiple_of(index * LANES, LANES), LANES)
         x = jnp.concatenate([product(a_ref[:, lanes], b_ref[:, lanes]), other_ref[:, lanes]], axis=0)
         taps = taps_scr[pl.ds(pl.multiple_of(index * per_tile, per_tile), per_tile), :]
-        tables = jnp.concatenate([table(taps[g : g + 1]) for g in range(per_tile)], axis=0)
-        every = jnp.dot(tables, x, preferred_element_type=jnp.float32)
-        y = every[:rows]
-        for g in range(1, per_tile):
-            y = jnp.where(group == g, every[g * rows : (g + 1) * rows], y)
+        y = jnp.zeros((rows, LANES), jnp.float32)
+        for g in range(per_tile):
+            y = jnp.where(group == g, jnp.dot(table(taps[g : g + 1]), x, preferred_element_type=jnp.float32), y)
         out_c_ref[:, lanes] = (c_ref[:, lanes].astype(jnp.float32) * y).astype(jnp.bfloat16)
         out_d_ref[:, lanes] = (d_ref[:, lanes].astype(jnp.float32) * y).astype(jnp.bfloat16)
-        return carry
-
-    lax.fori_loop(0, a_ref.shape[1] // LANES, tile, 0)
+
+    each_tile(tile, a_ref.shape[1])
 
 
 VMEM = pl.BlockSpec(memory_space=pltpu.VMEM)
 
 
-def local_call(kernel, name, out_shape, scratch_shapes, flops, operands):
+def local_call(kernel, name, out_shape, scratch_shapes, flops, operands, placed=VMEM):
     outs = out_shape if isinstance(out_shape, list) else [out_shape]
     moved = sum(math.prod(x.shape) * x.dtype.itemsize for x in [*operands, *outs])
     return pl.pallas_call(
         kernel,
         out_shape=out_shape,
-        in_specs=[VMEM] * len(operands),
+        in_specs=[placed] * len(operands),
         out_specs=[VMEM] * len(outs) if isinstance(out_shape, list) else VMEM,
         scratch_shapes=scratch_shapes,
         cost_estimate=pl.CostEstimate(flops=flops, bytes_accessed=moved, transcendentals=0),
@@ -149,11 +175,19 @@
     )(*operands)
 
 
-def masked_product(a, b, starts, tail):
-    return local_call(
-        functools.partial(send_kernel, tail=tail),
-        "sent_kv" if tail else "sent_cot",
-        jax.ShapeDtypeStruct(a.shape, jnp.bfloat16), [], 2 * a.size, (a, b, starts),
+def sent_kv(k, v, starts):
+    whole = pltpu.VMEM(k.shape, k.dtype)
+    return local_call(
+        sent_kv_kernel, "sent_kv", jax.ShapeDtypeStruct(k.shape, jnp.bfloat16),
+        [whole, whole, pltpu.VMEM(starts.shape, starts.dtype), pltpu.SemaphoreType.DMA((5,))],
+        2 * k.size, (k, v, starts), pl.BlockSpec(memory_space=pltpu.HBM),
+    )
+
+
+def sent_cot(dy, q, starts):
+    return local_call(
+        sent_cot_kernel, "sent_cot", jax.ShapeDtypeStruct(q.shape, jnp.bfloat16),
+        [], 2 * q.size, (dy, q, starts),
     )
 
 
@@ -188,17 +222,31 @@
     return lax.ppermute(block, axis, route)
 
 
-def summed_everywhere(share):
-    groups, taps = share.shape
-    ctx, dp = lax.axis_size("ctx"), lax.axis_size("dp")
-    part = -(-groups // ctx)
-    padded = jnp.pad(share, ((0, part * ctx - groups), (0, 0))).reshape(ctx, part, taps)
-    mine = jnp.sum(lax.all_to_all(padded, "ctx", 0, 0, tiled=True), axis=0)
-    spread = jnp.broadcast_to(mine[None], (dp, part, taps))
-    mine = jnp.sum(lax.all_to_all(spread, "dp", 0, 0, tiled=True), axis=0)
-    spread = jnp.broadcast_to(mine[None], (ctx, part, taps))
-    every = lax.all_to_all(spread, "ctx", 0, 0, tiled=True)
-    return every.reshape(ctx * part, taps)[:groups]
+def factors(size):
+    found, p = [], 2
+    while size > 1:
+        while size % p == 0:
+            found.append(p)
+            size //= p
+        p += 1
+    return found
+
+
+def summed_along(total, axis):
+    size = lax.axis_size(axis)
+    stride = 1
+    for p in factors(size):
+        turned = lambda i, k: i + ((i // stride + k) % p - i // stride % p) * stride
+        got = [
+            lax.ppermute(total, axis, [(turned(i, k), i) for i in range(size)]) for k in range(1, p)
+        ]
+        if p == 2:
+            total = total + got[0]
+        else:
+            digit = lax.axis_index(axis) // stride % p
+            total = jnp.sum(jnp.roll(jnp.stack([total, *got]), digit, axis=0), axis=0)
+        stride *= p
+    return total
 
 
 def per_device(q_proj, k_proj, v_proj, out_grad, contig_starts, filters):
@@ -207,10 +255,10 @@
     groups, taps = filters.shape
     assert rows == taps == LANES
     scale = 1.0 / math.sqrt(rows * lax.axis_size("ctx") * lax.axis_size("dp") * GSIZE)
-    kv_prev = passed_along(masked_product(k, v, contig_starts, True), "ctx", 1)
-    cot_next = passed_along(masked_product(dy, q, contig_starts, False), "ctx", -1)
+    kv_prev = passed_along(sent_kv(k, v, contig_starts), "ctx", 1)
+    cot_next = passed_along(sent_cot(dy, q, contig_starts), "ctx", -1)
     share = filter_share(q, k, v, dy, kv_prev, contig_starts, groups, scale)
-    filter_grad = summed_everywhere(share)
+    filter_grad = summed_along(summed_along(share, "ctx"), "dp")
     mixed, grad_q = convolution(k, v, kv_prev, q, dy, contig_starts, filters, False)
     grad_k, grad_v = convolution(dy, q, cot_next, v, k, contig_starts, filters, True)
     return (mixed[None], grad_q[None], grad_k[None], grad_v[None], filter_grad)

time: 59.2 us -> 46.2 us (0.78)
  blocking collectives: 18.7 us -> 0 us
  starting transfers between devices: 12 us -> 22.8 us
  Pallas kernels: 21.4 us -> 13.2 us
  waiting for transfers between devices: 0.01 us -> 5.77 us
  local copies, waits for them, and re-layouts: 5.69 us -> 2.76 us
  other arithmetic: 0.02 us -> 0.67 us
    ppermute x0 -> x5, starting transfers between devices: none -> 19.1 us  [summed_along(): lax.ppermute(total, axis, [(turned(i, k), i) for i in range(size)])]
    all_to_all x1 -> x0, blocking collectives: 18.7 us -> none  [summed_everywhere(): mine = jnp.sum(lax.all_to_all(padded, 'ctx', 0, 0, tiled=True), axis=0)]
    all_to_all x2 -> x0, starting transfers between devices: 8.33 us -> none  [the longest x1 4.98 us: summed_everywhere(): mine = jnp.sum(lax.all_to_all(spread, 'dp', 0, 0, tiled=True), axis=0)]
    pallas_call x5, Pallas kernels: 21.4 us -> 13.2 us  [local_call(): pl.pallas_call(kernel, out_shape=out_shape, in_specs=[placed] * len(opera...]
    ppermute x0 -> x5, waiting for transfers between devices: none -> 5.76 us  [summed_along(): lax.ppermute(total, axis, [(turned(i, k), i) for i in range(size)])]
    unnamed x21 -> x16, local copies, waits for them, and re-layouts: 4.43 us -> 2.76 us
    broadcast_in_dim x2 -> x0, local copies, waits for them, and re-layouts: 1.25 us -> none  [the longest x1 0.64 us: summed_everywhere(): spread = jnp.broadcast_to(mine[None], (ctx, part, taps))]
    add x0 -> x5, other arithmetic: none -> 0.67 us  [summed_along(): total = total + got[0]]
  transfers between devices with their start and end apart: 4 -> 7, of which waited for: 0 -> 3; matrix products, arithmetic and copies ran while one was open for 2% -> 0% of each run, Pallas kernels for 36% -> 28%
where the time goes in v4:
time: 46.2 us; the launch traced here: 46 us
  starting transfers between devices  22.8 us (49%)
  Pallas kernels  13.2 us (29%)
  waiting for transfers between devices  5.77 us (12%)
  local copies, waits for them, and re-layouts  2.76 us (6%)
  between operations  0.76 us (2%)
  other arithmetic  0.67 us (1%)
    ppermute x5, starting transfers between devices, summed_along(): lax.ppermute(total, axis, [(turned(i, k), i) for i in range(size)])  19.1 us
    pallas_call x5, Pallas kernels, local_call(): pl.pallas_call(kernel, out_shape=out_shape, in_specs=[placed] * len(opera...  13.2 us
    ppermute x5, waiting for transfers between devices, summed_along(): lax.ppermute(total, axis, [(turned(i, k), i) for i in range(size)])  5.76 us
    ppermute x2, starting transfers between devices, passed_along(): return lax.ppermute(block, axis, route)  3.68 us
    unnamed x16, local copies, waits for them, and re-layouts  2.76 us
  transfers between devices with their start and end apart: 7, of which 3 were waited for; matrix products, arithmetic and copies ran while one was open for 0% of the time, Pallas kernels for 28%

profile of v4, /device:TPU:0, one launch (start us, length us, event | category | flops | bytes accessed | tf_op | source)
XLA Modules:
  0.0 46.0 jit_solution(14627987258088066914)
XLA Ops:
  0.6 0.0 copy-start.6
  0.6 0.6 %copy-done.6 = s32[1,128]{1,0:T(1,128)S(1)} copy-done((s32[1,128]{1,0:T(1,128)S(1)}, s32[1,128]{1,0:T(1,128)}, u32[]{:S(2)}) %copy-start.6) | copy-done | bytes 536
  1.3 0.0 copy-start
  1.3 1.0 %copy-done = bf16[1,128,2048]{2,1,0:T(8,128)(2,1)S(1)} copy-done((bf16[1,128,2048]{2,1,0:T(8,128)(2,1)S(1)}, bf16[1,128,2048]{2,1,0:T(8,128)(2,1)}, u32[]{:S(2)}) %copy-start) | copy-done | bytes 524312
  2.3 0.0 copy-start.2
  2.3 1.0 %copy-done.2 = bf16[1,128,2048]{2,1,0:T(8,128)(2,1)S(1)} copy-done((bf16[1,128,2048]{2,1,0:T(8,128)(2,1)S(1)}, bf16[1,128,2048]{2,1,0:T(8,128)(2,1)}, u32[]{:S(2)}) %copy-start.2) | copy-done | bytes 524312
  3.4 0.0 copy-start.4
  3.4 0.0 copy-start.5
  3.4 0.4 sent_kv.1
  3.8 2.4 %collective-permute-start = (bf16[128,2048]{1,0:T(8,128)(2,1)S(1)}, bf16[128,2048]{1,0:T(8,128)(2,1)S(1)}, u32[]{:S(2)}, u32[]{:S(2)}) collective-permute-start(bf16[128,2048]{1,0:T(8,128)(2,1)S(1)} %sent_kv.1), channel_id=1, source_target_pairs={{0,4},{4,8},{8,12},{12,16},{16,20},{20,24},{24,28},{1,5},{5,9},{9,... | collective-permute-start | bytes 1572872 | tf_op jit(solution)/shard_map/ppermute | solution.py:222
  6.2 0.0 copy-done.4
  6.2 0.0 copy-done.5
  6.2 0.0 copy-start.1
  6.3 0.0 copy-start.3
  6.3 0.4 sent_cot.1
  6.6 1.3 %collective-permute-start.1 = (bf16[128,2048]{1,0:T(8,128)(2,1)S(1)}, bf16[128,2048]{1,0:T(8,128)(2,1)S(1)}, u32[]{:S(2)}, u32[]{:S(2)}) collective-permute-start(bf16[128,2048]{1,0:T(8,128)(2,1)S(1)} %sent_cot.1), channel_id=1, source_target_pairs={{4,0},{8,4},{12,8},{16,12},{20,16},{24,20},{28,24},{5,1},{9,5},{13... | collective-permute-start | bytes 1572872 | tf_op jit(solution)/shard_map/ppermute | solution.py:222
  7.9 0.0 collective-permute-done.other_ref.kv_prev_ref
  8.0 0.0 copy-done.1
  8.0 0.0 copy-done.3
  8.0 3.7 %filter_share.1 = f32[128,128]{1,0:T(8,128)S(1)} custom-call(bf16[128,2048]{1,0:T(8,128)(2,1)S(1)} %bitcast.17, bf16[128,2048]{1,0:T(8,128)(2,1)S(1)} %bitcast.9, bf16[128,2048]{1,0:T(8,128)(2,1)S(1)} %bitcast.13, bf16[128,2048]{1,0:T(8,128)(2,1)S(1)} %bitcast.21, bf16[128,2048]{1,0:T(8,128)(2,1)S(1)} %collective-permute-done.other_ref.kv_prev_ref, ...), custom_call_target="tpu_custom_call" | custom-call | flops 1073741824 | bytes 2687488 | tf_op jit(solution)/shard_map/filter_share/pallas_call | solution.py:166
  11.7 7.0 %collective-permute-start.2 = (f32[128,128]{1,0:T(8,128)S(1)}, f32[128,128]{1,0:T(8,128)S(1)}, u32[]{:S(2)}, u32[]{:S(2)}) collective-permute-start(f32[128,128]{1,0:T(8,128)S(1)} %filter_share.1), channel_id=1, source_target_pairs={{4,0},{0,4},{12,8},{8,12},{20,16},{16,20},{28,24},{24,28},{5,1},{1... | collective-permute-start | bytes 196616 | tf_op jit(solution)/shard_map/ppermute | solution.py:241
  18.7 0.9 %collective-permute-done.2 = f32[128,128]{1,0:T(8,128)S(1)} collective-permute-done((f32[128,128]{1,0:T(8,128)S(1)}, f32[128,128]{1,0:T(8,128)S(1)}, u32[]{:S(2)}, u32[]{:S(2)}) %collective-permute-start.2) | collective-permute-done | bytes 65568 | tf_op jit(solution)/shard_map/ppermute | solution.py:241
  19.7 3.9 %collective-permute-start.3 = (f32[128,128]{1,0:T(8,128)S(1)}, f32[128,128]{1,0:T(8,128)S(1)}, u32[]{:S(2)}, u32[]{:S(2)}) collective-permute-start(f32[128,128]{1,0:T(8,128)S(1)} %add.15), channel_id=1, source_target_pairs={{8,0},{12,4},{0,8},{4,12},{24,16},{28,20},{16,24},{20,28},{9,1},{1... | collective-permute-start | bytes 196616 | tf_op jit(solution)/shard_map/ppermute | solution.py:241
  23.6 2.6 %collective-permute-done.3 = f32[128,128]{1,0:T(8,128)S(1)} collective-permute-done((f32[128,128]{1,0:T(8,128)S(1)}, f32[128,128]{1,0:T(8,128)S(1)}, u32[]{:S(2)}, u32[]{:S(2)}) %collective-permute-start.3) | collective-permute-done | bytes 65568 | tf_op jit(solution)/shard_map/ppermute | solution.py:241
  26.2 0.0 copy-start.7
  26.2 3.9 %collective-permute-start.4 = (f32[128,128]{1,0:T(8,128)S(1)}, f32[128,128]{1,0:T(8,128)S(1)}, u32[]{:S(2)}, u32[]{:S(2)}) collective-permute-start(f32[128,128]{1,0:T(8,128)S(1)} %add.16), channel_id=1, source_target_pairs={{16,0},{20,4},{24,8},{28,12},{0,16},{4,20},{8,24},{12,28},{17,1},{... | collective-permute-start | bytes 196616 | tf_op jit(solution)/shard_map/ppermute | solution.py:241
  30.1 2.2 %collective-permute-done.4 = f32[128,128]{1,0:T(8,128)S(1)} collective-permute-done((f32[128,128]{1,0:T(8,128)S(1)}, f32[128,128]{1,0:T(8,128)S(1)}, u32[]{:S(2)}, u32[]{:S(2)}) %collective-permute-start.4) | collective-permute-done | bytes 65568 | tf_op jit(solution)/shard_map/ppermute | solution.py:241
  32.3 1.7 %collective-permute-start.5 = (f32[128,128]{1,0:T(8,128)S(1)}, f32[128,128]{1,0:T(8,128)S(1)}, u32[]{:S(2)}, u32[]{:S(2)}) collective-permute-start(f32[128,128]{1,0:T(8,128)S(1)} %add.17), channel_id=1, source_target_pairs={{1,0},{0,1},{3,2},{2,3},{5,4},{4,5},{7,6},{6,7},{9,8},{8,9},{11,10... | collective-permute-start | bytes 196616 | tf_op jit(solution)/shard_map/ppermute | solution.py:241
  34.0 0.0 copy-done.7
  34.0 4.3 %forward.1 = (bf16[128,2048]{1,0:T(8,128)(2,1)}, bf16[128,2048]{1,0:T(8,128)(2,1)}) custom-call(bf16[128,2048]{1,0:T(8,128)(2,1)S(1)} %bitcast.10, bf16[128,2048]{1,0:T(8,128)(2,1)S(1)} %bitcast.14, bf16[128,2048]{1,0:T(8,128)(2,1)S(1)} %collective-permute-done.other_ref.kv_prev_ref, bf16[128,2048]{1,0:T(8,128)(2,1)S(1)} %bitcast.18, ...), custom_call_target="tpu_custom_call" | custom-call | flops 1073741824 | bytes 3703296 | tf_op jit(solution)/shard_map/forward/pallas_call | solution.py:166
  38.3 0.0 collective-permute-done.5
  38.3 2.6 %collective-permute-start.6 = (f32[128,128]{1,0:T(8,128)S(1)}, f32[128,128]{1,0:T(8,128)S(1)}, u32[]{:S(2)}, u32[]{:S(2)}) collective-permute-start(f32[128,128]{1,0:T(8,128)S(1)} %add.18), channel_id=1, source_target_pairs={{2,0},{3,1},{0,2},{1,3},{6,4},{7,5},{4,6},{5,7},{10,8},{11,9},{8,1... | collective-permute-start | bytes 196616 | tf_op jit(solution)/shard_map/ppermute | solution.py:241
  41.0 0.0 collective-permute-done.1.other_ref
  41.0 4.4 %backward.1 = (bf16[128,2048]{1,0:T(8,128)(2,1)}, bf16[128,2048]{1,0:T(8,128)(2,1)}) custom-call(bf16[128,2048]{1,0:T(8,128)(2,1)S(1)} %bitcast.23, bf16[128,2048]{1,0:T(8,128)(2,1)S(1)} %bitcast.19, bf16[128,2048]{1,0:T(8,128)(2,1)S(1)} %collective-permute-done.1.other_ref, bf16[128,2048]{1,0:T(8,128)(2,1)S(1)} %bitcast.15, bf16[128,2048]{1,0:T(8,128)(2,1)S(1)} %bitcast.11, ...), custom_call_target="tpu_custom_call" | custom-call | flops 1073741824 | bytes 3703296 | tf_op jit(solution)/shard_map/backward/pallas_call | solution.py:166
  45.3 0.0 collective-permute-done.6
  45.3 0.6 %add.19 = f32[128,128]{1,0:T(8,128)} add(f32[128,128]{1,0:T(8,128)S(1)} %add.18, f32[128,128]{1,0:T(8,128)S(1)} %collective-permute-done.6) | non-fusion elementwise | flops 16384 | bytes 196608 | tf_op jit(solution)/shard_map/add | solution.py:244
  (4 shorter events, 0.0 us)
Async XLA Ops:
  0.6 0.7 %copy-start.6 = (s32[1,128]{1,0:T(1,128)S(1)}, s32[1,128]{1,0:T(1,128)}, u32[]{:S(2)}) copy-start(s32[1,128]{1,0:T(1,128)} %starts_ref.7) | copy-start | bytes 1540
  1.3 1.0 %copy-start = (bf16[1,128,2048]{2,1,0:T(8,128)(2,1)S(1)}, bf16[1,128,2048]{2,1,0:T(8,128)(2,1)}, u32[]{:S(2)}) copy-start(bf16[1,128,2048]{2,1,0:T(8,128)(2,1)} %param.7) | copy-start | bytes 1572868
  2.3 1.0 %copy-start.2 = (bf16[1,128,2048]{2,1,0:T(8,128)(2,1)S(1)}, bf16[1,128,2048]{2,1,0:T(8,128)(2,1)}, u32[]{:S(2)}) copy-start(bf16[1,128,2048]{2,1,0:T(8,128)(2,1)} %param.8) | copy-start | bytes 1572868
  3.4 2.9 %copy-start.4 = (bf16[1,128,2048]{2,1,0:T(8,128)(2,1)S(1)}, bf16[1,128,2048]{2,1,0:T(8,128)(2,1)}, u32[]{:S(2)}) copy-start(bf16[1,128,2048]{2,1,0:T(8,128)(2,1)} %param.6) | copy-start | bytes 1572868
  3.4 2.9 %copy-start.5 = (bf16[1,128,2048]{2,1,0:T(8,128)(2,1)S(1)}, bf16[1,128,2048]{2,1,0:T(8,128)(2,1)}, u32[]{:S(2)}) copy-start(bf16[1,128,2048]{2,1,0:T(8,128)(2,1)} %param.9) | copy-start | bytes 1572868
  3.8 4.1 %collective-permute-start = (bf16[128,2048]{1,0:T(8,128)(2,1)S(1)}, bf16[128,2048]{1,0:T(8,128)(2,1)S(1)}, u32[]{:S(2)}, u32[]{:S(2)}) collective-permute-start(bf16[128,2048]{1,0:T(8,128)(2,1)S(1)} %sent_kv.1), channel_id=1, source_target_pairs={{0,4},{4,8},{8,12},{12,16},{16,20},{20,24},{24,28},{1,5},{5,9},{9,... | collective-permute-start | bytes 1572872 | tf_op jit(solution)/shard_map/ppermute | solution.py:222
  6.2 1.7 %copy-start.1 = (bf16[1,128,2048]{2,1,0:T(8,128)(2,1)S(1)}, bf16[1,128,2048]{2,1,0:T(8,128)(2,1)}, u32[]{:S(2)}) copy-start(bf16[1,128,2048]{2,1,0:T(8,128)(2,1)} %param.7) | copy-start | bytes 1572868
  6.3 1.7 %copy-start.3 = (bf16[1,128,2048]{2,1,0:T(8,128)(2,1)S(1)}, bf16[1,128,2048]{2,1,0:T(8,128)(2,1)}, u32[]{:S(2)}) copy-start(bf16[1,128,2048]{2,1,0:T(8,128)(2,1)} %param.8) | copy-start | bytes 1572868
  6.6 34.3 %collective-permute-start.1 = (bf16[128,2048]{1,0:T(8,128)(2,1)S(1)}, bf16[128,2048]{1,0:T(8,128)(2,1)S(1)}, u32[]{:S(2)}, u32[]{:S(2)}) collective-permute-start(bf16[128,2048]{1,0:T(8,128)(2,1)S(1)} %sent_cot.1), channel_id=1, source_target_pairs={{4,0},{8,4},{12,8},{16,12},{20,16},{24,20},{28,24},{5,1},{9,5},{13... | collective-permute-start | bytes 1572872 | tf_op jit(solution)/shard_map/ppermute | solution.py:222
  11.7 7.9 %collective-permute-start.2 = (f32[128,128]{1,0:T(8,128)S(1)}, f32[128,128]{1,0:T(8,128)S(1)}, u32[]{:S(2)}, u32[]{:S(2)}) collective-permute-start(f32[128,128]{1,0:T(8,128)S(1)} %filter_share.1), channel_id=1, source_target_pairs={{4,0},{0,4},{12,8},{8,12},{20,16},{16,20},{28,24},{24,28},{5,1},{1... | collective-permute-start | bytes 196616 | tf_op jit(solution)/shard_map/ppermute | solution.py:241
  19.7 6.5 %collective-permute-start.3 = (f32[128,128]{1,0:T(8,128)S(1)}, f32[128,128]{1,0:T(8,128)S(1)}, u32[]{:S(2)}, u32[]{:S(2)}) collective-permute-start(f32[128,128]{1,0:T(8,128)S(1)} %add.15), channel_id=1, source_target_pairs={{8,0},{12,4},{0,8},{4,12},{24,16},{28,20},{16,24},{20,28},{9,1},{1... | collective-permute-start | bytes 196616 | tf_op jit(solution)/shard_map/ppermute | solution.py:241
  26.2 7.8 %copy-start.7 = (bf16[128,128]{1,0:T(8,128)(2,1)S(1)}, bf16[128,128]{1,0:T(8,128)(2,1)}, u32[]{:S(2)}) copy-start(bf16[128,128]{1,0:T(8,128)(2,1)} %taps_ref.3) | copy-start | bytes 98308
  26.2 6.1 %collective-permute-start.4 = (f32[128,128]{1,0:T(8,128)S(1)}, f32[128,128]{1,0:T(8,128)S(1)}, u32[]{:S(2)}, u32[]{:S(2)}) collective-permute-start(f32[128,128]{1,0:T(8,128)S(1)} %add.16), channel_id=1, source_target_pairs={{16,0},{20,4},{24,8},{28,12},{0,16},{4,20},{8,24},{12,28},{17,1},{... | collective-permute-start | bytes 196616 | tf_op jit(solution)/shard_map/ppermute | solution.py:241
  32.3 6.0 %collective-permute-start.5 = (f32[128,128]{1,0:T(8,128)S(1)}, f32[128,128]{1,0:T(8,128)S(1)}, u32[]{:S(2)}, u32[]{:S(2)}) collective-permute-start(f32[128,128]{1,0:T(8,128)S(1)} %add.17), channel_id=1, source_target_pairs={{1,0},{0,1},{3,2},{2,3},{5,4},{4,5},{7,6},{6,7},{9,8},{8,9},{11,10... | collective-permute-start | bytes 196616 | tf_op jit(solution)/shard_map/ppermute | solution.py:241
  38.3 7.0 %collective-permute-start.6 = (f32[128,128]{1,0:T(8,128)S(1)}, f32[128,128]{1,0:T(8,128)S(1)}, u32[]{:S(2)}, u32[]{:S(2)}) collective-permute-start(f32[128,128]{1,0:T(8,128)S(1)} %add.18), channel_id=1, source_target_pairs={{2,0},{3,1},{0,2},{1,3},{6,4},{7,5},{4,6},{5,7},{10,8},{11,9},{8,1... | collective-permute-start | bytes 196616 | tf_op jit(solution)/shard_map/ppermute | solution.py:241

commit v5 on v4

--- a/solution.py
+++ b/solution.py
@@ -70,10 +70,6 @@
 def sent_product(a, b, keep):
     out = a.astype(jnp.float32) * b.astype(jnp.float32)
     return jnp.where(keep, out, 0.0).astype(jnp.bfloat16)
-
-
-def sent_cot_kernel(a_ref, b_ref, starts_ref, out_ref):
-    out_ref[...] = sent_product(a_ref[...], b_ref[...], kept_rows(starts_ref, a_ref.shape[0], False))
 
 
 def sent_kv_kernel(a_hbm, b_hbm, starts_hbm, out_ref, a_ref, b_ref, starts_ref, sems):
@@ -129,28 +125,48 @@
     out_ref[...] = reversed_taps(diagonal) * scale
 
 
-def conv_kernel(a_ref, b_ref, other_ref, c_ref, d_ref, starts_ref, taps_ref, out_c_ref, out_d_ref, mask_ref, taps_scr, *, backward):
+def tables_kernel(q_ref, dy_ref, starts_ref, taps_ref, sent_cot_ref, fwd_ref, back_ref, fwd_mask_ref, back_mask_ref):
+    rows = q_ref.shape[0]
+    groups = taps_ref.shape[0]
+    own, previous, following = contig_masks(starts_ref)
+    fwd_mask_ref[:, :rows] = own.astype(jnp.bfloat16)
+    fwd_mask_ref[:, rows:] = previous.astype(jnp.bfloat16)
+    back_mask_ref[:, :rows] = own.T.astype(jnp.bfloat16)
+    back_mask_ref[:, rows:] = following.astype(jnp.bfloat16)
+    sent_cot_ref[...] = sent_product(dy_ref[...], q_ref[...], kept_rows(starts_ref, rows, False))
+
+    def circulant(row):
+        wide = pltpu.roll(jnp.broadcast_to(row, (rows, rows)), 0, 1, stride=1, stride_axis=0)
+        return wide.astype(jnp.bfloat16)
+
+    def some(i, carry):
+        at = pl.multiple_of(i * 16, 16)
+        taps = taps_ref[pl.ds(at, 16), :].astype(jnp.float32)
+        flipped = reversed_taps(taps)
+        for g in range(16):
+            wide = circulant(flipped[g : g + 1])
+            fwd_ref[at + g, :, :rows] = wide * fwd_mask_ref[:, :rows]
+            fwd_ref[at + g, :, rows:] = wide * fwd_mask_ref[:, rows:]
+            wide = circulant(taps[g : g + 1])
+            back_ref[at + g, :, :rows] = wide * back_mask_ref[:, :rows]
+            back_ref[at + g, :, rows:] = wide * back_mask_ref[:, rows:]
+        return carry
+
+    lax.fori_loop(0, groups // 16, some, 0)
+
+
+def conv_kernel(a_ref, b_ref, other_ref, c_ref, d_ref, tables_ref, out_c_ref, out_d_ref):
     rows = a_ref.shape[0]
     per_tile = LANES // GSIZE
-
-    own, previous, following = contig_masks(starts_ref)
-    mask_ref[:, :rows] = (own.T if backward else own).astype(jnp.bfloat16)
-    mask_ref[:, rows:] = (following if backward else previous).astype(jnp.bfloat16)
-    taps_scr[...] = taps_ref[...].astype(jnp.float32) if backward else reversed_taps(taps_ref[...])
     group = lane_groups()
-
-    def table(row):
-        wide = pltpu.roll(jnp.broadcast_to(row, (rows, rows)), 0, 1, stride=1, stride_axis=0)
-        wide = wide.astype(jnp.bfloat16)
-        return jnp.concatenate([wide, wide], axis=1) * mask_ref[...]
 
     def tile(index):
         lanes = pl.ds(pl.multiple_of(index * LANES, LANES), LANES)
         x = jnp.concatenate([product(a_ref[:, lanes], b_ref[:, lanes]), other_ref[:, lanes]], axis=0)
-        taps = taps_scr[pl.ds(pl.multiple_of(index * per_tile, per_tile), per_tile), :]
         y = jnp.zeros((rows, LANES), jnp.float32)
         for g in range(per_tile):
-            y = jnp.where(group == g, jnp.dot(table(taps[g : g + 1]), x, preferred_element_type=jnp.float32), y)
+            table = tables_ref[index * per_tile + g]
+            y = jnp.where(group == g, jnp.dot(table, x, preferred_element_type=jnp.float32), y)
         out_c_ref[:, lanes] = (c_ref[:, lanes].astype(jnp.float32) * y).astype(jnp.bfloat16)
         out_d_ref[:, lanes] = (d_ref[:, lanes].astype(jnp.float32) * y).astype(jnp.bfloat16)
 
@@ -160,7 +176,7 @@
 VMEM = pl.BlockSpec(memory_space=pltpu.VMEM)
 
 
-def local_call(kernel, name, out_shape, scratch_shapes, flops, operands, placed=VMEM):
+def local_call(kernel, name, out_shape, scratch_shapes, flops, operands, placed=VMEM, limit=24):
     outs = out_shape if isinstance(out_shape, list) else [out_shape]
     moved = sum(math.prod(x.shape) * x.dtype.itemsize for x in [*operands, *outs])
     return pl.pallas_call(
@@ -170,7 +186,7 @@
         out_specs=[VMEM] * len(outs) if isinstance(out_shape, list) else VMEM,
         scratch_shapes=scratch_shapes,
         cost_estimate=pl.CostEstimate(flops=flops, bytes_accessed=moved, transcendentals=0),
-        compiler_params=pltpu.CompilerParams(vmem_limit_bytes=24 << 20),
+        compiler_params=pltpu.CompilerParams(vmem_limit_bytes=limit << 20),
         name=name,
     )(*operands)
 
@@ -180,14 +196,18 @@
     return local_call(
         sent_kv_kernel, "sent_kv", jax.ShapeDtypeStruct(k.shape, jnp.bfloat16),
         [whole, whole, pltpu.VMEM(starts.shape, starts.dtype), pltpu.SemaphoreType.DMA((5,))],
-        2 * k.size, (k, v, starts), pl.BlockSpec(memory_space=pltpu.HBM),
-    )
-
-
-def sent_cot(dy, q, starts):
-    return local_call(
-        sent_cot_kernel, "sent_cot", jax.ShapeDtypeStruct(q.shape, jnp.bfloat16),
-        [], 2 * q.size, (dy, q, starts),
+        2 * k.size, (k, v, starts), pl.BlockSpec(memory_space=pltpu.HBM), 60,
+    )
+
+
+def tables_and_cot(q, dy, starts, filters):
+    rows, width = q.shape
+    groups = filters.shape[0]
+    tables = jax.ShapeDtypeStruct((groups, rows, 2 * rows), jnp.bfloat16)
+    mask = pltpu.VMEM((rows, 2 * rows), jnp.bfloat16)
+    return local_call(
+        tables_kernel, "tables", [jax.ShapeDtypeStruct((rows, width), jnp.bfloat16), tables, tables],
+        [mask, mask], 64 * rows * rows * width, (q, dy, starts, filters),
     )
 
 
@@ -195,24 +215,18 @@
     rows, width = q.shape
     table = pltpu.VMEM((rows, rows), jnp.float32)
     return local_call(
-        functools.partial(filter_kernel, scale=scale),
-        "filter_share",
+        functools.partial(filter_kernel, scale=scale), "filter_share",
         jax.ShapeDtypeStruct((groups, rows), jnp.float32),
         [table, table, pltpu.VMEM((groups * 8, rows), jnp.float32)],
-        32 * rows * rows * width,
-        (q, k, v, dy, kv_prev, starts),
-    )
-
-
-def convolution(a, b, other, c, d, starts, filters, backward):
+        32 * rows * rows * width, (q, k, v, dy, kv_prev, starts),
+    )
+
+
+def convolution(a, b, other, c, d, tables, name):
     rows, width = a.shape
-    return local_call(
-        functools.partial(conv_kernel, backward=backward),
-        "backward" if backward else "forward",
-        [jax.ShapeDtypeStruct((rows, width), jnp.bfloat16)] * 2,
-        [pltpu.VMEM((rows, 2 * rows), jnp.bfloat16), pltpu.VMEM(filters.shape, jnp.float32)],
-        32 * rows * rows * width,
-        (a, b, other, c, d, starts, filters),
+    out = jax.ShapeDtypeStruct((rows, width), jnp.bfloat16)
+    return local_call(
+        conv_kernel, name, [out, out], [], 32 * rows * rows * width, (a, b, other, c, d, tables)
     )
 
 
@@ -232,20 +246,25 @@
     return found
 
 
-def summed_along(total, axis):
-    size = lax.axis_size(axis)
-    stride = 1
-    for p in factors(size):
-        turned = lambda i, k: i + ((i // stride + k) % p - i // stride % p) * stride
-        got = [
-            lax.ppermute(total, axis, [(turned(i, k), i) for i in range(size)]) for k in range(1, p)
-        ]
-        if p == 2:
-            total = total + got[0]
-        else:
-            digit = lax.axis_index(axis) // stride % p
-            total = jnp.sum(jnp.roll(jnp.stack([total, *got]), digit, axis=0), axis=0)
-        stride *= p
+def summed_everywhere(total, beside):
+    done = 0
+    for axis in ("ctx", "dp"):
+        size = lax.axis_size(axis)
+        stride = 1
+        for p in factors(size):
+            if done in beside:
+                total, _ = lax.optimization_barrier((total, beside[done]))
+            turned = lambda i, k: i + ((i // stride + k) % p - i // stride % p) * stride
+            got = [
+                lax.ppermute(total, axis, [(turned(i, k), i) for i in range(size)]) for k in range(1, p)
+            ]
+            if p == 2:
+                total = total + got[0]
+            else:
+                digit = lax.axis_index(axis) // stride % p
+                total = jnp.sum(jnp.roll(jnp.stack([total, *got]), digit, axis=0), axis=0)
+            stride *= p
+            done += 1
     return total
 
 
@@ -256,11 +275,13 @@
     assert rows == taps == LANES
     scale = 1.0 / math.sqrt(rows * lax.axis_size("ctx") * lax.axis_size("dp") * GSIZE)
     kv_prev = passed_along(sent_kv(k, v, contig_starts), "ctx", 1)
-    cot_next = passed_along(sent_cot(dy, q, contig_starts), "ctx", -1)
+    cot_out, fwd_tables, back_tables = tables_and_cot(q, dy, contig_starts, filters)
+    cot_next = passed_along(cot_out, "ctx", -1)
     share = filter_share(q, k, v, dy, kv_prev, contig_starts, groups, scale)
-    filter_grad = summed_along(summed_along(share, "ctx"), "dp")
-    mixed, grad_q = convolution(k, v, kv_prev, q, dy, contig_starts, filters, False)
-    grad_k, grad_v = convolution(dy, q, cot_next, v, k, contig_starts, filters, True)
+    mixed, grad_q = convolution(k, v, kv_prev, q, dy, fwd_tables, "forward")
+    grad_k, grad_v = convolution(dy, q, cot_next, v, k, back_tables, "backward")
+    beside = {2: (mixed, grad_q), 4: (grad_k, grad_v)}
+    filter_grad = summed_everywhere(share, beside)
     return (mixed[None], grad_q[None], grad_k[None], grad_v[None], filter_grad)
 
 

time: 46.2 us -> 46 us (level)
  starting transfers between devices: 22.8 us -> 14.8 us
  Pallas kernels: 13.2 us -> 19 us
  waiting for transfers between devices: 5.77 us -> 6.85 us
  local copies, waits for them, and re-layouts: 2.76 us -> 3.5 us
    ppermute x5, starting transfers between devices: 19.1 us -> 11.2 us  [summed_everywhere(): lax.ppermute(total, axis, [(turned(i, k), i) for i in range(size)])]
    pallas_call x5, Pallas kernels: 13.2 us -> 19 us  [local_call(): pl.pallas_call(kernel, out_shape=out_shape, in_specs=[placed] * len(opera...]
    ppermute x5, waiting for transfers between devices: 5.76 us -> 6.85 us  [summed_everywhere(): lax.ppermute(total, axis, [(turned(i, k), i) for i in range(size)])]
    unnamed x16 -> x14, local copies, waits for them, and re-layouts: 2.76 us -> 3.5 us
  transfers between devices with their start and end apart: 7 -> 7, of which waited for: 3 -> 3; matrix products, arithmetic and copies ran while one was open for 0% -> 0% of each run, Pallas kernels for 28% -> 37%
where the time goes in v5:
time: 46 us; the launch traced here: 45.6 us
  Pallas kernels  19 us (41%)
  starting transfers between devices  14.8 us (32%)
  waiting for transfers between devices  6.85 us (15%)
  local copies, waits for them, and re-layouts  3.5 us (8%)
  between operations  0.76 us (2%)
  other arithmetic  0.67 us (1%)
    pallas_call x5, Pallas kernels, local_call(): pl.pallas_call(kernel, out_shape=out_shape, in_specs=[placed] * len(opera...  19 us
    ppermute x5, starting transfers between devices, summed_everywhere(): lax.ppermute(total, axis, [(turned(i, k), i) for i in range(size)])  11.2 us
    ppermute x5, waiting for transfers between devices, summed_everywhere(): lax.ppermute(total, axis, [(turned(i, k), i) for i in range(size)])  6.85 us
    ppermute x2, starting transfers between devices, passed_along(): return lax.ppermute(block, axis, route)  3.68 us
    unnamed x14, local copies, waits for them, and re-layouts  3.5 us
  transfers between devices with their start and end apart: 7, of which 3 were waited for; matrix products, arithmetic and copies ran while one was open for 0% of the time, Pallas kernels for 37%

profile of v5, /device:TPU:0, one launch (start us, length us, event | category | flops | bytes accessed | tf_op | source)
XLA Modules:
  0.0 45.6 jit_solution(1859404083838798415)
XLA Ops:
  0.6 0.0 copy-start
  0.6 0.0 copy-start.1
  0.7 0.0 copy-start.4
  0.7 2.2 %sent_kv.1 = bf16[128,2048]{1,0:T(8,128)(2,1)} custom-call(bf16[128,2048]{1,0:T(8,128)(2,1)} %bitcast.8, bf16[128,2048]{1,0:T(8,128)(2,1)} %bitcast.12, s32[1,128]{1,0:T(1,128)} %starts_ref.3), custom_call_target="tpu_custom_call" | custom-call | flops 524288 | bytes 1573376 | tf_op jit(solution)/shard_map/sent_kv/pallas_call | solution.py:182
  2.9 2.4 %collective-permute-start = (bf16[128,2048]{1,0:T(8,128)(2,1)}, bf16[128,2048]{1,0:T(8,128)(2,1)S(1)}, u32[]{:S(2)}, u32[]{:S(2)}) collective-permute-start(bf16[128,2048]{1,0:T(8,128)(2,1)} %sent_kv.1), channel_id=1, source_target_pairs={{0,4},{4,8},{8,12},{12,16},{16,20},{20,24},{24,28},{1,5},{5,9},{9,... | collective-permute-start | bytes 1572872 | tf_op jit(solution)/shard_map/ppermute | solution.py:236
  5.3 0.0 copy-start.2
  5.3 1.0 %copy-done.2 = bf16[1,128,2048]{2,1,0:T(8,128)(2,1)S(1)} copy-done((bf16[1,128,2048]{2,1,0:T(8,128)(2,1)S(1)}, bf16[1,128,2048]{2,1,0:T(8,128)(2,1)}, u32[]{:S(2)}) %copy-start.2) | copy-done | bytes 524312
  6.3 0.0 copy-start.3
  6.3 1.0 %copy-done.3 = bf16[1,128,2048]{2,1,0:T(8,128)(2,1)S(1)} copy-done((bf16[1,128,2048]{2,1,0:T(8,128)(2,1)S(1)}, bf16[1,128,2048]{2,1,0:T(8,128)(2,1)}, u32[]{:S(2)}) %copy-start.3) | copy-done | bytes 524312
  7.4 0.0 copy-start.5
  7.4 0.7 %copy-done.5 = s32[1,128]{1,0:T(1,128)S(1)} copy-done((s32[1,128]{1,0:T(1,128)S(1)}, s32[1,128]{1,0:T(1,128)}, u32[]{:S(2)}) %copy-start.5) | copy-done | bytes 536
  8.0 0.0 copy-start.6
  8.0 0.8 %copy-done.6 = bf16[128,128]{1,0:T(8,128)(2,1)S(1)} copy-done((bf16[128,128]{1,0:T(8,128)(2,1)S(1)}, bf16[128,128]{1,0:T(8,128)(2,1)}, u32[]{:S(2)}) %copy-start.6) | copy-done | bytes 32792
  8.8 5.0 %tables.1 = (bf16[128,2048]{1,0:T(8,128)(2,1)S(1)}, bf16[128,128,256]{2,1,0:T(8,128)(2,1)S(1)}, bf16[128,128,256]{2,1,0:T(8,128)(2,1)S(1)}) custom-call(bf16[128,2048]{1,0:T(8,128)(2,1)S(1)} %bitcast.16, bf16[128,2048]{1,0:T(8,128)(2,1)S(1)} %bitcast.20, s32[1,128]{1,0:T(1,128)S(1)} %copy-done.5, bf16[128,128]{1,0:T(8,128)(2,1)S(1)} %copy-done.6), custom_call_target="tpu_custom_call" | custom-call | flops 2147483648 | bytes 18383360 | tf_op jit(solution)/shard_map/tables/pallas_call | solution.py:182
  13.9 1.3 %collective-permute-start.1 = (bf16[128,2048]{1,0:T(8,128)(2,1)S(1)}, bf16[128,2048]{1,0:T(8,128)(2,1)S(1)}, u32[]{:S(2)}, u32[]{:S(2)}) collective-permute-start(bf16[128,2048]{1,0:T(8,128)(2,1)S(1)} %get-tuple-element.17), channel_id=1, source_target_pairs={{4,0},{8,4},{12,8},{16,12},{20,16},{24,20},{28,24},{5,1},{9,5},{13... | collective-permute-start | bytes 1572872 | tf_op jit(solution)/shard_map/ppermute | solution.py:236
  15.2 0.0 collective-permute-done.other_ref.kv_prev_ref
  15.2 0.0 copy-done
  15.2 0.0 copy-done.1
  15.2 0.0 copy-done.4
  15.2 3.7 %filter_share.1 = f32[128,128]{1,0:T(8,128)S(1)} custom-call(bf16[128,2048]{1,0:T(8,128)(2,1)S(1)} %bitcast.17, bf16[128,2048]{1,0:T(8,128)(2,1)S(1)} %bitcast.9, bf16[128,2048]{1,0:T(8,128)(2,1)S(1)} %bitcast.13, bf16[128,2048]{1,0:T(8,128)(2,1)S(1)} %bitcast.21, bf16[128,2048]{1,0:T(8,128)(2,1)S(1)} %collective-permute-done.other_ref.kv_prev_ref, ...), custom_call_target="tpu_custom_call" | custom-call | flops 1073741824 | bytes 2687488 | tf_op jit(solution)/shard_map/filter_share/pallas_call | solution.py:182
  18.9 3.3 %collective-permute-start.2 = (f32[128,128]{1,0:T(8,128)S(1)}, f32[128,128]{1,0:T(8,128)S(1)}, u32[]{:S(2)}, u32[]{:S(2)}) collective-permute-start(f32[128,128]{1,0:T(8,128)S(1)} %filter_share.1), channel_id=1, source_target_pairs={{4,0},{0,4},{12,8},{8,12},{20,16},{16,20},{28,24},{24,28},{5,1},{1... | collective-permute-start | bytes 196616 | tf_op jit(solution)/shard_map/ppermute | solution.py:259
  22.2 0.9 %collective-permute-done.2 = f32[128,128]{1,0:T(8,128)S(1)} collective-permute-done((f32[128,128]{1,0:T(8,128)S(1)}, f32[128,128]{1,0:T(8,128)S(1)}, u32[]{:S(2)}, u32[]{:S(2)}) %collective-permute-start.2) | collective-permute-done | bytes 65568 | tf_op jit(solution)/shard_map/ppermute | solution.py:259
  23.1 2.0 %collective-permute-start.3 = (f32[128,128]{1,0:T(8,128)S(1)}, f32[128,128]{1,0:T(8,128)S(1)}, u32[]{:S(2)}, u32[]{:S(2)}) collective-permute-start(f32[128,128]{1,0:T(8,128)S(1)} %add.15), channel_id=1, source_target_pairs={{8,0},{12,4},{0,8},{4,12},{24,16},{28,20},{16,24},{20,28},{9,1},{1... | collective-permute-start | bytes 196616 | tf_op jit(solution)/shard_map/ppermute | solution.py:259
  25.2 4.0 %forward.1 = (bf16[128,2048]{1,0:T(8,128)(2,1)}, bf16[128,2048]{1,0:T(8,128)(2,1)}) custom-call(bf16[128,2048]{1,0:T(8,128)(2,1)S(1)} %bitcast.10, bf16[128,2048]{1,0:T(8,128)(2,1)S(1)} %bitcast.14, bf16[128,2048]{1,0:T(8,128)(2,1)S(1)} %collective-permute-done.other_ref.kv_prev_ref, bf16[128,2048]{1,0:T(8,128)(2,1)S(1)} %bitcast.18, ...), custom_call_target="tpu_custom_call" | custom-call | flops 1073741824 | bytes 12058624 | tf_op jit(solution)/shard_map/forward/pallas_call | solution.py:182
  29.2 0.0 collective-permute-done.3
  29.2 1.6 %collective-permute-start.4 = (f32[128,128]{1,0:T(8,128)S(1)}, f32[128,128]{1,0:T(8,128)S(1)}, u32[]{:S(2)}, u32[]{:S(2)}) collective-permute-start(f32[128,128]{1,0:T(8,128)S(1)} %add.16), channel_id=1, source_target_pairs={{16,0},{20,4},{24,8},{28,12},{0,16},{4,20},{8,24},{12,28},{17,1},{... | collective-permute-start | bytes 196616 | tf_op jit(solution)/shard_map/ppermute | solution.py:259
  30.8 2.8 %collective-permute-done.4 = f32[128,128]{1,0:T(8,128)S(1)} collective-permute-done((f32[128,128]{1,0:T(8,128)S(1)}, f32[128,128]{1,0:T(8,128)S(1)}, u32[]{:S(2)}, u32[]{:S(2)}) %collective-permute-start.4) | collective-permute-done | bytes 65568 | tf_op jit(solution)/shard_map/ppermute | solution.py:259
  33.5 1.6 %collective-permute-start.5 = (f32[128,128]{1,0:T(8,128)S(1)}, f32[128,128]{1,0:T(8,128)S(1)}, u32[]{:S(2)}, u32[]{:S(2)}) collective-permute-start(f32[128,128]{1,0:T(8,128)S(1)} %add.17), channel_id=1, source_target_pairs={{1,0},{0,1},{3,2},{2,3},{5,4},{4,5},{7,6},{6,7},{9,8},{8,9},{11,10... | collective-permute-start | bytes 196616 | tf_op jit(solution)/shard_map/ppermute | solution.py:259
  35.2 0.0 collective-permute-done.1.other_ref
  35.2 4.0 %backward.1 = (bf16[128,2048]{1,0:T(8,128)(2,1)}, bf16[128,2048]{1,0:T(8,128)(2,1)}) custom-call(bf16[128,2048]{1,0:T(8,128)(2,1)S(1)} %bitcast.23, bf16[128,2048]{1,0:T(8,128)(2,1)S(1)} %bitcast.19, bf16[128,2048]{1,0:T(8,128)(2,1)S(1)} %collective-permute-done.1.other_ref, bf16[128,2048]{1,0:T(8,128)(2,1)S(1)} %bitcast.15, bf16[128,2048]{1,0:T(8,128)(2,1)S(1)} %bitcast.11, ...), custom_call_target="tpu_custom_call" | custom-call | flops 1073741824 | bytes 12058624 | tf_op jit(solution)/shard_map/backward/pallas_call | solution.py:182
  39.1 0.0 collective-permute-done.5
  39.2 2.6 %collective-permute-start.6 = (f32[128,128]{1,0:T(8,128)S(1)}, f32[128,128]{1,0:T(8,128)S(1)}, u32[]{:S(2)}, u32[]{:S(2)}) collective-permute-start(f32[128,128]{1,0:T(8,128)S(1)} %add.18), channel_id=1, source_target_pairs={{2,0},{3,1},{0,2},{1,3},{6,4},{7,5},{4,6},{5,7},{10,8},{11,9},{8,1... | collective-permute-start | bytes 196616 | tf_op jit(solution)/shard_map/ppermute | solution.py:259
  41.8 3.2 %collective-permute-done.6 = f32[128,128]{1,0:T(8,128)S(1)} collective-permute-done((f32[128,128]{1,0:T(8,128)S(1)}, f32[128,128]{1,0:T(8,128)S(1)}, u32[]{:S(2)}, u32[]{:S(2)}) %collective-permute-start.6) | collective-permute-done | bytes 65568 | tf_op jit(solution)/shard_map/ppermute | solution.py:259
  45.0 0.6 %add.19 = f32[128,128]{1,0:T(8,128)} add(f32[128,128]{1,0:T(8,128)S(1)} %add.18, f32[128,128]{1,0:T(8,128)S(1)} %collective-permute-done.6) | non-fusion elementwise | flops 16384 | bytes 196608 | tf_op jit(solution)/shard_map/add | solution.py:262
  (4 shorter events, 0.0 us)
Async XLA Ops:
  0.6 14.5 %copy-start = (bf16[1,128,2048]{2,1,0:T(8,128)(2,1)S(1)}, bf16[1,128,2048]{2,1,0:T(8,128)(2,1)}, u32[]{:S(2)}) copy-start(bf16[1,128,2048]{2,1,0:T(8,128)(2,1)} %param.7) | copy-start | bytes 1572868
  0.6 14.5 %copy-start.1 = (bf16[1,128,2048]{2,1,0:T(8,128)(2,1)S(1)}, bf16[1,128,2048]{2,1,0:T(8,128)(2,1)}, u32[]{:S(2)}) copy-start(bf16[1,128,2048]{2,1,0:T(8,128)(2,1)} %param.8) | copy-start | bytes 1572868
  0.7 14.5 %copy-start.4 = (bf16[1,128,2048]{2,1,0:T(8,128)(2,1)S(1)}, bf16[1,128,2048]{2,1,0:T(8,128)(2,1)}, u32[]{:S(2)}) copy-start(bf16[1,128,2048]{2,1,0:T(8,128)(2,1)} %param.9) | copy-start | bytes 1572868
  2.9 12.3 %collective-permute-start = (bf16[128,2048]{1,0:T(8,128)(2,1)}, bf16[128,2048]{1,0:T(8,128)(2,1)S(1)}, u32[]{:S(2)}, u32[]{:S(2)}) collective-permute-start(bf16[128,2048]{1,0:T(8,128)(2,1)} %sent_kv.1), channel_id=1, source_target_pairs={{0,4},{4,8},{8,12},{12,16},{16,20},{20,24},{24,28},{1,5},{5,9},{9,... | collective-permute-start | bytes 1572872 | tf_op jit(solution)/shard_map/ppermute | solution.py:236
  5.3 1.0 %copy-start.2 = (bf16[1,128,2048]{2,1,0:T(8,128)(2,1)S(1)}, bf16[1,128,2048]{2,1,0:T(8,128)(2,1)}, u32[]{:S(2)}) copy-start(bf16[1,128,2048]{2,1,0:T(8,128)(2,1)} %param.6) | copy-start | bytes 1572868
  6.3 1.0 %copy-start.3 = (bf16[1,128,2048]{2,1,0:T(8,128)(2,1)S(1)}, bf16[1,128,2048]{2,1,0:T(8,128)(2,1)}, u32[]{:S(2)}) copy-start(bf16[1,128,2048]{2,1,0:T(8,128)(2,1)} %param.9) | copy-start | bytes 1572868
  7.4 0.7 %copy-start.5 = (s32[1,128]{1,0:T(1,128)S(1)}, s32[1,128]{1,0:T(1,128)}, u32[]{:S(2)}) copy-start(s32[1,128]{1,0:T(1,128)} %starts_ref.3) | copy-start | bytes 1540
  8.0 0.8 %copy-start.6 = (bf16[128,128]{1,0:T(8,128)(2,1)S(1)}, bf16[128,128]{1,0:T(8,128)(2,1)}, u32[]{:S(2)}) copy-start(bf16[128,128]{1,0:T(8,128)(2,1)} %taps_ref.1) | copy-start | bytes 98308
  13.9 21.3 %collective-permute-start.1 = (bf16[128,2048]{1,0:T(8,128)(2,1)S(1)}, bf16[128,2048]{1,0:T(8,128)(2,1)S(1)}, u32[]{:S(2)}, u32[]{:S(2)}) collective-permute-start(bf16[128,2048]{1,0:T(8,128)(2,1)S(1)} %get-tuple-element.17), channel_id=1, source_target_pairs={{4,0},{8,4},{12,8},{16,12},{20,16},{24,20},{28,24},{5,1},{9,5},{13... | collective-permute-start | bytes 1572872 | tf_op jit(solution)/shard_map/ppermute | solution.py:236
  18.9 4.2 %collective-permute-start.2 = (f32[128,128]{1,0:T(8,128)S(1)}, f32[128,128]{1,0:T(8,128)S(1)}, u32[]{:S(2)}, u32[]{:S(2)}) collective-permute-start(f32[128,128]{1,0:T(8,128)S(1)} %filter_share.1), channel_id=1, source_target_pairs={{4,0},{0,4},{12,8},{8,12},{20,16},{16,20},{28,24},{24,28},{5,1},{1... | collective-permute-start | bytes 196616 | tf_op jit(solution)/shard_map/ppermute | solution.py:259
  23.1 6.0 %collective-permute-start.3 = (f32[128,128]{1,0:T(8,128)S(1)}, f32[128,128]{1,0:T(8,128)S(1)}, u32[]{:S(2)}, u32[]{:S(2)}) collective-permute-start(f32[128,128]{1,0:T(8,128)S(1)} %add.15), channel_id=1, source_target_pairs={{8,0},{12,4},{0,8},{4,12},{24,16},{28,20},{16,24},{20,28},{9,1},{1... | collective-permute-start | bytes 196616 | tf_op jit(solution)/shard_map/ppermute | solution.py:259
  29.2 4.3 %collective-permute-start.4 = (f32[128,128]{1,0:T(8,128)S(1)}, f32[128,128]{1,0:T(8,128)S(1)}, u32[]{:S(2)}, u32[]{:S(2)}) collective-permute-start(f32[128,128]{1,0:T(8,128)S(1)} %add.16), channel_id=1, source_target_pairs={{16,0},{20,4},{24,8},{28,12},{0,16},{4,20},{8,24},{12,28},{17,1},{... | collective-permute-start | bytes 196616 | tf_op jit(solution)/shard_map/ppermute | solution.py:259
  33.5 5.6 %collective-permute-start.5 = (f32[128,128]{1,0:T(8,128)S(1)}, f32[128,128]{1,0:T(8,128)S(1)}, u32[]{:S(2)}, u32[]{:S(2)}) collective-permute-start(f32[128,128]{1,0:T(8,128)S(1)} %add.17), channel_id=1, source_target_pairs={{1,0},{0,1},{3,2},{2,3},{5,4},{4,5},{7,6},{6,7},{9,8},{8,9},{11,10... | collective-permute-start | bytes 196616 | tf_op jit(solution)/shard_map/ppermute | solution.py:259
  39.2 5.8 %collective-permute-start.6 = (f32[128,128]{1,0:T(8,128)S(1)}, f32[128,128]{1,0:T(8,128)S(1)}, u32[]{:S(2)}, u32[]{:S(2)}) collective-permute-start(f32[128,128]{1,0:T(8,128)S(1)} %add.18), channel_id=1, source_target_pairs={{2,0},{3,1},{0,2},{1,3},{6,4},{7,5},{4,6},{5,7},{10,8},{11,9},{8,1... | collective-permute-start | bytes 196616 | tf_op jit(solution)/shard_map/ppermute | solution.py:259

commit v6 on v4

v6 whole, which is shorter than its diff:
```python
import functools
import math

import jax
import jax.numpy as jnp
from jax import lax
from jax.experimental import pallas as pl
from jax.experimental.pallas import tpu as pltpu
from jax.sharding import PartitionSpec as P

GSIZE = 16
LANES = 128
STEP = 4


def product(a, b):
    return (a.astype(jnp.float32) * b.astype(jnp.float32)).astype(jnp.bfloat16)


def contig_masks(starts_ref):
    rows = starts_ref.shape[1]
    starts = jnp.broadcast_to(starts_ref[...], (rows, rows)) > 0
    t = lax.broadcasted_iota(jnp.int32, (rows, rows), 0)
    s = lax.broadcasted_iota(jnp.int32, (rows, rows), 1)
    began = jnp.max(jnp.where(starts & (s <= t), s, 0), axis=1, keepdims=True)
    own = (s <= t) & (s >= began)
    first = jnp.min(jnp.where(starts, s, rows), axis=1, keepdims=True)
    previous = (s > t) & (t < first)
    last = jnp.max(jnp.where(starts, s, 0), axis=1, keepdims=True)
    following = (s < t) & (t >= last)
    as_f32 = lambda mask: jnp.where(mask, 1.0, 0.0).astype(jnp.float32)
    return as_f32(own), as_f32(previous), as_f32(following)


def reversed_taps(rows_of_taps):
    taps = rows_of_taps.shape[1]
    i = lax.broadcasted_iota(jnp.int32, (taps, taps), 0)
    j = lax.broadcasted_iota(jnp.int32, (taps, taps), 1)
    flip = jnp.where((i + j == 0) | (i + j == taps), 1.0, 0.0).astype(jnp.float32)
    return jnp.dot(
        rows_of_taps.astype(jnp.float32), flip,
        preferred_element_type=jnp.float32, precision=lax.Precision.HIGHEST,
    )


def lane_groups():
    return lax.broadcasted_iota(jnp.int32, (1, LANES), 1) // GSIZE


def half_index(partner):
    core = lax.axis_index("ctx") % 2
    return 1 - core if partner else core


def each_tile(tile, width):
    count = width // LANES
    step = math.gcd(count, STEP)

    def body(i, carry):
        for j in range(step):
            tile(i * step + j)
        return carry

    lax.fori_loop(0, count // step, body, 0)


def filter_kernel(
    q_ref, k_ref, v_ref, dy_ref, kv_prev_ref, starts_ref, out_ref, own_ref, prev_ref, sums_ref, *, scale, partner
):
    rows = q_ref.shape[0]
    per_tile = LANES // GSIZE

    own_ref[...], prev_ref[...], _ = contig_masks(starts_ref)

    group = lane_groups()
    width = q_ref.shape[1] // 2
    base = half_index(partner) * width

    def tile(index):
        here = pl.ds(pl.multiple_of(index * LANES, LANES), LANES)
        lanes = pl.ds(pl.multiple_of(base + index * LANES, LANES), LANES)
        cot = product(dy_ref[:, lanes], q_ref[:, lanes])
        kv = jnp.concatenate([product(k_ref[:, lanes], v_ref[:, lanes]), kv_prev_ref[:, here]], axis=0)
        for g in range(per_tile):
            picked = jnp.where(group == g, cot, jnp.zeros_like(cot))
            pairs = lax.dot_general(
                picked, kv, (((1,), (1,)), ((), ())), preferred_element_type=jnp.float32
            )
            linked = pairs[:, :rows] * own_ref[...] + pairs[:, rows:] * prev_ref[...]
            total = linked[:8]
            for i in range(1, rows // 8):
                total = total + pltpu.roll(linked[8 * i : 8 * i + 8], rows - 8 * i, 1)
            at = pl.multiple_of((index * per_tile + g) * 8, 8)
            sums_ref[pl.ds(at, 8), :] = total

    each_tile(tile, width)
    groups = out_ref.shape[0]
    diagonal = sums_ref[pl.ds(0, groups, stride=8), :]
    for r in range(1, 8):
        diagonal = diagonal + pltpu.roll(sums_ref[pl.ds(r, groups, stride=8), :], rows - r, 1)
    out_ref[...] = reversed_taps(diagonal) * scale


def conv_kernel(
    a_ref, b_ref, other_ref, c_ref, d_ref, starts_ref, taps_ref, c_in_hbm, d_in_hbm, out_c_hbm, out_d_hbm,
    mask_ref, taps_scr, out_c_ref, out_d_ref, sems, *, backward, partner,
):
    del c_in_hbm, d_in_hbm
    rows = a_ref.shape[0]
    per_tile = LANES // GSIZE
    width = a_ref.shape[1] // 2
    half = half_index(partner)
    base = half * width
    own, previous, following = contig_masks(starts_ref)
    mask_ref[:, :rows] = (own.T if backward else own).astype(jnp.bfloat16)
    mask_ref[:, rows:] = (following if backward else previous).astype(jnp.bfloat16)
    groups = width // GSIZE
    taps = taps_ref[pl.ds(pl.multiple_of(half * groups, groups), groups), :]
    taps_scr[...] = taps.astype(jnp.float32) if backward else reversed_taps(taps)
    group = lane_groups()

    def table(row):
        wide = pltpu.roll(jnp.broadcast_to(row, (rows, rows)), 0, 1, stride=1, stride_axis=0)
        wide = wide.astype(jnp.bfloat16)
        return jnp.concatenate([wide, wide], axis=1) * mask_ref[...]

    def tile(index):
        here = pl.ds(pl.multiple_of(index * LANES, LANES), LANES)
        lanes = pl.ds(pl.multiple_of(base + index * LANES, LANES), LANES)
        other = other_ref[:, here if other_ref.shape[1] == width else lanes]
        x = jnp.concatenate([product(a_ref[:, lanes], b_ref[:, lanes]), other], axis=0)
        taps = taps_scr[pl.ds(pl.multiple_of(index * per_tile, per_tile), per_tile), :]
        y = jnp.zeros((rows, LANES), jnp.float32)
        for g in range(per_tile):
            y = jnp.where(group == g, jnp.dot(table(taps[g : g + 1]), x, preferred_element_type=jnp.float32), y)
        out_c_ref[:, here] = (c_ref[:, lanes].astype(jnp.float32) * y).astype(jnp.bfloat16)
        out_d_ref[:, here] = (d_ref[:, lanes].astype(jnp.float32) * y).astype(jnp.bfloat16)

    step = math.gcd(width // LANES, STEP) * LANES

    def stored(i):
        here = pl.ds(pl.multiple_of(i * step, step), step)
        there = pl.ds(pl.multiple_of(base + i * step, step), step)
        return [
            pltpu.make_async_copy(out_c_ref.at[:, here], out_c_hbm.at[:, there], sems.at[0, i]),
            pltpu.make_async_copy(out_d_ref.at[:, here], out_d_hbm.at[:, there], sems.at[1, i]),
        ]

    def body(i, carry):
        for j in range(step // LANES):
            tile(i * (step // LANES) + j)
        for copy in stored(i):
            copy.start()
        return carry

    lax.fori_loop(0, width // step, body, 0)
    for i in range(width // step):
        for copy in stored(i):
            copy.wait()


VMEM = pl.BlockSpec(memory_space=pltpu.VMEM)


def local_call(kernel, name, out_shape, scratch_shapes, flops, operands, in_specs=None, out_specs=VMEM, aliases={}):
    outs = out_shape if isinstance(out_shape, list) else [out_shape]
    moved = sum(math.prod(x.shape) * x.dtype.itemsize for x in [*operands, *outs])
    return pl.pallas_call(
        kernel,
        out_shape=out_shape,
        in_specs=in_specs or [VMEM] * len(operands),
        out_specs=out_specs,
        scratch_shapes=scratch_shapes,
        input_output_aliases=aliases,
        cost_estimate=pl.CostEstimate(flops=flops, bytes_accessed=moved, transcendentals=0),
        compiler_params=pltpu.CompilerParams(vmem_limit_bytes=24 << 20),
        name=name,
    )(*operands)


def filter_share(q, k, v, dy, kv_prev, starts, groups, scale, partner):
    rows, width = q.shape
    table = pltpu.VMEM((rows, rows), jnp.float32)
    return local_call(
        functools.partial(filter_kernel, scale=scale, partner=partner),
        "filter_partner" if partner else "filter_own",
        jax.ShapeDtypeStruct((groups // 2, rows), jnp.float32),
        [table, table, pltpu.VMEM((groups * 4, rows), jnp.float32)],
        16 * rows * rows * width, (q, k, v, dy, kv_prev, starts),
    )


def convolution(a, b, other, c, d, starts, filters, outs, backward, partner):
    rows, width = a.shape
    steps = width // 2 // LANES // math.gcd(width // 2 // LANES, STEP)
    out = jax.ShapeDtypeStruct((rows, width), jnp.bfloat16)
    half = pltpu.VMEM((rows, width // 2), jnp.bfloat16)
    anywhere = pl.BlockSpec(memory_space=pl.ANY)
    kernel = functools.partial(conv_kernel, backward=backward, partner=partner)
    operands = (a, b, other, c, d, starts, filters)
    if outs is None:
        body = kernel
        kernel = lambda *refs: body(*refs[:7], None, None, *refs[7:])
    return local_call(
        kernel,
        ("backward" if backward else "forward") + ("_partner" if partner else "_own"),
        [out, out],
        [
            pltpu.VMEM((rows, 2 * rows), jnp.bfloat16), pltpu.VMEM((filters.shape[0] // 2, rows), jnp.float32),
            half, half, pltpu.SemaphoreType.DMA((2, steps)),
        ],
        16 * rows * rows * width,
        operands + tuple(outs or ()),
        [VMEM] * 7 + [anywhere] * (2 if outs else 0),
        [anywhere] * 2,
        {7: 0, 8: 1} if outs else {},
    )


def passed_along(block, axis, distance):
    devices = range(lax.axis_size(axis))
    route = [(i - distance, i) for i in devices if i - distance in devices]
    return lax.ppermute(block, axis, route)


def factors(size):
    found, p = [], 2
    while size > 1:
        while size % p == 0:
            found.append(p)
            size //= p
        p += 1
    return found


def other_core(block):
    size = lax.axis_size("ctx")
    return lax.ppermute(block, "ctx", [(i, i ^ 1) for i in range(size)])


def rounds_over_chips():
    return [
        (axis, first * math.prod(factors(lax.axis_size(axis) // first)[:n]), p)
        for axis, first in (("ctx", 2), ("dp", 1))
        for n, p in enumerate(factors(lax.axis_size(axis) // first))
    ]


def summed_over(total, axis, stride, p):
    size = lax.axis_size(axis)
    turned = lambda i, k: i + ((i // stride + k) % p - i // stride % p) * stride
    got = [lax.ppermute(total, axis, [(turned(i, k), i) for i in range(size)]) for k in range(1, p)]
    if p == 2:
        return total + got[0]
    digit = lax.axis_index(axis) // stride % p
    return jnp.sum(jnp.roll(jnp.stack([total, *got]), digit, axis=0), axis=0)


def after(value, *others):
    return lax.optimization_barrier((value, *others))[0]


def per_device(q_proj, k_proj, v_proj, out_grad, contig_starts, filters):
    q, k, v, dy = q_proj[0], k_proj[0], v_proj[0], out_grad[0]
    rows = q.shape[0]
    groups, taps = filters.shape
    assert rows == taps == LANES and lax.axis_size("ctx") % 2 == 0
    scale = 1.0 / math.sqrt(rows * lax.axis_size("ctx") * lax.axis_size("dp") * GSIZE)
    starts = contig_starts[0] > 0
    token = jnp.arange(rows)
    tail = ~jnp.any(starts[None, :] & (token[None, :] > token[:, None]), axis=1)
    head = ~jnp.any(starts[None, :] & (token[None, :] <= token[:, None]), axis=1)
    core = lax.axis_index("ctx") % 2
    width = q.shape[1] // 2

    def sent(a, b, keep, half):
        part = lambda x: lax.dynamic_slice_in_dim(x, half * width, width, 1)
        return jnp.where(keep[:, None], product(part(a), part(b)), 0)

    kv_out = sent(k, v, tail, core)
    kv_theirs = passed_along(kv_out, "ctx", 1)
    kv_mine = passed_along(sent(after(k, kv_out), v, tail, 1 - core), "ctx", 1)
    theirs = filter_share(q, k, v, dy, kv_theirs, contig_starts, groups, scale, True)
    mine = filter_share(q, k, v, dy, after(kv_mine, theirs), contig_starts, groups, scale, False)
    mine = mine + other_core(theirs)

    def forward(other, outs, partner):
        return convolution(k, v, other, q, dy, contig_starts, filters, outs, False, partner)

    def backward(other, outs, partner):
        return convolution(dy, q, other, v, k, contig_starts, filters, outs, True, partner)

    cot_out = [sent(dy, q, head, core), sent(dy, q, head, 1 - core)]
    rounds = rounds_over_chips()
    for n, place in enumerate(rounds):
        if n == 0:
            cot_theirs = passed_along(after(cot_out[0], mine), "ctx", -1)
            half_forward = forward(kv_theirs, None, True)
        if n == 1:
            mine = after(mine, *half_forward)
            cot_mine = passed_along(after(cot_out[1], mine), "ctx", -1)
            mixed, grad_q = forward(kv_mine, half_forward, False)
        if n == 2:
            mine = after(mine, mixed, grad_q, cot_theirs)
            half_backward = backward(cot_theirs, None, True)
        if n == 3:
            mine = after(mine, *half_backward, cot_mine)
            grad_k, grad_v = backward(cot_mine, half_backward, False)
        mine = summed_over(mine, *place)
    mine = after(mine, grad_k, grad_v)
    halves = [mine, other_core(mine)]
    filter_grad = jnp.where(core == 0, jnp.concatenate(halves), jnp.concatenate(halves[::-1]))
    return (mixed[None], grad_q[None], grad_k[None], grad_v[None], filter_grad)


def solution(mesh):
    wide = P("dp", "ctx", None)
    return jax.shard_map(
        per_device,
        mesh=mesh,
        in_specs=(wide,) * 4 + (P("dp", "ctx"), P()),
        out_specs=(wide,) * 4 + (P(),),
        check_vma=False,
    )
```

time: 46.2 us -> 42.2 us (0.913)
  the two profiles are of different devices: /device:TPU:0 before, /device:TPU:3 now
where the time goes in v6:
time: 42.2 us; the launch traced here: 41.9 us
  starting transfers between devices  18.9 us (45%)
  Pallas kernels  14.3 us (34%)
  other arithmetic  3.92 us (9%)
  waiting for transfers between devices  3.05 us (7%)
  between operations  0.93 us (2%)
  local copies, waits for them, and re-layouts  0.82 us (2%)
    pallas_call x6, Pallas kernels, local_call(): pl.pallas_call(kernel, out_shape=out_shape, in_specs=in_specs or [VMEM] *...  14.3 us
    ppermute x4, starting transfers between devices, passed_along(): return lax.ppermute(block, axis, route)  11.4 us
    ppermute x4, starting transfers between devices, summed_over(): lax.ppermute(total, axis, [(turned(i, k), i) for i in range(size)])  5.11 us
    ppermute x2, starting transfers between devices, other_core(): return lax.ppermute(block, 'ctx', [(i, i ^ 1) for i in range(size)])  2.42 us
    select_n x3, other arithmetic, sent(): return jnp.where(keep[:, None], product(part(a), part(b)), 0)  2.42 us
    ppermute x4, waiting for transfers between devices, summed_over(): lax.ppermute(total, axis, [(turned(i, k), i) for i in range(size)])  2.11 us
    ppermute x2, waiting for transfers between devices, other_core(): return lax.ppermute(block, 'ctx', [(i, i ^ 1) for i in range(size)])  0.86 us
  transfers between devices with their start and end apart: 10, of which 3 were waited for; matrix products, arithmetic and copies ran while one was open for 3% of the time, Pallas kernels for 34%

profile of v6, /device:TPU:3, one launch (start us, length us, event | category | flops | bytes accessed | tf_op | source)
XLA Modules:
  0.0 41.9 jit_solution(17983050603685944063)
XLA Ops:
  0.6 0.0 copy-start
  0.7 0.7 %compare_bitcast_fusion = pred[128]{0:T(512)(128)(4,1)S(1)} fusion(s32[1,128]{1,0:T(1,128)} %starts_ref.7), kind=kLoop, calls=%fused_computation.19 | loop fusion | flops 128 | bytes 640 | tf_op jit(solution)/shard_map/and | solution.py:271
  1.4 0.1 fusion.11
  1.5 0.0 copy-start.3
  1.5 1.2 %fusion.2 = bf16[128,1024]{1,0:T(8,128)(2,1)S(1)} fusion(bf16[1,128,2048]{2,1,0:T(8,128)(2,1)} %param.8, s32[]{:T(128)S(6)} %select_n.41, bf16[1,128,2048]{2,1,0:T(8,128)(2,1)} %param.7, pred[128]{0:T(512)(128)(4,1)S(1)} %not.14), kind=kLoop, calls=%fused_computation.6 | loop fusion | flops 655360 | bytes 786564 | tf_op jit(solution)/shard_map/jit(_where)/select_n | solution.py:278
  2.7 0.0 copy-start.2
  2.7 3.8 %collective-permute-start.1 = (bf16[128,1024]{1,0:T(8,128)(2,1)S(1)}, bf16[128,1024]{1,0:T(8,128)(2,1)S(1)}, u32[]{:S(2)}, u32[]{:S(2)}) collective-permute-start(bf16[128,1024]{1,0:T(8,128)(2,1)S(1)} %fusion.2), channel_id=1, source_target_pairs={{0,4},{4,8},{8,12},{12,16},{16,20},{20,24},{24,28},{1,5},{5,9},{9,... | collective-permute-start | bytes 786440 | tf_op jit(solution)/shard_map/ppermute | solution.py:223
  6.5 0.0 copy-done
  6.6 1.1 %fusion.7 = bf16[128,1024]{1,0:T(8,128)(2,1)S(1)} fusion(bf16[1,128,2048]{2,1,0:T(8,128)(2,1)} %param.8, s32[]{:T(128)S(6)} %select_n.43, bf16[128,2048]{1,0:T(8,128)(2,1)S(1)} %bitcast.25, pred[128]{0:T(512)(128)(4,1)S(1)} %not.14), kind=kLoop, calls=%fused_computation.11 | loop fusion | flops 655360 | bytes 786564 | tf_op jit(solution)/shard_map/jit(_where)/select_n | solution.py:278
  7.6 1.9 %collective-permute-start = (bf16[128,1024]{1,0:T(8,128)(2,1)S(1)}, bf16[128,1024]{1,0:T(8,128)(2,1)S(1)}, u32[]{:S(2)}, u32[]{:S(2)}) collective-permute-start(bf16[128,1024]{1,0:T(8,128)(2,1)S(1)} %fusion.7), channel_id=1, source_target_pairs={{0,4},{4,8},{8,12},{12,16},{16,20},{20,24},{24,28},{1,5},{5,9},{9,... | collective-permute-start | bytes 786440 | tf_op jit(solution)/shard_map/ppermute | solution.py:223
  9.6 0.0 copy-done.3
  9.6 0.0 copy-done.2
  9.6 0.0 copy-start.1
  9.6 0.2 fusion.6
  9.8 0.1 collective-permute-done.1.refs_2_.kv_prev_ref
  9.8 0.0 copy-start.5
  9.8 0.8 %copy-done.1 = bf16[1,128,2048]{2,1,0:T(8,128)(2,1)S(1)} copy-done((bf16[1,128,2048]{2,1,0:T(8,128)(2,1)S(1)}, bf16[1,128,2048]{2,1,0:T(8,128)(2,1)}, u32[]{:S(2)}) %copy-start.1) | copy-done | bytes 524312
  10.6 0.0 copy-done.5
  10.6 2.1 %filter_partner.1 = f32[64,128]{1,0:T(8,128)S(1)} custom-call(bf16[128,2048]{1,0:T(8,128)(2,1)S(1)} %bitcast.38, bf16[128,2048]{1,0:T(8,128)(2,1)S(1)} %bitcast.26, bf16[128,2048]{1,0:T(8,128)(2,1)S(1)} %bitcast.32, bf16[128,2048]{1,0:T(8,128)(2,1)S(1)} %bitcast.44, bf16[128,1024]{1,0:T(8,128)(2,1)S(1)} %collective-permute-done.1.refs_2_.kv_prev_ref, ...), custom_call_target="tpu_custom_call" | custom-call | flops 536870912 | bytes 2392576 | tf_op jit(solution)/shard_map/filter_partner/pallas_call | solution.py:168
  12.7 1.3 %collective-permute-start.2 = (f32[64,128]{1,0:T(8,128)S(1)}, f32[64,128]{1,0:T(8,128)S(1)}, u32[]{:S(2)}, u32[]{:S(2)}) collective-permute-start(f32[64,128]{1,0:T(8,128)S(1)} %filter_partner.1), channel_id=1, source_target_pairs={{0,4},{4,0},{8,12},{12,8},{16,20},{20,16},{24,28},{28,24},{1,5},{5... | collective-permute-start | bytes 98312 | tf_op jit(solution)/shard_map/ppermute | solution.py:238
  14.0 0.0 collective-permute-done.other_ref.kv_prev_ref
  14.0 2.1 %filter_own.1 = f32[64,128]{1,0:T(8,128)S(1)} custom-call(bf16[128,2048]{1,0:T(8,128)(2,1)S(1)} %bitcast.39, bf16[128,2048]{1,0:T(8,128)(2,1)S(1)} %bitcast.27, bf16[128,2048]{1,0:T(8,128)(2,1)S(1)} %bitcast.33, bf16[128,2048]{1,0:T(8,128)(2,1)S(1)} %bitcast.45, bf16[128,1024]{1,0:T(8,128)(2,1)S(1)} %collective-permute-done.other_ref.kv_prev_ref, ...), custom_call_target="tpu_custom_call" | custom-call | flops 536870912 | bytes 2392576 | tf_op jit(solution)/shard_map/filter_own/pallas_call | solution.py:168
  16.1 0.0 copy-start.4
  16.1 0.0 collective-permute-done.2
  16.1 0.1 collective-permute-start.3
  16.2 2.1 %collective-permute-start.5 = (bf16[128,1024]{1,0:T(8,128)(2,1)S(1)}, bf16[128,1024]{1,0:T(8,128)(2,1)S(1)}, u32[]{:S(2)}, u32[]{:S(2)}) collective-permute-start(bf16[128,1024]{1,0:T(8,128)(2,1)S(1)} %get-tuple-element.29), channel_id=1, source_target_pairs={{4,0},{8,4},{12,8},{16,12},{20,16},{24,20},{28,24},{5,1},{9,5},{13... | collective-permute-start | bytes 786440 | tf_op jit(solution)/shard_map/ppermute | solution.py:223
  18.3 0.0 copy-done.4
  18.3 2.5 %forward_partner.1 = (bf16[128,2048]{1,0:T(8,128)(2,1)}, bf16[128,2048]{1,0:T(8,128)(2,1)}) custom-call(bf16[128,2048]{1,0:T(8,128)(2,1)S(1)} %bitcast.28, bf16[128,2048]{1,0:T(8,128)(2,1)S(1)} %bitcast.34, bf16[128,1024]{1,0:T(8,128)(2,1)S(1)} %collective-permute-done.1.refs_2_.kv_prev_ref, bf16[128,2048]{1,0:T(8,128)(2,1)S(1)} %bitcast.40, ...), custom_call_target="tpu_custom_call" | custom-call | flops 536870912 | bytes 3441152 | tf_op jit(solution)/shard_map/forward_partner/pallas_call | solution.py:168
  20.9 0.0 collective-permute-done.3
  20.9 3.5 %collective-permute-start.4 = (bf16[128,1024]{1,0:T(8,128)(2,1)S(1)}, bf16[128,1024]{1,0:T(8,128)(2,1)S(1)}, u32[]{:S(2)}, u32[]{:S(2)}) collective-permute-start(bf16[128,1024]{1,0:T(8,128)(2,1)S(1)} %get-tuple-element.28), channel_id=1, source_target_pairs={{4,0},{8,4},{12,8},{16,12},{20,16},{24,20},{28,24},{5,1},{9,5},{13... | collective-permute-start | bytes 786440 | tf_op jit(solution)/shard_map/ppermute | solution.py:223
  24.4 1.3 %collective-permute-start.6 = (f32[64,128]{1,0:T(8,128)S(1)}, f32[64,128]{1,0:T(8,128)S(1)}, u32[]{:S(2)}, u32[]{:S(2)}) collective-permute-start(f32[64,128]{1,0:T(8,128)S(1)} %add.35), channel_id=1, source_target_pairs={{16,0},{20,4},{24,8},{28,12},{0,16},{4,20},{8,24},{12,28},{17,1},{... | collective-permute-start | bytes 98312 | tf_op jit(solution)/shard_map/ppermute | solution.py:252
  25.7 2.5 %forward_own.1 = (bf16[128,2048]{1,0:T(8,128)(2,1)}, bf16[128,2048]{1,0:T(8,128)(2,1)}) custom-call(bf16[128,2048]{1,0:T(8,128)(2,1)S(1)} %bitcast.29, bf16[128,2048]{1,0:T(8,128)(2,1)S(1)} %bitcast.35, bf16[128,1024]{1,0:T(8,128)(2,1)S(1)} %collective-permute-done.other_ref.kv_prev_ref, ...), custom_call_target="tpu_custom_call", output_to_operand_aliasing={{0}: (7, {}), {1}: (8, {})} | custom-call | flops 536870912 | bytes 4489728 | tf_op jit(solution)/shard_map/forward_own/pallas_call | solution.py:168
  28.3 2.1 %collective-permute-done.6 = f32[64,128]{1,0:T(8,128)S(1)} collective-permute-done((f32[64,128]{1,0:T(8,128)S(1)}, f32[64,128]{1,0:T(8,128)S(1)}, u32[]{:S(2)}, u32[]{:S(2)}) %collective-permute-start.6) | collective-permute-done | bytes 32800 | tf_op jit(solution)/shard_map/ppermute | solution.py:252
  30.4 0.0 collective-permute-done.5.refs_2_
  30.4 1.4 %collective-permute-start.7 = (f32[64,128]{1,0:T(8,128)S(1)}, f32[64,128]{1,0:T(8,128)S(1)}, u32[]{:S(2)}, u32[]{:S(2)}) collective-permute-start(f32[64,128]{1,0:T(8,128)S(1)} %add.36), channel_id=1, source_target_pairs={{1,0},{0,1},{3,2},{2,3},{5,4},{4,5},{7,6},{6,7},{9,8},{8,9},{11,10... | collective-permute-start | bytes 98312 | tf_op jit(solution)/shard_map/ppermute | solution.py:252
  31.8 2.6 %backward_partner.1 = (bf16[128,2048]{1,0:T(8,128)(2,1)}, bf16[128,2048]{1,0:T(8,128)(2,1)}) custom-call(bf16[128,2048]{1,0:T(8,128)(2,1)S(1)} %bitcast.48, bf16[128,2048]{1,0:T(8,128)(2,1)S(1)} %bitcast.42, bf16[128,1024]{1,0:T(8,128)(2,1)S(1)} %collective-permute-done.5.refs_2_, bf16[128,2048]{1,0:T(8,128)(2,1)S(1)} %bitcast.36, ...), custom_call_target="tpu_custom_call" | custom-call | flops 536870912 | bytes 3441152 | tf_op jit(solution)/shard_map/backward_partner/pallas_call | solution.py:168
  34.3 0.0 collective-permute-done.7
  34.3 0.0 collective-permute-done.4.other_ref
  34.4 2.4 %collective-permute-start.8 = (f32[64,128]{1,0:T(8,128)S(1)}, f32[64,128]{1,0:T(8,128)S(1)}, u32[]{:S(2)}, u32[]{:S(2)}) collective-permute-start(f32[64,128]{1,0:T(8,128)S(1)} %add.37), channel_id=1, source_target_pairs={{2,0},{3,1},{0,2},{1,3},{6,4},{7,5},{4,6},{5,7},{10,8},{11,9},{8,1... | collective-permute-start | bytes 98312 | tf_op jit(solution)/shard_map/ppermute | solution.py:252
  36.7 2.6 %backward_own.1 = (bf16[128,2048]{1,0:T(8,128)(2,1)}, bf16[128,2048]{1,0:T(8,128)(2,1)}) custom-call(bf16[128,2048]{1,0:T(8,128)(2,1)S(1)} %bitcast.49, bf16[128,2048]{1,0:T(8,128)(2,1)S(1)} %bitcast.43, bf16[128,1024]{1,0:T(8,128)(2,1)S(1)} %collective-permute-done.4.other_ref, ...), custom_call_target="tpu_custom_call", output_to_operand_aliasing={{0}: (7, {}), {1}: (8, {})} | custom-call | flops 536870912 | bytes 4489728 | tf_op jit(solution)/shard_map/backward_own/pallas_call | solution.py:168
  39.3 0.0 collective-permute-done.8
  39.3 1.1 %collective-permute-start.9 = (f32[64,128]{1,0:T(8,128)S(1)}, f32[64,128]{1,0:T(8,128)S(1)}, u32[]{:S(2)}, u32[]{:S(2)}) collective-permute-start(f32[64,128]{1,0:T(8,128)S(1)} %add.38), channel_id=1, source_target_pairs={{0,4},{4,0},{8,12},{12,8},{16,20},{20,16},{24,28},{28,24},{1,5},{5... | collective-permute-start | bytes 98312 | tf_op jit(solution)/shard_map/ppermute | solution.py:238
  40.4 0.9 %collective-permute-done.9 = f32[64,128]{1,0:T(8,128)S(1)} collective-permute-done((f32[64,128]{1,0:T(8,128)S(1)}, f32[64,128]{1,0:T(8,128)S(1)}, u32[]{:S(2)}, u32[]{:S(2)}) %collective-permute-start.9) | collective-permute-done | bytes 32800 | tf_op jit(solution)/shard_map/ppermute | solution.py:238
  41.3 0.6 %maximum_select_fusion = f32[128,128]{1,0:T(8,128)} fusion(f32[64,128]{1,0:T(8,128)S(1)} %collective-permute-done.9, f32[64,128]{1,0:T(8,128)S(1)} %add.38, pred[]{:T(512)S(6)} %eq.5), kind=kLoop, calls=%fused_computation.12 | loop fusion | flops 49152 | bytes 131073 | tf_op jit(solution)/shard_map/jit(_where)/select_n | solution.py:312
  (7 shorter events, 0.0 us)
Async XLA Ops:
  0.6 5.9 %copy-start = (bf16[1,128,2048]{2,1,0:T(8,128)(2,1)S(1)}, bf16[1,128,2048]{2,1,0:T(8,128)(2,1)}, u32[]{:S(2)}) copy-start(bf16[1,128,2048]{2,1,0:T(8,128)(2,1)} %param.7) | copy-start | bytes 1572868
  1.5 8.1 %copy-start.3 = (bf16[1,128,2048]{2,1,0:T(8,128)(2,1)S(1)}, bf16[1,128,2048]{2,1,0:T(8,128)(2,1)}, u32[]{:S(2)}) copy-start(bf16[1,128,2048]{2,1,0:T(8,128)(2,1)} %param.9) | copy-start | bytes 1572868
  2.7 6.9 %copy-start.2 = (bf16[1,128,2048]{2,1,0:T(8,128)(2,1)S(1)}, bf16[1,128,2048]{2,1,0:T(8,128)(2,1)}, u32[]{:S(2)}) copy-start(bf16[1,128,2048]{2,1,0:T(8,128)(2,1)} %param.6) | copy-start | bytes 1572868
  2.7 7.1 %collective-permute-start.1 = (bf16[128,1024]{1,0:T(8,128)(2,1)S(1)}, bf16[128,1024]{1,0:T(8,128)(2,1)S(1)}, u32[]{:S(2)}, u32[]{:S(2)}) collective-permute-start(bf16[128,1024]{1,0:T(8,128)(2,1)S(1)} %fusion.2), channel_id=1, source_target_pairs={{0,4},{4,8},{8,12},{12,16},{16,20},{20,24},{24,28},{1,5},{5,9},{9,... | collective-permute-start | bytes 786440 | tf_op jit(solution)/shard_map/ppermute | solution.py:223
  7.6 6.4 %collective-permute-start = (bf16[128,1024]{1,0:T(8,128)(2,1)S(1)}, bf16[128,1024]{1,0:T(8,128)(2,1)S(1)}, u32[]{:S(2)}, u32[]{:S(2)}) collective-permute-start(bf16[128,1024]{1,0:T(8,128)(2,1)S(1)} %fusion.7), channel_id=1, source_target_pairs={{0,4},{4,8},{8,12},{12,16},{16,20},{20,24},{24,28},{1,5},{5,9},{9,... | collective-permute-start | bytes 786440 | tf_op jit(solution)/shard_map/ppermute | solution.py:223
  9.6 1.0 %copy-start.1 = (bf16[1,128,2048]{2,1,0:T(8,128)(2,1)S(1)}, bf16[1,128,2048]{2,1,0:T(8,128)(2,1)}, u32[]{:S(2)}) copy-start(bf16[1,128,2048]{2,1,0:T(8,128)(2,1)} %param.8) | copy-start | bytes 1572868
  9.8 0.8 %copy-start.5 = (s32[1,128]{1,0:T(1,128)S(1)}, s32[1,128]{1,0:T(1,128)}, u32[]{:S(2)}) copy-start(s32[1,128]{1,0:T(1,128)} %starts_ref.7) | copy-start | bytes 1540
  12.7 3.4 %collective-permute-start.2 = (f32[64,128]{1,0:T(8,128)S(1)}, f32[64,128]{1,0:T(8,128)S(1)}, u32[]{:S(2)}, u32[]{:S(2)}) collective-permute-start(f32[64,128]{1,0:T(8,128)S(1)} %filter_partner.1), channel_id=1, source_target_pairs={{0,4},{4,0},{8,12},{12,8},{16,20},{20,16},{24,28},{28,24},{1,5},{5... | collective-permute-start | bytes 98312 | tf_op jit(solution)/shard_map/ppermute | solution.py:238
  16.1 2.2 %copy-start.4 = (bf16[128,128]{1,0:T(8,128)(2,1)S(1)}, bf16[128,128]{1,0:T(8,128)(2,1)}, u32[]{:S(2)}) copy-start(bf16[128,128]{1,0:T(8,128)(2,1)} %taps_ref.3) | copy-start | bytes 98308
  16.1 4.7 %collective-permute-start.3 = (f32[64,128]{1,0:T(8,128)S(1)}, f32[64,128]{1,0:T(8,128)S(1)}, u32[]{:S(2)}, u32[]{:S(2)}) collective-permute-start(f32[64,128]{1,0:T(8,128)S(1)} %add.34), channel_id=1, source_target_pairs={{8,0},{12,4},{0,8},{4,12},{24,16},{28,20},{16,24},{20,28},{9,1},{1... | collective-permute-start | bytes 98312 | tf_op jit(solution)/shard_map/ppermute | solution.py:252
  16.2 14.2 %collective-permute-start.5 = (bf16[128,1024]{1,0:T(8,128)(2,1)S(1)}, bf16[128,1024]{1,0:T(8,128)(2,1)S(1)}, u32[]{:S(2)}, u32[]{:S(2)}) collective-permute-start(bf16[128,1024]{1,0:T(8,128)(2,1)S(1)} %get-tuple-element.29), channel_id=1, source_target_pairs={{4,0},{8,4},{12,8},{16,12},{20,16},{24,20},{28,24},{5,1},{9,5},{13... | collective-permute-start | bytes 786440 | tf_op jit(solution)/shard_map/ppermute | solution.py:223
  20.9 13.5 %collective-permute-start.4 = (bf16[128,1024]{1,0:T(8,128)(2,1)S(1)}, bf16[128,1024]{1,0:T(8,128)(2,1)S(1)}, u32[]{:S(2)}, u32[]{:S(2)}) collective-permute-start(bf16[128,1024]{1,0:T(8,128)(2,1)S(1)} %get-tuple-element.28), channel_id=1, source_target_pairs={{4,0},{8,4},{12,8},{16,12},{20,16},{24,20},{28,24},{5,1},{9,5},{13... | collective-permute-start | bytes 786440 | tf_op jit(solution)/shard_map/ppermute | solution.py:223
  24.4 5.9 %collective-permute-start.6 = (f32[64,128]{1,0:T(8,128)S(1)}, f32[64,128]{1,0:T(8,128)S(1)}, u32[]{:S(2)}, u32[]{:S(2)}) collective-permute-start(f32[64,128]{1,0:T(8,128)S(1)} %add.35), channel_id=1, source_target_pairs={{16,0},{20,4},{24,8},{28,12},{0,16},{4,20},{8,24},{12,28},{17,1},{... | collective-permute-start | bytes 98312 | tf_op jit(solution)/shard_map/ppermute | solution.py:252
  30.4 3.9 %collective-permute-start.7 = (f32[64,128]{1,0:T(8,128)S(1)}, f32[64,128]{1,0:T(8,128)S(1)}, u32[]{:S(2)}, u32[]{:S(2)}) collective-permute-start(f32[64,128]{1,0:T(8,128)S(1)} %add.36), channel_id=1, source_target_pairs={{1,0},{0,1},{3,2},{2,3},{5,4},{4,5},{7,6},{6,7},{9,8},{8,9},{11,10... | collective-permute-start | bytes 98312 | tf_op jit(solution)/shard_map/ppermute | solution.py:252
  34.4 4.9 %collective-permute-start.8 = (f32[64,128]{1,0:T(8,128)S(1)}, f32[64,128]{1,0:T(8,128)S(1)}, u32[]{:S(2)}, u32[]{:S(2)}) collective-permute-start(f32[64,128]{1,0:T(8,128)S(1)} %add.37), channel_id=1, source_target_pairs={{2,0},{3,1},{0,2},{1,3},{6,4},{7,5},{4,6},{5,7},{10,8},{11,9},{8,1... | collective-permute-start | bytes 98312 | tf_op jit(solution)/shard_map/ppermute | solution.py:252
  39.3 2.0 %collective-permute-start.9 = (f32[64,128]{1,0:T(8,128)S(1)}, f32[64,128]{1,0:T(8,128)S(1)}, u32[]{:S(2)}, u32[]{:S(2)}) collective-permute-start(f32[64,128]{1,0:T(8,128)S(1)} %add.38), channel_id=1, source_target_pairs={{0,4},{4,0},{8,12},{12,8},{16,20},{20,16},{24,28},{28,24},{1,5},{5... | collective-permute-start | bytes 98312 | tf_op jit(solution)/shard_map/ppermute | solution.py:238

commit v7 on v6

--- a/solution.py
+++ b/solution.py
@@ -47,11 +47,6 @@
     return lax.broadcasted_iota(jnp.int32, (1, LANES), 1) // GSIZE
 
 
-def half_index(partner):
-    core = lax.axis_index("ctx") % 2
-    return 1 - core if partner else core
-
-
 def each_tile(tile, width):
     count = width // LANES
     step = math.gcd(count, STEP)
@@ -65,28 +60,35 @@
 
 
 def filter_kernel(
-    q_ref, k_ref, v_ref, dy_ref, kv_prev_ref, starts_ref, out_ref, own_ref, prev_ref, sums_ref, *, scale, partner
+    q_ref, k_ref, v_ref, dy_ref, other_ref, starts_ref, out_ref, own_ref, other_mask_ref, sums_ref, *, scale, partner
 ):
     rows = q_ref.shape[0]
     per_tile = LANES // GSIZE
-
-    own_ref[...], prev_ref[...], _ = contig_masks(starts_ref)
-
+    width = q_ref.shape[1] // 2
+    core = lax.axis_index("ctx") % 2
+    half = 1 - core if partner else core
+    low = half == 0
+    base = half * width
+    own, previous, following = contig_masks(starts_ref)
+    own_ref[...] = jnp.where(low, own, own.T)
+    other_mask_ref[...] = jnp.where(low, previous, following)
     group = lane_groups()
-    width = q_ref.shape[1] // 2
-    base = half_index(partner) * width
 
     def tile(index):
         here = pl.ds(pl.multiple_of(index * LANES, LANES), LANES)
         lanes = pl.ds(pl.multiple_of(base + index * LANES, LANES), LANES)
         cot = product(dy_ref[:, lanes], q_ref[:, lanes])
-        kv = jnp.concatenate([product(k_ref[:, lanes], v_ref[:, lanes]), kv_prev_ref[:, here]], axis=0)
+        kv = product(k_ref[:, lanes], v_ref[:, lanes])
+        left = jnp.where(low, cot, kv)
+        right = jnp.concatenate(
+            [jnp.where(low, kv, cot), other_ref[:, here if other_ref.shape[1] == width else lanes]], axis=0
+        )
         for g in range(per_tile):
-            picked = jnp.where(group == g, cot, jnp.zeros_like(cot))
+            picked = jnp.where(group == g, left, jnp.zeros_like(left))
             pairs = lax.dot_general(
-                picked, kv, (((1,), (1,)), ((), ())), preferred_element_type=jnp.float32
+                picked, right, (((1,), (1,)), ((), ())), preferred_element_type=jnp.float32
             )
-            linked = pairs[:, :rows] * own_ref[...] + pairs[:, rows:] * prev_ref[...]
+            linked = pairs[:, :rows] * own_ref[...] + pairs[:, rows:] * other_mask_ref[...]
             total = linked[:8]
             for i in range(1, rows // 8):
                 total = total + pltpu.roll(linked[8 * i : 8 * i + 8], rows - 8 * i, 1)
@@ -98,24 +100,24 @@
     diagonal = sums_ref[pl.ds(0, groups, stride=8), :]
     for r in range(1, 8):
         diagonal = diagonal + pltpu.roll(sums_ref[pl.ds(r, groups, stride=8), :], rows - r, 1)
-    out_ref[...] = reversed_taps(diagonal) * scale
+    out_ref[...] = jnp.where(low, reversed_taps(diagonal), diagonal) * scale
 
 
 def conv_kernel(
-    a_ref, b_ref, other_ref, c_ref, d_ref, starts_ref, taps_ref, c_in_hbm, d_in_hbm, out_c_hbm, out_d_hbm,
-    mask_ref, taps_scr, out_c_ref, out_d_ref, sems, *, backward, partner,
+    a_ref, b_ref, pair_ref, far_ref, c_ref, d_ref, starts_ref, taps_ref, c_in_hbm, d_in_hbm, out_c_hbm, out_d_hbm,
+    mask_ref, taps_scr, out_c_ref, out_d_ref, sems, *, backward, half,
 ):
     del c_in_hbm, d_in_hbm
     rows = a_ref.shape[0]
     per_tile = LANES // GSIZE
     width = a_ref.shape[1] // 2
-    half = half_index(partner)
     base = half * width
+    even = lax.axis_index("ctx") % 2 == 0
     own, previous, following = contig_masks(starts_ref)
     mask_ref[:, :rows] = (own.T if backward else own).astype(jnp.bfloat16)
     mask_ref[:, rows:] = (following if backward else previous).astype(jnp.bfloat16)
     groups = width // GSIZE
-    taps = taps_ref[pl.ds(pl.multiple_of(half * groups, groups), groups), :]
+    taps = taps_ref[half * groups : (half + 1) * groups, :]
     taps_scr[...] = taps.astype(jnp.float32) if backward else reversed_taps(taps)
     group = lane_groups()
 
@@ -127,7 +129,8 @@
     def tile(index):
         here = pl.ds(pl.multiple_of(index * LANES, LANES), LANES)
         lanes = pl.ds(pl.multiple_of(base + index * LANES, LANES), LANES)
-        other = other_ref[:, here if other_ref.shape[1] == width else lanes]
+        from_pair = even if backward else jnp.logical_not(even)
+        other = jnp.where(from_pair, pair_ref[:, lanes], far_ref[:, here])
         x = jnp.concatenate([product(a_ref[:, lanes], b_ref[:, lanes]), other], axis=0)
         taps = taps_scr[pl.ds(pl.multiple_of(index * per_tile, per_tile), per_tile), :]
         y = jnp.zeros((rows, LANES), jnp.float32)
@@ -162,9 +165,10 @@
 VMEM = pl.BlockSpec(memory_space=pltpu.VMEM)
 
 
-def local_call(kernel, name, out_shape, scratch_shapes, flops, operands, in_specs=None, out_specs=VMEM, aliases={}):
+def local_call(kernel, name, out_shape, scratch_shapes, flops, operands, in_specs=None, out_specs=VMEM, aliases={}, moved=None):
     outs = out_shape if isinstance(out_shape, list) else [out_shape]
-    moved = sum(math.prod(x.shape) * x.dtype.itemsize for x in [*operands, *outs])
+    if moved is None:
+        moved = sum(math.prod(x.shape) * x.dtype.itemsize for x in [*operands, *outs])
     return pl.pallas_call(
         kernel,
         out_shape=out_shape,
@@ -178,7 +182,7 @@
     )(*operands)
 
 
-def filter_share(q, k, v, dy, kv_prev, starts, groups, scale, partner):
+def filter_share(q, k, v, dy, other, starts, groups, scale, partner):
     rows, width = q.shape
     table = pltpu.VMEM((rows, rows), jnp.float32)
     return local_call(
@@ -186,41 +190,43 @@
         "filter_partner" if partner else "filter_own",
         jax.ShapeDtypeStruct((groups // 2, rows), jnp.float32),
         [table, table, pltpu.VMEM((groups * 4, rows), jnp.float32)],
-        16 * rows * rows * width, (q, k, v, dy, kv_prev, starts),
+        0, (q, k, v, dy, other, starts), moved=0,
     )
 
 
-def convolution(a, b, other, c, d, starts, filters, outs, backward, partner):
+def convolution(a, b, pair, far, c, d, starts, filters, outs, backward, half):
     rows, width = a.shape
     steps = width // 2 // LANES // math.gcd(width // 2 // LANES, STEP)
     out = jax.ShapeDtypeStruct((rows, width), jnp.bfloat16)
-    half = pltpu.VMEM((rows, width // 2), jnp.bfloat16)
+    part = pltpu.VMEM((rows, width // 2), jnp.bfloat16)
     anywhere = pl.BlockSpec(memory_space=pl.ANY)
-    kernel = functools.partial(conv_kernel, backward=backward, partner=partner)
-    operands = (a, b, other, c, d, starts, filters)
-    if outs is None:
-        body = kernel
-        kernel = lambda *refs: body(*refs[:7], None, None, *refs[7:])
+    body = functools.partial(conv_kernel, backward=backward, half=half)
+    operands = (a, b, pair, far, c, d, starts, filters)
+    n = len(operands)
     return local_call(
-        kernel,
-        ("backward" if backward else "forward") + ("_partner" if partner else "_own"),
+        body if outs else lambda *refs: body(*refs[:n], None, None, *refs[n:]),
+        ("backward" if backward else "forward") + ("_high" if half else "_low"),
         [out, out],
         [
             pltpu.VMEM((rows, 2 * rows), jnp.bfloat16), pltpu.VMEM((filters.shape[0] // 2, rows), jnp.float32),
-            half, half, pltpu.SemaphoreType.DMA((2, steps)),
+            part, part, pltpu.SemaphoreType.DMA((2, steps)),
         ],
         16 * rows * rows * width,
         operands + tuple(outs or ()),
-        [VMEM] * 7 + [anywhere] * (2 if outs else 0),
+        [VMEM] * n + [anywhere] * (2 if outs else 0),
         [anywhere] * 2,
-        {7: 0, 8: 1} if outs else {},
+        {n: 0, n + 1: 1} if outs else {},
     )
 
 
-def passed_along(block, axis, distance):
-    devices = range(lax.axis_size(axis))
-    route = [(i - distance, i) for i in devices if i - distance in devices]
-    return lax.ppermute(block, axis, route)
+def other_core(block):
+    return lax.ppermute(block, "ctx", [(i, i ^ 1) for i in range(lax.axis_size("ctx"))])
+
+
+def next_chip(block):
+    size = lax.axis_size("ctx")
+    pairs = [(i, i + 1) for i in range(1, size - 1, 2)]
+    return lax.ppermute(block, "ctx", pairs + [(j, i) for i, j in pairs])
 
 
 def factors(size):
@@ -233,11 +239,6 @@
     return found
 
 
-def other_core(block):
-    size = lax.axis_size("ctx")
-    return lax.ppermute(block, "ctx", [(i, i ^ 1) for i in range(size)])
-
-
 def rounds_over_chips():
     return [
         (axis, first * math.prod(factors(lax.axis_size(axis) // first)[:n]), p)
@@ -266,50 +267,55 @@
     groups, taps = filters.shape
     assert rows == taps == LANES and lax.axis_size("ctx") % 2 == 0
     scale = 1.0 / math.sqrt(rows * lax.axis_size("ctx") * lax.axis_size("dp") * GSIZE)
-    starts = contig_starts[0] > 0
+    flags = lax.optimization_barrier(jnp.minimum(contig_starts, 1))
+    starts = flags[0] > 0
     token = jnp.arange(rows)
     tail = ~jnp.any(starts[None, :] & (token[None, :] > token[:, None]), axis=1)
     head = ~jnp.any(starts[None, :] & (token[None, :] <= token[:, None]), axis=1)
-    core = lax.axis_index("ctx") % 2
+    even = lax.axis_index("ctx") % 2 == 0
     width = q.shape[1] // 2
-
-    def sent(a, b, keep, half):
-        part = lambda x: lax.dynamic_slice_in_dim(x, half * width, width, 1)
-        return jnp.where(keep[:, None], product(part(a), part(b)), 0)
-
-    kv_out = sent(k, v, tail, core)
-    kv_theirs = passed_along(kv_out, "ctx", 1)
-    kv_mine = passed_along(sent(after(k, kv_out), v, tail, 1 - core), "ctx", 1)
-    theirs = filter_share(q, k, v, dy, kv_theirs, contig_starts, groups, scale, True)
-    mine = filter_share(q, k, v, dy, after(kv_mine, theirs), contig_starts, groups, scale, False)
+    low, high, every = slice(0, width), slice(width, None), slice(None)
+
+    def sent(from_even, kv_part, cot_part, earlier=()):
+        to_next = even if from_even else ~even
+        q_, k_, v_, dy_ = lax.optimization_barrier((q, k, v, dy, *earlier))[:4]
+        kv = product(k_[:, kv_part], v_[:, kv_part])
+        cot = product(dy_[:, cot_part], q_[:, cot_part])
+        keep = jnp.where(to_next, tail, head)
+        return jnp.where(keep[:, None], jnp.where(to_next, kv, cot), 0)
+
+    far_out = sent(False, low, high)
+    far_first = next_chip(far_out)
+    pair_out = sent(True, every, every, (far_out,))
+    pair = other_core(pair_out)
+    theirs = filter_share(q, k, v, dy, pair, flags, groups, scale, True)
+    mine = filter_share(q, k, v, dy, after(far_first, theirs), flags, groups, scale, False)
     mine = mine + other_core(theirs)
 
-    def forward(other, outs, partner):
-        return convolution(k, v, other, q, dy, contig_starts, filters, outs, False, partner)
-
-    def backward(other, outs, partner):
-        return convolution(dy, q, other, v, k, contig_starts, filters, outs, True, partner)
-
-    cot_out = [sent(dy, q, head, core), sent(dy, q, head, 1 - core)]
-    rounds = rounds_over_chips()
-    for n, place in enumerate(rounds):
+    def forward(far, outs, half):
+        return convolution(k, v, pair, far, q, dy, flags, filters, outs, False, half)
+
+    def backward(far, outs, half):
+        return convolution(dy, q, pair, far, v, k, flags, filters, outs, True, half)
+
+    far_out = sent(False, high, low, (pair_out,))
+    for n, place in enumerate(rounds_over_chips()):
         if n == 0:
-            cot_theirs = passed_along(after(cot_out[0], mine), "ctx", -1)
-            half_forward = forward(kv_theirs, None, True)
+            far_second = next_chip(after(far_out, mine))
+            half_forward = forward(far_first, None, 0)
         if n == 1:
             mine = after(mine, *half_forward)
-            cot_mine = passed_along(after(cot_out[1], mine), "ctx", -1)
-            mixed, grad_q = forward(kv_mine, half_forward, False)
+            half_backward = backward(far_first, None, 1)
         if n == 2:
-            mine = after(mine, mixed, grad_q, cot_theirs)
-            half_backward = backward(cot_theirs, None, True)
+            mine = after(mine, *half_backward, far_second)
+            mixed, grad_q = forward(far_second, half_forward, 1)
         if n == 3:
-            mine = after(mine, *half_backward, cot_mine)
-            grad_k, grad_v = backward(cot_mine, half_backward, False)
+            mine = after(mine, mixed, grad_q)
+            grad_k, grad_v = backward(far_second, half_backward, 0)
         mine = summed_over(mine, *place)
     mine = after(mine, grad_k, grad_v)
     halves = [mine, other_core(mine)]
-    filter_grad = jnp.where(core == 0, jnp.concatenate(halves), jnp.concatenate(halves[::-1]))
+    filter_grad = jnp.where(even, jnp.concatenate(halves), jnp.concatenate(halves[::-1]))
     return (mixed[None], grad_q[None], grad_k[None], grad_v[None], filter_grad)
 
 

time: 42.2 us -> 45 us (1.066)
  the two profiles are of different devices: /device:TPU:3 before, /device:TPU:0 now
where the time goes in v7:
time: 45 us; the launch traced here: 44.8 us
  starting transfers between devices  19.1 us (42%)
  Pallas kernels  14.6 us (32%)
  waiting for transfers between devices  5.44 us (12%)
  other arithmetic  4.03 us (9%)
  between operations  0.86 us (2%)
  local copies, waits for them, and re-layouts  0.73 us (2%)
    pallas_call x6, Pallas kernels, local_call(): pl.pallas_call(kernel, out_shape=out_shape, in_specs=in_specs or [VMEM] *...  14.6 us
    ppermute x4, starting transfers between devices, summed_over(): lax.ppermute(total, axis, [(turned(i, k), i) for i in range(size)])  14.1 us
    ppermute x3, starting transfers between devices, other_core(): lax.ppermute(block, 'ctx', [(i, i ^ 1) for i in range(lax.axis_size('ctx'...  3.69 us
    ppermute x4, waiting for transfers between devices, summed_over(): lax.ppermute(total, axis, [(turned(i, k), i) for i in range(size)])  3.38 us
    select_n x3, other arithmetic, sent(): return jnp.where(keep[:, None], jnp.where(to_next, kv, cot), 0)  3.24 us
    ppermute x3, waiting for transfers between devices, other_core(): lax.ppermute(block, 'ctx', [(i, i ^ 1) for i in range(lax.axis_size('ctx'...  2.06 us
    ppermute x2, starting transfers between devices, next_chip(): return lax.ppermute(block, 'ctx', pairs + [(j, i) for i, j in pairs])  1.34 us
  transfers between devices with their start and end apart: 9, of which 3 were waited for; matrix products, arithmetic and copies ran while one was open for 0% of the time, Pallas kernels for 33%

profile of v7, /device:TPU:0, one launch (start us, length us, event | category | flops | bytes accessed | tf_op | source)
XLA Modules:
  0.0 44.8 jit_solution(388266967862328266)
XLA Ops:
  0.6 0.0 copy-start.5
  0.7 0.6 %copy-done.5 = s32[1,128]{1,0:T(1,128)S(1)} copy-done((s32[1,128]{1,0:T(1,128)S(1)}, s32[1,128]{1,0:T(1,128)}, u32[]{:S(2)}) %copy-start.5) | copy-done | bytes 536
  1.3 0.1 fusion.7
  1.4 0.0 copy-start
  1.5 0.0 copy-start.1
  1.5 1.4 %fusion.3 = bf16[128,1024]{1,0:T(8,128)(2,1)S(1)} fusion(bf16[128,2048]{1,0:T(8,128)(2,1)} %bitcast.28, bf16[128,2048]{1,0:T(8,128)(2,1)} %bitcast.37, bf16[128,2048]{1,0:T(8,128)(2,1)} %bitcast.19, bf16[128,2048]{1,0:T(8,128)(2,1)} %bitcast.10, pred[128]{0:T(512)(128)(4,1)S(1)} %get-tuple-element.60, pred[]{:T(512)S(6)} %not.26), kind=kLoop, calls=%fused_computation.9 | loop fusion | flops 1310720 | bytes 1310849 | tf_op jit(solution)/shard_map/jit(_where)/select_n | solution.py:285
  2.9 0.0 copy-done
  2.9 0.1 copy-done.1
  3.0 0.0 copy-start.2
  3.0 0.0 copy-start.3
  3.0 1.7 %fusion.1 = bf16[128,2048]{1,0:T(8,128)(2,1)S(1)} fusion(bf16[128,2048]{1,0:T(8,128)(2,1)S(1)} %bitcast.20, bf16[128,2048]{1,0:T(8,128)(2,1)S(1)} %bitcast.11, bf16[128,2048]{1,0:T(8,128)(2,1)} %bitcast.29, bf16[128,2048]{1,0:T(8,128)(2,1)} %bitcast.38, pred[128]{0:T(512)(128)(4,1)S(1)} %get-tuple-element.59, pred[]{:T(512)S(6)} %eq.5), kind=kLoop, calls=%fused_computation.3 | loop fusion | flops 2621440 | bytes 2621569 | tf_op jit(solution)/shard_map/jit(_where)/select_n | solution.py:285
  4.6 0.5 %collective-permute-start = (bf16[128,2048]{1,0:T(8,128)(2,1)S(1)}, bf16[128,2048]{1,0:T(8,128)(2,1)S(1)}, u32[]{:S(2)}, u32[]{:S(2)}) collective-permute-start(bf16[128,2048]{1,0:T(8,128)(2,1)S(1)} %fusion.1), channel_id=1, source_target_pairs={{0,4},{4,0},{8,12},{12,8},{16,20},{20,16},{24,28},{28,24},{1,5},{5... | collective-permute-start | bytes 1572872 | tf_op jit(solution)/shard_map/ppermute | solution.py:223
  5.1 0.7 %collective-permute-start.1 = (bf16[128,1024]{1,0:T(8,128)(2,1)S(1)}, bf16[128,1024]{1,0:T(8,128)(2,1)S(1)}, u32[]{:S(2)}, u32[]{:S(2)}) collective-permute-start(bf16[128,1024]{1,0:T(8,128)(2,1)S(1)} %fusion.3), channel_id=1, source_target_pairs={{4,8},{12,16},{20,24},{8,4},{16,12},{24,20},{5,9},{13,17},{21,25},... | collective-permute-start | bytes 786440 | tf_op jit(solution)/shard_map/ppermute | solution.py:229
  5.8 0.9 %collective-permute-done.other_ref.refs_2_.pair_ref = bf16[128,2048]{1,0:T(8,128)(2,1)S(1)} collective-permute-done((bf16[128,2048]{1,0:T(8,128)(2,1)S(1)}, bf16[128,2048]{1,0:T(8,128)(2,1)S(1)}, u32[]{:S(2)}, u32[]{:S(2)}) %collective-permute-start) | collective-permute-done | bytes 524320 | tf_op jit(solution)/shard_map/ppermute | solution.py:223
  6.7 0.0 copy-done.2
  6.7 0.0 copy-done.3
  6.7 2.2 %filter_partner.1 = f32[64,128]{1,0:T(8,128)S(1)} custom-call(bf16[128,2048]{1,0:T(8,128)(2,1)S(1)} %bitcast.30, bf16[128,2048]{1,0:T(8,128)(2,1)S(1)} %bitcast.12, bf16[128,2048]{1,0:T(8,128)(2,1)S(1)} %bitcast.21, bf16[128,2048]{1,0:T(8,128)(2,1)S(1)} %bitcast.39, bf16[128,2048]{1,0:T(8,128)(2,1)S(1)} %collective-permute-done.other_ref.refs_2_.pair_ref, ...), custom_call_target="tpu_custom_call" | custom-call | tf_op jit(solution)/shard_map/filter_partner/pallas_call | solution.py:172
  8.9 3.1 %collective-permute-start.2 = (f32[64,128]{1,0:T(8,128)S(1)}, f32[64,128]{1,0:T(8,128)S(1)}, u32[]{:S(2)}, u32[]{:S(2)}) collective-permute-start(f32[64,128]{1,0:T(8,128)S(1)} %filter_partner.1), channel_id=1, source_target_pairs={{0,4},{4,0},{8,12},{12,8},{16,20},{20,16},{24,28},{28,24},{1,5},{5... | collective-permute-start | bytes 98312 | tf_op jit(solution)/shard_map/ppermute | solution.py:223
  12.0 0.2 fusion.5
  12.1 0.0 collective-permute-done.1.other_ref.refs_3_
  12.1 2.2 %filter_own.1 = f32[64,128]{1,0:T(8,128)S(1)} custom-call(bf16[128,2048]{1,0:T(8,128)(2,1)S(1)} %bitcast.32, bf16[128,2048]{1,0:T(8,128)(2,1)S(1)} %bitcast.14, bf16[128,2048]{1,0:T(8,128)(2,1)S(1)} %bitcast.23, bf16[128,2048]{1,0:T(8,128)(2,1)S(1)} %bitcast.41, bf16[128,1024]{1,0:T(8,128)(2,1)S(1)} %collective-permute-done.1.other_ref.refs_3_, ...), custom_call_target="tpu_custom_call" | custom-call | tf_op jit(solution)/shard_map/filter_own/pallas_call | solution.py:172
  14.3 0.0 copy-start.4
  14.3 0.0 collective-permute-done.2
  14.4 0.7 %collective-permute-start.3 = (bf16[128,1024]{1,0:T(8,128)(2,1)S(1)}, bf16[128,1024]{1,0:T(8,128)(2,1)S(1)}, u32[]{:S(2)}, u32[]{:S(2)}) collective-permute-start(bf16[128,1024]{1,0:T(8,128)(2,1)S(1)} %fusion.5), channel_id=1, source_target_pairs={{4,8},{12,16},{20,24},{8,4},{16,12},{24,20},{5,9},{13,17},{21,25},... | collective-permute-start | bytes 786440 | tf_op jit(solution)/shard_map/ppermute | solution.py:229
  15.0 6.4 %collective-permute-start.4 = (f32[64,128]{1,0:T(8,128)S(1)}, f32[64,128]{1,0:T(8,128)S(1)}, u32[]{:S(2)}, u32[]{:S(2)}) collective-permute-start(f32[64,128]{1,0:T(8,128)S(1)} %add.20), channel_id=1, source_target_pairs={{8,0},{12,4},{0,8},{4,12},{24,16},{28,20},{16,24},{20,28},{9,1},{1... | collective-permute-start | bytes 98312 | tf_op jit(solution)/shard_map/ppermute | solution.py:253
  21.5 0.0 copy-done.4
  21.5 2.5 %forward_low.1 = (bf16[128,2048]{1,0:T(8,128)(2,1)}, bf16[128,2048]{1,0:T(8,128)(2,1)}) custom-call(bf16[128,2048]{1,0:T(8,128)(2,1)S(1)} %bitcast.15, bf16[128,2048]{1,0:T(8,128)(2,1)S(1)} %bitcast.24, bf16[128,2048]{1,0:T(8,128)(2,1)S(1)} %collective-permute-done.other_ref.refs_2_.pair_ref, bf16[128,1024]{1,0:T(8,128)(2,1)S(1)} %collective-permute-done.1.other_ref.refs_3_, ...), custom_call_target="tpu_custom_call" | custom-call | flops 536870912 | bytes 3965440 | tf_op jit(solution)/shard_map/forward_low/pallas_call | solution.py:172
  24.0 3.4 %collective-permute-done.4 = f32[64,128]{1,0:T(8,128)S(1)} collective-permute-done((f32[64,128]{1,0:T(8,128)S(1)}, f32[64,128]{1,0:T(8,128)S(1)}, u32[]{:S(2)}, u32[]{:S(2)}) %collective-permute-start.4) | collective-permute-done | bytes 32800 | tf_op jit(solution)/shard_map/ppermute | solution.py:253
  27.4 2.6 %collective-permute-start.5 = (f32[64,128]{1,0:T(8,128)S(1)}, f32[64,128]{1,0:T(8,128)S(1)}, u32[]{:S(2)}, u32[]{:S(2)}) collective-permute-start(f32[64,128]{1,0:T(8,128)S(1)} %add.21), channel_id=1, source_target_pairs={{16,0},{20,4},{24,8},{28,12},{0,16},{4,20},{8,24},{12,28},{17,1},{... | collective-permute-start | bytes 98312 | tf_op jit(solution)/shard_map/ppermute | solution.py:253
  30.0 2.6 %backward_high.1 = (bf16[128,2048]{1,0:T(8,128)(2,1)}, bf16[128,2048]{1,0:T(8,128)(2,1)}) custom-call(bf16[128,2048]{1,0:T(8,128)(2,1)S(1)} %bitcast.43, bf16[128,2048]{1,0:T(8,128)(2,1)S(1)} %bitcast.34, bf16[128,2048]{1,0:T(8,128)(2,1)S(1)} %collective-permute-done.other_ref.refs_2_.pair_ref, ...), custom_call_target="tpu_custom_call" | custom-call | flops 536870912 | bytes 3965440 | tf_op jit(solution)/shard_map/backward_high/pallas_call | solution.py:172
  32.6 0.0 collective-permute-done.5
  32.7 0.0 collective-permute-done.3.far_ref
  32.7 2.4 %collective-permute-start.6 = (f32[64,128]{1,0:T(8,128)S(1)}, f32[64,128]{1,0:T(8,128)S(1)}, u32[]{:S(2)}, u32[]{:S(2)}) collective-permute-start(f32[64,128]{1,0:T(8,128)S(1)} %add.22), channel_id=1, source_target_pairs={{1,0},{0,1},{3,2},{2,3},{5,4},{4,5},{7,6},{6,7},{9,8},{8,9},{11,10... | collective-permute-start | bytes 98312 | tf_op jit(solution)/shard_map/ppermute | solution.py:253
  35.1 2.5 %forward_high.1 = (bf16[128,2048]{1,0:T(8,128)(2,1)}, bf16[128,2048]{1,0:T(8,128)(2,1)}) custom-call(bf16[128,2048]{1,0:T(8,128)(2,1)S(1)} %bitcast.17, bf16[128,2048]{1,0:T(8,128)(2,1)S(1)} %bitcast.26, bf16[128,2048]{1,0:T(8,128)(2,1)S(1)} %collective-permute-done.other_ref.refs_2_.pair_ref, ...), custom_call_target="tpu_custom_call", output_to_operand_aliasing={{0}: (8, {}), {1}: (9, {})} | custom-call | flops 536870912 | bytes 5014016 | tf_op jit(solution)/shard_map/forward_high/pallas_call | solution.py:172
  37.6 0.0 collective-permute-done.6
  37.6 2.6 %collective-permute-start.7 = (f32[64,128]{1,0:T(8,128)S(1)}, f32[64,128]{1,0:T(8,128)S(1)}, u32[]{:S(2)}, u32[]{:S(2)}) collective-permute-start(f32[64,128]{1,0:T(8,128)S(1)} %add.23), channel_id=1, source_target_pairs={{2,0},{3,1},{0,2},{1,3},{6,4},{7,5},{4,6},{5,7},{10,8},{11,9},{8,1... | collective-permute-start | bytes 98312 | tf_op jit(solution)/shard_map/ppermute | solution.py:253
  40.2 2.6 %backward_low.1 = (bf16[128,2048]{1,0:T(8,128)(2,1)}, bf16[128,2048]{1,0:T(8,128)(2,1)}) custom-call(bf16[128,2048]{1,0:T(8,128)(2,1)S(1)} %bitcast.45, bf16[128,2048]{1,0:T(8,128)(2,1)S(1)} %bitcast.36, bf16[128,2048]{1,0:T(8,128)(2,1)S(1)} %collective-permute-done.other_ref.refs_2_.pair_ref, ...), custom_call_target="tpu_custom_call", output_to_operand_aliasing={{0}: (8, {}), {1}: (9, {})} | custom-call | flops 536870912 | bytes 5014016 | tf_op jit(solution)/shard_map/backward_low/pallas_call | solution.py:172
  42.8 0.0 collective-permute-done.7
  42.9 0.1 collective-permute-start.8
  43.0 1.2 %collective-permute-done.8 = f32[64,128]{1,0:T(8,128)S(1)} collective-permute-done((f32[64,128]{1,0:T(8,128)S(1)}, f32[64,128]{1,0:T(8,128)S(1)}, u32[]{:S(2)}, u32[]{:S(2)}) %collective-permute-start.8) | collective-permute-done | bytes 32800 | tf_op jit(solution)/shard_map/ppermute | solution.py:223
  44.1 0.6 %maximum_select_fusion = f32[128,128]{1,0:T(8,128)} fusion(f32[64,128]{1,0:T(8,128)S(1)} %collective-permute-done.8, f32[64,128]{1,0:T(8,128)S(1)} %add.24, pred[]{:T(512)S(6)} %eq.5), kind=kLoop, calls=%fused_computation.12 | loop fusion | flops 49152 | bytes 131073 | tf_op jit(solution)/shard_map/jit(_where)/select_n | solution.py:318
  (8 shorter events, 0.1 us)
Async XLA Ops:
  0.6 0.7 %copy-start.5 = (s32[1,128]{1,0:T(1,128)S(1)}, s32[1,128]{1,0:T(1,128)}, u32[]{:S(2)}) copy-start(s32[1,128]{1,0:T(1,128)} %param.10) | copy-start | bytes 1540
  1.4 1.5 %copy-start = (bf16[1,128,2048]{2,1,0:T(8,128)(2,1)S(1)}, bf16[1,128,2048]{2,1,0:T(8,128)(2,1)}, u32[]{:S(2)}) copy-start(bf16[1,128,2048]{2,1,0:T(8,128)(2,1)} %param.7) | copy-start | bytes 1572868
  1.5 1.5 %copy-start.1 = (bf16[1,128,2048]{2,1,0:T(8,128)(2,1)S(1)}, bf16[1,128,2048]{2,1,0:T(8,128)(2,1)}, u32[]{:S(2)}) copy-start(bf16[1,128,2048]{2,1,0:T(8,128)(2,1)} %param.8) | copy-start | bytes 1572868
  3.0 3.7 %copy-start.2 = (bf16[1,128,2048]{2,1,0:T(8,128)(2,1)S(1)}, bf16[1,128,2048]{2,1,0:T(8,128)(2,1)}, u32[]{:S(2)}) copy-start(bf16[1,128,2048]{2,1,0:T(8,128)(2,1)} %param.6) | copy-start | bytes 1572868
  3.0 3.7 %copy-start.3 = (bf16[1,128,2048]{2,1,0:T(8,128)(2,1)S(1)}, bf16[1,128,2048]{2,1,0:T(8,128)(2,1)}, u32[]{:S(2)}) copy-start(bf16[1,128,2048]{2,1,0:T(8,128)(2,1)} %param.9) | copy-start | bytes 1572868
  4.6 2.1 %collective-permute-start = (bf16[128,2048]{1,0:T(8,128)(2,1)S(1)}, bf16[128,2048]{1,0:T(8,128)(2,1)S(1)}, u32[]{:S(2)}, u32[]{:S(2)}) collective-permute-start(bf16[128,2048]{1,0:T(8,128)(2,1)S(1)} %fusion.1), channel_id=1, source_target_pairs={{0,4},{4,0},{8,12},{12,8},{16,20},{20,16},{24,28},{28,24},{1,5},{5... | collective-permute-start | bytes 1572872 | tf_op jit(solution)/shard_map/ppermute | solution.py:223
  5.1 7.0 %collective-permute-start.1 = (bf16[128,1024]{1,0:T(8,128)(2,1)S(1)}, bf16[128,1024]{1,0:T(8,128)(2,1)S(1)}, u32[]{:S(2)}, u32[]{:S(2)}) collective-permute-start(bf16[128,1024]{1,0:T(8,128)(2,1)S(1)} %fusion.3), channel_id=1, source_target_pairs={{4,8},{12,16},{20,24},{8,4},{16,12},{24,20},{5,9},{13,17},{21,25},... | collective-permute-start | bytes 786440 | tf_op jit(solution)/shard_map/ppermute | solution.py:229
  8.9 5.5 %collective-permute-start.2 = (f32[64,128]{1,0:T(8,128)S(1)}, f32[64,128]{1,0:T(8,128)S(1)}, u32[]{:S(2)}, u32[]{:S(2)}) collective-permute-start(f32[64,128]{1,0:T(8,128)S(1)} %filter_partner.1), channel_id=1, source_target_pairs={{0,4},{4,0},{8,12},{12,8},{16,20},{20,16},{24,28},{28,24},{1,5},{5... | collective-permute-start | bytes 98312 | tf_op jit(solution)/shard_map/ppermute | solution.py:223
  14.3 7.2 %copy-start.4 = (bf16[128,128]{1,0:T(8,128)(2,1)S(1)}, bf16[128,128]{1,0:T(8,128)(2,1)}, u32[]{:S(2)}) copy-start(bf16[128,128]{1,0:T(8,128)(2,1)} %taps_ref.3) | copy-start | bytes 98308
  14.4 18.3 %collective-permute-start.3 = (bf16[128,1024]{1,0:T(8,128)(2,1)S(1)}, bf16[128,1024]{1,0:T(8,128)(2,1)S(1)}, u32[]{:S(2)}, u32[]{:S(2)}) collective-permute-start(bf16[128,1024]{1,0:T(8,128)(2,1)S(1)} %fusion.5), channel_id=1, source_target_pairs={{4,8},{12,16},{20,24},{8,4},{16,12},{24,20},{5,9},{13,17},{21,25},... | collective-permute-start | bytes 786440 | tf_op jit(solution)/shard_map/ppermute | solution.py:229
  15.0 12.4 %collective-permute-start.4 = (f32[64,128]{1,0:T(8,128)S(1)}, f32[64,128]{1,0:T(8,128)S(1)}, u32[]{:S(2)}, u32[]{:S(2)}) collective-permute-start(f32[64,128]{1,0:T(8,128)S(1)} %add.20), channel_id=1, source_target_pairs={{8,0},{12,4},{0,8},{4,12},{24,16},{28,20},{16,24},{20,28},{9,1},{1... | collective-permute-start | bytes 98312 | tf_op jit(solution)/shard_map/ppermute | solution.py:253
  27.4 5.2 %collective-permute-start.5 = (f32[64,128]{1,0:T(8,128)S(1)}, f32[64,128]{1,0:T(8,128)S(1)}, u32[]{:S(2)}, u32[]{:S(2)}) collective-permute-start(f32[64,128]{1,0:T(8,128)S(1)} %add.21), channel_id=1, source_target_pairs={{16,0},{20,4},{24,8},{28,12},{0,16},{4,20},{8,24},{12,28},{17,1},{... | collective-permute-start | bytes 98312 | tf_op jit(solution)/shard_map/ppermute | solution.py:253
  32.7 4.9 %collective-permute-start.6 = (f32[64,128]{1,0:T(8,128)S(1)}, f32[64,128]{1,0:T(8,128)S(1)}, u32[]{:S(2)}, u32[]{:S(2)}) collective-permute-start(f32[64,128]{1,0:T(8,128)S(1)} %add.22), channel_id=1, source_target_pairs={{1,0},{0,1},{3,2},{2,3},{5,4},{4,5},{7,6},{6,7},{9,8},{8,9},{11,10... | collective-permute-start | bytes 98312 | tf_op jit(solution)/shard_map/ppermute | solution.py:253
  37.6 5.2 %collective-permute-start.7 = (f32[64,128]{1,0:T(8,128)S(1)}, f32[64,128]{1,0:T(8,128)S(1)}, u32[]{:S(2)}, u32[]{:S(2)}) collective-permute-start(f32[64,128]{1,0:T(8,128)S(1)} %add.23), channel_id=1, source_target_pairs={{2,0},{3,1},{0,2},{1,3},{6,4},{7,5},{4,6},{5,7},{10,8},{11,9},{8,1... | collective-permute-start | bytes 98312 | tf_op jit(solution)/shard_map/ppermute | solution.py:253
  42.9 1.3 %collective-permute-start.8 = (f32[64,128]{1,0:T(8,128)S(1)}, f32[64,128]{1,0:T(8,128)S(1)}, u32[]{:S(2)}, u32[]{:S(2)}) collective-permute-start(f32[64,128]{1,0:T(8,128)S(1)} %add.24), channel_id=1, source_target_pairs={{0,4},{4,0},{8,12},{12,8},{16,20},{20,16},{24,28},{28,24},{1,5},{5... | collective-permute-start | bytes 98312 | tf_op jit(solution)/shard_map/ppermute | solution.py:223

commit v8 on v7

--- a/solution.py
+++ b/solution.py
@@ -81,7 +81,7 @@
         kv = product(k_ref[:, lanes], v_ref[:, lanes])
         left = jnp.where(low, cot, kv)
         right = jnp.concatenate(
-            [jnp.where(low, kv, cot), other_ref[:, here if other_ref.shape[1] == width else lanes]], axis=0
+            [jnp.where(low, kv, cot), other_ref[:, here]], axis=0
         )
         for g in range(per_tile):
             picked = jnp.where(group == g, left, jnp.zeros_like(left))
@@ -130,7 +130,7 @@
         here = pl.ds(pl.multiple_of(index * LANES, LANES), LANES)
         lanes = pl.ds(pl.multiple_of(base + index * LANES, LANES), LANES)
         from_pair = even if backward else jnp.logical_not(even)
-        other = jnp.where(from_pair, pair_ref[:, lanes], far_ref[:, here])
+        other = jnp.where(from_pair, pair_ref[:, here], far_ref[:, here])
         x = jnp.concatenate([product(a_ref[:, lanes], b_ref[:, lanes]), other], axis=0)
         taps = taps_scr[pl.ds(pl.multiple_of(index * per_tile, per_tile), per_tile), :]
         y = jnp.zeros((rows, LANES), jnp.float32)
@@ -190,7 +190,7 @@
         "filter_partner" if partner else "filter_own",
         jax.ShapeDtypeStruct((groups // 2, rows), jnp.float32),
         [table, table, pltpu.VMEM((groups * 4, rows), jnp.float32)],
-        0, (q, k, v, dy, other, starts), moved=0,
+        1000, (q, k, v, dy, other, starts), moved=1000,
     )
 
 
@@ -242,7 +242,7 @@
 def rounds_over_chips():
     return [
         (axis, first * math.prod(factors(lax.axis_size(axis) // first)[:n]), p)
-        for axis, first in (("ctx", 2), ("dp", 1))
+        for axis, first in (("dp", 1), ("ctx", 2))
         for n, p in enumerate(factors(lax.axis_size(axis) // first))
     ]
 
@@ -276,7 +276,7 @@
     width = q.shape[1] // 2
     low, high, every = slice(0, width), slice(width, None), slice(None)
 
-    def sent(from_even, kv_part, cot_part, earlier=()):
+    def sent(from_even, kv_part, cot_part, *earlier):
         to_next = even if from_even else ~even
         q_, k_, v_, dy_ = lax.optimization_barrier((q, k, v, dy, *earlier))[:4]
         kv = product(k_[:, kv_part], v_[:, kv_part])
@@ -285,33 +285,34 @@
         return jnp.where(keep[:, None], jnp.where(to_next, kv, cot), 0)
 
     far_out = sent(False, low, high)
-    far_first = next_chip(far_out)
-    pair_out = sent(True, every, every, (far_out,))
+    far = next_chip(far_out)
+    pair_out = sent(True, low, high)
     pair = other_core(pair_out)
     theirs = filter_share(q, k, v, dy, pair, flags, groups, scale, True)
-    mine = filter_share(q, k, v, dy, after(far_first, theirs), flags, groups, scale, False)
+    mine = filter_share(q, k, v, dy, after(far, theirs), flags, groups, scale, False)
     mine = mine + other_core(theirs)
-
-    def forward(far, outs, half):
+    later_out = sent(False, high, low, pair_out, far_out), sent(True, high, low, pair_out, far_out)
+
+    def forward(pair, far, outs, half):
         return convolution(k, v, pair, far, q, dy, flags, filters, outs, False, half)
 
-    def backward(far, outs, half):
+    def backward(pair, far, outs, half):
         return convolution(dy, q, pair, far, v, k, flags, filters, outs, True, half)
 
-    far_out = sent(False, high, low, (pair_out,))
     for n, place in enumerate(rounds_over_chips()):
         if n == 0:
-            far_second = next_chip(after(far_out, mine))
-            half_forward = forward(far_first, None, 0)
+            later_far = next_chip(after(later_out[0], mine))
+            later_pair = other_core(after(later_out[1], mine))
+            half_forward = forward(pair, far, None, 0)
         if n == 1:
             mine = after(mine, *half_forward)
-            half_backward = backward(far_first, None, 1)
+            half_backward = backward(pair, far, None, 1)
         if n == 2:
-            mine = after(mine, *half_backward, far_second)
-            mixed, grad_q = forward(far_second, half_forward, 1)
+            mine = after(mine, *half_backward, later_far, later_pair)
+            mixed, grad_q = forward(later_pair, later_far, half_forward, 1)
         if n == 3:
             mine = after(mine, mixed, grad_q)
-            grad_k, grad_v = backward(far_second, half_backward, 0)
+            grad_k, grad_v = backward(later_pair, later_far, half_backward, 0)
         mine = summed_over(mine, *place)
     mine = after(mine, grad_k, grad_v)
     halves = [mine, other_core(mine)]

time: 45 us -> 41.1 us (0.913)
  waiting for transfers between devices: 5.44 us -> 2.01 us
  other arithmetic: 4.03 us -> 2.49 us
  local copies, waits for them, and re-layouts: 0.73 us -> 1.72 us
    ppermute x4, starting transfers between devices: 14.1 us -> 10.1 us  [summed_over(): lax.ppermute(total, axis, [(turned(i, k), i) for i in range(size)])]
    ppermute x3 -> x4, starting transfers between devices: 3.69 us -> 7.71 us  [other_core(): lax.ppermute(block, 'ctx', [(i, i ^ 1) for i in range(lax.axis_size('ctx'...]
    ppermute x4, waiting for transfers between devices: 3.38 us -> 0.31 us  [summed_over(): lax.ppermute(total, axis, [(turned(i, k), i) for i in range(size)])]
    select_n x3 -> x2, other arithmetic: 3.24 us -> 1.69 us  [sent(): return jnp.where(keep[:, None], jnp.where(to_next, kv, cot), 0)]
    unnamed x12 -> x14, local copies, waits for them, and re-layouts: 0.73 us -> 1.72 us
    ppermute x3 -> x4, waiting for transfers between devices: 2.06 us -> 1.69 us  [other_core(): lax.ppermute(block, 'ctx', [(i, i ^ 1) for i in range(lax.axis_size('ctx'...]
  transfers between devices with their start and end apart: 9 -> 10, of which waited for: 3 -> 3; matrix products, arithmetic and copies ran while one was open for 0% -> 1% of each run, Pallas kernels for 33% -> 36%
where the time goes in v8:
time: 41.1 us; the launch traced here: 40.8 us
  starting transfers between devices  19.1 us (46%)
  Pallas kernels  14.6 us (36%)
  other arithmetic  2.49 us (6%)
  waiting for transfers between devices  2.01 us (5%)
  local copies, waits for them, and re-layouts  1.72 us (4%)
  between operations  0.88 us (2%)
    pallas_call x6, Pallas kernels, local_call(): pl.pallas_call(kernel, out_shape=out_shape, in_specs=in_specs or [VMEM] *...  14.6 us
    ppermute x4, starting transfers between devices, summed_over(): lax.ppermute(total, axis, [(turned(i, k), i) for i in range(size)])  10.1 us
    ppermute x4, starting transfers between devices, other_core(): lax.ppermute(block, 'ctx', [(i, i ^ 1) for i in range(lax.axis_size('ctx'...  7.71 us
    unnamed x14, local copies, waits for them, and re-layouts  1.72 us
    select_n x2, other arithmetic, sent(): return jnp.where(keep[:, None], jnp.where(to_next, kv, cot), 0)  1.69 us
    ppermute x4, waiting for transfers between devices, other_core(): lax.ppermute(block, 'ctx', [(i, i ^ 1) for i in range(lax.axis_size('ctx'...  1.69 us
    ppermute x2, starting transfers between devices, next_chip(): return lax.ppermute(block, 'ctx', pairs + [(j, i) for i, j in pairs])  1.34 us
  transfers between devices with their start and end apart: 10, of which 3 were waited for; matrix products, arithmetic and copies ran while one was open for 1% of the time, Pallas kernels for 36%

profile of v8, /device:TPU:0, one launch (start us, length us, event | category | flops | bytes accessed | tf_op | source)
XLA Modules:
  0.0 40.8 jit_solution(2393491340993450387)
XLA Ops:
  0.6 0.0 copy-start.6
  0.7 0.6 %copy-done.6 = s32[1,128]{1,0:T(1,128)S(1)} copy-done((s32[1,128]{1,0:T(1,128)S(1)}, s32[1,128]{1,0:T(1,128)}, u32[]{:S(2)}) %copy-start.6) | copy-done | bytes 536
  1.3 0.1 fusion.1
  1.4 0.0 copy-start
  1.5 0.0 copy-start.1
  1.5 0.0 copy-start.2
  1.5 1.5 %select_select_fusion.2 = (bf16[128,1024]{1,0:T(8,128)(2,1)S(1)}, bf16[128,1024]{1,0:T(8,128)(2,1)S(1)}) fusion(pred[128]{0:T(512)(128)(4,1)S(1)} %get-tuple-element.57, pred[]{:T(512)S(6)} %not.26, bf16[128,2048]{1,0:T(8,128)(2,1)} %bitcast.18, bf16[128,2048]{1,0:T(8,128)(2,1)} %bitcast.10, bf16[128,2048]{1,0:T(8,128)(2,1)} %bitcast.26, ...), kind=kLoop, calls=%fused_computation.6 | loop fusion | flops 1572864 | bytes 1573122 | tf_op jit(solution)/shard_map/jit(_where)/select_n | solution.py:285
  3.0 0.5 %collective-permute-start.1 = (bf16[128,1024]{1,0:T(8,128)(2,1)S(1)}, bf16[128,1024]{1,0:T(8,128)(2,1)S(1)}, u32[]{:S(2)}, u32[]{:S(2)}) collective-permute-start(bf16[128,1024]{1,0:T(8,128)(2,1)S(1)} %get-tuple-element.56), channel_id=1, source_target_pairs={{0,4},{4,0},{8,12},{12,8},{16,20},{20,16},{24,28},{28,24},{1,5},{5... | collective-permute-start | bytes 786440 | tf_op jit(solution)/shard_map/ppermute | solution.py:223
  3.5 0.7 %collective-permute-start = (bf16[128,1024]{1,0:T(8,128)(2,1)S(1)}, bf16[128,1024]{1,0:T(8,128)(2,1)S(1)}, u32[]{:S(2)}, u32[]{:S(2)}) collective-permute-start(bf16[128,1024]{1,0:T(8,128)(2,1)S(1)} %get-tuple-element.55), channel_id=1, source_target_pairs={{4,8},{12,16},{20,24},{8,4},{16,12},{24,20},{5,9},{13,17},{21,25},... | collective-permute-start | bytes 786440 | tf_op jit(solution)/shard_map/ppermute | solution.py:229
  4.2 0.5 %collective-permute-done.1.other_ref.refs_2_ = bf16[128,1024]{1,0:T(8,128)(2,1)S(1)} collective-permute-done((bf16[128,1024]{1,0:T(8,128)(2,1)S(1)}, bf16[128,1024]{1,0:T(8,128)(2,1)S(1)}, u32[]{:S(2)}, u32[]{:S(2)}) %collective-permute-start.1) | collective-permute-done | bytes 262176 | tf_op jit(solution)/shard_map/ppermute | solution.py:223
  4.7 0.0 copy-done
  4.7 0.0 copy-done.1
  4.7 0.0 copy-done.2
  4.7 0.0 copy-start.3
  4.7 1.0 %copy-done.3 = bf16[1,128,2048]{2,1,0:T(8,128)(2,1)S(1)} copy-done((bf16[1,128,2048]{2,1,0:T(8,128)(2,1)S(1)}, bf16[1,128,2048]{2,1,0:T(8,128)(2,1)}, u32[]{:S(2)}) %copy-start.3) | copy-done | bytes 524312
  5.7 2.2 %filter_partner.1 = f32[64,128]{1,0:T(8,128)S(1)} custom-call(bf16[128,2048]{1,0:T(8,128)(2,1)S(1)} %bitcast.27, bf16[128,2048]{1,0:T(8,128)(2,1)S(1)} %bitcast.11, bf16[128,2048]{1,0:T(8,128)(2,1)S(1)} %bitcast.19, bf16[128,2048]{1,0:T(8,128)(2,1)S(1)} %bitcast.35, bf16[128,1024]{1,0:T(8,128)(2,1)S(1)} %collective-permute-done.1.other_ref.refs_2_, ...), custom_call_target="tpu_custom_call" | custom-call | flops 1000 | bytes 1000 | tf_op jit(solution)/shard_map/filter_partner/pallas_call | solution.py:172
  7.9 3.5 %collective-permute-start.2 = (f32[64,128]{1,0:T(8,128)S(1)}, f32[64,128]{1,0:T(8,128)S(1)}, u32[]{:S(2)}, u32[]{:S(2)}) collective-permute-start(f32[64,128]{1,0:T(8,128)S(1)} %filter_partner.1), channel_id=1, source_target_pairs={{0,4},{4,0},{8,12},{12,8},{16,20},{20,16},{24,28},{28,24},{1,5},{5... | collective-permute-start | bytes 98312 | tf_op jit(solution)/shard_map/ppermute | solution.py:223
  11.4 0.2 select_select_fusion
  11.6 0.0 copy-start.4
  11.6 0.0 collective-permute-done.other_ref.refs_3_
  11.6 2.2 %filter_own.1 = f32[64,128]{1,0:T(8,128)S(1)} custom-call(bf16[128,2048]{1,0:T(8,128)(2,1)S(1)} %bitcast.29, bf16[128,2048]{1,0:T(8,128)(2,1)S(1)} %bitcast.13, bf16[128,2048]{1,0:T(8,128)(2,1)S(1)} %bitcast.21, bf16[128,2048]{1,0:T(8,128)(2,1)S(1)} %bitcast.37, bf16[128,1024]{1,0:T(8,128)(2,1)S(1)} %collective-permute-done.other_ref.refs_3_, ...), custom_call_target="tpu_custom_call" | custom-call | flops 1000 | bytes 1000 | tf_op jit(solution)/shard_map/filter_own/pallas_call | solution.py:172
  13.8 0.0 copy-start.5
  13.8 0.0 collective-permute-done.2
  13.8 0.7 %collective-permute-start.4 = (bf16[128,1024]{1,0:T(8,128)(2,1)S(1)}, bf16[128,1024]{1,0:T(8,128)(2,1)S(1)}, u32[]{:S(2)}, u32[]{:S(2)}) collective-permute-start(bf16[128,1024]{1,0:T(8,128)(2,1)S(1)} %get-tuple-element.38), channel_id=1, source_target_pairs={{4,8},{12,16},{20,24},{8,4},{16,12},{24,20},{5,9},{13,17},{21,25},... | collective-permute-start | bytes 786440 | tf_op jit(solution)/shard_map/ppermute | solution.py:229
  14.5 3.7 %collective-permute-start.3 = (bf16[128,1024]{1,0:T(8,128)(2,1)S(1)}, bf16[128,1024]{1,0:T(8,128)(2,1)S(1)}, u32[]{:S(2)}, u32[]{:S(2)}) collective-permute-start(bf16[128,1024]{1,0:T(8,128)(2,1)S(1)} %get-tuple-element.37), channel_id=1, source_target_pairs={{0,4},{4,0},{8,12},{12,8},{16,20},{20,16},{24,28},{28,24},{1,5},{5... | collective-permute-start | bytes 786440 | tf_op jit(solution)/shard_map/ppermute | solution.py:223
  18.2 2.8 %collective-permute-start.5 = (f32[64,128]{1,0:T(8,128)S(1)}, f32[64,128]{1,0:T(8,128)S(1)}, u32[]{:S(2)}, u32[]{:S(2)}) collective-permute-start(f32[64,128]{1,0:T(8,128)S(1)} %add.20), channel_id=1, source_target_pairs={{1,0},{0,1},{3,2},{2,3},{5,4},{4,5},{7,6},{6,7},{9,8},{8,9},{11,10... | collective-permute-start | bytes 98312 | tf_op jit(solution)/shard_map/ppermute | solution.py:253
  21.0 0.0 copy-done.4
  21.0 0.0 copy-done.5
  21.0 2.5 %forward_low.1 = (bf16[128,2048]{1,0:T(8,128)(2,1)}, bf16[128,2048]{1,0:T(8,128)(2,1)}) custom-call(bf16[128,2048]{1,0:T(8,128)(2,1)S(1)} %bitcast.14, bf16[128,2048]{1,0:T(8,128)(2,1)S(1)} %bitcast.22, bf16[128,1024]{1,0:T(8,128)(2,1)S(1)} %collective-permute-done.1.other_ref.refs_2_, bf16[128,1024]{1,0:T(8,128)(2,1)S(1)} %collective-permute-done.other_ref.refs_3_, ...), custom_call_target="tpu_custom_call" | custom-call | flops 536870912 | bytes 3703296 | tf_op jit(solution)/shard_map/forward_low/pallas_call | solution.py:172
  23.5 0.0 collective-permute-done.5
  23.6 2.7 %collective-permute-start.6 = (f32[64,128]{1,0:T(8,128)S(1)}, f32[64,128]{1,0:T(8,128)S(1)}, u32[]{:S(2)}, u32[]{:S(2)}) collective-permute-start(f32[64,128]{1,0:T(8,128)S(1)} %add.21), channel_id=1, source_target_pairs={{2,0},{3,1},{0,2},{1,3},{6,4},{7,5},{4,6},{5,7},{10,8},{11,9},{8,1... | collective-permute-start | bytes 98312 | tf_op jit(solution)/shard_map/ppermute | solution.py:253
  26.2 2.6 %backward_high.1 = (bf16[128,2048]{1,0:T(8,128)(2,1)}, bf16[128,2048]{1,0:T(8,128)(2,1)}) custom-call(bf16[128,2048]{1,0:T(8,128)(2,1)S(1)} %bitcast.39, bf16[128,2048]{1,0:T(8,128)(2,1)S(1)} %bitcast.31, bf16[128,1024]{1,0:T(8,128)(2,1)S(1)} %collective-permute-done.1.other_ref.refs_2_, bf16[128,1024]{1,0:T(8,128)(2,1)S(1)} %collective-permute-done.other_ref.refs_3_, ...), custom_call_target="tpu_custom_call" | custom-call | flops 536870912 | bytes 3703296 | tf_op jit(solution)/shard_map/backward_high/pallas_call | solution.py:172
  28.8 0.0 collective-permute-done.6
  28.9 0.0 collective-permute-done.4.far_ref
  28.9 0.0 collective-permute-done.3.pair_ref
  28.9 3.5 %collective-permute-start.7 = (f32[64,128]{1,0:T(8,128)S(1)}, f32[64,128]{1,0:T(8,128)S(1)}, u32[]{:S(2)}, u32[]{:S(2)}) collective-permute-start(f32[64,128]{1,0:T(8,128)S(1)} %add.22), channel_id=1, source_target_pairs={{8,0},{12,4},{0,8},{4,12},{24,16},{28,20},{16,24},{20,28},{9,1},{1... | collective-permute-start | bytes 98312 | tf_op jit(solution)/shard_map/ppermute | solution.py:253
  32.4 2.5 %forward_high.1 = (bf16[128,2048]{1,0:T(8,128)(2,1)}, bf16[128,2048]{1,0:T(8,128)(2,1)}) custom-call(bf16[128,2048]{1,0:T(8,128)(2,1)S(1)} %bitcast.16, bf16[128,2048]{1,0:T(8,128)(2,1)S(1)} %bitcast.24, bf16[128,1024]{1,0:T(8,128)(2,1)S(1)} %collective-permute-done.3.pair_ref, ...), custom_call_target="tpu_custom_call", output_to_operand_aliasing={{0}: (8, {}), {1}: (9, {})} | custom-call | flops 536870912 | bytes 4751872 | tf_op jit(solution)/shard_map/forward_high/pallas_call | solution.py:172
  35.0 0.0 collective-permute-done.7
  35.0 1.1 %collective-permute-start.8 = (f32[64,128]{1,0:T(8,128)S(1)}, f32[64,128]{1,0:T(8,128)S(1)}, u32[]{:S(2)}, u32[]{:S(2)}) collective-permute-start(f32[64,128]{1,0:T(8,128)S(1)} %add.23), channel_id=1, source_target_pairs={{16,0},{20,4},{24,8},{28,12},{0,16},{4,20},{8,24},{12,28},{17,1},{... | collective-permute-start | bytes 98312 | tf_op jit(solution)/shard_map/ppermute | solution.py:253
  36.1 2.6 %backward_low.1 = (bf16[128,2048]{1,0:T(8,128)(2,1)}, bf16[128,2048]{1,0:T(8,128)(2,1)}) custom-call(bf16[128,2048]{1,0:T(8,128)(2,1)S(1)} %bitcast.41, bf16[128,2048]{1,0:T(8,128)(2,1)S(1)} %bitcast.33, bf16[128,1024]{1,0:T(8,128)(2,1)S(1)} %collective-permute-done.3.pair_ref, ...), custom_call_target="tpu_custom_call", output_to_operand_aliasing={{0}: (8, {}), {1}: (9, {})} | custom-call | flops 536870912 | bytes 4751872 | tf_op jit(solution)/shard_map/backward_low/pallas_call | solution.py:172
  38.7 0.3 collective-permute-done.8
  39.0 0.0 collective-permute-start.9
  39.0 1.2 %collective-permute-done.9 = f32[64,128]{1,0:T(8,128)S(1)} collective-permute-done((f32[64,128]{1,0:T(8,128)S(1)}, f32[64,128]{1,0:T(8,128)S(1)}, u32[]{:S(2)}, u32[]{:S(2)}) %collective-permute-start.9) | collective-permute-done | bytes 32800 | tf_op jit(solution)/shard_map/ppermute | solution.py:223
  40.2 0.6 %maximum_select_fusion = f32[128,128]{1,0:T(8,128)} fusion(f32[64,128]{1,0:T(8,128)S(1)} %collective-permute-done.9, f32[64,128]{1,0:T(8,128)S(1)} %add.24, pred[]{:T(512)S(6)} %eq.5), kind=kLoop, calls=%fused_computation.8 | loop fusion | flops 49152 | bytes 131073 | tf_op jit(solution)/shard_map/jit(_where)/select_n | solution.py:319
  (8 shorter events, 0.1 us)
Async XLA Ops:
  0.6 0.7 %copy-start.6 = (s32[1,128]{1,0:T(1,128)S(1)}, s32[1,128]{1,0:T(1,128)}, u32[]{:S(2)}) copy-start(s32[1,128]{1,0:T(1,128)} %param.10) | copy-start | bytes 1540
  1.4 3.2 %copy-start = (bf16[1,128,2048]{2,1,0:T(8,128)(2,1)S(1)}, bf16[1,128,2048]{2,1,0:T(8,128)(2,1)}, u32[]{:S(2)}) copy-start(bf16[1,128,2048]{2,1,0:T(8,128)(2,1)} %param.7) | copy-start | bytes 1572868
  1.5 3.2 %copy-start.1 = (bf16[1,128,2048]{2,1,0:T(8,128)(2,1)S(1)}, bf16[1,128,2048]{2,1,0:T(8,128)(2,1)}, u32[]{:S(2)}) copy-start(bf16[1,128,2048]{2,1,0:T(8,128)(2,1)} %param.8) | copy-start | bytes 1572868
  1.5 3.2 %copy-start.2 = (bf16[1,128,2048]{2,1,0:T(8,128)(2,1)S(1)}, bf16[1,128,2048]{2,1,0:T(8,128)(2,1)}, u32[]{:S(2)}) copy-start(bf16[1,128,2048]{2,1,0:T(8,128)(2,1)} %param.6) | copy-start | bytes 1572868
  3.0 1.7 %collective-permute-start.1 = (bf16[128,1024]{1,0:T(8,128)(2,1)S(1)}, bf16[128,1024]{1,0:T(8,128)(2,1)S(1)}, u32[]{:S(2)}, u32[]{:S(2)}) collective-permute-start(bf16[128,1024]{1,0:T(8,128)(2,1)S(1)} %get-tuple-element.56), channel_id=1, source_target_pairs={{0,4},{4,0},{8,12},{12,8},{16,20},{20,16},{24,28},{28,24},{1,5},{5... | collective-permute-start | bytes 786440 | tf_op jit(solution)/shard_map/ppermute | solution.py:223
  3.5 8.1 %collective-permute-start = (bf16[128,1024]{1,0:T(8,128)(2,1)S(1)}, bf16[128,1024]{1,0:T(8,128)(2,1)S(1)}, u32[]{:S(2)}, u32[]{:S(2)}) collective-permute-start(bf16[128,1024]{1,0:T(8,128)(2,1)S(1)} %get-tuple-element.55), channel_id=1, source_target_pairs={{4,8},{12,16},{20,24},{8,4},{16,12},{24,20},{5,9},{13,17},{21,25},... | collective-permute-start | bytes 786440 | tf_op jit(solution)/shard_map/ppermute | solution.py:229
  4.7 1.0 %copy-start.3 = (bf16[1,128,2048]{2,1,0:T(8,128)(2,1)S(1)}, bf16[1,128,2048]{2,1,0:T(8,128)(2,1)}, u32[]{:S(2)}) copy-start(bf16[1,128,2048]{2,1,0:T(8,128)(2,1)} %param.9) | copy-start | bytes 1572868
  7.9 5.9 %collective-permute-start.2 = (f32[64,128]{1,0:T(8,128)S(1)}, f32[64,128]{1,0:T(8,128)S(1)}, u32[]{:S(2)}, u32[]{:S(2)}) collective-permute-start(f32[64,128]{1,0:T(8,128)S(1)} %filter_partner.1), channel_id=1, source_target_pairs={{0,4},{4,0},{8,12},{12,8},{16,20},{20,16},{24,28},{28,24},{1,5},{5... | collective-permute-start | bytes 98312 | tf_op jit(solution)/shard_map/ppermute | solution.py:223
  11.6 9.4 %copy-start.4 = (bf16[1,128,2048]{2,1,0:T(8,128)(2,1)S(1)}, bf16[1,128,2048]{2,1,0:T(8,128)(2,1)}, u32[]{:S(2)}) copy-start(bf16[1,128,2048]{2,1,0:T(8,128)(2,1)} %param.9) | copy-start | bytes 1572868
  13.8 7.2 %copy-start.5 = (bf16[128,128]{1,0:T(8,128)(2,1)S(1)}, bf16[128,128]{1,0:T(8,128)(2,1)}, u32[]{:S(2)}) copy-start(bf16[128,128]{1,0:T(8,128)(2,1)} %taps_ref.3) | copy-start | bytes 98308
  13.8 15.1 %collective-permute-start.4 = (bf16[128,1024]{1,0:T(8,128)(2,1)S(1)}, bf16[128,1024]{1,0:T(8,128)(2,1)S(1)}, u32[]{:S(2)}, u32[]{:S(2)}) collective-permute-start(bf16[128,1024]{1,0:T(8,128)(2,1)S(1)} %get-tuple-element.38), channel_id=1, source_target_pairs={{4,8},{12,16},{20,24},{8,4},{16,12},{24,20},{5,9},{13,17},{21,25},... | collective-permute-start | bytes 786440 | tf_op jit(solution)/shard_map/ppermute | solution.py:229
  14.5 14.4 %collective-permute-start.3 = (bf16[128,1024]{1,0:T(8,128)(2,1)S(1)}, bf16[128,1024]{1,0:T(8,128)(2,1)S(1)}, u32[]{:S(2)}, u32[]{:S(2)}) collective-permute-start(bf16[128,1024]{1,0:T(8,128)(2,1)S(1)} %get-tuple-element.37), channel_id=1, source_target_pairs={{0,4},{4,0},{8,12},{12,8},{16,20},{20,16},{24,28},{28,24},{1,5},{5... | collective-permute-start | bytes 786440 | tf_op jit(solution)/shard_map/ppermute | solution.py:223
  18.2 5.3 %collective-permute-start.5 = (f32[64,128]{1,0:T(8,128)S(1)}, f32[64,128]{1,0:T(8,128)S(1)}, u32[]{:S(2)}, u32[]{:S(2)}) collective-permute-start(f32[64,128]{1,0:T(8,128)S(1)} %add.20), channel_id=1, source_target_pairs={{1,0},{0,1},{3,2},{2,3},{5,4},{4,5},{7,6},{6,7},{9,8},{8,9},{11,10... | collective-permute-start | bytes 98312 | tf_op jit(solution)/shard_map/ppermute | solution.py:253
  23.6 5.3 %collective-permute-start.6 = (f32[64,128]{1,0:T(8,128)S(1)}, f32[64,128]{1,0:T(8,128)S(1)}, u32[]{:S(2)}, u32[]{:S(2)}) collective-permute-start(f32[64,128]{1,0:T(8,128)S(1)} %add.21), channel_id=1, source_target_pairs={{2,0},{3,1},{0,2},{1,3},{6,4},{7,5},{4,6},{5,7},{10,8},{11,9},{8,1... | collective-permute-start | bytes 98312 | tf_op jit(solution)/shard_map/ppermute | solution.py:253
  28.9 6.1 %collective-permute-start.7 = (f32[64,128]{1,0:T(8,128)S(1)}, f32[64,128]{1,0:T(8,128)S(1)}, u32[]{:S(2)}, u32[]{:S(2)}) collective-permute-start(f32[64,128]{1,0:T(8,128)S(1)} %add.22), channel_id=1, source_target_pairs={{8,0},{12,4},{0,8},{4,12},{24,16},{28,20},{16,24},{20,28},{9,1},{1... | collective-permute-start | bytes 98312 | tf_op jit(solution)/shard_map/ppermute | solution.py:253
  35.0 4.0 %collective-permute-start.8 = (f32[64,128]{1,0:T(8,128)S(1)}, f32[64,128]{1,0:T(8,128)S(1)}, u32[]{:S(2)}, u32[]{:S(2)}) collective-permute-start(f32[64,128]{1,0:T(8,128)S(1)} %add.23), channel_id=1, source_target_pairs={{16,0},{20,4},{24,8},{28,12},{0,16},{4,20},{8,24},{12,28},{17,1},{... | collective-permute-start | bytes 98312 | tf_op jit(solution)/shard_map/ppermute | solution.py:253
  39.0 1.2 %collective-permute-start.9 = (f32[64,128]{1,0:T(8,128)S(1)}, f32[64,128]{1,0:T(8,128)S(1)}, u32[]{:S(2)}, u32[]{:S(2)}) collective-permute-start(f32[64,128]{1,0:T(8,128)S(1)} %add.24), channel_id=1, source_target_pairs={{0,4},{4,0},{8,12},{12,8},{16,20},{20,16},{24,28},{28,24},{1,5},{5... | collective-permute-start | bytes 98312 | tf_op jit(solution)/shard_map/ppermute | solution.py:223

commit v9 on v8

--- a/solution.py
+++ b/solution.py
@@ -289,9 +289,10 @@
     pair_out = sent(True, low, high)
     pair = other_core(pair_out)
     theirs = filter_share(q, k, v, dy, pair, flags, groups, scale, True)
+    later_far = next_chip(sent(False, high, low, theirs))
+    later_pair = other_core(sent(True, high, low, theirs))
     mine = filter_share(q, k, v, dy, after(far, theirs), flags, groups, scale, False)
     mine = mine + other_core(theirs)
-    later_out = sent(False, high, low, pair_out, far_out), sent(True, high, low, pair_out, far_out)
 
     def forward(pair, far, outs, half):
         return convolution(k, v, pair, far, q, dy, flags, filters, outs, False, half)
@@ -301,8 +302,6 @@
 
     for n, place in enumerate(rounds_over_chips()):
         if n == 0:
-            later_far = next_chip(after(later_out[0], mine))
-            later_pair = other_core(after(later_out[1], mine))
             half_forward = forward(pair, far, None, 0)
         if n == 1:
             mine = after(mine, *half_forward)

time: 41.1 us -> 37.7 us (0.917)
  starting transfers between devices: 19.1 us -> 16 us
    ppermute x4, starting transfers between devices: 10.1 us -> 7.56 us  [summed_over(): lax.ppermute(total, axis, [(turned(i, k), i) for i in range(size)])]
    ppermute x4, starting transfers between devices: 7.71 us -> 6.95 us  [other_core(): lax.ppermute(block, 'ctx', [(i, i ^ 1) for i in range(lax.axis_size('ctx'...]
  transfers between devices with their start and end apart: 10 -> 10, of which waited for: 3 -> 2; matrix products, arithmetic and copies ran while one was open for 1% -> 1% of each run, Pallas kernels for 36% -> 39%
where the time goes in v9:
time: 37.7 us; the launch traced here: 37.4 us
  starting transfers between devices  16 us (42%)
  Pallas kernels  14.6 us (39%)
  other arithmetic  2.5 us (7%)
  local copies, waits for them, and re-layouts  1.71 us (5%)
  waiting for transfers between devices  1.7 us (5%)
  between operations  0.89 us (2%)
    pallas_call x6, Pallas kernels, local_call(): pl.pallas_call(kernel, out_shape=out_shape, in_specs=in_specs or [VMEM] *...  14.6 us
    ppermute x4, starting transfers between devices, summed_over(): lax.ppermute(total, axis, [(turned(i, k), i) for i in range(size)])  7.56 us
    ppermute x4, starting transfers between devices, other_core(): lax.ppermute(block, 'ctx', [(i, i ^ 1) for i in range(lax.axis_size('ctx'...  6.95 us
    unnamed x14, local copies, waits for them, and re-layouts  1.71 us
    select_n x2, other arithmetic, sent(): return jnp.where(keep[:, None], jnp.where(to_next, kv, cot), 0)  1.7 us
    ppermute x4, waiting for transfers between devices, other_core(): lax.ppermute(block, 'ctx', [(i, i ^ 1) for i in range(lax.axis_size('ctx'...  1.69 us
    ppermute x2, starting transfers between devices, next_chip(): return lax.ppermute(block, 'ctx', pairs + [(j, i) for i, j in pairs])  1.46 us
  transfers between devices with their start and end apart: 10, of which 2 were waited for; matrix products, arithmetic and copies ran while one was open for 1% of the time, Pallas kernels for 39%

profile of v9, /device:TPU:0, one launch (start us, length us, event | category | flops | bytes accessed | tf_op | source)
XLA Modules:
  0.0 37.4 jit_solution(2251936212890541314)
XLA Ops:
  0.6 0.0 copy-start.6
  0.7 0.6 %copy-done.6 = s32[1,128]{1,0:T(1,128)S(1)} copy-done((s32[1,128]{1,0:T(1,128)S(1)}, s32[1,128]{1,0:T(1,128)}, u32[]{:S(2)}) %copy-start.6) | copy-done | bytes 536
  1.3 0.1 fusion.1
  1.4 0.0 copy-start
  1.5 0.0 copy-start.1
  1.5 0.0 copy-start.2
  1.5 1.5 %select_select_fusion = (bf16[128,1024]{1,0:T(8,128)(2,1)S(1)}, bf16[128,1024]{1,0:T(8,128)(2,1)S(1)}) fusion(pred[128]{0:T(512)(128)(4,1)S(1)} %get-tuple-element.53, pred[]{:T(512)S(6)} %not.26, bf16[128,2048]{1,0:T(8,128)(2,1)} %bitcast.18, bf16[128,2048]{1,0:T(8,128)(2,1)} %bitcast.10, bf16[128,2048]{1,0:T(8,128)(2,1)} %bitcast.26, ...), kind=kLoop, calls=%fused_computation.4 | loop fusion | flops 1572864 | bytes 1573122 | tf_op jit(solution)/shard_map/jit(_where)/select_n | solution.py:285
  3.0 0.5 %collective-permute-start = (bf16[128,1024]{1,0:T(8,128)(2,1)S(1)}, bf16[128,1024]{1,0:T(8,128)(2,1)S(1)}, u32[]{:S(2)}, u32[]{:S(2)}) collective-permute-start(bf16[128,1024]{1,0:T(8,128)(2,1)S(1)} %get-tuple-element.50), channel_id=1, source_target_pairs={{0,4},{4,0},{8,12},{12,8},{16,20},{20,16},{24,28},{28,24},{1,5},{5... | collective-permute-start | bytes 786440 | tf_op jit(solution)/shard_map/ppermute | solution.py:223
  3.5 0.7 %collective-permute-start.3 = (bf16[128,1024]{1,0:T(8,128)(2,1)S(1)}, bf16[128,1024]{1,0:T(8,128)(2,1)S(1)}, u32[]{:S(2)}, u32[]{:S(2)}) collective-permute-start(bf16[128,1024]{1,0:T(8,128)(2,1)S(1)} %get-tuple-element.49), channel_id=1, source_target_pairs={{4,8},{12,16},{20,24},{8,4},{16,12},{24,20},{5,9},{13,17},{21,25},... | collective-permute-start | bytes 786440 | tf_op jit(solution)/shard_map/ppermute | solution.py:229
  4.2 0.5 %collective-permute-done.other_ref.refs_2_ = bf16[128,1024]{1,0:T(8,128)(2,1)S(1)} collective-permute-done((bf16[128,1024]{1,0:T(8,128)(2,1)S(1)}, bf16[128,1024]{1,0:T(8,128)(2,1)S(1)}, u32[]{:S(2)}, u32[]{:S(2)}) %collective-permute-start) | collective-permute-done | bytes 262176 | tf_op jit(solution)/shard_map/ppermute | solution.py:223
  4.7 0.0 copy-done
  4.7 0.0 copy-done.1
  4.7 0.0 copy-done.2
  4.7 0.0 copy-start.3
  4.7 1.0 %copy-done.3 = bf16[1,128,2048]{2,1,0:T(8,128)(2,1)S(1)} copy-done((bf16[1,128,2048]{2,1,0:T(8,128)(2,1)S(1)}, bf16[1,128,2048]{2,1,0:T(8,128)(2,1)}, u32[]{:S(2)}) %copy-start.3) | copy-done | bytes 524312
  5.7 2.2 %filter_partner.1 = f32[64,128]{1,0:T(8,128)S(1)} custom-call(bf16[128,2048]{1,0:T(8,128)(2,1)S(1)} %bitcast.27, bf16[128,2048]{1,0:T(8,128)(2,1)S(1)} %bitcast.11, bf16[128,2048]{1,0:T(8,128)(2,1)S(1)} %bitcast.19, bf16[128,2048]{1,0:T(8,128)(2,1)S(1)} %bitcast.35, bf16[128,1024]{1,0:T(8,128)(2,1)S(1)} %collective-permute-done.other_ref.refs_2_, ...), custom_call_target="tpu_custom_call" | custom-call | flops 1000 | bytes 1000 | tf_op jit(solution)/shard_map/filter_partner/pallas_call | solution.py:172
  7.9 0.2 select_select_fusion.1
  8.1 3.5 %collective-permute-start.1 = (bf16[128,1024]{1,0:T(8,128)(2,1)S(1)}, bf16[128,1024]{1,0:T(8,128)(2,1)S(1)}, u32[]{:S(2)}, u32[]{:S(2)}) collective-permute-start(bf16[128,1024]{1,0:T(8,128)(2,1)S(1)} %get-tuple-element.52), channel_id=1, source_target_pairs={{0,4},{4,0},{8,12},{12,8},{16,20},{20,16},{24,28},{28,24},{1,5},{5... | collective-permute-start | bytes 786440 | tf_op jit(solution)/shard_map/ppermute | solution.py:223
  11.6 0.0 copy-start.4
  11.6 0.8 %collective-permute-start.2 = (bf16[128,1024]{1,0:T(8,128)(2,1)S(1)}, bf16[128,1024]{1,0:T(8,128)(2,1)S(1)}, u32[]{:S(2)}, u32[]{:S(2)}) collective-permute-start(bf16[128,1024]{1,0:T(8,128)(2,1)S(1)} %get-tuple-element.51), channel_id=1, source_target_pairs={{4,8},{12,16},{20,24},{8,4},{16,12},{24,20},{5,9},{13,17},{21,25},... | collective-permute-start | bytes 786440 | tf_op jit(solution)/shard_map/ppermute | solution.py:229
  12.4 2.9 %collective-permute-start.4 = (f32[64,128]{1,0:T(8,128)S(1)}, f32[64,128]{1,0:T(8,128)S(1)}, u32[]{:S(2)}, u32[]{:S(2)}) collective-permute-start(f32[64,128]{1,0:T(8,128)S(1)} %filter_partner.1), channel_id=1, source_target_pairs={{0,4},{4,0},{8,12},{12,8},{16,20},{20,16},{24,28},{28,24},{1,5},{5... | collective-permute-start | bytes 98312 | tf_op jit(solution)/shard_map/ppermute | solution.py:223
  15.3 0.0 collective-permute-done.3.refs_3_.other_ref
  15.3 2.2 %filter_own.1 = f32[64,128]{1,0:T(8,128)S(1)} custom-call(bf16[128,2048]{1,0:T(8,128)(2,1)S(1)} %bitcast.29, bf16[128,2048]{1,0:T(8,128)(2,1)S(1)} %bitcast.13, bf16[128,2048]{1,0:T(8,128)(2,1)S(1)} %bitcast.21, bf16[128,2048]{1,0:T(8,128)(2,1)S(1)} %bitcast.37, bf16[128,1024]{1,0:T(8,128)(2,1)S(1)} %collective-permute-done.3.refs_3_.other_ref, ...), custom_call_target="tpu_custom_call" | custom-call | flops 1000 | bytes 1000 | tf_op jit(solution)/shard_map/filter_own/pallas_call | solution.py:172
  17.5 0.0 copy-start.5
  17.5 0.0 collective-permute-done.4
  17.5 1.7 %collective-permute-start.5 = (f32[64,128]{1,0:T(8,128)S(1)}, f32[64,128]{1,0:T(8,128)S(1)}, u32[]{:S(2)}, u32[]{:S(2)}) collective-permute-start(f32[64,128]{1,0:T(8,128)S(1)} %add.20), channel_id=1, source_target_pairs={{1,0},{0,1},{3,2},{2,3},{5,4},{4,5},{7,6},{6,7},{9,8},{8,9},{11,10... | collective-permute-start | bytes 98312 | tf_op jit(solution)/shard_map/ppermute | solution.py:253
  19.1 0.0 copy-done.4
  19.2 0.0 copy-done.5
  19.2 2.5 %forward_low.1 = (bf16[128,2048]{1,0:T(8,128)(2,1)}, bf16[128,2048]{1,0:T(8,128)(2,1)}) custom-call(bf16[128,2048]{1,0:T(8,128)(2,1)S(1)} %bitcast.14, bf16[128,2048]{1,0:T(8,128)(2,1)S(1)} %bitcast.22, bf16[128,1024]{1,0:T(8,128)(2,1)S(1)} %collective-permute-done.other_ref.refs_2_, bf16[128,1024]{1,0:T(8,128)(2,1)S(1)} %collective-permute-done.3.refs_3_.other_ref, ...), custom_call_target="tpu_custom_call" | custom-call | flops 536870912 | bytes 3703296 | tf_op jit(solution)/shard_map/forward_low/pallas_call | solution.py:172
  21.7 0.0 collective-permute-done.5
  21.7 2.6 %collective-permute-start.6 = (f32[64,128]{1,0:T(8,128)S(1)}, f32[64,128]{1,0:T(8,128)S(1)}, u32[]{:S(2)}, u32[]{:S(2)}) collective-permute-start(f32[64,128]{1,0:T(8,128)S(1)} %add.21), channel_id=1, source_target_pairs={{2,0},{3,1},{0,2},{1,3},{6,4},{7,5},{4,6},{5,7},{10,8},{11,9},{8,1... | collective-permute-start | bytes 98312 | tf_op jit(solution)/shard_map/ppermute | solution.py:253
  24.4 2.6 %backward_high.1 = (bf16[128,2048]{1,0:T(8,128)(2,1)}, bf16[128,2048]{1,0:T(8,128)(2,1)}) custom-call(bf16[128,2048]{1,0:T(8,128)(2,1)S(1)} %bitcast.39, bf16[128,2048]{1,0:T(8,128)(2,1)S(1)} %bitcast.31, bf16[128,1024]{1,0:T(8,128)(2,1)S(1)} %collective-permute-done.other_ref.refs_2_, bf16[128,1024]{1,0:T(8,128)(2,1)S(1)} %collective-permute-done.3.refs_3_.other_ref, ...), custom_call_target="tpu_custom_call" | custom-call | flops 536870912 | bytes 3703296 | tf_op jit(solution)/shard_map/backward_high/pallas_call | solution.py:172
  27.0 0.0 collective-permute-done.6
  27.0 0.0 collective-permute-done.1.pair_ref
  27.0 0.0 collective-permute-done.2.far_ref
  27.0 1.6 %collective-permute-start.7 = (f32[64,128]{1,0:T(8,128)S(1)}, f32[64,128]{1,0:T(8,128)S(1)}, u32[]{:S(2)}, u32[]{:S(2)}) collective-permute-start(f32[64,128]{1,0:T(8,128)S(1)} %add.22), channel_id=1, source_target_pairs={{8,0},{12,4},{0,8},{4,12},{24,16},{28,20},{16,24},{20,28},{9,1},{1... | collective-permute-start | bytes 98312 | tf_op jit(solution)/shard_map/ppermute | solution.py:253
  28.6 2.5 %forward_high.1 = (bf16[128,2048]{1,0:T(8,128)(2,1)}, bf16[128,2048]{1,0:T(8,128)(2,1)}) custom-call(bf16[128,2048]{1,0:T(8,128)(2,1)S(1)} %bitcast.16, bf16[128,2048]{1,0:T(8,128)(2,1)S(1)} %bitcast.24, bf16[128,1024]{1,0:T(8,128)(2,1)S(1)} %collective-permute-done.1.pair_ref, ...), custom_call_target="tpu_custom_call", output_to_operand_aliasing={{0}: (8, {}), {1}: (9, {})} | custom-call | flops 536870912 | bytes 4751872 | tf_op jit(solution)/shard_map/forward_high/pallas_call | solution.py:172
  31.1 0.0 collective-permute-done.7
  31.2 1.7 %collective-permute-start.8 = (f32[64,128]{1,0:T(8,128)S(1)}, f32[64,128]{1,0:T(8,128)S(1)}, u32[]{:S(2)}, u32[]{:S(2)}) collective-permute-start(f32[64,128]{1,0:T(8,128)S(1)} %add.23), channel_id=1, source_target_pairs={{16,0},{20,4},{24,8},{28,12},{0,16},{4,20},{8,24},{12,28},{17,1},{... | collective-permute-start | bytes 98312 | tf_op jit(solution)/shard_map/ppermute | solution.py:253
  32.9 2.6 %backward_low.1 = (bf16[128,2048]{1,0:T(8,128)(2,1)}, bf16[128,2048]{1,0:T(8,128)(2,1)}) custom-call(bf16[128,2048]{1,0:T(8,128)(2,1)S(1)} %bitcast.41, bf16[128,2048]{1,0:T(8,128)(2,1)S(1)} %bitcast.33, bf16[128,1024]{1,0:T(8,128)(2,1)S(1)} %collective-permute-done.1.pair_ref, ...), custom_call_target="tpu_custom_call", output_to_operand_aliasing={{0}: (8, {}), {1}: (9, {})} | custom-call | flops 536870912 | bytes 4751872 | tf_op jit(solution)/shard_map/backward_low/pallas_call | solution.py:172
  35.4 0.0 collective-permute-done.8
  35.5 0.1 collective-permute-start.9
  35.5 1.2 %collective-permute-done.9 = f32[64,128]{1,0:T(8,128)S(1)} collective-permute-done((f32[64,128]{1,0:T(8,128)S(1)}, f32[64,128]{1,0:T(8,128)S(1)}, u32[]{:S(2)}, u32[]{:S(2)}) %collective-permute-start.9) | collective-permute-done | bytes 32800 | tf_op jit(solution)/shard_map/ppermute | solution.py:223
  36.7 0.6 %maximum_select_fusion = f32[128,128]{1,0:T(8,128)} fusion(f32[64,128]{1,0:T(8,128)S(1)} %collective-permute-done.9, f32[64,128]{1,0:T(8,128)S(1)} %add.24, pred[]{:T(512)S(6)} %eq.5), kind=kLoop, calls=%fused_computation.8 | loop fusion | flops 49152 | bytes 131073 | tf_op jit(solution)/shard_map/jit(_where)/select_n | solution.py:318
  (8 shorter events, 0.1 us)
Async XLA Ops:
  0.6 0.7 %copy-start.6 = (s32[1,128]{1,0:T(1,128)S(1)}, s32[1,128]{1,0:T(1,128)}, u32[]{:S(2)}) copy-start(s32[1,128]{1,0:T(1,128)} %param.10) | copy-start | bytes 1540
  1.4 3.2 %copy-start = (bf16[1,128,2048]{2,1,0:T(8,128)(2,1)S(1)}, bf16[1,128,2048]{2,1,0:T(8,128)(2,1)}, u32[]{:S(2)}) copy-start(bf16[1,128,2048]{2,1,0:T(8,128)(2,1)} %param.7) | copy-start | bytes 1572868
  1.5 3.2 %copy-start.1 = (bf16[1,128,2048]{2,1,0:T(8,128)(2,1)S(1)}, bf16[1,128,2048]{2,1,0:T(8,128)(2,1)}, u32[]{:S(2)}) copy-start(bf16[1,128,2048]{2,1,0:T(8,128)(2,1)} %param.8) | copy-start | bytes 1572868
  1.5 3.2 %copy-start.2 = (bf16[1,128,2048]{2,1,0:T(8,128)(2,1)S(1)}, bf16[1,128,2048]{2,1,0:T(8,128)(2,1)}, u32[]{:S(2)}) copy-start(bf16[1,128,2048]{2,1,0:T(8,128)(2,1)} %param.6) | copy-start | bytes 1572868
  3.0 1.7 %collective-permute-start = (bf16[128,1024]{1,0:T(8,128)(2,1)S(1)}, bf16[128,1024]{1,0:T(8,128)(2,1)S(1)}, u32[]{:S(2)}, u32[]{:S(2)}) collective-permute-start(bf16[128,1024]{1,0:T(8,128)(2,1)S(1)} %get-tuple-element.50), channel_id=1, source_target_pairs={{0,4},{4,0},{8,12},{12,8},{16,20},{20,16},{24,28},{28,24},{1,5},{5... | collective-permute-start | bytes 786440 | tf_op jit(solution)/shard_map/ppermute | solution.py:223
  3.5 11.8 %collective-permute-start.3 = (bf16[128,1024]{1,0:T(8,128)(2,1)S(1)}, bf16[128,1024]{1,0:T(8,128)(2,1)S(1)}, u32[]{:S(2)}, u32[]{:S(2)}) collective-permute-start(bf16[128,1024]{1,0:T(8,128)(2,1)S(1)} %get-tuple-element.49), channel_id=1, source_target_pairs={{4,8},{12,16},{20,24},{8,4},{16,12},{24,20},{5,9},{13,17},{21,25},... | collective-permute-start | bytes 786440 | tf_op jit(solution)/shard_map/ppermute | solution.py:229
  4.7 1.0 %copy-start.3 = (bf16[1,128,2048]{2,1,0:T(8,128)(2,1)S(1)}, bf16[1,128,2048]{2,1,0:T(8,128)(2,1)}, u32[]{:S(2)}) copy-start(bf16[1,128,2048]{2,1,0:T(8,128)(2,1)} %param.9) | copy-start | bytes 1572868
  8.1 18.9 %collective-permute-start.1 = (bf16[128,1024]{1,0:T(8,128)(2,1)S(1)}, bf16[128,1024]{1,0:T(8,128)(2,1)S(1)}, u32[]{:S(2)}, u32[]{:S(2)}) collective-permute-start(bf16[128,1024]{1,0:T(8,128)(2,1)S(1)} %get-tuple-element.52), channel_id=1, source_target_pairs={{0,4},{4,0},{8,12},{12,8},{16,20},{20,16},{24,28},{28,24},{1,5},{5... | collective-permute-start | bytes 786440 | tf_op jit(solution)/shard_map/ppermute | solution.py:223
  11.6 7.6 %copy-start.4 = (bf16[1,128,2048]{2,1,0:T(8,128)(2,1)S(1)}, bf16[1,128,2048]{2,1,0:T(8,128)(2,1)}, u32[]{:S(2)}) copy-start(bf16[1,128,2048]{2,1,0:T(8,128)(2,1)} %param.9) | copy-start | bytes 1572868
  11.6 15.4 %collective-permute-start.2 = (bf16[128,1024]{1,0:T(8,128)(2,1)S(1)}, bf16[128,1024]{1,0:T(8,128)(2,1)S(1)}, u32[]{:S(2)}, u32[]{:S(2)}) collective-permute-start(bf16[128,1024]{1,0:T(8,128)(2,1)S(1)} %get-tuple-element.51), channel_id=1, source_target_pairs={{4,8},{12,16},{20,24},{8,4},{16,12},{24,20},{5,9},{13,17},{21,25},... | collective-permute-start | bytes 786440 | tf_op jit(solution)/shard_map/ppermute | solution.py:229
  12.4 5.1 %collective-permute-start.4 = (f32[64,128]{1,0:T(8,128)S(1)}, f32[64,128]{1,0:T(8,128)S(1)}, u32[]{:S(2)}, u32[]{:S(2)}) collective-permute-start(f32[64,128]{1,0:T(8,128)S(1)} %filter_partner.1), channel_id=1, source_target_pairs={{0,4},{4,0},{8,12},{12,8},{16,20},{20,16},{24,28},{28,24},{1,5},{5... | collective-permute-start | bytes 98312 | tf_op jit(solution)/shard_map/ppermute | solution.py:223
  17.5 1.7 %copy-start.5 = (bf16[128,128]{1,0:T(8,128)(2,1)S(1)}, bf16[128,128]{1,0:T(8,128)(2,1)}, u32[]{:S(2)}) copy-start(bf16[128,128]{1,0:T(8,128)(2,1)} %taps_ref.3) | copy-start | bytes 98308
  17.5 4.2 %collective-permute-start.5 = (f32[64,128]{1,0:T(8,128)S(1)}, f32[64,128]{1,0:T(8,128)S(1)}, u32[]{:S(2)}, u32[]{:S(2)}) collective-permute-start(f32[64,128]{1,0:T(8,128)S(1)} %add.20), channel_id=1, source_target_pairs={{1,0},{0,1},{3,2},{2,3},{5,4},{4,5},{7,6},{6,7},{9,8},{8,9},{11,10... | collective-permute-start | bytes 98312 | tf_op jit(solution)/shard_map/ppermute | solution.py:253
  21.7 5.2 %collective-permute-start.6 = (f32[64,128]{1,0:T(8,128)S(1)}, f32[64,128]{1,0:T(8,128)S(1)}, u32[]{:S(2)}, u32[]{:S(2)}) collective-permute-start(f32[64,128]{1,0:T(8,128)S(1)} %add.21), channel_id=1, source_target_pairs={{2,0},{3,1},{0,2},{1,3},{6,4},{7,5},{4,6},{5,7},{10,8},{11,9},{8,1... | collective-permute-start | bytes 98312 | tf_op jit(solution)/shard_map/ppermute | solution.py:253
  27.0 4.1 %collective-permute-start.7 = (f32[64,128]{1,0:T(8,128)S(1)}, f32[64,128]{1,0:T(8,128)S(1)}, u32[]{:S(2)}, u32[]{:S(2)}) collective-permute-start(f32[64,128]{1,0:T(8,128)S(1)} %add.22), channel_id=1, source_target_pairs={{8,0},{12,4},{0,8},{4,12},{24,16},{28,20},{16,24},{20,28},{9,1},{1... | collective-permute-start | bytes 98312 | tf_op jit(solution)/shard_map/ppermute | solution.py:253
  31.2 4.3 %collective-permute-start.8 = (f32[64,128]{1,0:T(8,128)S(1)}, f32[64,128]{1,0:T(8,128)S(1)}, u32[]{:S(2)}, u32[]{:S(2)}) collective-permute-start(f32[64,128]{1,0:T(8,128)S(1)} %add.23), channel_id=1, source_target_pairs={{16,0},{20,4},{24,8},{28,12},{0,16},{4,20},{8,24},{12,28},{17,1},{... | collective-permute-start | bytes 98312 | tf_op jit(solution)/shard_map/ppermute | solution.py:253
  35.5 1.3 %collective-permute-start.9 = (f32[64,128]{1,0:T(8,128)S(1)}, f32[64,128]{1,0:T(8,128)S(1)}, u32[]{:S(2)}, u32[]{:S(2)}) collective-permute-start(f32[64,128]{1,0:T(8,128)S(1)} %add.24), channel_id=1, source_target_pairs={{0,4},{4,0},{8,12},{12,8},{16,20},{20,16},{24,28},{28,24},{1,5},{5... | collective-permute-start | bytes 98312 | tf_op jit(solution)/shard_map/ppermute | solution.py:223

commit v10 on v9

--- a/solution.py
+++ b/solution.py
@@ -60,11 +60,11 @@
 
 
 def filter_kernel(
-    q_ref, k_ref, v_ref, dy_ref, other_ref, starts_ref, out_ref, own_ref, other_mask_ref, sums_ref, *, scale, partner
+    kv_ref, cot_ref, other_ref, starts_ref, out_ref, own_ref, other_mask_ref, sums_ref, *, scale, partner
 ):
-    rows = q_ref.shape[0]
+    rows = kv_ref.shape[0]
     per_tile = LANES // GSIZE
-    width = q_ref.shape[1] // 2
+    width = kv_ref.shape[1] // 2
     core = lax.axis_index("ctx") % 2
     half = 1 - core if partner else core
     low = half == 0
@@ -77,8 +77,8 @@
     def tile(index):
         here = pl.ds(pl.multiple_of(index * LANES, LANES), LANES)
         lanes = pl.ds(pl.multiple_of(base + index * LANES, LANES), LANES)
-        cot = product(dy_ref[:, lanes], q_ref[:, lanes])
-        kv = product(k_ref[:, lanes], v_ref[:, lanes])
+        cot = cot_ref[:, lanes]
+        kv = kv_ref[:, lanes]
         left = jnp.where(low, cot, kv)
         right = jnp.concatenate(
             [jnp.where(low, kv, cot), other_ref[:, here]], axis=0
@@ -182,15 +182,15 @@
     )(*operands)
 
 
-def filter_share(q, k, v, dy, other, starts, groups, scale, partner):
-    rows, width = q.shape
+def filter_share(kv, cot, other, starts, groups, scale, partner):
+    rows, width = kv.shape
     table = pltpu.VMEM((rows, rows), jnp.float32)
     return local_call(
         functools.partial(filter_kernel, scale=scale, partner=partner),
         "filter_partner" if partner else "filter_own",
         jax.ShapeDtypeStruct((groups // 2, rows), jnp.float32),
         [table, table, pltpu.VMEM((groups * 4, rows), jnp.float32)],
-        1000, (q, k, v, dy, other, starts), moved=1000,
+        1000, (kv, cot, other, starts), moved=1000,
     )
 
 
@@ -267,31 +267,28 @@
     groups, taps = filters.shape
     assert rows == taps == LANES and lax.axis_size("ctx") % 2 == 0
     scale = 1.0 / math.sqrt(rows * lax.axis_size("ctx") * lax.axis_size("dp") * GSIZE)
-    flags = lax.optimization_barrier(jnp.minimum(contig_starts, 1))
+    kv, cot = lax.optimization_barrier((product(k, v), product(dy, q)))
+    flags = lax.optimization_barrier(jnp.minimum(contig_starts, after(jnp.ones_like(contig_starts), kv)))
     starts = flags[0] > 0
     token = jnp.arange(rows)
     tail = ~jnp.any(starts[None, :] & (token[None, :] > token[:, None]), axis=1)
     head = ~jnp.any(starts[None, :] & (token[None, :] <= token[:, None]), axis=1)
     even = lax.axis_index("ctx") % 2 == 0
     width = q.shape[1] // 2
-    low, high, every = slice(0, width), slice(width, None), slice(None)
-
-    def sent(from_even, kv_part, cot_part, *earlier):
+    low, high = slice(0, width), slice(width, None)
+
+    def sent(kv, cot, from_even):
         to_next = even if from_even else ~even
-        q_, k_, v_, dy_ = lax.optimization_barrier((q, k, v, dy, *earlier))[:4]
-        kv = product(k_[:, kv_part], v_[:, kv_part])
-        cot = product(dy_[:, cot_part], q_[:, cot_part])
         keep = jnp.where(to_next, tail, head)
         return jnp.where(keep[:, None], jnp.where(to_next, kv, cot), 0)
 
-    far_out = sent(False, low, high)
-    far = next_chip(far_out)
-    pair_out = sent(True, low, high)
-    pair = other_core(pair_out)
-    theirs = filter_share(q, k, v, dy, pair, flags, groups, scale, True)
-    later_far = next_chip(sent(False, high, low, theirs))
-    later_pair = other_core(sent(True, high, low, theirs))
-    mine = filter_share(q, k, v, dy, after(far, theirs), flags, groups, scale, False)
+    far = next_chip(sent(kv[:, low], cot[:, high], False))
+    pair = other_core(sent(kv[:, low], cot[:, high], True))
+    theirs = filter_share(kv, cot, pair, flags, groups, scale, True)
+    later_kv, later_cot, _ = lax.optimization_barrier((kv, cot, theirs))
+    later_far = next_chip(sent(later_kv[:, high], later_cot[:, low], False))
+    later_pair = other_core(sent(later_kv[:, high], later_cot[:, low], True))
+    mine = filter_share(kv, cot, after(far, theirs), flags, groups, scale, False)
     mine = mine + other_core(theirs)
 
     def forward(pair, far, outs, half):

time: 37.7 us -> 38.3 us (1.016)
  starting transfers between devices: 16 us -> 17.2 us
  local copies, waits for them, and re-layouts: 1.71 us -> 0.67 us
  other arithmetic: 2.5 us -> 3 us
    ppermute x4, starting transfers between devices: 7.56 us -> 10.4 us  [summed_over(): lax.ppermute(total, axis, [(turned(i, k), i) for i in range(size)])]
    convert_element_type x0 -> x1, other arithmetic: none -> 1.98 us  [product(): return (a.astype(jnp.float32) * b.astype(jnp.float32)).astype(jnp.bfloat16)]
    ppermute x4, starting transfers between devices: 6.95 us -> 5.35 us  [other_core(): lax.ppermute(block, 'ctx', [(i, i ^ 1) for i in range(lax.axis_size('ctx'...]
    select_n x2, other arithmetic: 1.7 us -> 0.22 us  [sent(): return jnp.where(keep[:, None], jnp.where(to_next, kv, cot), 0)]
    unnamed x14 -> x12, local copies, waits for them, and re-layouts: 1.71 us -> 0.67 us
  transfers between devices with their start and end apart: 10 -> 10, of which waited for: 2 -> 2; matrix products, arithmetic and copies ran while one was open for 1% -> 0% of each run, Pallas kernels for 39% -> 38%
where the time goes in v10:
time: 38.3 us; the launch traced here: 38.1 us
  starting transfers between devices  17.2 us (45%)
  Pallas kernels  14.6 us (38%)
  other arithmetic  3 us (8%)
  waiting for transfers between devices  1.7 us (4%)
  between operations  0.92 us (2%)
  local copies, waits for them, and re-layouts  0.67 us (2%)
    pallas_call x6, Pallas kernels, local_call(): pl.pallas_call(kernel, out_shape=out_shape, in_specs=in_specs or [VMEM] *...  14.6 us
    ppermute x4, starting transfers between devices, summed_over(): lax.ppermute(total, axis, [(turned(i, k), i) for i in range(size)])  10.4 us
    ppermute x4, starting transfers between devices, other_core(): lax.ppermute(block, 'ctx', [(i, i ^ 1) for i in range(lax.axis_size('ctx'...  5.35 us
    convert_element_type x1, other arithmetic, product(): return (a.astype(jnp.float32) * b.astype(jnp.float32)).astype(jnp.bfloat16)  1.98 us
    ppermute x4, waiting for transfers between devices, other_core(): lax.ppermute(block, 'ctx', [(i, i ^ 1) for i in range(lax.axis_size('ctx'...  1.69 us
    ppermute x2, starting transfers between devices, next_chip(): return lax.ppermute(block, 'ctx', pairs + [(j, i) for i, j in pairs])  1.47 us
  transfers between devices with their start and end apart: 10, of which 2 were waited for; matrix products, arithmetic and copies ran while one was open for 0% of the time, Pallas kernels for 38%

profile of v10, /device:TPU:0, one launch (start us, length us, event | category | flops | bytes accessed | tf_op | source)
XLA Modules:
  0.0 38.1 jit_solution(2353087410318787667)
XLA Ops:
  0.6 2.0 %multiply_convert_fusion = (bf16[128,2048]{1,0:T(8,128)(2,1)S(1)}, bf16[128,2048]{1,0:T(8,128)(2,1)S(1)}) fusion(bf16[1,128,2048]{2,1,0:T(8,128)(2,1)} %param.6, bf16[1,128,2048]{2,1,0:T(8,128)(2,1)} %param.9, bf16[1,128,2048]{2,1,0:T(8,128)(2,1)} %param.8, bf16[1,128,2048]{2,1,0:T(8,128)(2,1)} %param.7), kind=kLoop, calls=%fused_computation | loop fusion | flops 2097152 | bytes 3145728 | tf_op jit(solution)/shard_map/convert_element_type | solution.py:17
  2.6 0.0 copy-start.5
  2.7 0.6 %copy-done.5 = s32[1,128]{1,0:T(1,128)S(1)} copy-done((s32[1,128]{1,0:T(1,128)S(1)}, s32[1,128]{1,0:T(1,128)}, u32[]{:S(2)}) %copy-start.5) | copy-done | bytes 536
  3.3 0.1 fusion.1
  3.4 0.1 select_select_fusion
  3.6 0.5 %collective-permute-start = (bf16[128,1024]{1,0:T(8,128)(2,1)S(1)}, bf16[128,1024]{1,0:T(8,128)(2,1)S(1)}, u32[]{:S(2)}, u32[]{:S(2)}) collective-permute-start(bf16[128,1024]{1,0:T(8,128)(2,1)S(1)} %get-tuple-element.44), channel_id=1, source_target_pairs={{0,4},{4,0},{8,12},{12,8},{16,20},{20,16},{24,28},{28,24},{1,5},{5... | collective-permute-start | bytes 786440 | tf_op jit(solution)/shard_map/ppermute | solution.py:223
  4.1 0.7 %collective-permute-start.3 = (bf16[128,1024]{1,0:T(8,128)(2,1)S(1)}, bf16[128,1024]{1,0:T(8,128)(2,1)S(1)}, u32[]{:S(2)}, u32[]{:S(2)}) collective-permute-start(bf16[128,1024]{1,0:T(8,128)(2,1)S(1)} %get-tuple-element.43), channel_id=1, source_target_pairs={{4,8},{12,16},{20,24},{8,4},{16,12},{24,20},{5,9},{13,17},{21,25},... | collective-permute-start | bytes 786440 | tf_op jit(solution)/shard_map/ppermute | solution.py:229
  4.7 0.5 %collective-permute-done.other_ref.refs_2_ = bf16[128,1024]{1,0:T(8,128)(2,1)S(1)} collective-permute-done((bf16[128,1024]{1,0:T(8,128)(2,1)S(1)}, bf16[128,1024]{1,0:T(8,128)(2,1)S(1)}, u32[]{:S(2)}, u32[]{:S(2)}) %collective-permute-start) | collective-permute-done | bytes 262176 | tf_op jit(solution)/shard_map/ppermute | solution.py:223
  5.2 2.1 %filter_partner.1 = f32[64,128]{1,0:T(8,128)S(1)} custom-call(bf16[128,2048]{1,0:T(8,128)(2,1)S(1)} %get-tuple-element.26.kv_ref, bf16[128,2048]{1,0:T(8,128)(2,1)S(1)} %get-tuple-element.27.cot_ref, bf16[128,1024]{1,0:T(8,128)(2,1)S(1)} %collective-permute-done.other_ref.refs_2_, s32[1,128]{1,0:T(1,128)S(1)} %min.3.starts_ref.refs_6_), custom_call_target="tpu_custom_call" | custom-call | flops 1000 | bytes 1000 | tf_op jit(solution)/shard_map/filter_partner/pallas_call | solution.py:172
  7.4 0.0 copy-start.2
  7.4 0.0 copy-start.3
  7.4 0.1 select_select_fusion.1
  7.5 0.8 %collective-permute-start.2 = (bf16[128,1024]{1,0:T(8,128)(2,1)S(1)}, bf16[128,1024]{1,0:T(8,128)(2,1)S(1)}, u32[]{:S(2)}, u32[]{:S(2)}) collective-permute-start(bf16[128,1024]{1,0:T(8,128)(2,1)S(1)} %get-tuple-element.45), channel_id=1, source_target_pairs={{4,8},{12,16},{20,24},{8,4},{16,12},{24,20},{5,9},{13,17},{21,25},... | collective-permute-start | bytes 786440 | tf_op jit(solution)/shard_map/ppermute | solution.py:229
  8.3 0.0 copy-start
  8.4 0.0 copy-start.1
  8.4 4.7 %collective-permute-start.1 = (bf16[128,1024]{1,0:T(8,128)(2,1)S(1)}, bf16[128,1024]{1,0:T(8,128)(2,1)S(1)}, u32[]{:S(2)}, u32[]{:S(2)}) collective-permute-start(bf16[128,1024]{1,0:T(8,128)(2,1)S(1)} %get-tuple-element.46), channel_id=1, source_target_pairs={{0,4},{4,0},{8,12},{12,8},{16,20},{20,16},{24,28},{28,24},{1,5},{5... | collective-permute-start | bytes 786440 | tf_op jit(solution)/shard_map/ppermute | solution.py:223
  13.1 0.1 collective-permute-start.4
  13.1 0.0 collective-permute-done.3.refs_3_.other_ref
  13.1 2.1 %filter_own.1 = f32[64,128]{1,0:T(8,128)S(1)} custom-call(bf16[128,2048]{1,0:T(8,128)(2,1)S(1)} %get-tuple-element.26.kv_ref, bf16[128,2048]{1,0:T(8,128)(2,1)S(1)} %get-tuple-element.27.cot_ref, bf16[128,1024]{1,0:T(8,128)(2,1)S(1)} %collective-permute-done.3.refs_3_.other_ref, s32[1,128]{1,0:T(1,128)S(1)} %min.3.starts_ref.refs_6_), custom_call_target="tpu_custom_call" | custom-call | flops 1000 | bytes 1000 | tf_op jit(solution)/shard_map/filter_own/pallas_call | solution.py:172
  15.3 0.0 copy-start.4
  15.3 0.0 collective-permute-done.4
  15.3 2.3 %collective-permute-start.5 = (f32[64,128]{1,0:T(8,128)S(1)}, f32[64,128]{1,0:T(8,128)S(1)}, u32[]{:S(2)}, u32[]{:S(2)}) collective-permute-start(f32[64,128]{1,0:T(8,128)S(1)} %add.20), channel_id=1, source_target_pairs={{1,0},{0,1},{3,2},{2,3},{5,4},{4,5},{7,6},{6,7},{9,8},{8,9},{11,10... | collective-permute-start | bytes 98312 | tf_op jit(solution)/shard_map/ppermute | solution.py:253
  17.6 0.0 copy-done.2
  17.6 0.0 copy-done.3
  17.6 0.0 copy-done
  17.6 0.0 copy-done.1
  17.6 0.0 copy-done.4
  17.6 2.5 %forward_low.1 = (bf16[128,2048]{1,0:T(8,128)(2,1)}, bf16[128,2048]{1,0:T(8,128)(2,1)}) custom-call(bf16[128,2048]{1,0:T(8,128)(2,1)S(1)} %bitcast.14, bf16[128,2048]{1,0:T(8,128)(2,1)S(1)} %bitcast.18, bf16[128,1024]{1,0:T(8,128)(2,1)S(1)} %collective-permute-done.other_ref.refs_2_, bf16[128,1024]{1,0:T(8,128)(2,1)S(1)} %collective-permute-done.3.refs_3_.other_ref, ...), custom_call_target="tpu_custom_call" | custom-call | flops 536870912 | bytes 3703296 | tf_op jit(solution)/shard_map/forward_low/pallas_call | solution.py:172
  20.1 0.0 collective-permute-done.5
  20.2 2.7 %collective-permute-start.6 = (f32[64,128]{1,0:T(8,128)S(1)}, f32[64,128]{1,0:T(8,128)S(1)}, u32[]{:S(2)}, u32[]{:S(2)}) collective-permute-start(f32[64,128]{1,0:T(8,128)S(1)} %add.21), channel_id=1, source_target_pairs={{2,0},{3,1},{0,2},{1,3},{6,4},{7,5},{4,6},{5,7},{10,8},{11,9},{8,1... | collective-permute-start | bytes 98312 | tf_op jit(solution)/shard_map/ppermute | solution.py:253
  22.8 2.6 %backward_high.1 = (bf16[128,2048]{1,0:T(8,128)(2,1)}, bf16[128,2048]{1,0:T(8,128)(2,1)}) custom-call(bf16[128,2048]{1,0:T(8,128)(2,1)S(1)} %bitcast.27, bf16[128,2048]{1,0:T(8,128)(2,1)S(1)} %bitcast.23, bf16[128,1024]{1,0:T(8,128)(2,1)S(1)} %collective-permute-done.other_ref.refs_2_, bf16[128,1024]{1,0:T(8,128)(2,1)S(1)} %collective-permute-done.3.refs_3_.other_ref, ...), custom_call_target="tpu_custom_call" | custom-call | flops 536870912 | bytes 3703296 | tf_op jit(solution)/shard_map/backward_high/pallas_call | solution.py:172
  25.5 0.0 collective-permute-done.6
  25.5 0.0 collective-permute-done.2.far_ref
  25.5 0.0 collective-permute-done.1.pair_ref
  25.5 2.4 %collective-permute-start.7 = (f32[64,128]{1,0:T(8,128)S(1)}, f32[64,128]{1,0:T(8,128)S(1)}, u32[]{:S(2)}, u32[]{:S(2)}) collective-permute-start(f32[64,128]{1,0:T(8,128)S(1)} %add.22), channel_id=1, source_target_pairs={{8,0},{12,4},{0,8},{4,12},{24,16},{28,20},{16,24},{20,28},{9,1},{1... | collective-permute-start | bytes 98312 | tf_op jit(solution)/shard_map/ppermute | solution.py:253
  27.9 2.5 %forward_high.1 = (bf16[128,2048]{1,0:T(8,128)(2,1)}, bf16[128,2048]{1,0:T(8,128)(2,1)}) custom-call(bf16[128,2048]{1,0:T(8,128)(2,1)S(1)} %bitcast.16, bf16[128,2048]{1,0:T(8,128)(2,1)S(1)} %bitcast.20, bf16[128,1024]{1,0:T(8,128)(2,1)S(1)} %collective-permute-done.1.pair_ref, ...), custom_call_target="tpu_custom_call", output_to_operand_aliasing={{0}: (8, {}), {1}: (9, {})} | custom-call | flops 536870912 | bytes 4751872 | tf_op jit(solution)/shard_map/forward_high/pallas_call | solution.py:172
  30.5 0.0 collective-permute-done.7
  30.5 3.0 %collective-permute-start.8 = (f32[64,128]{1,0:T(8,128)S(1)}, f32[64,128]{1,0:T(8,128)S(1)}, u32[]{:S(2)}, u32[]{:S(2)}) collective-permute-start(f32[64,128]{1,0:T(8,128)S(1)} %add.23), channel_id=1, source_target_pairs={{16,0},{20,4},{24,8},{28,12},{0,16},{4,20},{8,24},{12,28},{17,1},{... | collective-permute-start | bytes 98312 | tf_op jit(solution)/shard_map/ppermute | solution.py:253
  33.5 2.6 %backward_low.1 = (bf16[128,2048]{1,0:T(8,128)(2,1)}, bf16[128,2048]{1,0:T(8,128)(2,1)}) custom-call(bf16[128,2048]{1,0:T(8,128)(2,1)S(1)} %bitcast.29, bf16[128,2048]{1,0:T(8,128)(2,1)S(1)} %bitcast.25, bf16[128,1024]{1,0:T(8,128)(2,1)S(1)} %collective-permute-done.1.pair_ref, ...), custom_call_target="tpu_custom_call", output_to_operand_aliasing={{0}: (8, {}), {1}: (9, {})} | custom-call | flops 536870912 | bytes 4751872 | tf_op jit(solution)/shard_map/backward_low/pallas_call | solution.py:172
  36.1 0.0 collective-permute-done.8
  36.1 0.1 collective-permute-start.9
  36.2 1.2 %collective-permute-done.9 = f32[64,128]{1,0:T(8,128)S(1)} collective-permute-done((f32[64,128]{1,0:T(8,128)S(1)}, f32[64,128]{1,0:T(8,128)S(1)}, u32[]{:S(2)}, u32[]{:S(2)}) %collective-permute-start.9) | collective-permute-done | bytes 32800 | tf_op jit(solution)/shard_map/ppermute | solution.py:223
  37.4 0.6 %maximum_select_fusion = f32[128,128]{1,0:T(8,128)} fusion(f32[64,128]{1,0:T(8,128)S(1)} %collective-permute-done.9, f32[64,128]{1,0:T(8,128)S(1)} %add.24, pred[]{:T(512)S(6)} %eq.5), kind=kLoop, calls=%fused_computation.6 | loop fusion | flops 49152 | bytes 131073 | tf_op jit(solution)/shard_map/jit(_where)/select_n | solution.py:315
  (9 shorter events, 0.1 us)
Async XLA Ops:
  2.6 0.7 %copy-start.5 = (s32[1,128]{1,0:T(1,128)S(1)}, s32[1,128]{1,0:T(1,128)}, u32[]{:S(2)}) copy-start(s32[1,128]{1,0:T(1,128)} %param.10) | copy-start | bytes 1540
  3.6 1.7 %collective-permute-start = (bf16[128,1024]{1,0:T(8,128)(2,1)S(1)}, bf16[128,1024]{1,0:T(8,128)(2,1)S(1)}, u32[]{:S(2)}, u32[]{:S(2)}) collective-permute-start(bf16[128,1024]{1,0:T(8,128)(2,1)S(1)} %get-tuple-element.44), channel_id=1, source_target_pairs={{0,4},{4,0},{8,12},{12,8},{16,20},{20,16},{24,28},{28,24},{1,5},{5... | collective-permute-start | bytes 786440 | tf_op jit(solution)/shard_map/ppermute | solution.py:223
  4.1 9.1 %collective-permute-start.3 = (bf16[128,1024]{1,0:T(8,128)(2,1)S(1)}, bf16[128,1024]{1,0:T(8,128)(2,1)S(1)}, u32[]{:S(2)}, u32[]{:S(2)}) collective-permute-start(bf16[128,1024]{1,0:T(8,128)(2,1)S(1)} %get-tuple-element.43), channel_id=1, source_target_pairs={{4,8},{12,16},{20,24},{8,4},{16,12},{24,20},{5,9},{13,17},{21,25},... | collective-permute-start | bytes 786440 | tf_op jit(solution)/shard_map/ppermute | solution.py:229
  7.4 10.2 %copy-start.2 = (bf16[1,128,2048]{2,1,0:T(8,128)(2,1)S(1)}, bf16[1,128,2048]{2,1,0:T(8,128)(2,1)}, u32[]{:S(2)}) copy-start(bf16[1,128,2048]{2,1,0:T(8,128)(2,1)} %param.6) | copy-start | bytes 1572868
  7.4 10.2 %copy-start.3 = (bf16[1,128,2048]{2,1,0:T(8,128)(2,1)S(1)}, bf16[1,128,2048]{2,1,0:T(8,128)(2,1)}, u32[]{:S(2)}) copy-start(bf16[1,128,2048]{2,1,0:T(8,128)(2,1)} %param.9) | copy-start | bytes 1572868
  7.5 18.0 %collective-permute-start.2 = (bf16[128,1024]{1,0:T(8,128)(2,1)S(1)}, bf16[128,1024]{1,0:T(8,128)(2,1)S(1)}, u32[]{:S(2)}, u32[]{:S(2)}) collective-permute-start(bf16[128,1024]{1,0:T(8,128)(2,1)S(1)} %get-tuple-element.45), channel_id=1, source_target_pairs={{4,8},{12,16},{20,24},{8,4},{16,12},{24,20},{5,9},{13,17},{21,25},... | collective-permute-start | bytes 786440 | tf_op jit(solution)/shard_map/ppermute | solution.py:229
  8.3 9.2 %copy-start = (bf16[1,128,2048]{2,1,0:T(8,128)(2,1)S(1)}, bf16[1,128,2048]{2,1,0:T(8,128)(2,1)}, u32[]{:S(2)}) copy-start(bf16[1,128,2048]{2,1,0:T(8,128)(2,1)} %param.7) | copy-start | bytes 1572868
  8.4 9.2 %copy-start.1 = (bf16[1,128,2048]{2,1,0:T(8,128)(2,1)S(1)}, bf16[1,128,2048]{2,1,0:T(8,128)(2,1)}, u32[]{:S(2)}) copy-start(bf16[1,128,2048]{2,1,0:T(8,128)(2,1)} %param.8) | copy-start | bytes 1572868
  8.4 17.1 %collective-permute-start.1 = (bf16[128,1024]{1,0:T(8,128)(2,1)S(1)}, bf16[128,1024]{1,0:T(8,128)(2,1)S(1)}, u32[]{:S(2)}, u32[]{:S(2)}) collective-permute-start(bf16[128,1024]{1,0:T(8,128)(2,1)S(1)} %get-tuple-element.46), channel_id=1, source_target_pairs={{0,4},{4,0},{8,12},{12,8},{16,20},{20,16},{24,28},{28,24},{1,5},{5... | collective-permute-start | bytes 786440 | tf_op jit(solution)/shard_map/ppermute | solution.py:223
  13.1 2.2 %collective-permute-start.4 = (f32[64,128]{1,0:T(8,128)S(1)}, f32[64,128]{1,0:T(8,128)S(1)}, u32[]{:S(2)}, u32[]{:S(2)}) collective-permute-start(f32[64,128]{1,0:T(8,128)S(1)} %filter_partner.1), channel_id=1, source_target_pairs={{0,4},{4,0},{8,12},{12,8},{16,20},{20,16},{24,28},{28,24},{1,5},{5... | collective-permute-start | bytes 98312 | tf_op jit(solution)/shard_map/ppermute | solution.py:223
  15.3 2.3 %copy-start.4 = (bf16[128,128]{1,0:T(8,128)(2,1)S(1)}, bf16[128,128]{1,0:T(8,128)(2,1)}, u32[]{:S(2)}) copy-start(bf16[128,128]{1,0:T(8,128)(2,1)} %taps_ref.3) | copy-start | bytes 98308
  15.3 4.8 %collective-permute-start.5 = (f32[64,128]{1,0:T(8,128)S(1)}, f32[64,128]{1,0:T(8,128)S(1)}, u32[]{:S(2)}, u32[]{:S(2)}) collective-permute-start(f32[64,128]{1,0:T(8,128)S(1)} %add.20), channel_id=1, source_target_pairs={{1,0},{0,1},{3,2},{2,3},{5,4},{4,5},{7,6},{6,7},{9,8},{8,9},{11,10... | collective-permute-start | bytes 98312 | tf_op jit(solution)/shard_map/ppermute | solution.py:253
  20.2 5.3 %collective-permute-start.6 = (f32[64,128]{1,0:T(8,128)S(1)}, f32[64,128]{1,0:T(8,128)S(1)}, u32[]{:S(2)}, u32[]{:S(2)}) collective-permute-start(f32[64,128]{1,0:T(8,128)S(1)} %add.21), channel_id=1, source_target_pairs={{2,0},{3,1},{0,2},{1,3},{6,4},{7,5},{4,6},{5,7},{10,8},{11,9},{8,1... | collective-permute-start | bytes 98312 | tf_op jit(solution)/shard_map/ppermute | solution.py:253
  25.5 5.0 %collective-permute-start.7 = (f32[64,128]{1,0:T(8,128)S(1)}, f32[64,128]{1,0:T(8,128)S(1)}, u32[]{:S(2)}, u32[]{:S(2)}) collective-permute-start(f32[64,128]{1,0:T(8,128)S(1)} %add.22), channel_id=1, source_target_pairs={{8,0},{12,4},{0,8},{4,12},{24,16},{28,20},{16,24},{20,28},{9,1},{1... | collective-permute-start | bytes 98312 | tf_op jit(solution)/shard_map/ppermute | solution.py:253
  30.5 5.6 %collective-permute-start.8 = (f32[64,128]{1,0:T(8,128)S(1)}, f32[64,128]{1,0:T(8,128)S(1)}, u32[]{:S(2)}, u32[]{:S(2)}) collective-permute-start(f32[64,128]{1,0:T(8,128)S(1)} %add.23), channel_id=1, source_target_pairs={{16,0},{20,4},{24,8},{28,12},{0,16},{4,20},{8,24},{12,28},{17,1},{... | collective-permute-start | bytes 98312 | tf_op jit(solution)/shard_map/ppermute | solution.py:253
  36.1 1.3 %collective-permute-start.9 = (f32[64,128]{1,0:T(8,128)S(1)}, f32[64,128]{1,0:T(8,128)S(1)}, u32[]{:S(2)}, u32[]{:S(2)}) collective-permute-start(f32[64,128]{1,0:T(8,128)S(1)} %add.24), channel_id=1, source_target_pairs={{0,4},{4,0},{8,12},{12,8},{16,20},{20,16},{24,28},{28,24},{1,5},{5... | collective-permute-start | bytes 98312 | tf_op jit(solution)/shard_map/ppermute | solution.py:223

commit v11 on v9

--- a/solution.py
+++ b/solution.py
@@ -11,25 +11,11 @@
 GSIZE = 16
 LANES = 128
 STEP = 4
+VMEM = pl.BlockSpec(memory_space=pltpu.VMEM)
 
 
 def product(a, b):
     return (a.astype(jnp.float32) * b.astype(jnp.float32)).astype(jnp.bfloat16)
-
-
-def contig_masks(starts_ref):
-    rows = starts_ref.shape[1]
-    starts = jnp.broadcast_to(starts_ref[...], (rows, rows)) > 0
-    t = lax.broadcasted_iota(jnp.int32, (rows, rows), 0)
-    s = lax.broadcasted_iota(jnp.int32, (rows, rows), 1)
-    began = jnp.max(jnp.where(starts & (s <= t), s, 0), axis=1, keepdims=True)
-    own = (s <= t) & (s >= began)
-    first = jnp.min(jnp.where(starts, s, rows), axis=1, keepdims=True)
-    previous = (s > t) & (t < first)
-    last = jnp.max(jnp.where(starts, s, 0), axis=1, keepdims=True)
-    following = (s < t) & (t >= last)
-    as_f32 = lambda mask: jnp.where(mask, 1.0, 0.0).astype(jnp.float32)
-    return as_f32(own), as_f32(previous), as_f32(following)
 
 
 def reversed_taps(rows_of_taps):
@@ -59,8 +45,66 @@
     lax.fori_loop(0, count // step, body, 0)
 
 
+def first_kernel(
+    q_hbm, k_hbm, v_hbm, dy_hbm, starts_hbm, filters_hbm,
+    q_ref, k_ref, v_ref, dy_ref, far_ref, pair_ref, later_far_ref, later_pair_ref,
+    masks_ref, table_masks_ref, taps_ref, starts_ref, filters_ref, sems,
+):
+    rows, width = q_ref.shape
+    half = rows // 2
+    copies = [
+        pltpu.make_async_copy(starts_hbm, starts_ref, sems.at[0]),
+        pltpu.make_async_copy(filters_hbm, filters_ref, sems.at[1]),
+    ]
+    inputs = [(k_hbm, k_ref), (v_hbm, v_ref), (dy_hbm, dy_ref), (q_hbm, q_ref)]
+    for n in range(2):
+        part = pl.ds(n * half, half)
+        for source, target in inputs:
+            copies.append(pltpu.make_async_copy(source.at[part], target.at[part], sems.at[len(copies)]))
+    for copy in copies:
+        copy.start()
+
+    copies[0].wait()
+    starts = jnp.broadcast_to(starts_ref[...], (rows, rows)) > 0
+    t = lax.broadcasted_iota(jnp.int32, (rows, rows), 0)
+    s = lax.broadcasted_iota(jnp.int32, (rows, rows), 1)
+    began = jnp.max(jnp.where(starts & (s <= t), s, 0), axis=1, keepdims=True)
+    first = jnp.min(jnp.where(starts, s, rows), axis=1, keepdims=True)
+    last = jnp.max(jnp.where(starts, s, 0), axis=1, keepdims=True)
+    as_f32 = lambda mask: jnp.where(mask, 1.0, 0.0).astype(jnp.float32)
+    own = as_f32((s <= t) & (s >= began))
+    previous = as_f32((s > t) & (t < first))
+    following = as_f32((s < t) & (t >= last))
+    for n, mask in enumerate((own, own.T, previous, following)):
+        masks_ref[n] = mask
+    for n, parts in enumerate(((own, previous), (own.T, following))):
+        for m, mask in enumerate(parts):
+            table_masks_ref[n, :, m * rows : (m + 1) * rows] = mask.astype(jnp.bfloat16)
+    token = t[:, :1]
+    head, tail = token < first, token >= last
+    copies[1].wait()
+    taps_ref[0] = reversed_taps(filters_ref[...])
+    taps_ref[1] = filters_ref[...].astype(jnp.float32)
+
+    even = lax.axis_index("ctx") % 2 == 0
+    low, high = slice(0, width // 2), slice(width // 2, width)
+    for n in range(2):
+        for copy in copies[2 + 4 * n : 6 + 4 * n]:
+            copy.wait()
+        at = slice(n * half, (n + 1) * half)
+        for kv_part, cot_part, far, pair in (
+            (low, high, far_ref, pair_ref), (high, low, later_far_ref, later_pair_ref)
+        ):
+            kv = product(k_ref[at, kv_part], v_ref[at, kv_part])
+            cot = product(dy_ref[at, cot_part], q_ref[at, cot_part])
+            kv = jnp.where(tail[at], kv, jnp.zeros_like(kv))
+            cot = jnp.where(head[at], cot, jnp.zeros_like(cot))
+            far[at, :] = jnp.where(even, cot, kv)
+            pair[at, :] = jnp.where(even, kv, cot)
+
+
 def filter_kernel(
-    q_ref, k_ref, v_ref, dy_ref, other_ref, starts_ref, out_ref, own_ref, other_mask_ref, sums_ref, *, scale, partner
+    q_ref, k_ref, v_ref, dy_ref, other_ref, masks_ref, out_ref, own_ref, other_mask_ref, sums_ref, *, scale, partner
 ):
     rows = q_ref.shape[0]
     per_tile = LANES // GSIZE
@@ -69,9 +113,8 @@
     half = 1 - core if partner else core
     low = half == 0
     base = half * width
-    own, previous, following = contig_masks(starts_ref)
-    own_ref[...] = jnp.where(low, own, own.T)
-    other_mask_ref[...] = jnp.where(low, previous, following)
+    own_ref[...] = jnp.where(low, masks_ref[0], masks_ref[1])
+    other_mask_ref[...] = jnp.where(low, masks_ref[2], masks_ref[3])
     group = lane_groups()
 
     def tile(index):
@@ -104,8 +147,8 @@
 
 
 def conv_kernel(
-    a_ref, b_ref, pair_ref, far_ref, c_ref, d_ref, starts_ref, taps_ref, c_in_hbm, d_in_hbm, out_c_hbm, out_d_hbm,
-    mask_ref, taps_scr, out_c_ref, out_d_ref, sems, *, backward, half,
+    a_ref, b_ref, pair_ref, far_ref, c_ref, d_ref, masks_ref, taps_ref, c_in_hbm, d_in_hbm, out_c_hbm, out_d_hbm,
+    out_c_ref, out_d_ref, sems, *, backward, half,
 ):
     del c_in_hbm, d_in_hbm
     rows = a_ref.shape[0]
@@ -113,13 +156,9 @@
     width = a_ref.shape[1] // 2
     base = half * width
     even = lax.axis_index("ctx") % 2 == 0
-    own, previous, following = contig_masks(starts_ref)
-    mask_ref[:, :rows] = (own.T if backward else own).astype(jnp.bfloat16)
-    mask_ref[:, rows:] = (following if backward else previous).astype(jnp.bfloat16)
+    group = lane_groups()
     groups = width // GSIZE
-    taps = taps_ref[half * groups : (half + 1) * groups, :]
-    taps_scr[...] = taps.astype(jnp.float32) if backward else reversed_taps(taps)
-    group = lane_groups()
+    mask_ref = masks_ref.at[1 if backward else 0]
 
     def table(row):
         wide = pltpu.roll(jnp.broadcast_to(row, (rows, rows)), 0, 1, stride=1, stride_axis=0)
@@ -132,7 +171,8 @@
         from_pair = even if backward else jnp.logical_not(even)
         other = jnp.where(from_pair, pair_ref[:, here], far_ref[:, here])
         x = jnp.concatenate([product(a_ref[:, lanes], b_ref[:, lanes]), other], axis=0)
-        taps = taps_scr[pl.ds(pl.multiple_of(index * per_tile, per_tile), per_tile), :]
+        at = pl.multiple_of(half * groups + index * per_tile, per_tile)
+        taps = taps_ref[1 if backward else 0, pl.ds(at, per_tile), :]
         y = jnp.zeros((rows, LANES), jnp.float32)
         for g in range(per_tile):
             y = jnp.where(group == g, jnp.dot(table(taps[g : g + 1]), x, preferred_element_type=jnp.float32), y)
@@ -160,9 +200,6 @@
     for i in range(width // step):
         for copy in stored(i):
             copy.wait()
-
-
-VMEM = pl.BlockSpec(memory_space=pltpu.VMEM)
 
 
 def local_call(kernel, name, out_shape, scratch_shapes, flops, operands, in_specs=None, out_specs=VMEM, aliases={}, moved=None):
@@ -182,7 +219,30 @@
     )(*operands)
 
 
-def filter_share(q, k, v, dy, other, starts, groups, scale, partner):
+def first(q, k, v, dy, starts, filters):
+    rows, width = q.shape
+    wide = pltpu.VMEM((rows, width), jnp.bfloat16)
+    sent = pltpu.VMEM((rows, width // 2), jnp.bfloat16)
+    operands = [pltpu.with_memory_space_constraint(x, pltpu.HBM) for x in (q, k, v, dy, starts, filters)]
+    return pl.pallas_call(
+        first_kernel,
+        out_shape=[wide] * 4 + [sent] * 4 + [
+            pltpu.VMEM((4, rows, rows), jnp.float32),
+            pltpu.VMEM((2, rows, 2 * rows), jnp.bfloat16),
+            pltpu.VMEM((2, *filters.shape), jnp.float32),
+        ],
+        in_specs=[pl.BlockSpec(memory_space=pltpu.HBM)] * 6,
+        out_specs=[VMEM] * 11,
+        scratch_shapes=[
+            pltpu.VMEM(starts.shape, starts.dtype), pltpu.VMEM(filters.shape, filters.dtype),
+            pltpu.SemaphoreType.DMA((10,)),
+        ],
+        compiler_params=pltpu.CompilerParams(vmem_limit_bytes=24 << 20),
+        name="first",
+    )(*operands)
+
+
+def filter_share(q, k, v, dy, other, masks, groups, scale, partner):
     rows, width = q.shape
     table = pltpu.VMEM((rows, rows), jnp.float32)
     return local_call(
@@ -190,27 +250,24 @@
         "filter_partner" if partner else "filter_own",
         jax.ShapeDtypeStruct((groups // 2, rows), jnp.float32),
         [table, table, pltpu.VMEM((groups * 4, rows), jnp.float32)],
-        1000, (q, k, v, dy, other, starts), moved=1000,
-    )
-
-
-def convolution(a, b, pair, far, c, d, starts, filters, outs, backward, half):
+        1000, (q, k, v, dy, other, masks), moved=1000,
+    )
+
+
+def convolution(a, b, pair, far, c, d, masks, taps, outs, backward, half):
     rows, width = a.shape
     steps = width // 2 // LANES // math.gcd(width // 2 // LANES, STEP)
     out = jax.ShapeDtypeStruct((rows, width), jnp.bfloat16)
     part = pltpu.VMEM((rows, width // 2), jnp.bfloat16)
     anywhere = pl.BlockSpec(memory_space=pl.ANY)
     body = functools.partial(conv_kernel, backward=backward, half=half)
-    operands = (a, b, pair, far, c, d, starts, filters)
+    operands = (a, b, pair, far, c, d, masks, taps)
     n = len(operands)
     return local_call(
         body if outs else lambda *refs: body(*refs[:n], None, None, *refs[n:]),
         ("backward" if backward else "forward") + ("_high" if half else "_low"),
         [out, out],
-        [
-            pltpu.VMEM((rows, 2 * rows), jnp.bfloat16), pltpu.VMEM((filters.shape[0] // 2, rows), jnp.float32),
-            part, part, pltpu.SemaphoreType.DMA((2, steps)),
-        ],
+        [part, part, pltpu.SemaphoreType.DMA((2, steps))],
         16 * rows * rows * width,
         operands + tuple(outs or ()),
         [VMEM] * n + [anywhere] * (2 if outs else 0),
@@ -267,38 +324,22 @@
     groups, taps = filters.shape
     assert rows == taps == LANES and lax.axis_size("ctx") % 2 == 0
     scale = 1.0 / math.sqrt(rows * lax.axis_size("ctx") * lax.axis_size("dp") * GSIZE)
-    flags = lax.optimization_barrier(jnp.minimum(contig_starts, 1))
-    starts = flags[0] > 0
-    token = jnp.arange(rows)
-    tail = ~jnp.any(starts[None, :] & (token[None, :] > token[:, None]), axis=1)
-    head = ~jnp.any(starts[None, :] & (token[None, :] <= token[:, None]), axis=1)
-    even = lax.axis_index("ctx") % 2 == 0
-    width = q.shape[1] // 2
-    low, high, every = slice(0, width), slice(width, None), slice(None)
-
-    def sent(from_even, kv_part, cot_part, *earlier):
-        to_next = even if from_even else ~even
-        q_, k_, v_, dy_ = lax.optimization_barrier((q, k, v, dy, *earlier))[:4]
-        kv = product(k_[:, kv_part], v_[:, kv_part])
-        cot = product(dy_[:, cot_part], q_[:, cot_part])
-        keep = jnp.where(to_next, tail, head)
-        return jnp.where(keep[:, None], jnp.where(to_next, kv, cot), 0)
-
-    far_out = sent(False, low, high)
+    q, k, v, dy, far_out, pair_out, later_far_out, later_pair_out, masks, table_masks, tap_rows = first(
+        q, k, v, dy, contig_starts, filters
+    )
     far = next_chip(far_out)
-    pair_out = sent(True, low, high)
     pair = other_core(pair_out)
-    theirs = filter_share(q, k, v, dy, pair, flags, groups, scale, True)
-    later_far = next_chip(sent(False, high, low, theirs))
-    later_pair = other_core(sent(True, high, low, theirs))
-    mine = filter_share(q, k, v, dy, after(far, theirs), flags, groups, scale, False)
+    theirs = filter_share(q, k, v, dy, pair, masks, groups, scale, True)
+    later_far = next_chip(after(later_far_out, theirs))
+    later_pair = other_core(after(later_pair_out, theirs))
+    mine = filter_share(q, k, v, dy, after(far, theirs), masks, groups, scale, False)
     mine = mine + other_core(theirs)
 
     def forward(pair, far, outs, half):
-        return convolution(k, v, pair, far, q, dy, flags, filters, outs, False, half)
+        return convolution(k, v, pair, far, q, dy, table_masks, tap_rows, outs, False, half)
 
     def backward(pair, far, outs, half):
-        return convolution(dy, q, pair, far, v, k, flags, filters, outs, True, half)
+        return convolution(dy, q, pair, far, v, k, table_masks, tap_rows, outs, True, half)
 
     for n, place in enumerate(rounds_over_chips()):
         if n == 0:
@@ -315,7 +356,7 @@
         mine = summed_over(mine, *place)
     mine = after(mine, grad_k, grad_v)
     halves = [mine, other_core(mine)]
-    filter_grad = jnp.where(even, jnp.concatenate(halves), jnp.concatenate(halves[::-1]))
+    filter_grad = jnp.where(lax.axis_index("ctx") % 2 == 0, jnp.concatenate(halves), jnp.concatenate(halves[::-1]))
     return (mixed[None], grad_q[None], grad_k[None], grad_v[None], filter_grad)
 
 

time: 37.7 us -> 36.3 us (0.963)
  starting transfers between devices: 16 us -> 17.9 us
  other arithmetic: 2.5 us -> 0.67 us
  local copies, waits for them, and re-layouts: 1.71 us -> 0 us
  Pallas kernels: 14.6 us -> 15 us
    ppermute x4, starting transfers between devices: 7.56 us -> 11.3 us  [summed_over(): lax.ppermute(total, axis, [(turned(i, k), i) for i in range(size)])]
    pallas_call x0 -> x1, Pallas kernels: none -> 1.81 us  [first(): pl.pallas_call(first_kernel, out_shape=[wide] * 4 + [sent] * 4 + [pltpu.V...]
    unnamed x14 -> x0, local copies, waits for them, and re-layouts: 1.71 us -> none
    select_n x4 -> x1, other arithmetic: 2.34 us -> 0.64 us  [per_device(): jnp.where(lax.axis_index('ctx') % 2 == 0, jnp.concatenate(halves), jnp.co...]
    ppermute x4, starting transfers between devices: 6.95 us -> 5.33 us  [other_core(): lax.ppermute(block, 'ctx', [(i, i ^ 1) for i in range(lax.axis_size('ctx'...]
    pallas_call x6, Pallas kernels: 14.6 us -> 13.2 us  [local_call(): pl.pallas_call(kernel, out_shape=out_shape, in_specs=in_specs or [VMEM] *...]
  transfers between devices with their start and end apart: 10 -> 10, of which waited for: 2 -> 2; matrix products, arithmetic and copies ran while one was open for 1% -> 0% of each run, Pallas kernels for 39% -> 37%
where the time goes in v11:
time: 36.3 us; the launch traced here: 36.1 us
  starting transfers between devices  17.9 us (49%)
  Pallas kernels  15 us (41%)
  waiting for transfers between devices  1.69 us (5%)
  between operations  0.82 us (2%)
  other arithmetic  0.67 us (2%)
    pallas_call x6, Pallas kernels, local_call(): pl.pallas_call(kernel, out_shape=out_shape, in_specs=in_specs or [VMEM] *...  13.2 us
    ppermute x4, starting transfers between devices, summed_over(): lax.ppermute(total, axis, [(turned(i, k), i) for i in range(size)])  11.3 us
    ppermute x4, starting transfers between devices, other_core(): lax.ppermute(block, 'ctx', [(i, i ^ 1) for i in range(lax.axis_size('ctx'...  5.33 us
    pallas_call x1, Pallas kernels, first(): pl.pallas_call(first_kernel, out_shape=[wide] * 4 + [sent] * 4 + [pltpu.V...  1.81 us
    ppermute x4, waiting for transfers between devices, other_core(): lax.ppermute(block, 'ctx', [(i, i ^ 1) for i in range(lax.axis_size('ctx'...  1.68 us
    ppermute x2, starting transfers between devices, next_chip(): return lax.ppermute(block, 'ctx', pairs + [(j, i) for i, j in pairs])  1.34 us
  transfers between devices with their start and end apart: 10, of which 2 were waited for; matrix products, arithmetic and copies ran while one was open for 0% of the time, Pallas kernels for 37%

profile of v11, /device:TPU:0, one launch (start us, length us, event | category | flops | bytes accessed | tf_op | source)
XLA Modules:
  0.0 36.1 jit_solution(6167454225069477257)
XLA Ops:
  0.6 1.8 %first.1 = (bf16[128,2048]{1,0:T(8,128)(2,1)S(1)}, bf16[128,2048]{1,0:T(8,128)(2,1)S(1)}, bf16[128,2048]{1,0:T(8,128)(2,1)S(1)}, bf16[128,2048]{1,0:T(8,128)(2,1...) custom-call(bf16[128,2048]{1,0:T(8,128)(2,1)} %bitcast.8, ...), custom_call_target="tpu_custom_call" | custom-call | tf_op jit(solution)/shard_map/first/pallas_call | solution.py:227
  2.5 0.5 %collective-permute-start = (bf16[128,1024]{1,0:T(8,128)(2,1)S(1)}, bf16[128,1024]{1,0:T(8,128)(2,1)S(1)}, u32[]{:S(2)}, u32[]{:S(2)}) collective-permute-start(bf16[128,1024]{1,0:T(8,128)(2,1)S(1)} %get-tuple-element.36), channel_id=1, source_target_pairs={{0,4},{4,0},{8,12},{12,8},{16,20},{20,16},{24,28},{28,24},{1,5},{5... | collective-permute-start | bytes 786440 | tf_op jit(solution)/shard_map/ppermute | solution.py:280
  3.0 0.7 %collective-permute-start.3 = (bf16[128,1024]{1,0:T(8,128)(2,1)S(1)}, bf16[128,1024]{1,0:T(8,128)(2,1)S(1)}, u32[]{:S(2)}, u32[]{:S(2)}) collective-permute-start(bf16[128,1024]{1,0:T(8,128)(2,1)S(1)} %get-tuple-element.43), channel_id=1, source_target_pairs={{4,8},{12,16},{20,24},{8,4},{16,12},{24,20},{5,9},{13,17},{21,25},... | collective-permute-start | bytes 786440 | tf_op jit(solution)/shard_map/ppermute | solution.py:286
  3.6 0.5 %collective-permute-done.other_ref.refs_2_ = bf16[128,1024]{1,0:T(8,128)(2,1)S(1)} collective-permute-done((bf16[128,1024]{1,0:T(8,128)(2,1)S(1)}, bf16[128,1024]{1,0:T(8,128)(2,1)S(1)}, u32[]{:S(2)}, u32[]{:S(2)}) %collective-permute-start) | collective-permute-done | bytes 262176 | tf_op jit(solution)/shard_map/ppermute | solution.py:280
  4.1 2.0 %filter_partner.1 = f32[64,128]{1,0:T(8,128)S(1)} custom-call(bf16[128,2048]{1,0:T(8,128)(2,1)S(1)} %get-tuple-element.34.q_ref.refs_4_.c_ref.refs_1_.b_ref, bf16[128,2048]{1,0:T(8,128)(2,1)S(1)} %get-tuple-element.31.k_ref.refs_0_.a_ref.refs_5_.d_ref, bf16[128,2048]{1,0:T(8,128)(2,1)S(1)} %get-tuple-element.32.v_ref.refs_1_.b_ref.refs_4_.c_ref, ...), custom_call_target="tpu_custom_call" | custom-call | flops 1000 | bytes 1000 | tf_op jit(solution)/shard_map/filter_partner/pallas_call | solution.py:209
  6.1 0.7 %collective-permute-start.2 = (bf16[128,1024]{1,0:T(8,128)(2,1)S(1)}, bf16[128,1024]{1,0:T(8,128)(2,1)S(1)}, u32[]{:S(2)}, u32[]{:S(2)}) collective-permute-start(bf16[128,1024]{1,0:T(8,128)(2,1)S(1)} %get-tuple-element.40), channel_id=1, source_target_pairs={{4,8},{12,16},{20,24},{8,4},{16,12},{24,20},{5,9},{13,17},{21,25},... | collective-permute-start | bytes 786440 | tf_op jit(solution)/shard_map/ppermute | solution.py:286
  6.8 4.7 %collective-permute-start.1 = (bf16[128,1024]{1,0:T(8,128)(2,1)S(1)}, bf16[128,1024]{1,0:T(8,128)(2,1)S(1)}, u32[]{:S(2)}, u32[]{:S(2)}) collective-permute-start(bf16[128,1024]{1,0:T(8,128)(2,1)S(1)} %get-tuple-element.38), channel_id=1, source_target_pairs={{0,4},{4,0},{8,12},{12,8},{16,20},{20,16},{24,28},{28,24},{1,5},{5... | collective-permute-start | bytes 786440 | tf_op jit(solution)/shard_map/ppermute | solution.py:280
  11.4 0.1 collective-permute-start.4
  11.5 0.0 collective-permute-done.3.refs_3_.other_ref
  11.5 1.9 %filter_own.1 = f32[64,128]{1,0:T(8,128)S(1)} custom-call(bf16[128,2048]{1,0:T(8,128)(2,1)S(1)} %get-tuple-element.34.q_ref.refs_4_.c_ref.refs_1_.b_ref, bf16[128,2048]{1,0:T(8,128)(2,1)S(1)} %get-tuple-element.31.k_ref.refs_0_.a_ref.refs_5_.d_ref, bf16[128,2048]{1,0:T(8,128)(2,1)S(1)} %get-tuple-element.32.v_ref.refs_1_.b_ref.refs_4_.c_ref, ...), custom_call_target="tpu_custom_call" | custom-call | flops 1000 | bytes 1000 | tf_op jit(solution)/shard_map/filter_own/pallas_call | solution.py:209
  13.5 0.0 collective-permute-done.4
  13.5 2.2 %collective-permute-start.5 = (f32[64,128]{1,0:T(8,128)S(1)}, f32[64,128]{1,0:T(8,128)S(1)}, u32[]{:S(2)}, u32[]{:S(2)}) collective-permute-start(f32[64,128]{1,0:T(8,128)S(1)} %add.20), channel_id=1, source_target_pairs={{1,0},{0,1},{3,2},{2,3},{5,4},{4,5},{7,6},{6,7},{9,8},{8,9},{11,10... | collective-permute-start | bytes 98312 | tf_op jit(solution)/shard_map/ppermute | solution.py:310
  15.7 2.3 %forward_low.1 = (bf16[128,2048]{1,0:T(8,128)(2,1)}, bf16[128,2048]{1,0:T(8,128)(2,1)}) custom-call(bf16[128,2048]{1,0:T(8,128)(2,1)S(1)} %get-tuple-element.31.k_ref.refs_0_.a_ref.refs_5_.d_ref, bf16[128,2048]{1,0:T(8,128)(2,1)S(1)} %get-tuple-element.32.v_ref.refs_1_.b_ref.refs_4_.c_ref, bf16[128,1024]{1,0:T(8,128)(2,1)S(1)} %collective-permute-done.other_ref.refs_2_, ...), custom_call_target="tpu_custom_call" | custom-call | flops 536870912 | bytes 3932160 | tf_op jit(solution)/shard_map/forward_low/pallas_call | solution.py:209
  18.1 0.0 collective-permute-done.5
  18.1 2.7 %collective-permute-start.6 = (f32[64,128]{1,0:T(8,128)S(1)}, f32[64,128]{1,0:T(8,128)S(1)}, u32[]{:S(2)}, u32[]{:S(2)}) collective-permute-start(f32[64,128]{1,0:T(8,128)S(1)} %add.21), channel_id=1, source_target_pairs={{2,0},{3,1},{0,2},{1,3},{6,4},{7,5},{4,6},{5,7},{10,8},{11,9},{8,1... | collective-permute-start | bytes 98312 | tf_op jit(solution)/shard_map/ppermute | solution.py:310
  20.8 2.3 %backward_high.1 = (bf16[128,2048]{1,0:T(8,128)(2,1)}, bf16[128,2048]{1,0:T(8,128)(2,1)}) custom-call(bf16[128,2048]{1,0:T(8,128)(2,1)S(1)} %get-tuple-element.35.dy_ref.refs_5_.d_ref.refs_0_.a_ref, bf16[128,2048]{1,0:T(8,128)(2,1)S(1)} %get-tuple-element.34.q_ref.refs_4_.c_ref.refs_1_.b_ref, bf16[128,1024]{1,0:T(8,128)(2,1)S(1)} %collective-permute-done.other_ref.refs_2_, ...), custom_call_target="tpu_custom_call" | custom-call | flops 536870912 | bytes 3932160 | tf_op jit(solution)/shard_map/backward_high/pallas_call | solution.py:209
  23.1 0.0 collective-permute-done.6
  23.1 0.0 collective-permute-done.2.far_ref
  23.2 0.0 collective-permute-done.1.pair_ref
  23.2 2.4 %collective-permute-start.7 = (f32[64,128]{1,0:T(8,128)S(1)}, f32[64,128]{1,0:T(8,128)S(1)}, u32[]{:S(2)}, u32[]{:S(2)}) collective-permute-start(f32[64,128]{1,0:T(8,128)S(1)} %add.22), channel_id=1, source_target_pairs={{8,0},{12,4},{0,8},{4,12},{24,16},{28,20},{16,24},{20,28},{9,1},{1... | collective-permute-start | bytes 98312 | tf_op jit(solution)/shard_map/ppermute | solution.py:310
  25.6 2.3 %forward_high.1 = (bf16[128,2048]{1,0:T(8,128)(2,1)}, bf16[128,2048]{1,0:T(8,128)(2,1)}) custom-call(bf16[128,2048]{1,0:T(8,128)(2,1)S(1)} %get-tuple-element.31.k_ref.refs_0_.a_ref.refs_5_.d_ref, bf16[128,2048]{1,0:T(8,128)(2,1)S(1)} %get-tuple-element.32.v_ref.refs_1_.b_ref.refs_4_.c_ref, ...), custom_call_target="tpu_custom_call", output_to_operand_aliasing={{0}: (8, {}), {1}: (9, {})} | custom-call | flops 536870912 | bytes 4980736 | tf_op jit(solution)/shard_map/forward_high/pallas_call | solution.py:209
  28.0 0.0 collective-permute-done.7
  28.0 3.9 %collective-permute-start.8 = (f32[64,128]{1,0:T(8,128)S(1)}, f32[64,128]{1,0:T(8,128)S(1)}, u32[]{:S(2)}, u32[]{:S(2)}) collective-permute-start(f32[64,128]{1,0:T(8,128)S(1)} %add.23), channel_id=1, source_target_pairs={{16,0},{20,4},{24,8},{28,12},{0,16},{4,20},{8,24},{12,28},{17,1},{... | collective-permute-start | bytes 98312 | tf_op jit(solution)/shard_map/ppermute | solution.py:310
  31.9 2.3 %backward_low.1 = (bf16[128,2048]{1,0:T(8,128)(2,1)}, bf16[128,2048]{1,0:T(8,128)(2,1)}) custom-call(bf16[128,2048]{1,0:T(8,128)(2,1)S(1)} %get-tuple-element.35.dy_ref.refs_5_.d_ref.refs_0_.a_ref, bf16[128,2048]{1,0:T(8,128)(2,1)S(1)} %get-tuple-element.34.q_ref.refs_4_.c_ref.refs_1_.b_ref, ...), custom_call_target="tpu_custom_call", output_to_operand_aliasing={{0}: (8, {}), {1}: (9, {})} | custom-call | flops 536870912 | bytes 4980736 | tf_op jit(solution)/shard_map/backward_low/pallas_call | solution.py:209
  34.2 0.0 collective-permute-done.8
  34.2 0.1 collective-permute-start.9
  34.3 1.2 %collective-permute-done.9 = f32[64,128]{1,0:T(8,128)S(1)} collective-permute-done((f32[64,128]{1,0:T(8,128)S(1)}, f32[64,128]{1,0:T(8,128)S(1)}, u32[]{:S(2)}, u32[]{:S(2)}) %collective-permute-start.9) | collective-permute-done | bytes 32800 | tf_op jit(solution)/shard_map/ppermute | solution.py:280
  35.5 0.6 %maximum_select_fusion = f32[128,128]{1,0:T(8,128)} fusion(f32[64,128]{1,0:T(8,128)S(1)} %collective-permute-done.9, f32[64,128]{1,0:T(8,128)S(1)} %add.24, pred[]{:T(512)S(6)} %eq.5), kind=kLoop, calls=%fused_computation | loop fusion | flops 49152 | bytes 131073 | tf_op jit(solution)/shard_map/jit(_where)/select_n | solution.py:359
  (5 shorter events, 0.0 us)
Async XLA Ops:
  2.5 1.7 %collective-permute-start = (bf16[128,1024]{1,0:T(8,128)(2,1)S(1)}, bf16[128,1024]{1,0:T(8,128)(2,1)S(1)}, u32[]{:S(2)}, u32[]{:S(2)}) collective-permute-start(bf16[128,1024]{1,0:T(8,128)(2,1)S(1)} %get-tuple-element.36), channel_id=1, source_target_pairs={{0,4},{4,0},{8,12},{12,8},{16,20},{20,16},{24,28},{28,24},{1,5},{5... | collective-permute-start | bytes 786440 | tf_op jit(solution)/shard_map/ppermute | solution.py:280
  3.0 8.6 %collective-permute-start.3 = (bf16[128,1024]{1,0:T(8,128)(2,1)S(1)}, bf16[128,1024]{1,0:T(8,128)(2,1)S(1)}, u32[]{:S(2)}, u32[]{:S(2)}) collective-permute-start(bf16[128,1024]{1,0:T(8,128)(2,1)S(1)} %get-tuple-element.43), channel_id=1, source_target_pairs={{4,8},{12,16},{20,24},{8,4},{16,12},{24,20},{5,9},{13,17},{21,25},... | collective-permute-start | bytes 786440 | tf_op jit(solution)/shard_map/ppermute | solution.py:286
  6.1 17.1 %collective-permute-start.2 = (bf16[128,1024]{1,0:T(8,128)(2,1)S(1)}, bf16[128,1024]{1,0:T(8,128)(2,1)S(1)}, u32[]{:S(2)}, u32[]{:S(2)}) collective-permute-start(bf16[128,1024]{1,0:T(8,128)(2,1)S(1)} %get-tuple-element.40), channel_id=1, source_target_pairs={{4,8},{12,16},{20,24},{8,4},{16,12},{24,20},{5,9},{13,17},{21,25},... | collective-permute-start | bytes 786440 | tf_op jit(solution)/shard_map/ppermute | solution.py:286
  6.8 16.4 %collective-permute-start.1 = (bf16[128,1024]{1,0:T(8,128)(2,1)S(1)}, bf16[128,1024]{1,0:T(8,128)(2,1)S(1)}, u32[]{:S(2)}, u32[]{:S(2)}) collective-permute-start(bf16[128,1024]{1,0:T(8,128)(2,1)S(1)} %get-tuple-element.38), channel_id=1, source_target_pairs={{0,4},{4,0},{8,12},{12,8},{16,20},{20,16},{24,28},{28,24},{1,5},{5... | collective-permute-start | bytes 786440 | tf_op jit(solution)/shard_map/ppermute | solution.py:280
  11.4 2.0 %collective-permute-start.4 = (f32[64,128]{1,0:T(8,128)S(1)}, f32[64,128]{1,0:T(8,128)S(1)}, u32[]{:S(2)}, u32[]{:S(2)}) collective-permute-start(f32[64,128]{1,0:T(8,128)S(1)} %filter_partner.1), channel_id=1, source_target_pairs={{0,4},{4,0},{8,12},{12,8},{16,20},{20,16},{24,28},{28,24},{1,5},{5... | collective-permute-start | bytes 98312 | tf_op jit(solution)/shard_map/ppermute | solution.py:280
  13.5 4.6 %collective-permute-start.5 = (f32[64,128]{1,0:T(8,128)S(1)}, f32[64,128]{1,0:T(8,128)S(1)}, u32[]{:S(2)}, u32[]{:S(2)}) collective-permute-start(f32[64,128]{1,0:T(8,128)S(1)} %add.20), channel_id=1, source_target_pairs={{1,0},{0,1},{3,2},{2,3},{5,4},{4,5},{7,6},{6,7},{9,8},{8,9},{11,10... | collective-permute-start | bytes 98312 | tf_op jit(solution)/shard_map/ppermute | solution.py:310
  18.1 5.0 %collective-permute-start.6 = (f32[64,128]{1,0:T(8,128)S(1)}, f32[64,128]{1,0:T(8,128)S(1)}, u32[]{:S(2)}, u32[]{:S(2)}) collective-permute-start(f32[64,128]{1,0:T(8,128)S(1)} %add.21), channel_id=1, source_target_pairs={{2,0},{3,1},{0,2},{1,3},{6,4},{7,5},{4,6},{5,7},{10,8},{11,9},{8,1... | collective-permute-start | bytes 98312 | tf_op jit(solution)/shard_map/ppermute | solution.py:310
  23.2 4.8 %collective-permute-start.7 = (f32[64,128]{1,0:T(8,128)S(1)}, f32[64,128]{1,0:T(8,128)S(1)}, u32[]{:S(2)}, u32[]{:S(2)}) collective-permute-start(f32[64,128]{1,0:T(8,128)S(1)} %add.22), channel_id=1, source_target_pairs={{8,0},{12,4},{0,8},{4,12},{24,16},{28,20},{16,24},{20,28},{9,1},{1... | collective-permute-start | bytes 98312 | tf_op jit(solution)/shard_map/ppermute | solution.py:310
  28.0 6.2 %collective-permute-start.8 = (f32[64,128]{1,0:T(8,128)S(1)}, f32[64,128]{1,0:T(8,128)S(1)}, u32[]{:S(2)}, u32[]{:S(2)}) collective-permute-start(f32[64,128]{1,0:T(8,128)S(1)} %add.23), channel_id=1, source_target_pairs={{16,0},{20,4},{24,8},{28,12},{0,16},{4,20},{8,24},{12,28},{17,1},{... | collective-permute-start | bytes 98312 | tf_op jit(solution)/shard_map/ppermute | solution.py:310
  34.2 1.3 %collective-permute-start.9 = (f32[64,128]{1,0:T(8,128)S(1)}, f32[64,128]{1,0:T(8,128)S(1)}, u32[]{:S(2)}, u32[]{:S(2)}) collective-permute-start(f32[64,128]{1,0:T(8,128)S(1)} %add.24), channel_id=1, source_target_pairs={{0,4},{4,0},{8,12},{12,8},{16,20},{20,16},{24,28},{28,24},{1,5},{5... | collective-permute-start | bytes 98312 | tf_op jit(solution)/shard_map/ppermute | solution.py:280

commit v12 on v11

--- a/solution.py
+++ b/solution.py
@@ -15,7 +15,7 @@
 
 
 def product(a, b):
-    return (a.astype(jnp.float32) * b.astype(jnp.float32)).astype(jnp.bfloat16)
+    return a * b
 
 
 def reversed_taps(rows_of_taps):
@@ -75,7 +75,7 @@
     own = as_f32((s <= t) & (s >= began))
     previous = as_f32((s > t) & (t < first))
     following = as_f32((s < t) & (t >= last))
-    for n, mask in enumerate((own, own.T, previous, following)):
+    for n, mask in enumerate((own, own.T, previous, following, previous.T, following.T)):
         masks_ref[n] = mask
     for n, parts in enumerate(((own, previous), (own.T, following))):
         for m, mask in enumerate(parts):
@@ -103,47 +103,90 @@
             pair[at, :] = jnp.where(even, kv, cot)
 
 
-def filter_kernel(
-    q_ref, k_ref, v_ref, dy_ref, other_ref, masks_ref, out_ref, own_ref, other_mask_ref, sums_ref, *, scale, partner
-):
-    rows = q_ref.shape[0]
-    per_tile = LANES // GSIZE
+def masked_diagonals(left, sides, group):
+    rows = left.shape[0]
+    right = jnp.concatenate([side for side, _ in sides], axis=0)
+    for g in range(LANES // GSIZE):
+        picked = jnp.where(group == g, left, jnp.zeros_like(left))
+        pairs = lax.dot_general(picked, right, (((1,), (1,)), ((), ())), preferred_element_type=jnp.float32)
+        linked = pairs[:, :rows] * sides[0][1][...]
+        for n in range(1, len(sides)):
+            linked = linked + pairs[:, n * rows : (n + 1) * rows] * sides[n][1][...]
+        total = linked[:8]
+        for i in range(1, rows // 8):
+            total = total + pltpu.roll(linked[8 * i : 8 * i + 8], rows - 8 * i, 1)
+        yield g, total
+
+
+def diagonals(sums_ref, groups):
+    rows = sums_ref.shape[1]
+    total = sums_ref[pl.ds(0, groups, stride=8), :]
+    for r in range(1, 8):
+        total = total + pltpu.roll(sums_ref[pl.ds(r, groups, stride=8), :], rows - r, 1)
+    return total
+
+
+def lanes_of(half, width, index):
+    return pl.ds(pl.multiple_of(half * width + index * LANES, LANES), LANES)
+
+
+def sums_at(index, g):
+    return pl.ds(pl.multiple_of((index * (LANES // GSIZE) + g) * 8, 8), 8)
+
+
+def filter_partner_kernel(q_ref, k_ref, v_ref, dy_ref, masks_ref, out_ref, sums_ref, *, scale):
+    width = q_ref.shape[1] // 2
+    half = 1 - lax.axis_index("ctx") % 2
+    group = lane_groups()
+
+    def tile(index):
+        lanes = lanes_of(half, width, index)
+        cot = product(dy_ref[:, lanes], q_ref[:, lanes])
+        kv = product(k_ref[:, lanes], v_ref[:, lanes])
+        for g, total in masked_diagonals(kv, [(cot, masks_ref.at[1])], group):
+            sums_ref[sums_at(index, g), :] = total
+
+    each_tile(tile, width)
+    out_ref[...] = diagonals(sums_ref, out_ref.shape[0]) * scale
+
+
+def filter_own_kernel(q_ref, k_ref, v_ref, dy_ref, other_ref, masks_ref, sums_ref, own_ref, cross_ref):
     width = q_ref.shape[1] // 2
     core = lax.axis_index("ctx") % 2
-    half = 1 - core if partner else core
-    low = half == 0
-    base = half * width
-    own_ref[...] = jnp.where(low, masks_ref[0], masks_ref[1])
-    other_mask_ref[...] = jnp.where(low, masks_ref[2], masks_ref[3])
+    even = core == 0
+    own_ref[...] = jnp.where(even, masks_ref[1], masks_ref[0])
+    cross_ref[...] = jnp.where(even, masks_ref[3], masks_ref[2])
     group = lane_groups()
 
     def tile(index):
-        here = pl.ds(pl.multiple_of(index * LANES, LANES), LANES)
-        lanes = pl.ds(pl.multiple_of(base + index * LANES, LANES), LANES)
+        lanes = lanes_of(core, width, index)
         cot = product(dy_ref[:, lanes], q_ref[:, lanes])
         kv = product(k_ref[:, lanes], v_ref[:, lanes])
-        left = jnp.where(low, cot, kv)
-        right = jnp.concatenate(
-            [jnp.where(low, kv, cot), other_ref[:, here]], axis=0
-        )
-        for g in range(per_tile):
-            picked = jnp.where(group == g, left, jnp.zeros_like(left))
-            pairs = lax.dot_general(
-                picked, right, (((1,), (1,)), ((), ())), preferred_element_type=jnp.float32
-            )
-            linked = pairs[:, :rows] * own_ref[...] + pairs[:, rows:] * other_mask_ref[...]
-            total = linked[:8]
-            for i in range(1, rows // 8):
-                total = total + pltpu.roll(linked[8 * i : 8 * i + 8], rows - 8 * i, 1)
-            at = pl.multiple_of((index * per_tile + g) * 8, 8)
-            sums_ref[pl.ds(at, 8), :] = total
+        sides = [(jnp.where(even, cot, kv), own_ref), (other_ref[:, lanes_of(0, width, index)], cross_ref)]
+        for g, total in masked_diagonals(jnp.where(even, kv, cot), sides, group):
+            sums_ref[sums_at(index, g), :] = total
 
     each_tile(tile, width)
-    groups = out_ref.shape[0]
-    diagonal = sums_ref[pl.ds(0, groups, stride=8), :]
-    for r in range(1, 8):
-        diagonal = diagonal + pltpu.roll(sums_ref[pl.ds(r, groups, stride=8), :], rows - r, 1)
-    out_ref[...] = jnp.where(low, reversed_taps(diagonal), diagonal) * scale
+
+
+def filter_far_kernel(q_ref, k_ref, v_ref, dy_ref, other_ref, masks_ref, sums_ref, out_ref, total_ref, cross_ref, *, scale):
+    width = q_ref.shape[1] // 2
+    core = lax.axis_index("ctx") % 2
+    even = core == 0
+    cross_ref[...] = jnp.where(even, masks_ref[4], masks_ref[5])
+    group = lane_groups()
+
+    def tile(index):
+        lanes = lanes_of(core, width, index)
+        cot = product(dy_ref[:, lanes], q_ref[:, lanes])
+        kv = product(k_ref[:, lanes], v_ref[:, lanes])
+        left = other_ref[:, lanes_of(0, width, index)]
+        for g, total in masked_diagonals(left, [(jnp.where(even, cot, kv), cross_ref)], group):
+            total_ref[sums_at(index, g), :] = sums_ref[sums_at(index, g), :] + total
+
+    each_tile(tile, width)
+    total = diagonals(total_ref, out_ref.shape[0])
+    out_ref[...] = jnp.where(even, total, reversed_taps(total)) * scale
 
 
 def conv_kernel(
@@ -227,7 +270,7 @@
     return pl.pallas_call(
         first_kernel,
         out_shape=[wide] * 4 + [sent] * 4 + [
-            pltpu.VMEM((4, rows, rows), jnp.float32),
+            pltpu.VMEM((6, rows, rows), jnp.float32),
             pltpu.VMEM((2, rows, 2 * rows), jnp.bfloat16),
             pltpu.VMEM((2, *filters.shape), jnp.float32),
         ],
@@ -242,16 +285,8 @@
     )(*operands)
 
 
-def filter_share(q, k, v, dy, other, masks, groups, scale, partner):
-    rows, width = q.shape
-    table = pltpu.VMEM((rows, rows), jnp.float32)
-    return local_call(
-        functools.partial(filter_kernel, scale=scale, partner=partner),
-        "filter_partner" if partner else "filter_own",
-        jax.ShapeDtypeStruct((groups // 2, rows), jnp.float32),
-        [table, table, pltpu.VMEM((groups * 4, rows), jnp.float32)],
-        1000, (q, k, v, dy, other, masks), moved=1000,
-    )
+def filter_call(kernel, name, out_shape, scratch_shapes, *operands):
+    return local_call(kernel, name, out_shape, scratch_shapes, 0, operands, moved=0)
 
 
 def convolution(a, b, pair, far, c, d, masks, taps, outs, backward, half):
@@ -327,12 +362,24 @@
     q, k, v, dy, far_out, pair_out, later_far_out, later_pair_out, masks, table_masks, tap_rows = first(
         q, k, v, dy, contig_starts, filters
     )
+    square = pltpu.VMEM((rows, rows), jnp.float32)
+    part = jax.ShapeDtypeStruct((groups // 2, rows), jnp.float32)
+    unsummed = jax.ShapeDtypeStruct((groups * 4, rows), jnp.float32)
+    sums = pltpu.VMEM(unsummed.shape, unsummed.dtype)
     far = next_chip(far_out)
-    pair = other_core(pair_out)
-    theirs = filter_share(q, k, v, dy, pair, masks, groups, scale, True)
+    theirs = filter_call(
+        functools.partial(filter_partner_kernel, scale=scale), "filter_partner", part, [sums], q, k, v, dy, masks
+    )
+    later_pair = other_core(later_pair_out)
+    pair = other_core(after(pair_out, theirs))
     later_far = next_chip(after(later_far_out, theirs))
-    later_pair = other_core(after(later_pair_out, theirs))
-    mine = filter_share(q, k, v, dy, after(far, theirs), masks, groups, scale, False)
+    mine = filter_call(
+        filter_own_kernel, "filter_own", unsummed, [square, square], q, k, v, dy, later_pair, masks
+    )
+    mine = filter_call(
+        functools.partial(filter_far_kernel, scale=scale), "filter_far", part, [sums, square],
+        q, k, v, dy, far, masks, mine,
+    )
     mine = mine + other_core(theirs)
 
     def forward(pair, far, outs, half):

time: 36.3 us -> 36 us (level)
  Pallas kernels: 15 us -> 16.9 us
  starting transfers between devices: 17.9 us -> 16 us
    ppermute x4, starting transfers between devices: 11.3 us -> 7.34 us  [summed_over(): lax.ppermute(total, axis, [(turned(i, k), i) for i in range(size)])]
    pallas_call x6 -> x7, Pallas kernels: 13.2 us -> 15.2 us  [local_call(): pl.pallas_call(kernel, out_shape=out_shape, in_specs=in_specs or [VMEM] *...]
    ppermute x4, starting transfers between devices: 5.33 us -> 7.33 us  [other_core(): lax.ppermute(block, 'ctx', [(i, i ^ 1) for i in range(lax.axis_size('ctx'...]
    ppermute x4, waiting for transfers between devices: 1.68 us -> 1.19 us  [other_core(): lax.ppermute(block, 'ctx', [(i, i ^ 1) for i in range(lax.axis_size('ctx'...]
  transfers between devices with their start and end apart: 10 -> 10, of which waited for: 2 -> 2; matrix products, arithmetic and copies ran while one was open for 0% -> 0% of each run, Pallas kernels for 37% -> 43%
where the time goes in v12:
time: 36 us; the launch traced here: 35.8 us
  Pallas kernels  16.9 us (47%)
  starting transfers between devices  16 us (44%)
  waiting for transfers between devices  1.41 us (4%)
  between operations  0.79 us (2%)
  other arithmetic  0.67 us (2%)
    pallas_call x7, Pallas kernels, local_call(): pl.pallas_call(kernel, out_shape=out_shape, in_specs=in_specs or [VMEM] *...  15.2 us
    ppermute x4, starting transfers between devices, summed_over(): lax.ppermute(total, axis, [(turned(i, k), i) for i in range(size)])  7.34 us
    ppermute x4, starting transfers between devices, other_core(): lax.ppermute(block, 'ctx', [(i, i ^ 1) for i in range(lax.axis_size('ctx'...  7.33 us
    pallas_call x1, Pallas kernels, first(): pl.pallas_call(first_kernel, out_shape=[wide] * 4 + [sent] * 4 + [pltpu.V...  1.69 us
    ppermute x2, starting transfers between devices, next_chip(): return lax.ppermute(block, 'ctx', pairs + [(j, i) for i, j in pairs])  1.35 us
    ppermute x4, waiting for transfers between devices, other_core(): lax.ppermute(block, 'ctx', [(i, i ^ 1) for i in range(lax.axis_size('ctx'...  1.19 us
  transfers between devices with their start and end apart: 10, of which 2 were waited for; matrix products, arithmetic and copies ran while one was open for 0% of the time, Pallas kernels for 43%

profile of v12, /device:TPU:0, one launch (start us, length us, event | category | flops | bytes accessed | tf_op | source)
XLA Modules:
  0.0 35.8 jit_solution(13380004735644631993)
XLA Ops:
  0.6 1.7 %first.1 = (bf16[128,2048]{1,0:T(8,128)(2,1)S(1)}, bf16[128,2048]{1,0:T(8,128)(2,1)S(1)}, bf16[128,2048]{1,0:T(8,128)(2,1)S(1)}, bf16[128,2048]{1,0:T(8,128)(2,1...) custom-call(bf16[128,2048]{1,0:T(8,128)(2,1)} %bitcast.8, ...), custom_call_target="tpu_custom_call" | custom-call | tf_op jit(solution)/shard_map/first/pallas_call | solution.py:270
  2.3 0.7 %collective-permute-start.3 = (bf16[128,1024]{1,0:T(8,128)(2,1)S(1)}, bf16[128,1024]{1,0:T(8,128)(2,1)S(1)}, u32[]{:S(2)}, u32[]{:S(2)}) collective-permute-start(bf16[128,1024]{1,0:T(8,128)(2,1)S(1)} %get-tuple-element.42), channel_id=1, source_target_pairs={{4,8},{12,16},{20,24},{8,4},{16,12},{24,20},{5,9},{13,17},{21,25},... | collective-permute-start | bytes 786440 | tf_op jit(solution)/shard_map/ppermute | solution.py:321
  3.0 4.3 %collective-permute-start = (bf16[128,1024]{1,0:T(8,128)(2,1)S(1)}, bf16[128,1024]{1,0:T(8,128)(2,1)S(1)}, u32[]{:S(2)}, u32[]{:S(2)}) collective-permute-start(bf16[128,1024]{1,0:T(8,128)(2,1)S(1)} %get-tuple-element.32), channel_id=1, source_target_pairs={{0,4},{4,0},{8,12},{12,8},{16,20},{20,16},{24,28},{28,24},{1,5},{5... | collective-permute-start | bytes 786440 | tf_op jit(solution)/shard_map/ppermute | solution.py:315
  7.4 2.0 %filter_partner.1 = f32[64,128]{1,0:T(8,128)S(1)} custom-call(bf16[128,2048]{1,0:T(8,128)(2,1)S(1)} %get-tuple-element.34.q_ref.refs_4_.c_ref.refs_1_.b_ref, bf16[128,2048]{1,0:T(8,128)(2,1)S(1)} %get-tuple-element.30.k_ref.refs_0_.a_ref.refs_5_.d_ref, bf16[128,2048]{1,0:T(8,128)(2,1)S(1)} %get-tuple-element.31.v_ref.refs_1_.b_ref.refs_4_.c_ref, ...), custom_call_target="tpu_custom_call" | custom-call | tf_op jit(solution)/shard_map/filter_partner/pallas_call | solution.py:252
  9.4 0.1 collective-permute-start.2
  9.5 0.7 %collective-permute-start.1 = (bf16[128,1024]{1,0:T(8,128)(2,1)S(1)}, bf16[128,1024]{1,0:T(8,128)(2,1)S(1)}, u32[]{:S(2)}, u32[]{:S(2)}) collective-permute-start(bf16[128,1024]{1,0:T(8,128)(2,1)S(1)} %get-tuple-element.37), channel_id=1, source_target_pairs={{4,8},{12,16},{20,24},{8,4},{16,12},{24,20},{5,9},{13,17},{21,25},... | collective-permute-start | bytes 786440 | tf_op jit(solution)/shard_map/ppermute | solution.py:321
  10.2 2.9 %collective-permute-start.4 = (f32[64,128]{1,0:T(8,128)S(1)}, f32[64,128]{1,0:T(8,128)S(1)}, u32[]{:S(2)}, u32[]{:S(2)}) collective-permute-start(f32[64,128]{1,0:T(8,128)S(1)} %filter_partner.1), channel_id=1, source_target_pairs={{0,4},{4,0},{8,12},{12,8},{16,20},{20,16},{24,28},{28,24},{1,5},{5... | collective-permute-start | bytes 98312 | tf_op jit(solution)/shard_map/ppermute | solution.py:315
  13.1 0.0 collective-permute-done.pair_ref.other_ref
  13.1 1.7 %filter_own.1.sums_ref = f32[512,128]{1,0:T(8,128)S(1)} custom-call(bf16[128,2048]{1,0:T(8,128)(2,1)S(1)} %get-tuple-element.34.q_ref.refs_4_.c_ref.refs_1_.b_ref, bf16[128,2048]{1,0:T(8,128)(2,1)S(1)} %get-tuple-element.30.k_ref.refs_0_.a_ref.refs_5_.d_ref, bf16[128,2048]{1,0:T(8,128)(2,1)S(1)} %get-tuple-element.31.v_ref.refs_1_.b_ref.refs_4_.c_ref, ...), custom_call_target="tpu_custom_call" | custom-call | tf_op jit(solution)/shard_map/filter_own/pallas_call | solution.py:252
  14.7 0.0 collective-permute-done.3.refs_3_.other_ref
  14.7 2.2 %filter_far.1 = f32[64,128]{1,0:T(8,128)S(1)} custom-call(bf16[128,2048]{1,0:T(8,128)(2,1)S(1)} %get-tuple-element.34.q_ref.refs_4_.c_ref.refs_1_.b_ref, bf16[128,2048]{1,0:T(8,128)(2,1)S(1)} %get-tuple-element.30.k_ref.refs_0_.a_ref.refs_5_.d_ref, bf16[128,2048]{1,0:T(8,128)(2,1)S(1)} %get-tuple-element.31.v_ref.refs_1_.b_ref.refs_4_.c_ref, ...), custom_call_target="tpu_custom_call" | custom-call | tf_op jit(solution)/shard_map/filter_far/pallas_call | solution.py:252
  17.0 0.0 collective-permute-done.4
  17.0 1.7 %collective-permute-start.5 = (f32[64,128]{1,0:T(8,128)S(1)}, f32[64,128]{1,0:T(8,128)S(1)}, u32[]{:S(2)}, u32[]{:S(2)}) collective-permute-start(f32[64,128]{1,0:T(8,128)S(1)} %add.20), channel_id=1, source_target_pairs={{1,0},{0,1},{3,2},{2,3},{5,4},{4,5},{7,6},{6,7},{9,8},{8,9},{11,10... | collective-permute-start | bytes 98312 | tf_op jit(solution)/shard_map/ppermute | solution.py:345
  18.6 0.0 collective-permute-done.2.refs_2_
  18.6 2.3 %forward_low.1 = (bf16[128,2048]{1,0:T(8,128)(2,1)}, bf16[128,2048]{1,0:T(8,128)(2,1)}) custom-call(bf16[128,2048]{1,0:T(8,128)(2,1)S(1)} %get-tuple-element.30.k_ref.refs_0_.a_ref.refs_5_.d_ref, bf16[128,2048]{1,0:T(8,128)(2,1)S(1)} %get-tuple-element.31.v_ref.refs_1_.b_ref.refs_4_.c_ref, bf16[128,1024]{1,0:T(8,128)(2,1)S(1)} %collective-permute-done.2.refs_2_, ...), custom_call_target="tpu_custom_call" | custom-call | flops 536870912 | bytes 3932160 | tf_op jit(solution)/shard_map/forward_low/pallas_call | solution.py:252
  21.0 0.0 collective-permute-done.5
  21.0 2.6 %collective-permute-start.6 = (f32[64,128]{1,0:T(8,128)S(1)}, f32[64,128]{1,0:T(8,128)S(1)}, u32[]{:S(2)}, u32[]{:S(2)}) collective-permute-start(f32[64,128]{1,0:T(8,128)S(1)} %add.21), channel_id=1, source_target_pairs={{2,0},{3,1},{0,2},{1,3},{6,4},{7,5},{4,6},{5,7},{10,8},{11,9},{8,1... | collective-permute-start | bytes 98312 | tf_op jit(solution)/shard_map/ppermute | solution.py:345
  23.6 2.3 %backward_high.1 = (bf16[128,2048]{1,0:T(8,128)(2,1)}, bf16[128,2048]{1,0:T(8,128)(2,1)}) custom-call(bf16[128,2048]{1,0:T(8,128)(2,1)S(1)} %get-tuple-element.35.dy_ref.refs_5_.d_ref.refs_0_.a_ref, bf16[128,2048]{1,0:T(8,128)(2,1)S(1)} %get-tuple-element.34.q_ref.refs_4_.c_ref.refs_1_.b_ref, bf16[128,1024]{1,0:T(8,128)(2,1)S(1)} %collective-permute-done.2.refs_2_, ...), custom_call_target="tpu_custom_call" | custom-call | flops 536870912 | bytes 3932160 | tf_op jit(solution)/shard_map/backward_high/pallas_call | solution.py:252
  26.0 0.0 collective-permute-done.6
  26.0 0.0 collective-permute-done.1.far_ref
  26.0 1.6 %collective-permute-start.7 = (f32[64,128]{1,0:T(8,128)S(1)}, f32[64,128]{1,0:T(8,128)S(1)}, u32[]{:S(2)}, u32[]{:S(2)}) collective-permute-start(f32[64,128]{1,0:T(8,128)S(1)} %add.22), channel_id=1, source_target_pairs={{8,0},{12,4},{0,8},{4,12},{24,16},{28,20},{16,24},{20,28},{9,1},{1... | collective-permute-start | bytes 98312 | tf_op jit(solution)/shard_map/ppermute | solution.py:345
  27.6 2.3 %forward_high.1 = (bf16[128,2048]{1,0:T(8,128)(2,1)}, bf16[128,2048]{1,0:T(8,128)(2,1)}) custom-call(bf16[128,2048]{1,0:T(8,128)(2,1)S(1)} %get-tuple-element.30.k_ref.refs_0_.a_ref.refs_5_.d_ref, bf16[128,2048]{1,0:T(8,128)(2,1)S(1)} %get-tuple-element.31.v_ref.refs_1_.b_ref.refs_4_.c_ref, ...), custom_call_target="tpu_custom_call", output_to_operand_aliasing={{0}: (8, {}), {1}: (9, {})} | custom-call | flops 536870912 | bytes 4980736 | tf_op jit(solution)/shard_map/forward_high/pallas_call | solution.py:252
  30.0 0.1 collective-permute-done.7
  30.0 1.5 %collective-permute-start.8 = (f32[64,128]{1,0:T(8,128)S(1)}, f32[64,128]{1,0:T(8,128)S(1)}, u32[]{:S(2)}, u32[]{:S(2)}) collective-permute-start(f32[64,128]{1,0:T(8,128)S(1)} %add.23), channel_id=1, source_target_pairs={{16,0},{20,4},{24,8},{28,12},{0,16},{4,20},{8,24},{12,28},{17,1},{... | collective-permute-start | bytes 98312 | tf_op jit(solution)/shard_map/ppermute | solution.py:345
  31.5 2.3 %backward_low.1 = (bf16[128,2048]{1,0:T(8,128)(2,1)}, bf16[128,2048]{1,0:T(8,128)(2,1)}) custom-call(bf16[128,2048]{1,0:T(8,128)(2,1)S(1)} %get-tuple-element.35.dy_ref.refs_5_.d_ref.refs_0_.a_ref, bf16[128,2048]{1,0:T(8,128)(2,1)S(1)} %get-tuple-element.34.q_ref.refs_4_.c_ref.refs_1_.b_ref, ...), custom_call_target="tpu_custom_call", output_to_operand_aliasing={{0}: (8, {}), {1}: (9, {})} | custom-call | flops 536870912 | bytes 4980736 | tf_op jit(solution)/shard_map/backward_low/pallas_call | solution.py:252
  33.8 0.2 collective-permute-done.8
  34.0 0.0 collective-permute-start.9
  34.0 1.2 %collective-permute-done.9 = f32[64,128]{1,0:T(8,128)S(1)} collective-permute-done((f32[64,128]{1,0:T(8,128)S(1)}, f32[64,128]{1,0:T(8,128)S(1)}, u32[]{:S(2)}, u32[]{:S(2)}) %collective-permute-start.9) | collective-permute-done | bytes 32800 | tf_op jit(solution)/shard_map/ppermute | solution.py:315
  35.2 0.6 %maximum_select_fusion = f32[128,128]{1,0:T(8,128)} fusion(f32[64,128]{1,0:T(8,128)S(1)} %collective-permute-done.9, f32[64,128]{1,0:T(8,128)S(1)} %add.24, pred[]{:T(512)S(6)} %eq.5), kind=kLoop, calls=%fused_computation | loop fusion | flops 49152 | bytes 131073 | tf_op jit(solution)/shard_map/jit(_where)/select_n | solution.py:406
  (5 shorter events, 0.0 us)
Async XLA Ops:
  2.3 12.4 %collective-permute-start.3 = (bf16[128,1024]{1,0:T(8,128)(2,1)S(1)}, bf16[128,1024]{1,0:T(8,128)(2,1)S(1)}, u32[]{:S(2)}, u32[]{:S(2)}) collective-permute-start(bf16[128,1024]{1,0:T(8,128)(2,1)S(1)} %get-tuple-element.42), channel_id=1, source_target_pairs={{4,8},{12,16},{20,24},{8,4},{16,12},{24,20},{5,9},{13,17},{21,25},... | collective-permute-start | bytes 786440 | tf_op jit(solution)/shard_map/ppermute | solution.py:321
  3.0 10.1 %collective-permute-start = (bf16[128,1024]{1,0:T(8,128)(2,1)S(1)}, bf16[128,1024]{1,0:T(8,128)(2,1)S(1)}, u32[]{:S(2)}, u32[]{:S(2)}) collective-permute-start(bf16[128,1024]{1,0:T(8,128)(2,1)S(1)} %get-tuple-element.32), channel_id=1, source_target_pairs={{0,4},{4,0},{8,12},{12,8},{16,20},{20,16},{24,28},{28,24},{1,5},{5... | collective-permute-start | bytes 786440 | tf_op jit(solution)/shard_map/ppermute | solution.py:315
  9.4 9.2 %collective-permute-start.2 = (bf16[128,1024]{1,0:T(8,128)(2,1)S(1)}, bf16[128,1024]{1,0:T(8,128)(2,1)S(1)}, u32[]{:S(2)}, u32[]{:S(2)}) collective-permute-start(bf16[128,1024]{1,0:T(8,128)(2,1)S(1)} %get-tuple-element.41), channel_id=1, source_target_pairs={{0,4},{4,0},{8,12},{12,8},{16,20},{20,16},{24,28},{28,24},{1,5},{5... | collective-permute-start | bytes 786440 | tf_op jit(solution)/shard_map/ppermute | solution.py:315
  9.5 16.5 %collective-permute-start.1 = (bf16[128,1024]{1,0:T(8,128)(2,1)S(1)}, bf16[128,1024]{1,0:T(8,128)(2,1)S(1)}, u32[]{:S(2)}, u32[]{:S(2)}) collective-permute-start(bf16[128,1024]{1,0:T(8,128)(2,1)S(1)} %get-tuple-element.37), channel_id=1, source_target_pairs={{4,8},{12,16},{20,24},{8,4},{16,12},{24,20},{5,9},{13,17},{21,25},... | collective-permute-start | bytes 786440 | tf_op jit(solution)/shard_map/ppermute | solution.py:321
  10.2 6.8 %collective-permute-start.4 = (f32[64,128]{1,0:T(8,128)S(1)}, f32[64,128]{1,0:T(8,128)S(1)}, u32[]{:S(2)}, u32[]{:S(2)}) collective-permute-start(f32[64,128]{1,0:T(8,128)S(1)} %filter_partner.1), channel_id=1, source_target_pairs={{0,4},{4,0},{8,12},{12,8},{16,20},{20,16},{24,28},{28,24},{1,5},{5... | collective-permute-start | bytes 98312 | tf_op jit(solution)/shard_map/ppermute | solution.py:315
  17.0 4.0 %collective-permute-start.5 = (f32[64,128]{1,0:T(8,128)S(1)}, f32[64,128]{1,0:T(8,128)S(1)}, u32[]{:S(2)}, u32[]{:S(2)}) collective-permute-start(f32[64,128]{1,0:T(8,128)S(1)} %add.20), channel_id=1, source_target_pairs={{1,0},{0,1},{3,2},{2,3},{5,4},{4,5},{7,6},{6,7},{9,8},{8,9},{11,10... | collective-permute-start | bytes 98312 | tf_op jit(solution)/shard_map/ppermute | solution.py:345
  21.0 5.0 %collective-permute-start.6 = (f32[64,128]{1,0:T(8,128)S(1)}, f32[64,128]{1,0:T(8,128)S(1)}, u32[]{:S(2)}, u32[]{:S(2)}) collective-permute-start(f32[64,128]{1,0:T(8,128)S(1)} %add.21), channel_id=1, source_target_pairs={{2,0},{3,1},{0,2},{1,3},{6,4},{7,5},{4,6},{5,7},{10,8},{11,9},{8,1... | collective-permute-start | bytes 98312 | tf_op jit(solution)/shard_map/ppermute | solution.py:345
  26.0 4.0 %collective-permute-start.7 = (f32[64,128]{1,0:T(8,128)S(1)}, f32[64,128]{1,0:T(8,128)S(1)}, u32[]{:S(2)}, u32[]{:S(2)}) collective-permute-start(f32[64,128]{1,0:T(8,128)S(1)} %add.22), channel_id=1, source_target_pairs={{8,0},{12,4},{0,8},{4,12},{24,16},{28,20},{16,24},{20,28},{9,1},{1... | collective-permute-start | bytes 98312 | tf_op jit(solution)/shard_map/ppermute | solution.py:345
  30.0 4.0 %collective-permute-start.8 = (f32[64,128]{1,0:T(8,128)S(1)}, f32[64,128]{1,0:T(8,128)S(1)}, u32[]{:S(2)}, u32[]{:S(2)}) collective-permute-start(f32[64,128]{1,0:T(8,128)S(1)} %add.23), channel_id=1, source_target_pairs={{16,0},{20,4},{24,8},{28,12},{0,16},{4,20},{8,24},{12,28},{17,1},{... | collective-permute-start | bytes 98312 | tf_op jit(solution)/shard_map/ppermute | solution.py:345
  34.0 1.2 %collective-permute-start.9 = (f32[64,128]{1,0:T(8,128)S(1)}, f32[64,128]{1,0:T(8,128)S(1)}, u32[]{:S(2)}, u32[]{:S(2)}) collective-permute-start(f32[64,128]{1,0:T(8,128)S(1)} %add.24), channel_id=1, source_target_pairs={{0,4},{4,0},{8,12},{12,8},{16,20},{20,16},{24,28},{28,24},{1,5},{5... | collective-permute-start | bytes 98312 | tf_op jit(solution)/shard_map/ppermute | solution.py:315

commit v13 on v12

--- a/solution.py
+++ b/solution.py
@@ -45,26 +45,48 @@
     lax.fori_loop(0, count // step, body, 0)
 
 
+def half_copies(sources, targets, half, sems):
+    rows, width = sources[0].shape
+    lanes = pl.ds(pl.multiple_of(half * (width // 2), width // 2), width // 2)
+    copies = []
+    for n in range(2):
+        part = pl.ds(n * (rows // 2), rows // 2)
+        for source, target in zip(sources, targets):
+            copies.append(
+                pltpu.make_async_copy(source.at[part, lanes], target.at[part, lanes], sems.at[len(copies)])
+            )
+    return copies
+
+
+def sent_products(inputs, half, keep_ref, kv_out, cot_out, swapped):
+    q_ref, k_ref, v_ref, dy_ref = inputs
+    width = kv_out.shape[1]
+    lanes = pl.ds(pl.multiple_of(half * width, width), width)
+    kv = product(k_ref[:, lanes], v_ref[:, lanes])
+    cot = product(dy_ref[:, lanes], q_ref[:, lanes])
+    kv = jnp.where(keep_ref[1][:, :1] > 0, kv, jnp.zeros_like(kv))
+    cot = jnp.where(keep_ref[0][:, :1] > 0, cot, jnp.zeros_like(cot))
+    kv_out[...] = jnp.where(swapped, cot, kv)
+    cot_out[...] = jnp.where(swapped, kv, cot)
+
+
 def first_kernel(
     q_hbm, k_hbm, v_hbm, dy_hbm, starts_hbm, filters_hbm,
-    q_ref, k_ref, v_ref, dy_ref, far_ref, pair_ref, later_far_ref, later_pair_ref,
-    masks_ref, table_masks_ref, taps_ref, starts_ref, filters_ref, sems,
+    q_ref, k_ref, v_ref, dy_ref, far_ref, pair_ref, keep_ref, masks_ref, table_masks_ref, taps_ref,
+    starts_ref, filters_ref, sems,
 ):
-    rows, width = q_ref.shape
-    half = rows // 2
-    copies = [
-        pltpu.make_async_copy(starts_hbm, starts_ref, sems.at[0]),
-        pltpu.make_async_copy(filters_hbm, filters_ref, sems.at[1]),
+    rows = q_ref.shape[0]
+    core = lax.axis_index("ctx") % 2
+    small = [
+        pltpu.make_async_copy(starts_hbm, starts_ref, sems.at[8]),
+        pltpu.make_async_copy(filters_hbm, filters_ref, sems.at[9]),
     ]
-    inputs = [(k_hbm, k_ref), (v_hbm, v_ref), (dy_hbm, dy_ref), (q_hbm, q_ref)]
-    for n in range(2):
-        part = pl.ds(n * half, half)
-        for source, target in inputs:
-            copies.append(pltpu.make_async_copy(source.at[part], target.at[part], sems.at[len(copies)]))
-    for copy in copies:
+    inputs = (q_ref, k_ref, v_ref, dy_ref)
+    copies = half_copies((q_hbm, k_hbm, v_hbm, dy_hbm), inputs, 1 - core, sems)
+    for copy in small + copies:
         copy.start()
 
-    copies[0].wait()
+    small[0].wait()
     starts = jnp.broadcast_to(starts_ref[...], (rows, rows)) > 0
     t = lax.broadcasted_iota(jnp.int32, (rows, rows), 0)
     s = lax.broadcasted_iota(jnp.int32, (rows, rows), 1)
@@ -75,118 +97,118 @@
     own = as_f32((s <= t) & (s >= began))
     previous = as_f32((s > t) & (t < first))
     following = as_f32((s < t) & (t >= last))
-    for n, mask in enumerate((own, own.T, previous, following, previous.T, following.T)):
-        masks_ref[n] = mask
+    keep_ref[0] = as_f32(t < first)
+    keep_ref[1] = as_f32(t >= last)
     for n, parts in enumerate(((own, previous), (own.T, following))):
         for m, mask in enumerate(parts):
             table_masks_ref[n, :, m * rows : (m + 1) * rows] = mask.astype(jnp.bfloat16)
-    token = t[:, :1]
-    head, tail = token < first, token >= last
-    copies[1].wait()
+    flip = as_f32(s + t == rows - 1)
+    reverse = lambda mask: jnp.dot(mask, flip, preferred_element_type=jnp.float32)
+    for n, mask in enumerate((own, previous, following.T)):
+        mask = reverse(mask)
+        masks_ref[2 * n] = mask
+        masks_ref[2 * n + 1] = mask.T
+    small[1].wait()
     taps_ref[0] = reversed_taps(filters_ref[...])
     taps_ref[1] = filters_ref[...].astype(jnp.float32)
-
-    even = lax.axis_index("ctx") % 2 == 0
-    low, high = slice(0, width // 2), slice(width // 2, width)
-    for n in range(2):
-        for copy in copies[2 + 4 * n : 6 + 4 * n]:
-            copy.wait()
-        at = slice(n * half, (n + 1) * half)
-        for kv_part, cot_part, far, pair in (
-            (low, high, far_ref, pair_ref), (high, low, later_far_ref, later_pair_ref)
-        ):
-            kv = product(k_ref[at, kv_part], v_ref[at, kv_part])
-            cot = product(dy_ref[at, cot_part], q_ref[at, cot_part])
-            kv = jnp.where(tail[at], kv, jnp.zeros_like(kv))
-            cot = jnp.where(head[at], cot, jnp.zeros_like(cot))
-            far[at, :] = jnp.where(even, cot, kv)
-            pair[at, :] = jnp.where(even, kv, cot)
-
-
-def masked_diagonals(left, sides, group):
+    for copy in copies:
+        copy.wait()
+    sent_products(inputs, 1 - core, keep_ref, far_ref, pair_ref, core == 0)
+
+
+def tile_products(inputs, half, index):
+    q_ref, k_ref, v_ref, dy_ref = inputs
+    lanes = lanes_of(half, q_ref.shape[1] // 2, index)
+    return product(k_ref[:, lanes], v_ref[:, lanes]), product(dy_ref[:, lanes], q_ref[:, lanes])
+
+
+def reversed_rows(tile):
+    rows = tile.shape[0]
+    i = lax.broadcasted_iota(jnp.int32, (rows, rows), 0)
+    j = lax.broadcasted_iota(jnp.int32, (rows, rows), 1)
+    flip = jnp.where(i + j == rows - 1, 1.0, 0.0).astype(jnp.bfloat16)
+    return jnp.dot(flip, tile, preferred_element_type=jnp.float32).astype(jnp.bfloat16)
+
+
+def add_diagonals(out_ref, index, left, sides, group, scale=1.0, base_ref=None):
     rows = left.shape[0]
+    per_tile = LANES // GSIZE
     right = jnp.concatenate([side for side, _ in sides], axis=0)
-    for g in range(LANES // GSIZE):
+    for g in range(per_tile):
         picked = jnp.where(group == g, left, jnp.zeros_like(left))
         pairs = lax.dot_general(picked, right, (((1,), (1,)), ((), ())), preferred_element_type=jnp.float32)
         linked = pairs[:, :rows] * sides[0][1][...]
         for n in range(1, len(sides)):
             linked = linked + pairs[:, n * rows : (n + 1) * rows] * sides[n][1][...]
-        total = linked[:8]
-        for i in range(1, rows // 8):
-            total = total + pltpu.roll(linked[8 * i : 8 * i + 8], rows - 8 * i, 1)
-        yield g, total
-
-
-def diagonals(sums_ref, groups):
-    rows = sums_ref.shape[1]
-    total = sums_ref[pl.ds(0, groups, stride=8), :]
-    for r in range(1, 8):
-        total = total + pltpu.roll(sums_ref[pl.ds(r, groups, stride=8), :], rows - r, 1)
-    return total
+        total = jnp.sum(pltpu.roll(linked, 1, 1, stride=1, stride_axis=0), axis=0, keepdims=True)
+        at = pl.ds(index * per_tile + g, 1)
+        if base_ref is not None:
+            total = total + base_ref[at, :]
+        out_ref[at, :] = total * scale
 
 
 def lanes_of(half, width, index):
     return pl.ds(pl.multiple_of(half * width + index * LANES, LANES), LANES)
 
 
-def sums_at(index, g):
-    return pl.ds(pl.multiple_of((index * (LANES // GSIZE) + g) * 8, 8), 8)
-
-
-def filter_partner_kernel(q_ref, k_ref, v_ref, dy_ref, masks_ref, out_ref, sums_ref, *, scale):
-    width = q_ref.shape[1] // 2
-    half = 1 - lax.axis_index("ctx") % 2
+def filter_partner_kernel(
+    q_hbm, k_hbm, v_hbm, dy_hbm, q_in, k_in, v_in, dy_in, keep_ref, masks_ref,
+    q_ref, k_ref, v_ref, dy_ref, out_ref, pair_ref, far_ref, sems, *, scale
+):
+    del q_in, k_in, v_in, dy_in
+    core = lax.axis_index("ctx") % 2
+    inputs = (q_ref, k_ref, v_ref, dy_ref)
+    copies = half_copies((q_hbm, k_hbm, v_hbm, dy_hbm), inputs, core, sems)
+    for copy in copies:
+        copy.start()
     group = lane_groups()
 
     def tile(index):
-        lanes = lanes_of(half, width, index)
-        cot = product(dy_ref[:, lanes], q_ref[:, lanes])
-        kv = product(k_ref[:, lanes], v_ref[:, lanes])
-        for g, total in masked_diagonals(kv, [(cot, masks_ref.at[1])], group):
-            sums_ref[sums_at(index, g), :] = total
-
-    each_tile(tile, width)
-    out_ref[...] = diagonals(sums_ref, out_ref.shape[0]) * scale
-
-
-def filter_own_kernel(q_ref, k_ref, v_ref, dy_ref, other_ref, masks_ref, sums_ref, own_ref, cross_ref):
+        kv, cot = tile_products(inputs, 1 - core, index)
+        add_diagonals(out_ref, index, reversed_rows(kv), [(cot, masks_ref.at[1])], group, scale)
+
+    each_tile(tile, q_ref.shape[1] // 2)
+    for copy in copies:
+        copy.wait()
+    sent_products(inputs, core, keep_ref, pair_ref, far_ref, core == 1)
+
+
+def filter_own_kernel(q_ref, k_ref, v_ref, dy_ref, other_ref, masks_ref, out_ref, own_ref, cross_ref):
+    inputs = (q_ref, k_ref, v_ref, dy_ref)
     width = q_ref.shape[1] // 2
     core = lax.axis_index("ctx") % 2
     even = core == 0
     own_ref[...] = jnp.where(even, masks_ref[1], masks_ref[0])
-    cross_ref[...] = jnp.where(even, masks_ref[3], masks_ref[2])
+    cross_ref[...] = jnp.where(even, masks_ref[5], masks_ref[2])
     group = lane_groups()
 
     def tile(index):
-        lanes = lanes_of(core, width, index)
-        cot = product(dy_ref[:, lanes], q_ref[:, lanes])
-        kv = product(k_ref[:, lanes], v_ref[:, lanes])
-        sides = [(jnp.where(even, cot, kv), own_ref), (other_ref[:, lanes_of(0, width, index)], cross_ref)]
-        for g, total in masked_diagonals(jnp.where(even, kv, cot), sides, group):
-            sums_ref[sums_at(index, g), :] = total
+        kv, cot = tile_products(inputs, core, index)
+        kv = reversed_rows(kv)
+        other = other_ref[:, lanes_of(0, width, index)]
+        sides = [(jnp.where(even, cot, kv), own_ref), (jnp.where(even, other, reversed_rows(other)), cross_ref)]
+        add_diagonals(out_ref, index, jnp.where(even, kv, cot), sides, group)
 
     each_tile(tile, width)
 
 
-def filter_far_kernel(q_ref, k_ref, v_ref, dy_ref, other_ref, masks_ref, sums_ref, out_ref, total_ref, cross_ref, *, scale):
+def filter_far_kernel(q_ref, k_ref, v_ref, dy_ref, other_ref, masks_ref, base_ref, out_ref, cross_ref, *, scale):
+    inputs = (q_ref, k_ref, v_ref, dy_ref)
     width = q_ref.shape[1] // 2
     core = lax.axis_index("ctx") % 2
     even = core == 0
-    cross_ref[...] = jnp.where(even, masks_ref[4], masks_ref[5])
+    cross_ref[...] = jnp.where(even, masks_ref[3], masks_ref[4])
     group = lane_groups()
 
     def tile(index):
-        lanes = lanes_of(core, width, index)
-        cot = product(dy_ref[:, lanes], q_ref[:, lanes])
-        kv = product(k_ref[:, lanes], v_ref[:, lanes])
-        left = other_ref[:, lanes_of(0, width, index)]
-        for g, total in masked_diagonals(left, [(jnp.where(even, cot, kv), cross_ref)], group):
-            total_ref[sums_at(index, g), :] = sums_ref[sums_at(index, g), :] + total
+        kv, cot = tile_products(inputs, core, index)
+        other = other_ref[:, lanes_of(0, width, index)]
+        turned = reversed_rows(jnp.where(even, other, kv))
+        left = jnp.where(even, turned, other)
+        right = jnp.where(even, cot, turned)
+        add_diagonals(out_ref, index, left, [(right, cross_ref)], group, scale, base_ref)
 
     each_tile(tile, width)
-    total = diagonals(total_ref, out_ref.shape[0])
-    out_ref[...] = jnp.where(even, total, reversed_taps(total)) * scale
 
 
 def conv_kernel(
@@ -262,31 +284,42 @@
     )(*operands)
 
 
+def in_hbm(*arrays):
+    return [pltpu.with_memory_space_constraint(x, pltpu.HBM) for x in arrays]
+
+
+def own_call(kernel, name, out_shape, scratch_shapes, hbm_operands, operands, aliases={}):
+    return pl.pallas_call(
+        kernel,
+        out_shape=out_shape,
+        in_specs=[pl.BlockSpec(memory_space=pltpu.HBM)] * len(hbm_operands) + [VMEM] * len(operands),
+        out_specs=[VMEM] * len(out_shape) if isinstance(out_shape, list) else VMEM,
+        scratch_shapes=scratch_shapes,
+        input_output_aliases=aliases,
+        cost_estimate=pl.CostEstimate(flops=0, bytes_accessed=0, transcendentals=0),
+        compiler_params=pltpu.CompilerParams(vmem_limit_bytes=24 << 20),
+        name=name,
+    )(*in_hbm(*hbm_operands), *operands)
+
+
 def first(q, k, v, dy, starts, filters):
     rows, width = q.shape
     wide = pltpu.VMEM((rows, width), jnp.bfloat16)
     sent = pltpu.VMEM((rows, width // 2), jnp.bfloat16)
-    operands = [pltpu.with_memory_space_constraint(x, pltpu.HBM) for x in (q, k, v, dy, starts, filters)]
-    return pl.pallas_call(
-        first_kernel,
-        out_shape=[wide] * 4 + [sent] * 4 + [
+    return own_call(
+        first_kernel, "first",
+        [wide] * 4 + [sent] * 2 + [
+            pltpu.VMEM((2, rows, rows), jnp.float32),
             pltpu.VMEM((6, rows, rows), jnp.float32),
             pltpu.VMEM((2, rows, 2 * rows), jnp.bfloat16),
             pltpu.VMEM((2, *filters.shape), jnp.float32),
         ],
-        in_specs=[pl.BlockSpec(memory_space=pltpu.HBM)] * 6,
-        out_specs=[VMEM] * 11,
-        scratch_shapes=[
+        [
             pltpu.VMEM(starts.shape, starts.dtype), pltpu.VMEM(filters.shape, filters.dtype),
             pltpu.SemaphoreType.DMA((10,)),
         ],
-        compiler_params=pltpu.CompilerParams(vmem_limit_bytes=24 << 20),
-        name="first",
-    )(*operands)
-
-
-def filter_call(kernel, name, out_shape, scratch_shapes, *operands):
-    return local_call(kernel, name, out_shape, scratch_shapes, 0, operands, moved=0)
+        (q, k, v, dy, starts, filters), (),
+    )
 
 
 def convolution(a, b, pair, far, c, d, masks, taps, outs, backward, half):
@@ -359,26 +392,28 @@
     groups, taps = filters.shape
     assert rows == taps == LANES and lax.axis_size("ctx") % 2 == 0
     scale = 1.0 / math.sqrt(rows * lax.axis_size("ctx") * lax.axis_size("dp") * GSIZE)
-    q, k, v, dy, far_out, pair_out, later_far_out, later_pair_out, masks, table_masks, tap_rows = first(
-        q, k, v, dy, contig_starts, filters
-    )
+    inputs = q, k, v, dy
+    *partly, far_out, pair_out, keep, masks, table_masks, tap_rows = first(*inputs, contig_starts, filters)
     square = pltpu.VMEM((rows, rows), jnp.float32)
-    part = jax.ShapeDtypeStruct((groups // 2, rows), jnp.float32)
-    unsummed = jax.ShapeDtypeStruct((groups * 4, rows), jnp.float32)
-    sums = pltpu.VMEM(unsummed.shape, unsummed.dtype)
+    part = pltpu.VMEM((groups // 2, rows), jnp.float32)
+    wide = pltpu.VMEM(q.shape, q.dtype)
+    sent = pltpu.VMEM((rows, q.shape[1] // 2), q.dtype)
     far = next_chip(far_out)
-    theirs = filter_call(
-        functools.partial(filter_partner_kernel, scale=scale), "filter_partner", part, [sums], q, k, v, dy, masks
-    )
-    later_pair = other_core(later_pair_out)
-    pair = other_core(after(pair_out, theirs))
-    later_far = next_chip(after(later_far_out, theirs))
-    mine = filter_call(
-        filter_own_kernel, "filter_own", unsummed, [square, square], q, k, v, dy, later_pair, masks
-    )
-    mine = filter_call(
-        functools.partial(filter_far_kernel, scale=scale), "filter_far", part, [sums, square],
-        q, k, v, dy, far, masks, mine,
+    later_pair = other_core(pair_out)
+    q, k, v, dy, theirs, pair_out, far_out = own_call(
+        functools.partial(filter_partner_kernel, scale=scale), "filter_partner",
+        [wide] * 4 + [part, sent, sent], [pltpu.SemaphoreType.DMA((8,))],
+        inputs, (*partly, keep, masks), {4: 0, 5: 1, 6: 2, 7: 3},
+    )
+    pair = other_core(pair_out)
+    mine = own_call(
+        filter_own_kernel, "filter_own", part, [square, square],
+        (), (q, k, v, dy, later_pair, masks),
+    )
+    later_far = next_chip(after(far_out, mine))
+    mine = own_call(
+        functools.partial(filter_far_kernel, scale=scale), "filter_far", part, [square],
+        (), (q, k, v, dy, far, masks, mine),
     )
     mine = mine + other_core(theirs)
 

time: 36 us -> 39 us (1.083)
  Pallas kernels: 16.9 us -> 19.9 us
  starting transfers between devices: 16 us -> 15.5 us
  waiting for transfers between devices: 1.41 us -> 1.88 us
    pallas_call x1 -> x4, Pallas kernels: 1.69 us -> 10.6 us  [own_call(): pl.pallas_call(kernel, out_shape=out_shape, in_specs=[pl.BlockSpec(memory...]
    pallas_call x7 -> x4, Pallas kernels: 15.2 us -> 9.36 us  [local_call(): pl.pallas_call(kernel, out_shape=out_shape, in_specs=in_specs or [VMEM] *...]
    ppermute x4, starting transfers between devices: 7.34 us -> 6.84 us  [summed_over(): lax.ppermute(total, axis, [(turned(i, k), i) for i in range(size)])]
    ppermute x4, waiting for transfers between devices: 0.21 us -> 0.68 us  [summed_over(): lax.ppermute(total, axis, [(turned(i, k), i) for i in range(size)])]
  transfers between devices with their start and end apart: 10 -> 10, of which waited for: 2 -> 3; matrix products, arithmetic and copies ran while one was open for 0% -> 0% of each run, Pallas kernels for 43% -> 47%
where the time goes in v13:
time: 39 us; the launch traced here: 38.8 us
  Pallas kernels  19.9 us (51%)
  starting transfers between devices  15.5 us (40%)
  waiting for transfers between devices  1.88 us (5%)
  between operations  0.79 us (2%)
  other arithmetic  0.67 us (2%)
    pallas_call x4, Pallas kernels, own_call(): pl.pallas_call(kernel, out_shape=out_shape, in_specs=[pl.BlockSpec(memory...  10.6 us
    pallas_call x4, Pallas kernels, local_call(): pl.pallas_call(kernel, out_shape=out_shape, in_specs=in_specs or [VMEM] *...  9.36 us
    ppermute x4, starting transfers between devices, other_core(): lax.ppermute(block, 'ctx', [(i, i ^ 1) for i in range(lax.axis_size('ctx'...  7.35 us
    ppermute x4, starting transfers between devices, summed_over(): lax.ppermute(total, axis, [(turned(i, k), i) for i in range(size)])  6.84 us
    ppermute x2, starting transfers between devices, next_chip(): return lax.ppermute(block, 'ctx', pairs + [(j, i) for i, j in pairs])  1.34 us
    ppermute x4, waiting for transfers between devices, other_core(): lax.ppermute(block, 'ctx', [(i, i ^ 1) for i in range(lax.axis_size('ctx'...  1.19 us
  transfers between devices with their start and end apart: 10, of which 3 were waited for; matrix products, arithmetic and copies ran while one was open for 0% of the time, Pallas kernels for 47%

profile of v13, /device:TPU:0, one launch (start us, length us, event | category | flops | bytes accessed | tf_op | source)
XLA Modules:
  0.0 38.8 jit_solution(9408375095059211266)
XLA Ops:
  0.6 1.6 %first.1 = (bf16[128,2048]{1,0:T(8,128)(2,1)S(1)}, bf16[128,2048]{1,0:T(8,128)(2,1)S(1)}, bf16[128,2048]{1,0:T(8,128)(2,1)S(1)}, bf16[128,2048]{1,0:T(8,128)(2,1...) custom-call(bf16[128,2048]{1,0:T(8,128)(2,1)} %bitcast.8, ...), custom_call_target="tpu_custom_call" | custom-call | tf_op jit(solution)/shard_map/first/pallas_call | solution.py:292
  2.2 0.5 %collective-permute-start = (bf16[128,1024]{1,0:T(8,128)(2,1)S(1)}, bf16[128,1024]{1,0:T(8,128)(2,1)S(1)}, u32[]{:S(2)}, u32[]{:S(2)}) collective-permute-start(bf16[128,1024]{1,0:T(8,128)(2,1)S(1)} %get-tuple-element.43), channel_id=1, source_target_pairs={{0,4},{4,0},{8,12},{12,8},{16,20},{20,16},{24,28},{28,24},{1,5},{5... | collective-permute-start | bytes 786440 | tf_op jit(solution)/shard_map/ppermute | solution.py:348
  2.7 0.7 %collective-permute-start.3 = (bf16[128,1024]{1,0:T(8,128)(2,1)S(1)}, bf16[128,1024]{1,0:T(8,128)(2,1)S(1)}, u32[]{:S(2)}, u32[]{:S(2)}) collective-permute-start(bf16[128,1024]{1,0:T(8,128)(2,1)S(1)} %get-tuple-element.51), channel_id=1, source_target_pairs={{4,8},{12,16},{20,24},{8,4},{16,12},{24,20},{5,9},{13,17},{21,25},... | collective-permute-start | bytes 786440 | tf_op jit(solution)/shard_map/ppermute | solution.py:354
  3.4 3.0 %filter_partner.1 = (bf16[128,2048]{1,0:T(8,128)(2,1)S(1)}, bf16[128,2048]{1,0:T(8,128)(2,1)S(1)}, bf16[128,2048]{1,0:T(8,128)(2,1)S(1)}, bf16[128,2048]{1,0:T(8...) custom-call(bf16[128,2048]{1,0:T(8,128)(2,1)} %bitcast.9, ...), custom_call_target="tpu_custom_call", output_to_operand_aliasing={{0}: (4, {}), {1}: (5, {}), {2}: (6, {}), {3}: (7, {})} | custom-call | tf_op jit(solution)/shard_map/filter_partner/pallas_call | solution.py:292
  6.4 3.9 %collective-permute-start.2 = (bf16[128,1024]{1,0:T(8,128)(2,1)S(1)}, bf16[128,1024]{1,0:T(8,128)(2,1)S(1)}, u32[]{:S(2)}, u32[]{:S(2)}) collective-permute-start(bf16[128,1024]{1,0:T(8,128)(2,1)S(1)} %get-tuple-element.50), channel_id=1, source_target_pairs={{0,4},{4,0},{8,12},{12,8},{16,20},{20,16},{24,28},{28,24},{1,5},{5... | collective-permute-start | bytes 786440 | tf_op jit(solution)/shard_map/ppermute | solution.py:348
  10.3 0.0 collective-permute-done.other_ref.pair_ref
  10.3 3.0 %filter_own.1.base_ref = f32[64,128]{1,0:T(8,128)S(1)} custom-call(bf16[128,2048]{1,0:T(8,128)(2,1)S(1)} %get-tuple-element.45.q_ref.refs_4_.c_ref.refs_1_.b_ref, bf16[128,2048]{1,0:T(8,128)(2,1)S(1)} %get-tuple-element.41.k_ref.refs_0_.a_ref.refs_5_.d_ref, bf16[128,2048]{1,0:T(8,128)(2,1)S(1)} %get-tuple-element.42.v_ref.refs_1_.b_ref.refs_4_.c_ref, ...), custom_call_target="tpu_custom_call" | custom-call | tf_op jit(solution)/shard_map/filter_own/pallas_call | solution.py:292
  13.3 0.7 %collective-permute-start.1 = (bf16[128,1024]{1,0:T(8,128)(2,1)S(1)}, bf16[128,1024]{1,0:T(8,128)(2,1)S(1)}, u32[]{:S(2)}, u32[]{:S(2)}) collective-permute-start(bf16[128,1024]{1,0:T(8,128)(2,1)S(1)} %get-tuple-element.47), channel_id=1, source_target_pairs={{4,8},{12,16},{20,24},{8,4},{16,12},{24,20},{5,9},{13,17},{21,25},... | collective-permute-start | bytes 786440 | tf_op jit(solution)/shard_map/ppermute | solution.py:354
  14.0 2.9 %collective-permute-start.4 = (f32[64,128]{1,0:T(8,128)S(1)}, f32[64,128]{1,0:T(8,128)S(1)}, u32[]{:S(2)}, u32[]{:S(2)}) collective-permute-start(f32[64,128]{1,0:T(8,128)S(1)} %get-tuple-element.60), channel_id=1, source_target_pairs={{0,4},{4,0},{8,12},{12,8},{16,20},{20,16},{24,28},{28,24},{1,5},{5... | collective-permute-start | bytes 98312 | tf_op jit(solution)/shard_map/ppermute | solution.py:348
  16.9 0.0 collective-permute-done.3.refs_3_.other_ref
  16.9 3.0 %filter_far.1 = f32[64,128]{1,0:T(8,128)S(1)} custom-call(bf16[128,2048]{1,0:T(8,128)(2,1)S(1)} %get-tuple-element.45.q_ref.refs_4_.c_ref.refs_1_.b_ref, bf16[128,2048]{1,0:T(8,128)(2,1)S(1)} %get-tuple-element.41.k_ref.refs_0_.a_ref.refs_5_.d_ref, bf16[128,2048]{1,0:T(8,128)(2,1)S(1)} %get-tuple-element.42.v_ref.refs_1_.b_ref.refs_4_.c_ref, ...), custom_call_target="tpu_custom_call" | custom-call | tf_op jit(solution)/shard_map/filter_far/pallas_call | solution.py:292
  20.0 0.0 collective-permute-done.4
  20.0 1.6 %collective-permute-start.5 = (f32[64,128]{1,0:T(8,128)S(1)}, f32[64,128]{1,0:T(8,128)S(1)}, u32[]{:S(2)}, u32[]{:S(2)}) collective-permute-start(f32[64,128]{1,0:T(8,128)S(1)} %add.20), channel_id=1, source_target_pairs={{1,0},{0,1},{3,2},{2,3},{5,4},{4,5},{7,6},{6,7},{9,8},{8,9},{11,10... | collective-permute-start | bytes 98312 | tf_op jit(solution)/shard_map/ppermute | solution.py:378
  21.6 0.0 collective-permute-done.2.refs_2_
  21.6 2.3 %forward_low.1 = (bf16[128,2048]{1,0:T(8,128)(2,1)}, bf16[128,2048]{1,0:T(8,128)(2,1)}) custom-call(bf16[128,2048]{1,0:T(8,128)(2,1)S(1)} %get-tuple-element.41.k_ref.refs_0_.a_ref.refs_5_.d_ref, bf16[128,2048]{1,0:T(8,128)(2,1)S(1)} %get-tuple-element.42.v_ref.refs_1_.b_ref.refs_4_.c_ref, bf16[128,1024]{1,0:T(8,128)(2,1)S(1)} %collective-permute-done.2.refs_2_, ...), custom_call_target="tpu_custom_call" | custom-call | flops 536870912 | bytes 3932160 | tf_op jit(solution)/shard_map/forward_low/pallas_call | solution.py:274
  24.0 0.0 collective-permute-done.5
  24.0 2.7 %collective-permute-start.6 = (f32[64,128]{1,0:T(8,128)S(1)}, f32[64,128]{1,0:T(8,128)S(1)}, u32[]{:S(2)}, u32[]{:S(2)}) collective-permute-start(f32[64,128]{1,0:T(8,128)S(1)} %add.21), channel_id=1, source_target_pairs={{2,0},{3,1},{0,2},{1,3},{6,4},{7,5},{4,6},{5,7},{10,8},{11,9},{8,1... | collective-permute-start | bytes 98312 | tf_op jit(solution)/shard_map/ppermute | solution.py:378
  26.6 2.3 %backward_high.1 = (bf16[128,2048]{1,0:T(8,128)(2,1)}, bf16[128,2048]{1,0:T(8,128)(2,1)}) custom-call(bf16[128,2048]{1,0:T(8,128)(2,1)S(1)} %get-tuple-element.46.dy_ref.refs_5_.d_ref.refs_0_.a_ref, bf16[128,2048]{1,0:T(8,128)(2,1)S(1)} %get-tuple-element.45.q_ref.refs_4_.c_ref.refs_1_.b_ref, bf16[128,1024]{1,0:T(8,128)(2,1)S(1)} %collective-permute-done.2.refs_2_, ...), custom_call_target="tpu_custom_call" | custom-call | flops 536870912 | bytes 3932160 | tf_op jit(solution)/shard_map/backward_high/pallas_call | solution.py:274
  29.0 0.0 collective-permute-done.6
  29.0 0.0 collective-permute-done.1.far_ref
  29.0 1.6 %collective-permute-start.7 = (f32[64,128]{1,0:T(8,128)S(1)}, f32[64,128]{1,0:T(8,128)S(1)}, u32[]{:S(2)}, u32[]{:S(2)}) collective-permute-start(f32[64,128]{1,0:T(8,128)S(1)} %add.22), channel_id=1, source_target_pairs={{8,0},{12,4},{0,8},{4,12},{24,16},{28,20},{16,24},{20,28},{9,1},{1... | collective-permute-start | bytes 98312 | tf_op jit(solution)/shard_map/ppermute | solution.py:378
  30.6 2.3 %forward_high.1 = (bf16[128,2048]{1,0:T(8,128)(2,1)}, bf16[128,2048]{1,0:T(8,128)(2,1)}) custom-call(bf16[128,2048]{1,0:T(8,128)(2,1)S(1)} %get-tuple-element.41.k_ref.refs_0_.a_ref.refs_5_.d_ref, bf16[128,2048]{1,0:T(8,128)(2,1)S(1)} %get-tuple-element.42.v_ref.refs_1_.b_ref.refs_4_.c_ref, ...), custom_call_target="tpu_custom_call", output_to_operand_aliasing={{0}: (8, {}), {1}: (9, {})} | custom-call | flops 536870912 | bytes 4980736 | tf_op jit(solution)/shard_map/forward_high/pallas_call | solution.py:274
  32.9 0.1 collective-permute-done.7
  33.0 1.0 %collective-permute-start.8 = (f32[64,128]{1,0:T(8,128)S(1)}, f32[64,128]{1,0:T(8,128)S(1)}, u32[]{:S(2)}, u32[]{:S(2)}) collective-permute-start(f32[64,128]{1,0:T(8,128)S(1)} %add.23), channel_id=1, source_target_pairs={{16,0},{20,4},{24,8},{28,12},{0,16},{4,20},{8,24},{12,28},{17,1},{... | collective-permute-start | bytes 98312 | tf_op jit(solution)/shard_map/ppermute | solution.py:378
  34.0 2.3 %backward_low.1 = (bf16[128,2048]{1,0:T(8,128)(2,1)}, bf16[128,2048]{1,0:T(8,128)(2,1)}) custom-call(bf16[128,2048]{1,0:T(8,128)(2,1)S(1)} %get-tuple-element.46.dy_ref.refs_5_.d_ref.refs_0_.a_ref, bf16[128,2048]{1,0:T(8,128)(2,1)S(1)} %get-tuple-element.45.q_ref.refs_4_.c_ref.refs_1_.b_ref, ...), custom_call_target="tpu_custom_call", output_to_operand_aliasing={{0}: (8, {}), {1}: (9, {})} | custom-call | flops 536870912 | bytes 4980736 | tf_op jit(solution)/shard_map/backward_low/pallas_call | solution.py:274
  36.4 0.6 %collective-permute-done.8 = f32[64,128]{1,0:T(8,128)S(1)} collective-permute-done((f32[64,128]{1,0:T(8,128)S(1)}, f32[64,128]{1,0:T(8,128)S(1)}, u32[]{:S(2)}, u32[]{:S(2)}) %collective-permute-start.8) | collective-permute-done | bytes 32800 | tf_op jit(solution)/shard_map/ppermute | solution.py:378
  37.0 0.0 collective-permute-start.9
  37.0 1.2 %collective-permute-done.9 = f32[64,128]{1,0:T(8,128)S(1)} collective-permute-done((f32[64,128]{1,0:T(8,128)S(1)}, f32[64,128]{1,0:T(8,128)S(1)}, u32[]{:S(2)}, u32[]{:S(2)}) %collective-permute-start.9) | collective-permute-done | bytes 32800 | tf_op jit(solution)/shard_map/ppermute | solution.py:348
  38.2 0.6 %maximum_select_fusion = f32[128,128]{1,0:T(8,128)} fusion(f32[64,128]{1,0:T(8,128)S(1)} %collective-permute-done.9, f32[64,128]{1,0:T(8,128)S(1)} %add.24, pred[]{:T(512)S(6)} %eq.5), kind=kLoop, calls=%fused_computation | loop fusion | flops 49152 | bytes 131073 | tf_op jit(solution)/shard_map/jit(_where)/select_n | solution.py:441
  (5 shorter events, 0.0 us)
Async XLA Ops:
  2.2 8.1 %collective-permute-start = (bf16[128,1024]{1,0:T(8,128)(2,1)S(1)}, bf16[128,1024]{1,0:T(8,128)(2,1)S(1)}, u32[]{:S(2)}, u32[]{:S(2)}) collective-permute-start(bf16[128,1024]{1,0:T(8,128)(2,1)S(1)} %get-tuple-element.43), channel_id=1, source_target_pairs={{0,4},{4,0},{8,12},{12,8},{16,20},{20,16},{24,28},{28,24},{1,5},{5... | collective-permute-start | bytes 786440 | tf_op jit(solution)/shard_map/ppermute | solution.py:348
  2.7 14.2 %collective-permute-start.3 = (bf16[128,1024]{1,0:T(8,128)(2,1)S(1)}, bf16[128,1024]{1,0:T(8,128)(2,1)S(1)}, u32[]{:S(2)}, u32[]{:S(2)}) collective-permute-start(bf16[128,1024]{1,0:T(8,128)(2,1)S(1)} %get-tuple-element.51), channel_id=1, source_target_pairs={{4,8},{12,16},{20,24},{8,4},{16,12},{24,20},{5,9},{13,17},{21,25},... | collective-permute-start | bytes 786440 | tf_op jit(solution)/shard_map/ppermute | solution.py:354
  6.4 15.2 %collective-permute-start.2 = (bf16[128,1024]{1,0:T(8,128)(2,1)S(1)}, bf16[128,1024]{1,0:T(8,128)(2,1)S(1)}, u32[]{:S(2)}, u32[]{:S(2)}) collective-permute-start(bf16[128,1024]{1,0:T(8,128)(2,1)S(1)} %get-tuple-element.50), channel_id=1, source_target_pairs={{0,4},{4,0},{8,12},{12,8},{16,20},{20,16},{24,28},{28,24},{1,5},{5... | collective-permute-start | bytes 786440 | tf_op jit(solution)/shard_map/ppermute | solution.py:348
  13.3 15.7 %collective-permute-start.1 = (bf16[128,1024]{1,0:T(8,128)(2,1)S(1)}, bf16[128,1024]{1,0:T(8,128)(2,1)S(1)}, u32[]{:S(2)}, u32[]{:S(2)}) collective-permute-start(bf16[128,1024]{1,0:T(8,128)(2,1)S(1)} %get-tuple-element.47), channel_id=1, source_target_pairs={{4,8},{12,16},{20,24},{8,4},{16,12},{24,20},{5,9},{13,17},{21,25},... | collective-permute-start | bytes 786440 | tf_op jit(solution)/shard_map/ppermute | solution.py:354
  14.0 5.9 %collective-permute-start.4 = (f32[64,128]{1,0:T(8,128)S(1)}, f32[64,128]{1,0:T(8,128)S(1)}, u32[]{:S(2)}, u32[]{:S(2)}) collective-permute-start(f32[64,128]{1,0:T(8,128)S(1)} %get-tuple-element.60), channel_id=1, source_target_pairs={{0,4},{4,0},{8,12},{12,8},{16,20},{20,16},{24,28},{28,24},{1,5},{5... | collective-permute-start | bytes 98312 | tf_op jit(solution)/shard_map/ppermute | solution.py:348
  20.0 4.0 %collective-permute-start.5 = (f32[64,128]{1,0:T(8,128)S(1)}, f32[64,128]{1,0:T(8,128)S(1)}, u32[]{:S(2)}, u32[]{:S(2)}) collective-permute-start(f32[64,128]{1,0:T(8,128)S(1)} %add.20), channel_id=1, source_target_pairs={{1,0},{0,1},{3,2},{2,3},{5,4},{4,5},{7,6},{6,7},{9,8},{8,9},{11,10... | collective-permute-start | bytes 98312 | tf_op jit(solution)/shard_map/ppermute | solution.py:378
  24.0 5.0 %collective-permute-start.6 = (f32[64,128]{1,0:T(8,128)S(1)}, f32[64,128]{1,0:T(8,128)S(1)}, u32[]{:S(2)}, u32[]{:S(2)}) collective-permute-start(f32[64,128]{1,0:T(8,128)S(1)} %add.21), channel_id=1, source_target_pairs={{2,0},{3,1},{0,2},{1,3},{6,4},{7,5},{4,6},{5,7},{10,8},{11,9},{8,1... | collective-permute-start | bytes 98312 | tf_op jit(solution)/shard_map/ppermute | solution.py:378
  29.0 4.0 %collective-permute-start.7 = (f32[64,128]{1,0:T(8,128)S(1)}, f32[64,128]{1,0:T(8,128)S(1)}, u32[]{:S(2)}, u32[]{:S(2)}) collective-permute-start(f32[64,128]{1,0:T(8,128)S(1)} %add.22), channel_id=1, source_target_pairs={{8,0},{12,4},{0,8},{4,12},{24,16},{28,20},{16,24},{20,28},{9,1},{1... | collective-permute-start | bytes 98312 | tf_op jit(solution)/shard_map/ppermute | solution.py:378
  33.0 3.9 %collective-permute-start.8 = (f32[64,128]{1,0:T(8,128)S(1)}, f32[64,128]{1,0:T(8,128)S(1)}, u32[]{:S(2)}, u32[]{:S(2)}) collective-permute-start(f32[64,128]{1,0:T(8,128)S(1)} %add.23), channel_id=1, source_target_pairs={{16,0},{20,4},{24,8},{28,12},{0,16},{4,20},{8,24},{12,28},{17,1},{... | collective-permute-start | bytes 98312 | tf_op jit(solution)/shard_map/ppermute | solution.py:378
  37.0 1.2 %collective-permute-start.9 = (f32[64,128]{1,0:T(8,128)S(1)}, f32[64,128]{1,0:T(8,128)S(1)}, u32[]{:S(2)}, u32[]{:S(2)}) collective-permute-start(f32[64,128]{1,0:T(8,128)S(1)} %add.24), channel_id=1, source_target_pairs={{0,4},{4,0},{8,12},{12,8},{16,20},{20,16},{24,28},{28,24},{1,5},{5... | collective-permute-start | bytes 98312 | tf_op jit(solution)/shard_map/ppermute | solution.py:348

commit v14 on v13

--- a/solution.py
+++ b/solution.py
@@ -102,12 +102,8 @@
     for n, parts in enumerate(((own, previous), (own.T, following))):
         for m, mask in enumerate(parts):
             table_masks_ref[n, :, m * rows : (m + 1) * rows] = mask.astype(jnp.bfloat16)
-    flip = as_f32(s + t == rows - 1)
-    reverse = lambda mask: jnp.dot(mask, flip, preferred_element_type=jnp.float32)
-    for n, mask in enumerate((own, previous, following.T)):
-        mask = reverse(mask)
-        masks_ref[2 * n] = mask
-        masks_ref[2 * n + 1] = mask.T
+    for n, mask in enumerate((own, own.T, previous, following, previous.T, following.T)):
+        masks_ref[n] = mask
     small[1].wait()
     taps_ref[0] = reversed_taps(filters_ref[...])
     taps_ref[1] = filters_ref[...].astype(jnp.float32)
@@ -122,29 +118,45 @@
     return product(k_ref[:, lanes], v_ref[:, lanes]), product(dy_ref[:, lanes], q_ref[:, lanes])
 
 
-def reversed_rows(tile):
-    rows = tile.shape[0]
-    i = lax.broadcasted_iota(jnp.int32, (rows, rows), 0)
-    j = lax.broadcasted_iota(jnp.int32, (rows, rows), 1)
-    flip = jnp.where(i + j == rows - 1, 1.0, 0.0).astype(jnp.bfloat16)
-    return jnp.dot(flip, tile, preferred_element_type=jnp.float32).astype(jnp.bfloat16)
-
-
-def add_diagonals(out_ref, index, left, sides, group, scale=1.0, base_ref=None):
-    rows = left.shape[0]
-    per_tile = LANES // GSIZE
-    right = jnp.concatenate([side for side, _ in sides], axis=0)
-    for g in range(per_tile):
-        picked = jnp.where(group == g, left, jnp.zeros_like(left))
-        pairs = lax.dot_general(picked, right, (((1,), (1,)), ((), ())), preferred_element_type=jnp.float32)
-        linked = pairs[:, :rows] * sides[0][1][...]
-        for n in range(1, len(sides)):
-            linked = linked + pairs[:, n * rows : (n + 1) * rows] * sides[n][1][...]
-        total = jnp.sum(pltpu.roll(linked, 1, 1, stride=1, stride_axis=0), axis=0, keepdims=True)
-        at = pl.ds(index * per_tile + g, 1)
-        if base_ref is not None:
-            total = total + base_ref[at, :]
-        out_ref[at, :] = total * scale
+def wrapped(linked):
+    rows = linked.shape[0]
+    total = linked[:8]
+    for i in range(1, rows // 8):
+        total = total + pltpu.roll(linked[8 * i : 8 * i + 8], rows - 8 * i, 1)
+    return total
+
+
+def products(left, right):
+    return lax.dot_general(left, right, (((1,), (1,)), ((), ())), preferred_element_type=jnp.float32)
+
+
+def picked(group, g, *tiles):
+    return jnp.concatenate([jnp.where(group == g, tile, jnp.zeros_like(tile)) for tile in tiles], axis=1)
+
+
+def diagonals(sums_ref, groups):
+    rows = sums_ref.shape[1]
+    total = sums_ref[pl.ds(0, groups, stride=8), :]
+    for r in range(1, 8):
+        total = total + pltpu.roll(sums_ref[pl.ds(r, groups, stride=8), :], rows - r, 1)
+    return total
+
+
+def sums_at(index, g):
+    return pl.ds(pl.multiple_of((index * (LANES // GSIZE) + g) * 8, 8), 8)
+
+
+def two_tiles(index, sides, mask_ref, store, group):
+    rows = mask_ref.shape[0]
+    (left_a, right_a), (left_b, right_b) = sides(index), sides(index + 1)
+    zeros = jnp.zeros_like(right_a)
+    right = jnp.concatenate(
+        [jnp.concatenate([right_a, zeros], axis=1), jnp.concatenate([zeros, right_b], axis=1)], axis=0
+    )
+    for g in range(LANES // GSIZE):
+        pairs = products(picked(group, g, left_a, left_b), right)
+        for n in range(2):
+            store(sums_at(index + n, g), wrapped(pairs[:, n * rows : (n + 1) * rows] * mask_ref[...]))
 
 
 def lanes_of(half, width, index):
@@ -153,7 +165,7 @@
 
 def filter_partner_kernel(
     q_hbm, k_hbm, v_hbm, dy_hbm, q_in, k_in, v_in, dy_in, keep_ref, masks_ref,
-    q_ref, k_ref, v_ref, dy_ref, out_ref, pair_ref, far_ref, sems, *, scale
+    q_ref, k_ref, v_ref, dy_ref, out_ref, pair_ref, far_ref, sums_ref, sems, *, scale
 ):
     del q_in, k_in, v_in, dy_in
     core = lax.axis_index("ctx") % 2
@@ -163,52 +175,58 @@
         copy.start()
     group = lane_groups()
 
-    def tile(index):
-        kv, cot = tile_products(inputs, 1 - core, index)
-        add_diagonals(out_ref, index, reversed_rows(kv), [(cot, masks_ref.at[1])], group, scale)
-
-    each_tile(tile, q_ref.shape[1] // 2)
+    def store(at, total):
+        sums_ref[at, :] = total
+
+    def tiles(index):
+        two_tiles(2 * index, lambda i: tile_products(inputs, 1 - core, i), masks_ref.at[1], store, group)
+
+    each_tile(tiles, q_ref.shape[1] // 4)
+    out_ref[...] = diagonals(sums_ref, out_ref.shape[0]) * scale
     for copy in copies:
         copy.wait()
     sent_products(inputs, core, keep_ref, pair_ref, far_ref, core == 1)
 
 
-def filter_own_kernel(q_ref, k_ref, v_ref, dy_ref, other_ref, masks_ref, out_ref, own_ref, cross_ref):
+def filter_own_kernel(q_ref, k_ref, v_ref, dy_ref, other_ref, masks_ref, sums_ref, own_ref, cross_ref):
+    inputs = (q_ref, k_ref, v_ref, dy_ref)
+    rows, width = q_ref.shape[0], q_ref.shape[1] // 2
+    core = lax.axis_index("ctx") % 2
+    even = core == 0
+    own_ref[...] = jnp.where(even, masks_ref[1], masks_ref[0])
+    cross_ref[...] = jnp.where(even, masks_ref[3], masks_ref[2])
+    group = lane_groups()
+
+    def tile(index):
+        kv, cot = tile_products(inputs, core, index)
+        left = jnp.where(even, kv, cot)
+        right = jnp.concatenate([jnp.where(even, cot, kv), other_ref[:, lanes_of(0, width, index)]], axis=0)
+        for g in range(LANES // GSIZE):
+            pairs = products(picked(group, g, left), right)
+            linked = pairs[:, :rows] * own_ref[...] + pairs[:, rows:] * cross_ref[...]
+            sums_ref[sums_at(index, g), :] = wrapped(linked)
+
+    each_tile(tile, width)
+
+
+def filter_far_kernel(q_ref, k_ref, v_ref, dy_ref, other_ref, masks_ref, base_ref, out_ref, total_ref, cross_ref, *, scale):
     inputs = (q_ref, k_ref, v_ref, dy_ref)
     width = q_ref.shape[1] // 2
     core = lax.axis_index("ctx") % 2
     even = core == 0
-    own_ref[...] = jnp.where(even, masks_ref[1], masks_ref[0])
-    cross_ref[...] = jnp.where(even, masks_ref[5], masks_ref[2])
+    cross_ref[...] = jnp.where(even, masks_ref[4], masks_ref[5])
     group = lane_groups()
 
-    def tile(index):
+    def sides(index):
         kv, cot = tile_products(inputs, core, index)
-        kv = reversed_rows(kv)
-        other = other_ref[:, lanes_of(0, width, index)]
-        sides = [(jnp.where(even, cot, kv), own_ref), (jnp.where(even, other, reversed_rows(other)), cross_ref)]
-        add_diagonals(out_ref, index, jnp.where(even, kv, cot), sides, group)
-
-    each_tile(tile, width)
-
-
-def filter_far_kernel(q_ref, k_ref, v_ref, dy_ref, other_ref, masks_ref, base_ref, out_ref, cross_ref, *, scale):
-    inputs = (q_ref, k_ref, v_ref, dy_ref)
-    width = q_ref.shape[1] // 2
-    core = lax.axis_index("ctx") % 2
-    even = core == 0
-    cross_ref[...] = jnp.where(even, masks_ref[3], masks_ref[4])
-    group = lane_groups()
-
-    def tile(index):
-        kv, cot = tile_products(inputs, core, index)
-        other = other_ref[:, lanes_of(0, width, index)]
-        turned = reversed_rows(jnp.where(even, other, kv))
-        left = jnp.where(even, turned, other)
-        right = jnp.where(even, cot, turned)
-        add_diagonals(out_ref, index, left, [(right, cross_ref)], group, scale, base_ref)
-
-    each_tile(tile, width)
+        return other_ref[:, lanes_of(0, width, index)], jnp.where(even, cot, kv)
+
+    def store(at, total):
+        total_ref[at, :] = base_ref[at, :] + total
+
+    each_tile(lambda index: two_tiles(2 * index, sides, cross_ref, store, group), width // 2)
+    total = diagonals(total_ref, out_ref.shape[0])
+    out_ref[...] = jnp.where(even, total, reversed_taps(total)) * scale
 
 
 def conv_kernel(
@@ -226,7 +244,8 @@
     mask_ref = masks_ref.at[1 if backward else 0]
 
     def table(row):
-        wide = pltpu.roll(jnp.broadcast_to(row, (rows, rows)), 0, 1, stride=1, stride_axis=0)
+        first = pltpu.roll(jnp.broadcast_to(row, (8, rows)), 0, 1, stride=1, stride_axis=0)
+        wide = jnp.concatenate([first] + [pltpu.roll(first, 8 * i, 1) for i in range(1, rows // 8)], axis=0)
         wide = wide.astype(jnp.bfloat16)
         return jnp.concatenate([wide, wide], axis=1) * mask_ref[...]
 
@@ -238,9 +257,15 @@
         x = jnp.concatenate([product(a_ref[:, lanes], b_ref[:, lanes]), other], axis=0)
         at = pl.multiple_of(half * groups + index * per_tile, per_tile)
         taps = taps_ref[1 if backward else 0, pl.ds(at, per_tile), :]
-        y = jnp.zeros((rows, LANES), jnp.float32)
-        for g in range(per_tile):
-            y = jnp.where(group == g, jnp.dot(table(taps[g : g + 1]), x, preferred_element_type=jnp.float32), y)
+        tables = [table(taps[g : g + 1]) for g in range(per_tile)]
+        if backward:
+            each = [jnp.dot(one, x, preferred_element_type=jnp.float32) for one in tables]
+        else:
+            every = jnp.dot(jnp.concatenate(tables, axis=0), x, preferred_element_type=jnp.float32)
+            each = [every[g * rows : (g + 1) * rows] for g in range(per_tile)]
+        y = each[0]
+        for g in range(1, per_tile):
+            y = jnp.where(group == g, each[g], y)
         out_c_ref[:, here] = (c_ref[:, lanes].astype(jnp.float32) * y).astype(jnp.bfloat16)
         out_d_ref[:, here] = (d_ref[:, lanes].astype(jnp.float32) * y).astype(jnp.bfloat16)
 
@@ -396,23 +421,24 @@
     *partly, far_out, pair_out, keep, masks, table_masks, tap_rows = first(*inputs, contig_starts, filters)
     square = pltpu.VMEM((rows, rows), jnp.float32)
     part = pltpu.VMEM((groups // 2, rows), jnp.float32)
+    unsummed = pltpu.VMEM((groups * 4, rows), jnp.float32)
     wide = pltpu.VMEM(q.shape, q.dtype)
     sent = pltpu.VMEM((rows, q.shape[1] // 2), q.dtype)
     far = next_chip(far_out)
     later_pair = other_core(pair_out)
     q, k, v, dy, theirs, pair_out, far_out = own_call(
         functools.partial(filter_partner_kernel, scale=scale), "filter_partner",
-        [wide] * 4 + [part, sent, sent], [pltpu.SemaphoreType.DMA((8,))],
+        [wide] * 4 + [part, sent, sent], [unsummed, pltpu.SemaphoreType.DMA((8,))],
         inputs, (*partly, keep, masks), {4: 0, 5: 1, 6: 2, 7: 3},
     )
     pair = other_core(pair_out)
     mine = own_call(
-        filter_own_kernel, "filter_own", part, [square, square],
+        filter_own_kernel, "filter_own", unsummed, [square, square],
         (), (q, k, v, dy, later_pair, masks),
     )
     later_far = next_chip(after(far_out, mine))
     mine = own_call(
-        functools.partial(filter_far_kernel, scale=scale), "filter_far", part, [square],
+        functools.partial(filter_far_kernel, scale=scale), "filter_far", part, [unsummed, square],
         (), (q, k, v, dy, far, masks, mine),
     )
     mine = mine + other_core(theirs)

time: 39 us -> 37.6 us (0.964)
  Pallas kernels: 19.9 us -> 19 us
  waiting for transfers between devices: 1.88 us -> 1.21 us
    pallas_call x4, Pallas kernels: 10.6 us -> 7.26 us  [own_call(): pl.pallas_call(kernel, out_shape=out_shape, in_specs=[pl.BlockSpec(memory...]
    pallas_call x4, Pallas kernels: 9.36 us -> 11.7 us  [local_call(): pl.pallas_call(kernel, out_shape=out_shape, in_specs=in_specs or [VMEM] *...]
    ppermute x4, waiting for transfers between devices: 0.68 us -> 0.01 us  [summed_over(): lax.ppermute(total, axis, [(turned(i, k), i) for i in range(size)])]
  transfers between devices with their start and end apart: 10 -> 10, of which waited for: 3 -> 1; matrix products, arithmetic and copies ran while one was open for 0% -> 0% of each run, Pallas kernels for 47% -> 47%
where the time goes in v14:
time: 37.6 us; the launch traced here: 37.4 us
  Pallas kernels  19 us (51%)
  starting transfers between devices  15.8 us (42%)
  waiting for transfers between devices  1.21 us (3%)
  between operations  0.82 us (2%)
  other arithmetic  0.67 us (2%)
    pallas_call x4, Pallas kernels, local_call(): pl.pallas_call(kernel, out_shape=out_shape, in_specs=in_specs or [VMEM] *...  11.7 us
    ppermute x4, starting transfers between devices, other_core(): lax.ppermute(block, 'ctx', [(i, i ^ 1) for i in range(lax.axis_size('ctx'...  7.39 us
    pallas_call x4, Pallas kernels, own_call(): pl.pallas_call(kernel, out_shape=out_shape, in_specs=[pl.BlockSpec(memory...  7.26 us
    ppermute x4, starting transfers between devices, summed_over(): lax.ppermute(total, axis, [(turned(i, k), i) for i in range(size)])  7.03 us
    ppermute x2, starting transfers between devices, next_chip(): return lax.ppermute(block, 'ctx', pairs + [(j, i) for i, j in pairs])  1.34 us
    ppermute x4, waiting for transfers between devices, other_core(): lax.ppermute(block, 'ctx', [(i, i ^ 1) for i in range(lax.axis_size('ctx'...  1.19 us
  transfers between devices with their start and end apart: 10, of which 1 were waited for; matrix products, arithmetic and copies ran while one was open for 0% of the time, Pallas kernels for 47%

profile of v14, /device:TPU:0, one launch (start us, length us, event | category | flops | bytes accessed | tf_op | source)
XLA Modules:
  0.0 37.4 jit_solution(8408001025505051558)
XLA Ops:
  0.6 1.5 %first.1 = (bf16[128,2048]{1,0:T(8,128)(2,1)S(1)}, bf16[128,2048]{1,0:T(8,128)(2,1)S(1)}, bf16[128,2048]{1,0:T(8,128)(2,1)S(1)}, bf16[128,2048]{1,0:T(8,128)(2,1...) custom-call(bf16[128,2048]{1,0:T(8,128)(2,1)} %bitcast.8, ...), custom_call_target="tpu_custom_call" | custom-call | tf_op jit(solution)/shard_map/first/pallas_call | solution.py:317
  2.2 0.5 %collective-permute-start = (bf16[128,1024]{1,0:T(8,128)(2,1)S(1)}, bf16[128,1024]{1,0:T(8,128)(2,1)S(1)}, u32[]{:S(2)}, u32[]{:S(2)}) collective-permute-start(bf16[128,1024]{1,0:T(8,128)(2,1)S(1)} %get-tuple-element.43), channel_id=1, source_target_pairs={{0,4},{4,0},{8,12},{12,8},{16,20},{20,16},{24,28},{28,24},{1,5},{5... | collective-permute-start | bytes 786440 | tf_op jit(solution)/shard_map/ppermute | solution.py:373
  2.7 0.7 %collective-permute-start.3 = (bf16[128,1024]{1,0:T(8,128)(2,1)S(1)}, bf16[128,1024]{1,0:T(8,128)(2,1)S(1)}, u32[]{:S(2)}, u32[]{:S(2)}) collective-permute-start(bf16[128,1024]{1,0:T(8,128)(2,1)S(1)} %get-tuple-element.51), channel_id=1, source_target_pairs={{4,8},{12,16},{20,24},{8,4},{16,12},{24,20},{5,9},{13,17},{21,25},... | collective-permute-start | bytes 786440 | tf_op jit(solution)/shard_map/ppermute | solution.py:379
  3.4 2.1 %filter_partner.1 = (bf16[128,2048]{1,0:T(8,128)(2,1)S(1)}, bf16[128,2048]{1,0:T(8,128)(2,1)S(1)}, bf16[128,2048]{1,0:T(8,128)(2,1)S(1)}, bf16[128,2048]{1,0:T(8...) custom-call(bf16[128,2048]{1,0:T(8,128)(2,1)} %bitcast.9, ...), custom_call_target="tpu_custom_call", output_to_operand_aliasing={{0}: (4, {}), {1}: (5, {}), {2}: (6, {}), {3}: (7, {})} | custom-call | tf_op jit(solution)/shard_map/filter_partner/pallas_call | solution.py:317
  5.4 3.9 %collective-permute-start.2 = (bf16[128,1024]{1,0:T(8,128)(2,1)S(1)}, bf16[128,1024]{1,0:T(8,128)(2,1)S(1)}, u32[]{:S(2)}, u32[]{:S(2)}) collective-permute-start(bf16[128,1024]{1,0:T(8,128)(2,1)S(1)} %get-tuple-element.50), channel_id=1, source_target_pairs={{0,4},{4,0},{8,12},{12,8},{16,20},{20,16},{24,28},{28,24},{1,5},{5... | collective-permute-start | bytes 786440 | tf_op jit(solution)/shard_map/ppermute | solution.py:373
  9.4 0.0 collective-permute-done.other_ref.pair_ref
  9.4 1.7 %filter_own.1.base_ref = f32[512,128]{1,0:T(8,128)S(1)} custom-call(bf16[128,2048]{1,0:T(8,128)(2,1)S(1)} %get-tuple-element.45.q_ref.refs_4_.c_ref.refs_1_.b_ref, bf16[128,2048]{1,0:T(8,128)(2,1)S(1)} %get-tuple-element.41.k_ref.refs_0_.a_ref.refs_5_.d_ref, bf16[128,2048]{1,0:T(8,128)(2,1)S(1)} %get-tuple-element.42.v_ref.refs_1_.b_ref.refs_4_.c_ref, ...), custom_call_target="tpu_custom_call" | custom-call | tf_op jit(solution)/shard_map/filter_own/pallas_call | solution.py:317
  11.0 0.7 %collective-permute-start.1 = (bf16[128,1024]{1,0:T(8,128)(2,1)S(1)}, bf16[128,1024]{1,0:T(8,128)(2,1)S(1)}, u32[]{:S(2)}, u32[]{:S(2)}) collective-permute-start(bf16[128,1024]{1,0:T(8,128)(2,1)S(1)} %get-tuple-element.47), channel_id=1, source_target_pairs={{4,8},{12,16},{20,24},{8,4},{16,12},{24,20},{5,9},{13,17},{21,25},... | collective-permute-start | bytes 786440 | tf_op jit(solution)/shard_map/ppermute | solution.py:379
  11.7 2.9 %collective-permute-start.4 = (f32[64,128]{1,0:T(8,128)S(1)}, f32[64,128]{1,0:T(8,128)S(1)}, u32[]{:S(2)}, u32[]{:S(2)}) collective-permute-start(f32[64,128]{1,0:T(8,128)S(1)} %get-tuple-element.60), channel_id=1, source_target_pairs={{0,4},{4,0},{8,12},{12,8},{16,20},{20,16},{24,28},{28,24},{1,5},{5... | collective-permute-start | bytes 98312 | tf_op jit(solution)/shard_map/ppermute | solution.py:373
  14.6 0.0 collective-permute-done.3.refs_3_.other_ref
  14.6 2.0 %filter_far.1 = f32[64,128]{1,0:T(8,128)S(1)} custom-call(bf16[128,2048]{1,0:T(8,128)(2,1)S(1)} %get-tuple-element.45.q_ref.refs_4_.c_ref.refs_1_.b_ref, bf16[128,2048]{1,0:T(8,128)(2,1)S(1)} %get-tuple-element.41.k_ref.refs_0_.a_ref.refs_5_.d_ref, bf16[128,2048]{1,0:T(8,128)(2,1)S(1)} %get-tuple-element.42.v_ref.refs_1_.b_ref.refs_4_.c_ref, ...), custom_call_target="tpu_custom_call" | custom-call | tf_op jit(solution)/shard_map/filter_far/pallas_call | solution.py:317
  16.6 0.0 collective-permute-done.4
  16.6 1.6 %collective-permute-start.5 = (f32[64,128]{1,0:T(8,128)S(1)}, f32[64,128]{1,0:T(8,128)S(1)}, u32[]{:S(2)}, u32[]{:S(2)}) collective-permute-start(f32[64,128]{1,0:T(8,128)S(1)} %add.20), channel_id=1, source_target_pairs={{1,0},{0,1},{3,2},{2,3},{5,4},{4,5},{7,6},{6,7},{9,8},{8,9},{11,10... | collective-permute-start | bytes 98312 | tf_op jit(solution)/shard_map/ppermute | solution.py:403
  18.3 0.0 collective-permute-done.2.refs_2_
  18.3 2.9 %forward_low.1 = (bf16[128,2048]{1,0:T(8,128)(2,1)}, bf16[128,2048]{1,0:T(8,128)(2,1)}) custom-call(bf16[128,2048]{1,0:T(8,128)(2,1)S(1)} %get-tuple-element.41.k_ref.refs_0_.a_ref.refs_5_.d_ref, bf16[128,2048]{1,0:T(8,128)(2,1)S(1)} %get-tuple-element.42.v_ref.refs_1_.b_ref.refs_4_.c_ref, bf16[128,1024]{1,0:T(8,128)(2,1)S(1)} %collective-permute-done.2.refs_2_, ...), custom_call_target="tpu_custom_call" | custom-call | flops 536870912 | bytes 3932160 | tf_op jit(solution)/shard_map/forward_low/pallas_call | solution.py:299
  21.2 0.0 collective-permute-done.5
  21.2 2.7 %collective-permute-start.6 = (f32[64,128]{1,0:T(8,128)S(1)}, f32[64,128]{1,0:T(8,128)S(1)}, u32[]{:S(2)}, u32[]{:S(2)}) collective-permute-start(f32[64,128]{1,0:T(8,128)S(1)} %add.21), channel_id=1, source_target_pairs={{2,0},{3,1},{0,2},{1,3},{6,4},{7,5},{4,6},{5,7},{10,8},{11,9},{8,1... | collective-permute-start | bytes 98312 | tf_op jit(solution)/shard_map/ppermute | solution.py:403
  23.9 2.9 %backward_high.1 = (bf16[128,2048]{1,0:T(8,128)(2,1)}, bf16[128,2048]{1,0:T(8,128)(2,1)}) custom-call(bf16[128,2048]{1,0:T(8,128)(2,1)S(1)} %get-tuple-element.46.dy_ref.refs_5_.d_ref.refs_0_.a_ref, bf16[128,2048]{1,0:T(8,128)(2,1)S(1)} %get-tuple-element.45.q_ref.refs_4_.c_ref.refs_1_.b_ref, bf16[128,1024]{1,0:T(8,128)(2,1)S(1)} %collective-permute-done.2.refs_2_, ...), custom_call_target="tpu_custom_call" | custom-call | flops 536870912 | bytes 3932160 | tf_op jit(solution)/shard_map/backward_high/pallas_call | solution.py:299
  26.8 0.0 collective-permute-done.6
  26.9 0.0 collective-permute-done.1.far_ref
  26.9 1.6 %collective-permute-start.7 = (f32[64,128]{1,0:T(8,128)S(1)}, f32[64,128]{1,0:T(8,128)S(1)}, u32[]{:S(2)}, u32[]{:S(2)}) collective-permute-start(f32[64,128]{1,0:T(8,128)S(1)} %add.22), channel_id=1, source_target_pairs={{8,0},{12,4},{0,8},{4,12},{24,16},{28,20},{16,24},{20,28},{9,1},{1... | collective-permute-start | bytes 98312 | tf_op jit(solution)/shard_map/ppermute | solution.py:403
  28.4 2.9 %forward_high.1 = (bf16[128,2048]{1,0:T(8,128)(2,1)}, bf16[128,2048]{1,0:T(8,128)(2,1)}) custom-call(bf16[128,2048]{1,0:T(8,128)(2,1)S(1)} %get-tuple-element.41.k_ref.refs_0_.a_ref.refs_5_.d_ref, bf16[128,2048]{1,0:T(8,128)(2,1)S(1)} %get-tuple-element.42.v_ref.refs_1_.b_ref.refs_4_.c_ref, ...), custom_call_target="tpu_custom_call", output_to_operand_aliasing={{0}: (8, {}), {1}: (9, {})} | custom-call | flops 536870912 | bytes 4980736 | tf_op jit(solution)/shard_map/forward_high/pallas_call | solution.py:299
  31.4 0.0 collective-permute-done.7
  31.4 1.2 %collective-permute-start.8 = (f32[64,128]{1,0:T(8,128)S(1)}, f32[64,128]{1,0:T(8,128)S(1)}, u32[]{:S(2)}, u32[]{:S(2)}) collective-permute-start(f32[64,128]{1,0:T(8,128)S(1)} %add.23), channel_id=1, source_target_pairs={{16,0},{20,4},{24,8},{28,12},{0,16},{4,20},{8,24},{12,28},{17,1},{... | collective-permute-start | bytes 98312 | tf_op jit(solution)/shard_map/ppermute | solution.py:403
  32.6 2.9 %backward_low.1 = (bf16[128,2048]{1,0:T(8,128)(2,1)}, bf16[128,2048]{1,0:T(8,128)(2,1)}) custom-call(bf16[128,2048]{1,0:T(8,128)(2,1)S(1)} %get-tuple-element.46.dy_ref.refs_5_.d_ref.refs_0_.a_ref, bf16[128,2048]{1,0:T(8,128)(2,1)S(1)} %get-tuple-element.45.q_ref.refs_4_.c_ref.refs_1_.b_ref, ...), custom_call_target="tpu_custom_call", output_to_operand_aliasing={{0}: (8, {}), {1}: (9, {})} | custom-call | flops 536870912 | bytes 4980736 | tf_op jit(solution)/shard_map/backward_low/pallas_call | solution.py:299
  35.5 0.0 collective-permute-done.8
  35.5 0.1 collective-permute-start.9
  35.6 1.2 %collective-permute-done.9 = f32[64,128]{1,0:T(8,128)S(1)} collective-permute-done((f32[64,128]{1,0:T(8,128)S(1)}, f32[64,128]{1,0:T(8,128)S(1)}, u32[]{:S(2)}, u32[]{:S(2)}) %collective-permute-start.9) | collective-permute-done | bytes 32800 | tf_op jit(solution)/shard_map/ppermute | solution.py:373
  36.8 0.6 %maximum_select_fusion = f32[128,128]{1,0:T(8,128)} fusion(f32[64,128]{1,0:T(8,128)S(1)} %collective-permute-done.9, f32[64,128]{1,0:T(8,128)S(1)} %add.24, pred[]{:T(512)S(6)} %eq.5), kind=kLoop, calls=%fused_computation | loop fusion | flops 49152 | bytes 131073 | tf_op jit(solution)/shard_map/jit(_where)/select_n | solution.py:467
  (5 shorter events, 0.0 us)
Async XLA Ops:
  2.2 7.2 %collective-permute-start = (bf16[128,1024]{1,0:T(8,128)(2,1)S(1)}, bf16[128,1024]{1,0:T(8,128)(2,1)S(1)}, u32[]{:S(2)}, u32[]{:S(2)}) collective-permute-start(bf16[128,1024]{1,0:T(8,128)(2,1)S(1)} %get-tuple-element.43), channel_id=1, source_target_pairs={{0,4},{4,0},{8,12},{12,8},{16,20},{20,16},{24,28},{28,24},{1,5},{5... | collective-permute-start | bytes 786440 | tf_op jit(solution)/shard_map/ppermute | solution.py:373
  2.7 11.9 %collective-permute-start.3 = (bf16[128,1024]{1,0:T(8,128)(2,1)S(1)}, bf16[128,1024]{1,0:T(8,128)(2,1)S(1)}, u32[]{:S(2)}, u32[]{:S(2)}) collective-permute-start(bf16[128,1024]{1,0:T(8,128)(2,1)S(1)} %get-tuple-element.51), channel_id=1, source_target_pairs={{4,8},{12,16},{20,24},{8,4},{16,12},{24,20},{5,9},{13,17},{21,25},... | collective-permute-start | bytes 786440 | tf_op jit(solution)/shard_map/ppermute | solution.py:379
  5.4 12.8 %collective-permute-start.2 = (bf16[128,1024]{1,0:T(8,128)(2,1)S(1)}, bf16[128,1024]{1,0:T(8,128)(2,1)S(1)}, u32[]{:S(2)}, u32[]{:S(2)}) collective-permute-start(bf16[128,1024]{1,0:T(8,128)(2,1)S(1)} %get-tuple-element.50), channel_id=1, source_target_pairs={{0,4},{4,0},{8,12},{12,8},{16,20},{20,16},{24,28},{28,24},{1,5},{5... | collective-permute-start | bytes 786440 | tf_op jit(solution)/shard_map/ppermute | solution.py:373
  11.0 15.8 %collective-permute-start.1 = (bf16[128,1024]{1,0:T(8,128)(2,1)S(1)}, bf16[128,1024]{1,0:T(8,128)(2,1)S(1)}, u32[]{:S(2)}, u32[]{:S(2)}) collective-permute-start(bf16[128,1024]{1,0:T(8,128)(2,1)S(1)} %get-tuple-element.47), channel_id=1, source_target_pairs={{4,8},{12,16},{20,24},{8,4},{16,12},{24,20},{5,9},{13,17},{21,25},... | collective-permute-start | bytes 786440 | tf_op jit(solution)/shard_map/ppermute | solution.py:379
  11.7 4.9 %collective-permute-start.4 = (f32[64,128]{1,0:T(8,128)S(1)}, f32[64,128]{1,0:T(8,128)S(1)}, u32[]{:S(2)}, u32[]{:S(2)}) collective-permute-start(f32[64,128]{1,0:T(8,128)S(1)} %get-tuple-element.60), channel_id=1, source_target_pairs={{0,4},{4,0},{8,12},{12,8},{16,20},{20,16},{24,28},{28,24},{1,5},{5... | collective-permute-start | bytes 98312 | tf_op jit(solution)/shard_map/ppermute | solution.py:373
  16.6 4.6 %collective-permute-start.5 = (f32[64,128]{1,0:T(8,128)S(1)}, f32[64,128]{1,0:T(8,128)S(1)}, u32[]{:S(2)}, u32[]{:S(2)}) collective-permute-start(f32[64,128]{1,0:T(8,128)S(1)} %add.20), channel_id=1, source_target_pairs={{1,0},{0,1},{3,2},{2,3},{5,4},{4,5},{7,6},{6,7},{9,8},{8,9},{11,10... | collective-permute-start | bytes 98312 | tf_op jit(solution)/shard_map/ppermute | solution.py:403
  21.2 5.6 %collective-permute-start.6 = (f32[64,128]{1,0:T(8,128)S(1)}, f32[64,128]{1,0:T(8,128)S(1)}, u32[]{:S(2)}, u32[]{:S(2)}) collective-permute-start(f32[64,128]{1,0:T(8,128)S(1)} %add.21), channel_id=1, source_target_pairs={{2,0},{3,1},{0,2},{1,3},{6,4},{7,5},{4,6},{5,7},{10,8},{11,9},{8,1... | collective-permute-start | bytes 98312 | tf_op jit(solution)/shard_map/ppermute | solution.py:403
  26.9 4.5 %collective-permute-start.7 = (f32[64,128]{1,0:T(8,128)S(1)}, f32[64,128]{1,0:T(8,128)S(1)}, u32[]{:S(2)}, u32[]{:S(2)}) collective-permute-start(f32[64,128]{1,0:T(8,128)S(1)} %add.22), channel_id=1, source_target_pairs={{8,0},{12,4},{0,8},{4,12},{24,16},{28,20},{16,24},{20,28},{9,1},{1... | collective-permute-start | bytes 98312 | tf_op jit(solution)/shard_map/ppermute | solution.py:403
  31.4 4.1 %collective-permute-start.8 = (f32[64,128]{1,0:T(8,128)S(1)}, f32[64,128]{1,0:T(8,128)S(1)}, u32[]{:S(2)}, u32[]{:S(2)}) collective-permute-start(f32[64,128]{1,0:T(8,128)S(1)} %add.23), channel_id=1, source_target_pairs={{16,0},{20,4},{24,8},{28,12},{0,16},{4,20},{8,24},{12,28},{17,1},{... | collective-permute-start | bytes 98312 | tf_op jit(solution)/shard_map/ppermute | solution.py:403
  35.5 1.3 %collective-permute-start.9 = (f32[64,128]{1,0:T(8,128)S(1)}, f32[64,128]{1,0:T(8,128)S(1)}, u32[]{:S(2)}, u32[]{:S(2)}) collective-permute-start(f32[64,128]{1,0:T(8,128)S(1)} %add.24), channel_id=1, source_target_pairs={{0,4},{4,0},{8,12},{12,8},{16,20},{20,16},{24,28},{28,24},{1,5},{5... | collective-permute-start | bytes 98312 | tf_op jit(solution)/shard_map/ppermute | solution.py:373

commit v15 on v14

--- a/solution.py
+++ b/solution.py
@@ -10,6 +10,7 @@
 
 GSIZE = 16
 LANES = 128
+BLOCK = 16
 STEP = 4
 VMEM = pl.BlockSpec(memory_space=pltpu.VMEM)
 
@@ -43,6 +44,22 @@
         return carry
 
     lax.fori_loop(0, count // step, body, 0)
+
+
+def aligned(mask):
+    rows = mask.shape[0]
+    blocks = [mask[at : at + BLOCK] for at in range(0, rows, BLOCK)]
+    return jnp.concatenate(
+        blocks[:1] + [pltpu.roll(block, rows - BLOCK * (i + 1), 1) for i, block in enumerate(blocks[1:])], axis=0
+    )
+
+
+def turned(tile, at):
+    return jnp.concatenate([tile[at:], tile[:at]], axis=0) if at else tile
+
+
+def for_groups(block):
+    return jnp.concatenate([block] * (LANES // GSIZE), axis=0)
 
 
 def half_copies(sources, targets, half, sems):
@@ -101,9 +118,9 @@
     keep_ref[1] = as_f32(t >= last)
     for n, parts in enumerate(((own, previous), (own.T, following))):
         for m, mask in enumerate(parts):
-            table_masks_ref[n, :, m * rows : (m + 1) * rows] = mask.astype(jnp.bfloat16)
+            table_masks_ref[n, :, m * rows : (m + 1) * rows] = aligned(mask).astype(jnp.bfloat16)
     for n, mask in enumerate((own, own.T, previous, following, previous.T, following.T)):
-        masks_ref[n] = mask
+        masks_ref[n] = aligned(mask)
     small[1].wait()
     taps_ref[0] = reversed_taps(filters_ref[...])
     taps_ref[1] = filters_ref[...].astype(jnp.float32)
@@ -118,20 +135,38 @@
     return product(k_ref[:, lanes], v_ref[:, lanes]), product(dy_ref[:, lanes], q_ref[:, lanes])
 
 
-def wrapped(linked):
-    rows = linked.shape[0]
-    total = linked[:8]
-    for i in range(1, rows // 8):
-        total = total + pltpu.roll(linked[8 * i : 8 * i + 8], rows - 8 * i, 1)
-    return total
-
-
-def products(left, right):
-    return lax.dot_general(left, right, (((1,), (1,)), ((), ())), preferred_element_type=jnp.float32)
-
-
-def picked(group, g, *tiles):
-    return jnp.concatenate([jnp.where(group == g, tile, jnp.zeros_like(tile)) for tile in tiles], axis=1)
+def wrapped_products(left, rights, masks, group):
+    rows = left[0].shape[0]
+    zeros = jnp.zeros_like(left[0])
+    totals = [None] * len(masks)
+    for at in range(0, rows, BLOCK):
+        picked = jnp.concatenate(
+            [
+                jnp.concatenate([jnp.where(group == g, tile[at : at + BLOCK], zeros[:BLOCK]) for tile in left], axis=1)
+                for g in range(LANES // GSIZE)
+            ],
+            axis=0,
+        )
+        right = jnp.concatenate(
+            [
+                jnp.concatenate([zeros if tile is None else turned(tile, at) for tile in tiles], axis=1)
+                for tiles in rights
+            ],
+            axis=0,
+        )
+        pairs = lax.dot_general(picked, right, (((1,), (1,)), ((), ())), preferred_element_type=jnp.float32)
+        for n, columns in enumerate(masks):
+            for column, mask_ref in columns:
+                piece = pairs[:, column * rows : (column + 1) * rows] * for_groups(mask_ref[at : at + BLOCK, :])
+                totals[n] = piece if totals[n] is None else totals[n] + piece
+    for total in totals:
+        yield jnp.concatenate(
+            [
+                total[at : at + 8] + pltpu.roll(total[at + 8 : at + 16], rows - 8, 1)
+                for at in range(0, total.shape[0], BLOCK)
+            ],
+            axis=0,
+        )
 
 
 def diagonals(sums_ref, groups):
@@ -142,21 +177,17 @@
     return total
 
 
-def sums_at(index, g):
-    return pl.ds(pl.multiple_of((index * (LANES // GSIZE) + g) * 8, 8), 8)
+def sums_at(index):
+    count = LANES // GSIZE * 8
+    return pl.ds(pl.multiple_of(index * count, count), count)
 
 
 def two_tiles(index, sides, mask_ref, store, group):
-    rows = mask_ref.shape[0]
     (left_a, right_a), (left_b, right_b) = sides(index), sides(index + 1)
-    zeros = jnp.zeros_like(right_a)
-    right = jnp.concatenate(
-        [jnp.concatenate([right_a, zeros], axis=1), jnp.concatenate([zeros, right_b], axis=1)], axis=0
-    )
-    for g in range(LANES // GSIZE):
-        pairs = products(picked(group, g, left_a, left_b), right)
-        for n in range(2):
-            store(sums_at(index + n, g), wrapped(pairs[:, n * rows : (n + 1) * rows] * mask_ref[...]))
+    masks = [[(0, mask_ref)], [(1, mask_ref)]]
+    rights = [[right_a, None], [None, right_b]]
+    for n, total in enumerate(wrapped_products([left_a, left_b], rights, masks, group)):
+        store(sums_at(index + n), total)
 
 
 def lanes_of(half, width, index):
@@ -190,7 +221,7 @@
 
 def filter_own_kernel(q_ref, k_ref, v_ref, dy_ref, other_ref, masks_ref, sums_ref, own_ref, cross_ref):
     inputs = (q_ref, k_ref, v_ref, dy_ref)
-    rows, width = q_ref.shape[0], q_ref.shape[1] // 2
+    width = q_ref.shape[1] // 2
     core = lax.axis_index("ctx") % 2
     even = core == 0
     own_ref[...] = jnp.where(even, masks_ref[1], masks_ref[0])
@@ -200,11 +231,9 @@
     def tile(index):
         kv, cot = tile_products(inputs, core, index)
         left = jnp.where(even, kv, cot)
-        right = jnp.concatenate([jnp.where(even, cot, kv), other_ref[:, lanes_of(0, width, index)]], axis=0)
-        for g in range(LANES // GSIZE):
-            pairs = products(picked(group, g, left), right)
-            linked = pairs[:, :rows] * own_ref[...] + pairs[:, rows:] * cross_ref[...]
-            sums_ref[sums_at(index, g), :] = wrapped(linked)
+        rights = [[jnp.where(even, cot, kv)], [other_ref[:, lanes_of(0, width, index)]]]
+        for total in wrapped_products([left], rights, [[(0, own_ref), (1, cross_ref)]], group):
+            sums_ref[sums_at(index), :] = total
 
     each_tile(tile, width)
 
@@ -243,31 +272,29 @@
     groups = width // GSIZE
     mask_ref = masks_ref.at[1 if backward else 0]
 
-    def table(row):
-        first = pltpu.roll(jnp.broadcast_to(row, (8, rows)), 0, 1, stride=1, stride_axis=0)
-        wide = jnp.concatenate([first] + [pltpu.roll(first, 8 * i, 1) for i in range(1, rows // 8)], axis=0)
-        wide = wide.astype(jnp.bfloat16)
-        return jnp.concatenate([wide, wide], axis=1) * mask_ref[...]
+    def table_start(row):
+        start = pltpu.roll(jnp.broadcast_to(row, (BLOCK, rows)), 0, 1, stride=1, stride_axis=0).astype(jnp.bfloat16)
+        return jnp.concatenate([start, start], axis=1)
 
     def tile(index):
         here = pl.ds(pl.multiple_of(index * LANES, LANES), LANES)
         lanes = pl.ds(pl.multiple_of(base + index * LANES, LANES), LANES)
         from_pair = even if backward else jnp.logical_not(even)
+        own = product(a_ref[:, lanes], b_ref[:, lanes])
         other = jnp.where(from_pair, pair_ref[:, here], far_ref[:, here])
-        x = jnp.concatenate([product(a_ref[:, lanes], b_ref[:, lanes]), other], axis=0)
         at = pl.multiple_of(half * groups + index * per_tile, per_tile)
         taps = taps_ref[1 if backward else 0, pl.ds(at, per_tile), :]
-        tables = [table(taps[g : g + 1]) for g in range(per_tile)]
-        if backward:
-            each = [jnp.dot(one, x, preferred_element_type=jnp.float32) for one in tables]
-        else:
-            every = jnp.dot(jnp.concatenate(tables, axis=0), x, preferred_element_type=jnp.float32)
-            each = [every[g * rows : (g + 1) * rows] for g in range(per_tile)]
-        y = each[0]
-        for g in range(1, per_tile):
-            y = jnp.where(group == g, each[g], y)
-        out_c_ref[:, here] = (c_ref[:, lanes].astype(jnp.float32) * y).astype(jnp.bfloat16)
-        out_d_ref[:, here] = (d_ref[:, lanes].astype(jnp.float32) * y).astype(jnp.bfloat16)
+        tables = jnp.concatenate([table_start(taps[g : g + 1]) for g in range(per_tile)], axis=0)
+        for at in range(0, rows, BLOCK):
+            x = jnp.concatenate([turned(own, at), turned(other, at)], axis=0)
+            masked = tables * for_groups(mask_ref[at : at + BLOCK, :])
+            every = jnp.dot(masked, x, preferred_element_type=jnp.float32)
+            y = every[:BLOCK]
+            for g in range(1, per_tile):
+                y = jnp.where(group == g, every[g * BLOCK : (g + 1) * BLOCK], y)
+            block = slice(at, at + BLOCK)
+            out_c_ref[block, here] = (c_ref[block, lanes].astype(jnp.float32) * y).astype(jnp.bfloat16)
+            out_d_ref[block, here] = (d_ref[block, lanes].astype(jnp.float32) * y).astype(jnp.bfloat16)
 
     step = math.gcd(width // LANES, STEP) * LANES
 

time: 37.6 us -> 35.6 us (0.947)
  Pallas kernels: 19 us -> 16.2 us
  starting transfers between devices: 15.8 us -> 16.4 us
    pallas_call x4, Pallas kernels: 11.7 us -> 9.1 us  [local_call(): pl.pallas_call(kernel, out_shape=out_shape, in_specs=in_specs or [VMEM] *...]
    ppermute x4, starting transfers between devices: 7.03 us -> 7.6 us  [summed_over(): lax.ppermute(total, axis, [(turned(i, k), i) for i in range(size)])]
  transfers between devices with their start and end apart: 10 -> 10, of which waited for: 1 -> 2; matrix products, arithmetic and copies ran while one was open for 0% -> 0% of each run, Pallas kernels for 47% -> 41%
where the time goes in v15:
time: 35.6 us; the launch traced here: 35.4 us
  starting transfers between devices  16.4 us (46%)
  Pallas kernels  16.2 us (46%)
  waiting for transfers between devices  1.39 us (4%)
  between operations  0.79 us (2%)
  other arithmetic  0.67 us (2%)
    pallas_call x4, Pallas kernels, local_call(): pl.pallas_call(kernel, out_shape=out_shape, in_specs=in_specs or [VMEM] *...  9.1 us
    ppermute x4, starting transfers between devices, summed_over(): lax.ppermute(total, axis, [(turned(i, k), i) for i in range(size)])  7.6 us
    ppermute x4, starting transfers between devices, other_core(): lax.ppermute(block, 'ctx', [(i, i ^ 1) for i in range(lax.axis_size('ctx'...  7.42 us
    pallas_call x4, Pallas kernels, own_call(): pl.pallas_call(kernel, out_shape=out_shape, in_specs=[pl.BlockSpec(memory...  7.09 us
    ppermute x2, starting transfers between devices, next_chip(): return lax.ppermute(block, 'ctx', pairs + [(j, i) for i, j in pairs])  1.34 us
    ppermute x4, waiting for transfers between devices, other_core(): lax.ppermute(block, 'ctx', [(i, i ^ 1) for i in range(lax.axis_size('ctx'...  1.19 us
  transfers between devices with their start and end apart: 10, of which 2 were waited for; matrix products, arithmetic and copies ran while one was open for 0% of the time, Pallas kernels for 41%

profile of v15, /device:TPU:0, one launch (start us, length us, event | category | flops | bytes accessed | tf_op | source)
XLA Modules:
  0.0 35.4 jit_solution(8323020778328320118)
XLA Ops:
  0.6 1.6 %first.1 = (bf16[128,2048]{1,0:T(8,128)(2,1)S(1)}, bf16[128,2048]{1,0:T(8,128)(2,1)S(1)}, bf16[128,2048]{1,0:T(8,128)(2,1)S(1)}, bf16[128,2048]{1,0:T(8,128)(2,1...) custom-call(bf16[128,2048]{1,0:T(8,128)(2,1)} %bitcast.8, ...), custom_call_target="tpu_custom_call" | custom-call | tf_op jit(solution)/shard_map/first/pallas_call | solution.py:344
  2.2 0.5 %collective-permute-start = (bf16[128,1024]{1,0:T(8,128)(2,1)S(1)}, bf16[128,1024]{1,0:T(8,128)(2,1)S(1)}, u32[]{:S(2)}, u32[]{:S(2)}) collective-permute-start(bf16[128,1024]{1,0:T(8,128)(2,1)S(1)} %get-tuple-element.43), channel_id=1, source_target_pairs={{0,4},{4,0},{8,12},{12,8},{16,20},{20,16},{24,28},{28,24},{1,5},{5... | collective-permute-start | bytes 786440 | tf_op jit(solution)/shard_map/ppermute | solution.py:400
  2.8 0.7 %collective-permute-start.3 = (bf16[128,1024]{1,0:T(8,128)(2,1)S(1)}, bf16[128,1024]{1,0:T(8,128)(2,1)S(1)}, u32[]{:S(2)}, u32[]{:S(2)}) collective-permute-start(bf16[128,1024]{1,0:T(8,128)(2,1)S(1)} %get-tuple-element.51), channel_id=1, source_target_pairs={{4,8},{12,16},{20,24},{8,4},{16,12},{24,20},{5,9},{13,17},{21,25},... | collective-permute-start | bytes 786440 | tf_op jit(solution)/shard_map/ppermute | solution.py:406
  3.4 2.0 %filter_partner.1 = (bf16[128,2048]{1,0:T(8,128)(2,1)S(1)}, bf16[128,2048]{1,0:T(8,128)(2,1)S(1)}, bf16[128,2048]{1,0:T(8,128)(2,1)S(1)}, bf16[128,2048]{1,0:T(8...) custom-call(bf16[128,2048]{1,0:T(8,128)(2,1)} %bitcast.9, ...), custom_call_target="tpu_custom_call", output_to_operand_aliasing={{0}: (4, {}), {1}: (5, {}), {2}: (6, {}), {3}: (7, {})} | custom-call | tf_op jit(solution)/shard_map/filter_partner/pallas_call | solution.py:344
  5.4 3.9 %collective-permute-start.2 = (bf16[128,1024]{1,0:T(8,128)(2,1)S(1)}, bf16[128,1024]{1,0:T(8,128)(2,1)S(1)}, u32[]{:S(2)}, u32[]{:S(2)}) collective-permute-start(bf16[128,1024]{1,0:T(8,128)(2,1)S(1)} %get-tuple-element.50), channel_id=1, source_target_pairs={{0,4},{4,0},{8,12},{12,8},{16,20},{20,16},{24,28},{28,24},{1,5},{5... | collective-permute-start | bytes 786440 | tf_op jit(solution)/shard_map/ppermute | solution.py:400
  9.3 0.0 collective-permute-done.other_ref.pair_ref
  9.3 1.7 %filter_own.1.base_ref = f32[512,128]{1,0:T(8,128)S(1)} custom-call(bf16[128,2048]{1,0:T(8,128)(2,1)S(1)} %get-tuple-element.45.q_ref.refs_4_.c_ref.refs_1_.b_ref, bf16[128,2048]{1,0:T(8,128)(2,1)S(1)} %get-tuple-element.41.k_ref.refs_0_.a_ref.refs_5_.d_ref, bf16[128,2048]{1,0:T(8,128)(2,1)S(1)} %get-tuple-element.42.v_ref.refs_1_.b_ref.refs_4_.c_ref, ...), custom_call_target="tpu_custom_call" | custom-call | tf_op jit(solution)/shard_map/filter_own/pallas_call | solution.py:344
  11.0 0.7 %collective-permute-start.1 = (bf16[128,1024]{1,0:T(8,128)(2,1)S(1)}, bf16[128,1024]{1,0:T(8,128)(2,1)S(1)}, u32[]{:S(2)}, u32[]{:S(2)}) collective-permute-start(bf16[128,1024]{1,0:T(8,128)(2,1)S(1)} %get-tuple-element.47), channel_id=1, source_target_pairs={{4,8},{12,16},{20,24},{8,4},{16,12},{24,20},{5,9},{13,17},{21,25},... | collective-permute-start | bytes 786440 | tf_op jit(solution)/shard_map/ppermute | solution.py:406
  11.7 2.9 %collective-permute-start.4 = (f32[64,128]{1,0:T(8,128)S(1)}, f32[64,128]{1,0:T(8,128)S(1)}, u32[]{:S(2)}, u32[]{:S(2)}) collective-permute-start(f32[64,128]{1,0:T(8,128)S(1)} %get-tuple-element.60), channel_id=1, source_target_pairs={{0,4},{4,0},{8,12},{12,8},{16,20},{20,16},{24,28},{28,24},{1,5},{5... | collective-permute-start | bytes 98312 | tf_op jit(solution)/shard_map/ppermute | solution.py:400
  14.6 0.0 collective-permute-done.3.refs_3_.other_ref
  14.6 1.8 %filter_far.1 = f32[64,128]{1,0:T(8,128)S(1)} custom-call(bf16[128,2048]{1,0:T(8,128)(2,1)S(1)} %get-tuple-element.45.q_ref.refs_4_.c_ref.refs_1_.b_ref, bf16[128,2048]{1,0:T(8,128)(2,1)S(1)} %get-tuple-element.41.k_ref.refs_0_.a_ref.refs_5_.d_ref, bf16[128,2048]{1,0:T(8,128)(2,1)S(1)} %get-tuple-element.42.v_ref.refs_1_.b_ref.refs_4_.c_ref, ...), custom_call_target="tpu_custom_call" | custom-call | tf_op jit(solution)/shard_map/filter_far/pallas_call | solution.py:344
  16.5 0.0 collective-permute-done.4
  16.5 1.6 %collective-permute-start.5 = (f32[64,128]{1,0:T(8,128)S(1)}, f32[64,128]{1,0:T(8,128)S(1)}, u32[]{:S(2)}, u32[]{:S(2)}) collective-permute-start(f32[64,128]{1,0:T(8,128)S(1)} %add.20), channel_id=1, source_target_pairs={{1,0},{0,1},{3,2},{2,3},{5,4},{4,5},{7,6},{6,7},{9,8},{8,9},{11,10... | collective-permute-start | bytes 98312 | tf_op jit(solution)/shard_map/ppermute | solution.py:430
  18.1 0.0 collective-permute-done.2.refs_2_
  18.1 2.3 %forward_low.1 = (bf16[128,2048]{1,0:T(8,128)(2,1)}, bf16[128,2048]{1,0:T(8,128)(2,1)}) custom-call(bf16[128,2048]{1,0:T(8,128)(2,1)S(1)} %get-tuple-element.41.k_ref.refs_0_.a_ref.refs_5_.d_ref, bf16[128,2048]{1,0:T(8,128)(2,1)S(1)} %get-tuple-element.42.v_ref.refs_1_.b_ref.refs_4_.c_ref, bf16[128,1024]{1,0:T(8,128)(2,1)S(1)} %collective-permute-done.2.refs_2_, ...), custom_call_target="tpu_custom_call" | custom-call | flops 536870912 | bytes 3932160 | tf_op jit(solution)/shard_map/forward_low/pallas_call | solution.py:326
  20.4 0.0 collective-permute-done.5
  20.5 2.6 %collective-permute-start.6 = (f32[64,128]{1,0:T(8,128)S(1)}, f32[64,128]{1,0:T(8,128)S(1)}, u32[]{:S(2)}, u32[]{:S(2)}) collective-permute-start(f32[64,128]{1,0:T(8,128)S(1)} %add.21), channel_id=1, source_target_pairs={{2,0},{3,1},{0,2},{1,3},{6,4},{7,5},{4,6},{5,7},{10,8},{11,9},{8,1... | collective-permute-start | bytes 98312 | tf_op jit(solution)/shard_map/ppermute | solution.py:430
  23.1 2.3 %backward_high.1 = (bf16[128,2048]{1,0:T(8,128)(2,1)}, bf16[128,2048]{1,0:T(8,128)(2,1)}) custom-call(bf16[128,2048]{1,0:T(8,128)(2,1)S(1)} %get-tuple-element.46.dy_ref.refs_5_.d_ref.refs_0_.a_ref, bf16[128,2048]{1,0:T(8,128)(2,1)S(1)} %get-tuple-element.45.q_ref.refs_4_.c_ref.refs_1_.b_ref, bf16[128,1024]{1,0:T(8,128)(2,1)S(1)} %collective-permute-done.2.refs_2_, ...), custom_call_target="tpu_custom_call" | custom-call | flops 536870912 | bytes 3932160 | tf_op jit(solution)/shard_map/backward_high/pallas_call | solution.py:326
  25.4 0.0 collective-permute-done.6
  25.4 0.0 collective-permute-done.1.far_ref
  25.4 1.5 %collective-permute-start.7 = (f32[64,128]{1,0:T(8,128)S(1)}, f32[64,128]{1,0:T(8,128)S(1)}, u32[]{:S(2)}, u32[]{:S(2)}) collective-permute-start(f32[64,128]{1,0:T(8,128)S(1)} %add.22), channel_id=1, source_target_pairs={{8,0},{12,4},{0,8},{4,12},{24,16},{28,20},{16,24},{20,28},{9,1},{1... | collective-permute-start | bytes 98312 | tf_op jit(solution)/shard_map/ppermute | solution.py:430
  27.0 2.3 %forward_high.1 = (bf16[128,2048]{1,0:T(8,128)(2,1)}, bf16[128,2048]{1,0:T(8,128)(2,1)}) custom-call(bf16[128,2048]{1,0:T(8,128)(2,1)S(1)} %get-tuple-element.41.k_ref.refs_0_.a_ref.refs_5_.d_ref, bf16[128,2048]{1,0:T(8,128)(2,1)S(1)} %get-tuple-element.42.v_ref.refs_1_.b_ref.refs_4_.c_ref, ...), custom_call_target="tpu_custom_call", output_to_operand_aliasing={{0}: (8, {}), {1}: (9, {})} | custom-call | flops 536870912 | bytes 4980736 | tf_op jit(solution)/shard_map/forward_high/pallas_call | solution.py:326
  29.2 0.1 collective-permute-done.7
  29.4 1.8 %collective-permute-start.8 = (f32[64,128]{1,0:T(8,128)S(1)}, f32[64,128]{1,0:T(8,128)S(1)}, u32[]{:S(2)}, u32[]{:S(2)}) collective-permute-start(f32[64,128]{1,0:T(8,128)S(1)} %add.23), channel_id=1, source_target_pairs={{16,0},{20,4},{24,8},{28,12},{0,16},{4,20},{8,24},{12,28},{17,1},{... | collective-permute-start | bytes 98312 | tf_op jit(solution)/shard_map/ppermute | solution.py:430
  31.2 2.3 %backward_low.1 = (bf16[128,2048]{1,0:T(8,128)(2,1)}, bf16[128,2048]{1,0:T(8,128)(2,1)}) custom-call(bf16[128,2048]{1,0:T(8,128)(2,1)S(1)} %get-tuple-element.46.dy_ref.refs_5_.d_ref.refs_0_.a_ref, bf16[128,2048]{1,0:T(8,128)(2,1)S(1)} %get-tuple-element.45.q_ref.refs_4_.c_ref.refs_1_.b_ref, ...), custom_call_target="tpu_custom_call", output_to_operand_aliasing={{0}: (8, {}), {1}: (9, {})} | custom-call | flops 536870912 | bytes 4980736 | tf_op jit(solution)/shard_map/backward_low/pallas_call | solution.py:326
  33.5 0.0 collective-permute-done.8
  33.5 0.1 collective-permute-start.9
  33.6 1.2 %collective-permute-done.9 = f32[64,128]{1,0:T(8,128)S(1)} collective-permute-done((f32[64,128]{1,0:T(8,128)S(1)}, f32[64,128]{1,0:T(8,128)S(1)}, u32[]{:S(2)}, u32[]{:S(2)}) %collective-permute-start.9) | collective-permute-done | bytes 32800 | tf_op jit(solution)/shard_map/ppermute | solution.py:400
  34.8 0.6 %maximum_select_fusion = f32[128,128]{1,0:T(8,128)} fusion(f32[64,128]{1,0:T(8,128)S(1)} %collective-permute-done.9, f32[64,128]{1,0:T(8,128)S(1)} %add.24, pred[]{:T(512)S(6)} %eq.5), kind=kLoop, calls=%fused_computation | loop fusion | flops 49152 | bytes 131073 | tf_op jit(solution)/shard_map/jit(_where)/select_n | solution.py:494
  (5 shorter events, 0.0 us)
Async XLA Ops:
  2.2 7.1 %collective-permute-start = (bf16[128,1024]{1,0:T(8,128)(2,1)S(1)}, bf16[128,1024]{1,0:T(8,128)(2,1)S(1)}, u32[]{:S(2)}, u32[]{:S(2)}) collective-permute-start(bf16[128,1024]{1,0:T(8,128)(2,1)S(1)} %get-tuple-element.43), channel_id=1, source_target_pairs={{0,4},{4,0},{8,12},{12,8},{16,20},{20,16},{24,28},{28,24},{1,5},{5... | collective-permute-start | bytes 786440 | tf_op jit(solution)/shard_map/ppermute | solution.py:400
  2.8 11.8 %collective-permute-start.3 = (bf16[128,1024]{1,0:T(8,128)(2,1)S(1)}, bf16[128,1024]{1,0:T(8,128)(2,1)S(1)}, u32[]{:S(2)}, u32[]{:S(2)}) collective-permute-start(bf16[128,1024]{1,0:T(8,128)(2,1)S(1)} %get-tuple-element.51), channel_id=1, source_target_pairs={{4,8},{12,16},{20,24},{8,4},{16,12},{24,20},{5,9},{13,17},{21,25},... | collective-permute-start | bytes 786440 | tf_op jit(solution)/shard_map/ppermute | solution.py:406
  5.4 12.7 %collective-permute-start.2 = (bf16[128,1024]{1,0:T(8,128)(2,1)S(1)}, bf16[128,1024]{1,0:T(8,128)(2,1)S(1)}, u32[]{:S(2)}, u32[]{:S(2)}) collective-permute-start(bf16[128,1024]{1,0:T(8,128)(2,1)S(1)} %get-tuple-element.50), channel_id=1, source_target_pairs={{0,4},{4,0},{8,12},{12,8},{16,20},{20,16},{24,28},{28,24},{1,5},{5... | collective-permute-start | bytes 786440 | tf_op jit(solution)/shard_map/ppermute | solution.py:400
  11.0 14.4 %collective-permute-start.1 = (bf16[128,1024]{1,0:T(8,128)(2,1)S(1)}, bf16[128,1024]{1,0:T(8,128)(2,1)S(1)}, u32[]{:S(2)}, u32[]{:S(2)}) collective-permute-start(bf16[128,1024]{1,0:T(8,128)(2,1)S(1)} %get-tuple-element.47), channel_id=1, source_target_pairs={{4,8},{12,16},{20,24},{8,4},{16,12},{24,20},{5,9},{13,17},{21,25},... | collective-permute-start | bytes 786440 | tf_op jit(solution)/shard_map/ppermute | solution.py:406
  11.7 4.7 %collective-permute-start.4 = (f32[64,128]{1,0:T(8,128)S(1)}, f32[64,128]{1,0:T(8,128)S(1)}, u32[]{:S(2)}, u32[]{:S(2)}) collective-permute-start(f32[64,128]{1,0:T(8,128)S(1)} %get-tuple-element.60), channel_id=1, source_target_pairs={{0,4},{4,0},{8,12},{12,8},{16,20},{20,16},{24,28},{28,24},{1,5},{5... | collective-permute-start | bytes 98312 | tf_op jit(solution)/shard_map/ppermute | solution.py:400
  16.5 4.0 %collective-permute-start.5 = (f32[64,128]{1,0:T(8,128)S(1)}, f32[64,128]{1,0:T(8,128)S(1)}, u32[]{:S(2)}, u32[]{:S(2)}) collective-permute-start(f32[64,128]{1,0:T(8,128)S(1)} %add.20), channel_id=1, source_target_pairs={{1,0},{0,1},{3,2},{2,3},{5,4},{4,5},{7,6},{6,7},{9,8},{8,9},{11,10... | collective-permute-start | bytes 98312 | tf_op jit(solution)/shard_map/ppermute | solution.py:430
  20.5 4.9 %collective-permute-start.6 = (f32[64,128]{1,0:T(8,128)S(1)}, f32[64,128]{1,0:T(8,128)S(1)}, u32[]{:S(2)}, u32[]{:S(2)}) collective-permute-start(f32[64,128]{1,0:T(8,128)S(1)} %add.21), channel_id=1, source_target_pairs={{2,0},{3,1},{0,2},{1,3},{6,4},{7,5},{4,6},{5,7},{10,8},{11,9},{8,1... | collective-permute-start | bytes 98312 | tf_op jit(solution)/shard_map/ppermute | solution.py:430
  25.4 4.0 %collective-permute-start.7 = (f32[64,128]{1,0:T(8,128)S(1)}, f32[64,128]{1,0:T(8,128)S(1)}, u32[]{:S(2)}, u32[]{:S(2)}) collective-permute-start(f32[64,128]{1,0:T(8,128)S(1)} %add.22), channel_id=1, source_target_pairs={{8,0},{12,4},{0,8},{4,12},{24,16},{28,20},{16,24},{20,28},{9,1},{1... | collective-permute-start | bytes 98312 | tf_op jit(solution)/shard_map/ppermute | solution.py:430
  29.4 4.1 %collective-permute-start.8 = (f32[64,128]{1,0:T(8,128)S(1)}, f32[64,128]{1,0:T(8,128)S(1)}, u32[]{:S(2)}, u32[]{:S(2)}) collective-permute-start(f32[64,128]{1,0:T(8,128)S(1)} %add.23), channel_id=1, source_target_pairs={{16,0},{20,4},{24,8},{28,12},{0,16},{4,20},{8,24},{12,28},{17,1},{... | collective-permute-start | bytes 98312 | tf_op jit(solution)/shard_map/ppermute | solution.py:430
  33.5 1.3 %collective-permute-start.9 = (f32[64,128]{1,0:T(8,128)S(1)}, f32[64,128]{1,0:T(8,128)S(1)}, u32[]{:S(2)}, u32[]{:S(2)}) collective-permute-start(f32[64,128]{1,0:T(8,128)S(1)} %add.24), channel_id=1, source_target_pairs={{0,4},{4,0},{8,12},{12,8},{16,20},{20,16},{24,28},{28,24},{1,5},{5... | collective-permute-start | bytes 98312 | tf_op jit(solution)/shard_map/ppermute | solution.py:400

commit v16 on v15

--- a/solution.py
+++ b/solution.py
@@ -11,7 +11,7 @@
 GSIZE = 16
 LANES = 128
 BLOCK = 16
-STEP = 4
+STEP = 2
 VMEM = pl.BlockSpec(memory_space=pltpu.VMEM)
 
 

time: 35.6 us -> 37.4 us (1.051)
  Pallas kernels: 16.2 us -> 18.7 us
  starting transfers between devices: 16.4 us -> 15.4 us
    pallas_call x4, Pallas kernels: 9.1 us -> 10.7 us  [local_call(): pl.pallas_call(kernel, out_shape=out_shape, in_specs=in_specs or [VMEM] *...]
    pallas_call x4, Pallas kernels: 7.09 us -> 8.06 us  [own_call(): pl.pallas_call(kernel, out_shape=out_shape, in_specs=[pl.BlockSpec(memory...]
    ppermute x4, starting transfers between devices: 7.6 us -> 6.71 us  [summed_over(): lax.ppermute(total, axis, [(turned(i, k), i) for i in range(size)])]
  transfers between devices with their start and end apart: 10 -> 10, of which waited for: 2 -> 2; matrix products, arithmetic and copies ran while one was open for 0% -> 0% of each run, Pallas kernels for 41% -> 46%
where the time goes in v16:
time: 37.4 us; the launch traced here: 37.3 us
  Pallas kernels  18.7 us (50%)
  starting transfers between devices  15.4 us (41%)
  waiting for transfers between devices  1.64 us (4%)
  between operations  0.8 us (2%)
  other arithmetic  0.67 us (2%)
    pallas_call x4, Pallas kernels, local_call(): pl.pallas_call(kernel, out_shape=out_shape, in_specs=in_specs or [VMEM] *...  10.7 us
    pallas_call x4, Pallas kernels, own_call(): pl.pallas_call(kernel, out_shape=out_shape, in_specs=[pl.BlockSpec(memory...  8.06 us
    ppermute x4, starting transfers between devices, other_core(): lax.ppermute(block, 'ctx', [(i, i ^ 1) for i in range(lax.axis_size('ctx'...  7.35 us
    ppermute x4, starting transfers between devices, summed_over(): lax.ppermute(total, axis, [(turned(i, k), i) for i in range(size)])  6.71 us
    ppermute x2, starting transfers between devices, next_chip(): return lax.ppermute(block, 'ctx', pairs + [(j, i) for i, j in pairs])  1.34 us
    ppermute x4, waiting for transfers between devices, other_core(): lax.ppermute(block, 'ctx', [(i, i ^ 1) for i in range(lax.axis_size('ctx'...  1.19 us
  transfers between devices with their start and end apart: 10, of which 2 were waited for; matrix products, arithmetic and copies ran while one was open for 0% of the time, Pallas kernels for 46%

profile of v16, /device:TPU:0, one launch (start us, length us, event | category | flops | bytes accessed | tf_op | source)
XLA Modules:
  0.0 37.3 jit_solution(13846377784334649877)
XLA Ops:
  0.6 1.6 %first.1 = (bf16[128,2048]{1,0:T(8,128)(2,1)S(1)}, bf16[128,2048]{1,0:T(8,128)(2,1)S(1)}, bf16[128,2048]{1,0:T(8,128)(2,1)S(1)}, bf16[128,2048]{1,0:T(8,128)(2,1...) custom-call(bf16[128,2048]{1,0:T(8,128)(2,1)} %bitcast.8, ...), custom_call_target="tpu_custom_call" | custom-call | tf_op jit(solution)/shard_map/first/pallas_call | solution.py:344
  2.2 0.5 %collective-permute-start = (bf16[128,1024]{1,0:T(8,128)(2,1)S(1)}, bf16[128,1024]{1,0:T(8,128)(2,1)S(1)}, u32[]{:S(2)}, u32[]{:S(2)}) collective-permute-start(bf16[128,1024]{1,0:T(8,128)(2,1)S(1)} %get-tuple-element.43), channel_id=1, source_target_pairs={{0,4},{4,0},{8,12},{12,8},{16,20},{20,16},{24,28},{28,24},{1,5},{5... | collective-permute-start | bytes 786440 | tf_op jit(solution)/shard_map/ppermute | solution.py:400
  2.8 0.7 %collective-permute-start.3 = (bf16[128,1024]{1,0:T(8,128)(2,1)S(1)}, bf16[128,1024]{1,0:T(8,128)(2,1)S(1)}, u32[]{:S(2)}, u32[]{:S(2)}) collective-permute-start(bf16[128,1024]{1,0:T(8,128)(2,1)S(1)} %get-tuple-element.51), channel_id=1, source_target_pairs={{4,8},{12,16},{20,24},{8,4},{16,12},{24,20},{5,9},{13,17},{21,25},... | collective-permute-start | bytes 786440 | tf_op jit(solution)/shard_map/ppermute | solution.py:406
  3.4 2.2 %filter_partner.1 = (bf16[128,2048]{1,0:T(8,128)(2,1)S(1)}, bf16[128,2048]{1,0:T(8,128)(2,1)S(1)}, bf16[128,2048]{1,0:T(8,128)(2,1)S(1)}, bf16[128,2048]{1,0:T(8...) custom-call(bf16[128,2048]{1,0:T(8,128)(2,1)} %bitcast.9, ...), custom_call_target="tpu_custom_call", output_to_operand_aliasing={{0}: (4, {}), {1}: (5, {}), {2}: (6, {}), {3}: (7, {})} | custom-call | tf_op jit(solution)/shard_map/filter_partner/pallas_call | solution.py:344
  5.6 3.9 %collective-permute-start.2 = (bf16[128,1024]{1,0:T(8,128)(2,1)S(1)}, bf16[128,1024]{1,0:T(8,128)(2,1)S(1)}, u32[]{:S(2)}, u32[]{:S(2)}) collective-permute-start(bf16[128,1024]{1,0:T(8,128)(2,1)S(1)} %get-tuple-element.50), channel_id=1, source_target_pairs={{0,4},{4,0},{8,12},{12,8},{16,20},{20,16},{24,28},{28,24},{1,5},{5... | collective-permute-start | bytes 786440 | tf_op jit(solution)/shard_map/ppermute | solution.py:400
  9.6 0.0 collective-permute-done.other_ref.pair_ref
  9.6 2.1 %filter_own.1.base_ref = f32[512,128]{1,0:T(8,128)S(1)} custom-call(bf16[128,2048]{1,0:T(8,128)(2,1)S(1)} %get-tuple-element.45.q_ref.refs_4_.c_ref.refs_1_.b_ref, bf16[128,2048]{1,0:T(8,128)(2,1)S(1)} %get-tuple-element.41.k_ref.refs_0_.a_ref.refs_5_.d_ref, bf16[128,2048]{1,0:T(8,128)(2,1)S(1)} %get-tuple-element.42.v_ref.refs_1_.b_ref.refs_4_.c_ref, ...), custom_call_target="tpu_custom_call" | custom-call | tf_op jit(solution)/shard_map/filter_own/pallas_call | solution.py:344
  11.7 0.7 %collective-permute-start.1 = (bf16[128,1024]{1,0:T(8,128)(2,1)S(1)}, bf16[128,1024]{1,0:T(8,128)(2,1)S(1)}, u32[]{:S(2)}, u32[]{:S(2)}) collective-permute-start(bf16[128,1024]{1,0:T(8,128)(2,1)S(1)} %get-tuple-element.47), channel_id=1, source_target_pairs={{4,8},{12,16},{20,24},{8,4},{16,12},{24,20},{5,9},{13,17},{21,25},... | collective-permute-start | bytes 786440 | tf_op jit(solution)/shard_map/ppermute | solution.py:406
  12.4 2.9 %collective-permute-start.4 = (f32[64,128]{1,0:T(8,128)S(1)}, f32[64,128]{1,0:T(8,128)S(1)}, u32[]{:S(2)}, u32[]{:S(2)}) collective-permute-start(f32[64,128]{1,0:T(8,128)S(1)} %get-tuple-element.60), channel_id=1, source_target_pairs={{0,4},{4,0},{8,12},{12,8},{16,20},{20,16},{24,28},{28,24},{1,5},{5... | collective-permute-start | bytes 98312 | tf_op jit(solution)/shard_map/ppermute | solution.py:400
  15.3 0.0 collective-permute-done.3.refs_3_.other_ref
  15.3 2.1 %filter_far.1 = f32[64,128]{1,0:T(8,128)S(1)} custom-call(bf16[128,2048]{1,0:T(8,128)(2,1)S(1)} %get-tuple-element.45.q_ref.refs_4_.c_ref.refs_1_.b_ref, bf16[128,2048]{1,0:T(8,128)(2,1)S(1)} %get-tuple-element.41.k_ref.refs_0_.a_ref.refs_5_.d_ref, bf16[128,2048]{1,0:T(8,128)(2,1)S(1)} %get-tuple-element.42.v_ref.refs_1_.b_ref.refs_4_.c_ref, ...), custom_call_target="tpu_custom_call" | custom-call | tf_op jit(solution)/shard_map/filter_far/pallas_call | solution.py:344
  17.4 0.0 collective-permute-done.4
  17.4 1.6 %collective-permute-start.5 = (f32[64,128]{1,0:T(8,128)S(1)}, f32[64,128]{1,0:T(8,128)S(1)}, u32[]{:S(2)}, u32[]{:S(2)}) collective-permute-start(f32[64,128]{1,0:T(8,128)S(1)} %add.20), channel_id=1, source_target_pairs={{1,0},{0,1},{3,2},{2,3},{5,4},{4,5},{7,6},{6,7},{9,8},{8,9},{11,10... | collective-permute-start | bytes 98312 | tf_op jit(solution)/shard_map/ppermute | solution.py:430
  19.1 0.0 collective-permute-done.2.refs_2_
  19.1 2.7 %forward_low.1 = (bf16[128,2048]{1,0:T(8,128)(2,1)}, bf16[128,2048]{1,0:T(8,128)(2,1)}) custom-call(bf16[128,2048]{1,0:T(8,128)(2,1)S(1)} %get-tuple-element.41.k_ref.refs_0_.a_ref.refs_5_.d_ref, bf16[128,2048]{1,0:T(8,128)(2,1)S(1)} %get-tuple-element.42.v_ref.refs_1_.b_ref.refs_4_.c_ref, bf16[128,1024]{1,0:T(8,128)(2,1)S(1)} %collective-permute-done.2.refs_2_, ...), custom_call_target="tpu_custom_call" | custom-call | flops 536870912 | bytes 3932160 | tf_op jit(solution)/shard_map/forward_low/pallas_call | solution.py:326
  21.8 0.0 collective-permute-done.5
  21.8 2.7 %collective-permute-start.6 = (f32[64,128]{1,0:T(8,128)S(1)}, f32[64,128]{1,0:T(8,128)S(1)}, u32[]{:S(2)}, u32[]{:S(2)}) collective-permute-start(f32[64,128]{1,0:T(8,128)S(1)} %add.21), channel_id=1, source_target_pairs={{2,0},{3,1},{0,2},{1,3},{6,4},{7,5},{4,6},{5,7},{10,8},{11,9},{8,1... | collective-permute-start | bytes 98312 | tf_op jit(solution)/shard_map/ppermute | solution.py:430
  24.5 2.7 %backward_high.1 = (bf16[128,2048]{1,0:T(8,128)(2,1)}, bf16[128,2048]{1,0:T(8,128)(2,1)}) custom-call(bf16[128,2048]{1,0:T(8,128)(2,1)S(1)} %get-tuple-element.46.dy_ref.refs_5_.d_ref.refs_0_.a_ref, bf16[128,2048]{1,0:T(8,128)(2,1)S(1)} %get-tuple-element.45.q_ref.refs_4_.c_ref.refs_1_.b_ref, bf16[128,1024]{1,0:T(8,128)(2,1)S(1)} %collective-permute-done.2.refs_2_, ...), custom_call_target="tpu_custom_call" | custom-call | flops 536870912 | bytes 3932160 | tf_op jit(solution)/shard_map/backward_high/pallas_call | solution.py:326
  27.2 0.0 collective-permute-done.6
  27.2 0.0 collective-permute-done.1.far_ref
  27.2 1.5 %collective-permute-start.7 = (f32[64,128]{1,0:T(8,128)S(1)}, f32[64,128]{1,0:T(8,128)S(1)}, u32[]{:S(2)}, u32[]{:S(2)}) collective-permute-start(f32[64,128]{1,0:T(8,128)S(1)} %add.22), channel_id=1, source_target_pairs={{8,0},{12,4},{0,8},{4,12},{24,16},{28,20},{16,24},{20,28},{9,1},{1... | collective-permute-start | bytes 98312 | tf_op jit(solution)/shard_map/ppermute | solution.py:430
  28.7 2.7 %forward_high.1 = (bf16[128,2048]{1,0:T(8,128)(2,1)}, bf16[128,2048]{1,0:T(8,128)(2,1)}) custom-call(bf16[128,2048]{1,0:T(8,128)(2,1)S(1)} %get-tuple-element.41.k_ref.refs_0_.a_ref.refs_5_.d_ref, bf16[128,2048]{1,0:T(8,128)(2,1)S(1)} %get-tuple-element.42.v_ref.refs_1_.b_ref.refs_4_.c_ref, ...), custom_call_target="tpu_custom_call", output_to_operand_aliasing={{0}: (8, {}), {1}: (9, {})} | custom-call | flops 536870912 | bytes 4980736 | tf_op jit(solution)/shard_map/forward_high/pallas_call | solution.py:326
  31.4 0.0 collective-permute-done.7
  31.4 0.9 %collective-permute-start.8 = (f32[64,128]{1,0:T(8,128)S(1)}, f32[64,128]{1,0:T(8,128)S(1)}, u32[]{:S(2)}, u32[]{:S(2)}) collective-permute-start(f32[64,128]{1,0:T(8,128)S(1)} %add.23), channel_id=1, source_target_pairs={{16,0},{20,4},{24,8},{28,12},{0,16},{4,20},{8,24},{12,28},{17,1},{... | collective-permute-start | bytes 98312 | tf_op jit(solution)/shard_map/ppermute | solution.py:430
  32.3 2.7 %backward_low.1 = (bf16[128,2048]{1,0:T(8,128)(2,1)}, bf16[128,2048]{1,0:T(8,128)(2,1)}) custom-call(bf16[128,2048]{1,0:T(8,128)(2,1)S(1)} %get-tuple-element.46.dy_ref.refs_5_.d_ref.refs_0_.a_ref, bf16[128,2048]{1,0:T(8,128)(2,1)S(1)} %get-tuple-element.45.q_ref.refs_4_.c_ref.refs_1_.b_ref, ...), custom_call_target="tpu_custom_call", output_to_operand_aliasing={{0}: (8, {}), {1}: (9, {})} | custom-call | flops 536870912 | bytes 4980736 | tf_op jit(solution)/shard_map/backward_low/pallas_call | solution.py:326
  35.0 0.4 %collective-permute-done.8 = f32[64,128]{1,0:T(8,128)S(1)} collective-permute-done((f32[64,128]{1,0:T(8,128)S(1)}, f32[64,128]{1,0:T(8,128)S(1)}, u32[]{:S(2)}, u32[]{:S(2)}) %collective-permute-start.8) | collective-permute-done | bytes 32800 | tf_op jit(solution)/shard_map/ppermute | solution.py:430
  35.4 0.0 collective-permute-start.9
  35.4 1.2 %collective-permute-done.9 = f32[64,128]{1,0:T(8,128)S(1)} collective-permute-done((f32[64,128]{1,0:T(8,128)S(1)}, f32[64,128]{1,0:T(8,128)S(1)}, u32[]{:S(2)}, u32[]{:S(2)}) %collective-permute-start.9) | collective-permute-done | bytes 32800 | tf_op jit(solution)/shard_map/ppermute | solution.py:400
  36.6 0.6 %maximum_select_fusion = f32[128,128]{1,0:T(8,128)} fusion(f32[64,128]{1,0:T(8,128)S(1)} %collective-permute-done.9, f32[64,128]{1,0:T(8,128)S(1)} %add.24, pred[]{:T(512)S(6)} %eq.5), kind=kLoop, calls=%fused_computation | loop fusion | flops 49152 | bytes 131073 | tf_op jit(solution)/shard_map/jit(_where)/select_n | solution.py:494
  (5 shorter events, 0.0 us)
Async XLA Ops:
  2.2 7.3 %collective-permute-start = (bf16[128,1024]{1,0:T(8,128)(2,1)S(1)}, bf16[128,1024]{1,0:T(8,128)(2,1)S(1)}, u32[]{:S(2)}, u32[]{:S(2)}) collective-permute-start(bf16[128,1024]{1,0:T(8,128)(2,1)S(1)} %get-tuple-element.43), channel_id=1, source_target_pairs={{0,4},{4,0},{8,12},{12,8},{16,20},{20,16},{24,28},{28,24},{1,5},{5... | collective-permute-start | bytes 786440 | tf_op jit(solution)/shard_map/ppermute | solution.py:400
  2.8 12.5 %collective-permute-start.3 = (bf16[128,1024]{1,0:T(8,128)(2,1)S(1)}, bf16[128,1024]{1,0:T(8,128)(2,1)S(1)}, u32[]{:S(2)}, u32[]{:S(2)}) collective-permute-start(bf16[128,1024]{1,0:T(8,128)(2,1)S(1)} %get-tuple-element.51), channel_id=1, source_target_pairs={{4,8},{12,16},{20,24},{8,4},{16,12},{24,20},{5,9},{13,17},{21,25},... | collective-permute-start | bytes 786440 | tf_op jit(solution)/shard_map/ppermute | solution.py:406
  5.6 13.4 %collective-permute-start.2 = (bf16[128,1024]{1,0:T(8,128)(2,1)S(1)}, bf16[128,1024]{1,0:T(8,128)(2,1)S(1)}, u32[]{:S(2)}, u32[]{:S(2)}) collective-permute-start(bf16[128,1024]{1,0:T(8,128)(2,1)S(1)} %get-tuple-element.50), channel_id=1, source_target_pairs={{0,4},{4,0},{8,12},{12,8},{16,20},{20,16},{24,28},{28,24},{1,5},{5... | collective-permute-start | bytes 786440 | tf_op jit(solution)/shard_map/ppermute | solution.py:400
  11.7 15.5 %collective-permute-start.1 = (bf16[128,1024]{1,0:T(8,128)(2,1)S(1)}, bf16[128,1024]{1,0:T(8,128)(2,1)S(1)}, u32[]{:S(2)}, u32[]{:S(2)}) collective-permute-start(bf16[128,1024]{1,0:T(8,128)(2,1)S(1)} %get-tuple-element.47), channel_id=1, source_target_pairs={{4,8},{12,16},{20,24},{8,4},{16,12},{24,20},{5,9},{13,17},{21,25},... | collective-permute-start | bytes 786440 | tf_op jit(solution)/shard_map/ppermute | solution.py:406
  12.4 5.0 %collective-permute-start.4 = (f32[64,128]{1,0:T(8,128)S(1)}, f32[64,128]{1,0:T(8,128)S(1)}, u32[]{:S(2)}, u32[]{:S(2)}) collective-permute-start(f32[64,128]{1,0:T(8,128)S(1)} %get-tuple-element.60), channel_id=1, source_target_pairs={{0,4},{4,0},{8,12},{12,8},{16,20},{20,16},{24,28},{28,24},{1,5},{5... | collective-permute-start | bytes 98312 | tf_op jit(solution)/shard_map/ppermute | solution.py:400
  17.4 4.3 %collective-permute-start.5 = (f32[64,128]{1,0:T(8,128)S(1)}, f32[64,128]{1,0:T(8,128)S(1)}, u32[]{:S(2)}, u32[]{:S(2)}) collective-permute-start(f32[64,128]{1,0:T(8,128)S(1)} %add.20), channel_id=1, source_target_pairs={{1,0},{0,1},{3,2},{2,3},{5,4},{4,5},{7,6},{6,7},{9,8},{8,9},{11,10... | collective-permute-start | bytes 98312 | tf_op jit(solution)/shard_map/ppermute | solution.py:430
  21.8 5.3 %collective-permute-start.6 = (f32[64,128]{1,0:T(8,128)S(1)}, f32[64,128]{1,0:T(8,128)S(1)}, u32[]{:S(2)}, u32[]{:S(2)}) collective-permute-start(f32[64,128]{1,0:T(8,128)S(1)} %add.21), channel_id=1, source_target_pairs={{2,0},{3,1},{0,2},{1,3},{6,4},{7,5},{4,6},{5,7},{10,8},{11,9},{8,1... | collective-permute-start | bytes 98312 | tf_op jit(solution)/shard_map/ppermute | solution.py:430
  27.2 4.2 %collective-permute-start.7 = (f32[64,128]{1,0:T(8,128)S(1)}, f32[64,128]{1,0:T(8,128)S(1)}, u32[]{:S(2)}, u32[]{:S(2)}) collective-permute-start(f32[64,128]{1,0:T(8,128)S(1)} %add.22), channel_id=1, source_target_pairs={{8,0},{12,4},{0,8},{4,12},{24,16},{28,20},{16,24},{20,28},{9,1},{1... | collective-permute-start | bytes 98312 | tf_op jit(solution)/shard_map/ppermute | solution.py:430
  31.4 4.0 %collective-permute-start.8 = (f32[64,128]{1,0:T(8,128)S(1)}, f32[64,128]{1,0:T(8,128)S(1)}, u32[]{:S(2)}, u32[]{:S(2)}) collective-permute-start(f32[64,128]{1,0:T(8,128)S(1)} %add.23), channel_id=1, source_target_pairs={{16,0},{20,4},{24,8},{28,12},{0,16},{4,20},{8,24},{12,28},{17,1},{... | collective-permute-start | bytes 98312 | tf_op jit(solution)/shard_map/ppermute | solution.py:430
  35.4 1.2 %collective-permute-start.9 = (f32[64,128]{1,0:T(8,128)S(1)}, f32[64,128]{1,0:T(8,128)S(1)}, u32[]{:S(2)}, u32[]{:S(2)}) collective-permute-start(f32[64,128]{1,0:T(8,128)S(1)} %add.24), channel_id=1, source_target_pairs={{0,4},{4,0},{8,12},{12,8},{16,20},{20,16},{24,28},{28,24},{1,5},{5... | collective-permute-start | bytes 98312 | tf_op jit(solution)/shard_map/ppermute | solution.py:400

commit v17 on v15

--- a/solution.py
+++ b/solution.py
@@ -119,7 +119,7 @@
     for n, parts in enumerate(((own, previous), (own.T, following))):
         for m, mask in enumerate(parts):
             table_masks_ref[n, :, m * rows : (m + 1) * rows] = aligned(mask).astype(jnp.bfloat16)
-    for n, mask in enumerate((own, own.T, previous, following, previous.T, following.T)):
+    for n, mask in enumerate((own.T, following, previous.T)):
         masks_ref[n] = aligned(mask)
     small[1].wait()
     taps_ref[0] = reversed_taps(filters_ref[...])
@@ -210,7 +210,7 @@
         sums_ref[at, :] = total
 
     def tiles(index):
-        two_tiles(2 * index, lambda i: tile_products(inputs, 1 - core, i), masks_ref.at[1], store, group)
+        two_tiles(2 * index, lambda i: tile_products(inputs, 1 - core, i), masks_ref.at[0], store, group)
 
     each_tile(tiles, q_ref.shape[1] // 4)
     out_ref[...] = diagonals(sums_ref, out_ref.shape[0]) * scale
@@ -219,20 +219,20 @@
     sent_products(inputs, core, keep_ref, pair_ref, far_ref, core == 1)
 
 
-def filter_own_kernel(q_ref, k_ref, v_ref, dy_ref, other_ref, masks_ref, sums_ref, own_ref, cross_ref):
+def filter_own_kernel(q_ref, k_ref, v_ref, dy_ref, other_ref, masks_ref, sums_ref, cross_ref):
     inputs = (q_ref, k_ref, v_ref, dy_ref)
     width = q_ref.shape[1] // 2
     core = lax.axis_index("ctx") % 2
     even = core == 0
-    own_ref[...] = jnp.where(even, masks_ref[1], masks_ref[0])
-    cross_ref[...] = jnp.where(even, masks_ref[3], masks_ref[2])
+    cross_ref[...] = jnp.where(even, masks_ref[1], masks_ref[2])
     group = lane_groups()
 
     def tile(index):
         kv, cot = tile_products(inputs, core, index)
-        left = jnp.where(even, kv, cot)
-        rights = [[jnp.where(even, cot, kv)], [other_ref[:, lanes_of(0, width, index)]]]
-        for total in wrapped_products([left], rights, [[(0, own_ref), (1, cross_ref)]], group):
+        other = other_ref[:, lanes_of(0, width, index)]
+        left = [kv, jnp.where(even, kv, other)]
+        rights = [[cot, None], [None, jnp.where(even, other, cot)]]
+        for total in wrapped_products(left, rights, [[(0, masks_ref.at[0]), (1, cross_ref)]], group):
             sums_ref[sums_at(index), :] = total
 
     each_tile(tile, width)
@@ -243,47 +243,48 @@
     width = q_ref.shape[1] // 2
     core = lax.axis_index("ctx") % 2
     even = core == 0
-    cross_ref[...] = jnp.where(even, masks_ref[4], masks_ref[5])
+    cross_ref[...] = jnp.where(even, masks_ref[2], masks_ref[1])
     group = lane_groups()
 
     def sides(index):
         kv, cot = tile_products(inputs, core, index)
-        return other_ref[:, lanes_of(0, width, index)], jnp.where(even, cot, kv)
+        other = other_ref[:, lanes_of(0, width, index)]
+        return jnp.where(even, other, kv), jnp.where(even, cot, other)
 
     def store(at, total):
         total_ref[at, :] = base_ref[at, :] + total
 
     each_tile(lambda index: two_tiles(2 * index, sides, cross_ref, store, group), width // 2)
-    total = diagonals(total_ref, out_ref.shape[0])
-    out_ref[...] = jnp.where(even, total, reversed_taps(total)) * scale
+    out_ref[...] = diagonals(total_ref, out_ref.shape[0]) * scale
 
 
 def conv_kernel(
-    a_ref, b_ref, pair_ref, far_ref, c_ref, d_ref, masks_ref, taps_ref, c_in_hbm, d_in_hbm, out_c_hbm, out_d_hbm,
-    out_c_ref, out_d_ref, sems, *, backward, half,
+    a_ref, b_ref, c_ref, d_ref, masks_ref, taps_ref, pair_ref, far_ref, *rest, backward, spans
 ):
-    del c_in_hbm, d_in_hbm
+    later = rest[: 2 * len(spans) - 2]
+    others = [(pair_ref, far_ref), *zip(later[::2], later[1::2])]
+    out_c_hbm, out_d_hbm, out_c_ref, out_d_ref, sems = rest[-5:]
     rows = a_ref.shape[0]
     per_tile = LANES // GSIZE
-    width = a_ref.shape[1] // 2
-    base = half * width
+    half_tiles = a_ref.shape[1] // 2 // LANES
     even = lax.axis_index("ctx") % 2 == 0
+    from_pair = even if backward else jnp.logical_not(even)
     group = lane_groups()
-    groups = width // GSIZE
     mask_ref = masks_ref.at[1 if backward else 0]
 
     def table_start(row):
         start = pltpu.roll(jnp.broadcast_to(row, (BLOCK, rows)), 0, 1, stride=1, stride_axis=0).astype(jnp.bfloat16)
         return jnp.concatenate([start, start], axis=1)
 
-    def tile(index):
-        here = pl.ds(pl.multiple_of(index * LANES, LANES), LANES)
-        lanes = pl.ds(pl.multiple_of(base + index * LANES, LANES), LANES)
-        from_pair = even if backward else jnp.logical_not(even)
+    def lanes_at(index):
+        return pl.ds(pl.multiple_of(index * LANES, LANES), LANES)
+
+    def tile(index, near, distant):
+        lanes = lanes_at(index)
+        here = lanes_at(index % half_tiles)
         own = product(a_ref[:, lanes], b_ref[:, lanes])
-        other = jnp.where(from_pair, pair_ref[:, here], far_ref[:, here])
-        at = pl.multiple_of(half * groups + index * per_tile, per_tile)
-        taps = taps_ref[1 if backward else 0, pl.ds(at, per_tile), :]
+        other = jnp.where(from_pair, near[:, here], distant[:, here])
+        taps = taps_ref[1 if backward else 0, pl.ds(pl.multiple_of(index * per_tile, per_tile), per_tile), :]
         tables = jnp.concatenate([table_start(taps[g : g + 1]) for g in range(per_tile)], axis=0)
         for at in range(0, rows, BLOCK):
             x = jnp.concatenate([turned(own, at), turned(other, at)], axis=0)
@@ -293,29 +294,31 @@
             for g in range(1, per_tile):
                 y = jnp.where(group == g, every[g * BLOCK : (g + 1) * BLOCK], y)
             block = slice(at, at + BLOCK)
-            out_c_ref[block, here] = (c_ref[block, lanes].astype(jnp.float32) * y).astype(jnp.bfloat16)
-            out_d_ref[block, here] = (d_ref[block, lanes].astype(jnp.float32) * y).astype(jnp.bfloat16)
-
-    step = math.gcd(width // LANES, STEP) * LANES
-
-    def stored(i):
-        here = pl.ds(pl.multiple_of(i * step, step), step)
-        there = pl.ds(pl.multiple_of(base + i * step, step), step)
+            out_c_ref[block, lanes] = (c_ref[block, lanes].astype(jnp.float32) * y).astype(jnp.bfloat16)
+            out_d_ref[block, lanes] = (d_ref[block, lanes].astype(jnp.float32) * y).astype(jnp.bfloat16)
+
+    def stored(start, count, sem):
+        lanes = pl.ds(pl.multiple_of(start * LANES, count * LANES), count * LANES)
         return [
-            pltpu.make_async_copy(out_c_ref.at[:, here], out_c_hbm.at[:, there], sems.at[0, i]),
-            pltpu.make_async_copy(out_d_ref.at[:, here], out_d_hbm.at[:, there], sems.at[1, i]),
+            pltpu.make_async_copy(out_c_ref.at[:, lanes], out_c_hbm.at[:, lanes], sems.at[0, sem]),
+            pltpu.make_async_copy(out_d_ref.at[:, lanes], out_d_hbm.at[:, lanes], sems.at[1, sem]),
         ]
 
-    def body(i, carry):
-        for j in range(step // LANES):
-            tile(i * (step // LANES) + j)
-        for copy in stored(i):
-            copy.start()
-        return carry
-
-    lax.fori_loop(0, width // step, body, 0)
-    for i in range(width // step):
-        for copy in stored(i):
+    bodies = []
+    for (first, count), (near, distant) in zip(spans, others):
+        step = math.gcd(count, STEP)
+
+        def body(i, carry, first=first, step=step, near=near, distant=distant, sem=len(bodies)):
+            for j in range(step):
+                tile(first + i * step + j, near, distant)
+            for copy in stored(first + i * step, step, sem + i):
+                copy.start()
+            return carry
+
+        lax.fori_loop(0, count // step, body, 0)
+        bodies += [(first + i * step, step) for i in range(count // step)]
+    for n, (start, count) in enumerate(bodies):
+        for copy in stored(start, count, n):
             copy.wait()
 
 
@@ -362,7 +365,7 @@
         first_kernel, "first",
         [wide] * 4 + [sent] * 2 + [
             pltpu.VMEM((2, rows, rows), jnp.float32),
-            pltpu.VMEM((6, rows, rows), jnp.float32),
+            pltpu.VMEM((3, rows, rows), jnp.float32),
             pltpu.VMEM((2, rows, 2 * rows), jnp.bfloat16),
             pltpu.VMEM((2, *filters.shape), jnp.float32),
         ],
@@ -374,20 +377,20 @@
     )
 
 
-def convolution(a, b, pair, far, c, d, masks, taps, outs, backward, half):
+def convolution(a, b, c, d, masks, taps, spans, others, outs, backward):
     rows, width = a.shape
-    steps = width // 2 // LANES // math.gcd(width // 2 // LANES, STEP)
+    count = sum(tiles // math.gcd(tiles, STEP) for _, tiles in spans)
     out = jax.ShapeDtypeStruct((rows, width), jnp.bfloat16)
-    part = pltpu.VMEM((rows, width // 2), jnp.bfloat16)
+    whole = pltpu.VMEM((rows, width), jnp.bfloat16)
     anywhere = pl.BlockSpec(memory_space=pl.ANY)
-    body = functools.partial(conv_kernel, backward=backward, half=half)
-    operands = (a, b, pair, far, c, d, masks, taps)
+    body = functools.partial(conv_kernel, backward=backward, spans=spans)
+    operands = (a, b, c, d, masks, taps, *[x for pair in others for x in pair])
     n = len(operands)
     return local_call(
-        body if outs else lambda *refs: body(*refs[:n], None, None, *refs[n:]),
-        ("backward" if backward else "forward") + ("_high" if half else "_low"),
+        (lambda *refs: body(*refs[:n], *refs[n + 2 :])) if outs else body,
+        "backward" if backward else "forward",
         [out, out],
-        [part, part, pltpu.SemaphoreType.DMA((2, steps))],
+        [whole, whole, pltpu.SemaphoreType.DMA((2, count))],
         16 * rows * rows * width,
         operands + tuple(outs or ()),
         [VMEM] * n + [anywhere] * (2 if outs else 0),
@@ -460,7 +463,7 @@
     )
     pair = other_core(pair_out)
     mine = own_call(
-        filter_own_kernel, "filter_own", unsummed, [square, square],
+        filter_own_kernel, "filter_own", unsummed, [square],
         (), (q, k, v, dy, later_pair, masks),
     )
     later_far = next_chip(after(far_out, mine))
@@ -470,24 +473,32 @@
     )
     mine = mine + other_core(theirs)
 
-    def forward(pair, far, outs, half):
-        return convolution(k, v, pair, far, q, dy, table_masks, tap_rows, outs, False, half)
-
-    def backward(pair, far, outs, half):
-        return convolution(dy, q, pair, far, v, k, table_masks, tap_rows, outs, True, half)
+    half_tiles = q.shape[1] // 2 // LANES
+    few = max(half_tiles // 2, 1)
+    first_others, later_others = (pair, far), (later_pair, later_far)
+
+    def forward(spans, others, outs=None):
+        return convolution(k, v, q, dy, table_masks, tap_rows, spans, others, outs, False)
+
+    def backward(spans, others, outs=None):
+        return convolution(dy, q, v, k, table_masks, tap_rows, spans, others, outs, True)
 
     for n, place in enumerate(rounds_over_chips()):
         if n == 0:
-            half_forward = forward(pair, far, None, 0)
+            some_forward = forward([(0, few)], [first_others])
         if n == 1:
-            mine = after(mine, *half_forward)
-            half_backward = backward(pair, far, None, 1)
+            mine = after(mine, *some_forward)
+            some_backward = backward([(half_tiles, few)], [first_others])
         if n == 2:
-            mine = after(mine, *half_backward, later_far, later_pair)
-            mixed, grad_q = forward(later_pair, later_far, half_forward, 1)
+            mine = after(mine, *some_backward, later_far, later_pair)
+            mixed, grad_q = forward(
+                [(few, half_tiles - few), (half_tiles, half_tiles)], [first_others, later_others], some_forward
+            )
         if n == 3:
             mine = after(mine, mixed, grad_q)
-            grad_k, grad_v = backward(later_pair, later_far, half_backward, 0)
+            grad_k, grad_v = backward(
+                [(half_tiles + few, half_tiles - few), (0, half_tiles)], [first_others, later_others], some_backward
+            )
         mine = summed_over(mine, *place)
     mine = after(mine, grad_k, grad_v)
     halves = [mine, other_core(mine)]

time: 35.6 us -> 37.3 us (1.048)
  waiting for transfers between devices: 1.39 us -> 3.12 us
  Pallas kernels: 16.2 us -> 17.5 us
  starting transfers between devices: 16.4 us -> 15.1 us
    ppermute x4, waiting for transfers between devices: 0.2 us -> 1.92 us  [summed_over(): lax.ppermute(total, axis, [(turned(i, k), i) for i in range(size)])]
    pallas_call x4, Pallas kernels: 7.09 us -> 8.43 us  [own_call(): pl.pallas_call(kernel, out_shape=out_shape, in_specs=[pl.BlockSpec(memory...]
    ppermute x4, starting transfers between devices: 7.6 us -> 6.41 us  [summed_over(): lax.ppermute(total, axis, [(turned(i, k), i) for i in range(size)])]
  transfers between devices with their start and end apart: 10 -> 10, of which waited for: 2 -> 4; matrix products, arithmetic and copies ran while one was open for 0% -> 0% of each run, Pallas kernels for 41% -> 43%
where the time goes in v17:
time: 37.3 us; the launch traced here: 37.1 us
  Pallas kernels  17.5 us (47%)
  starting transfers between devices  15.1 us (40%)
  waiting for transfers between devices  3.12 us (8%)
  between operations  0.76 us (2%)
  other arithmetic  0.67 us (2%)
    pallas_call x4, Pallas kernels, local_call(): pl.pallas_call(kernel, out_shape=out_shape, in_specs=in_specs or [VMEM] *...  9.02 us
    pallas_call x4, Pallas kernels, own_call(): pl.pallas_call(kernel, out_shape=out_shape, in_specs=[pl.BlockSpec(memory...  8.43 us
    ppermute x4, starting transfers between devices, other_core(): lax.ppermute(block, 'ctx', [(i, i ^ 1) for i in range(lax.axis_size('ctx'...  7.34 us
    ppermute x4, starting transfers between devices, summed_over(): lax.ppermute(total, axis, [(turned(i, k), i) for i in range(size)])  6.41 us
    ppermute x4, waiting for transfers between devices, summed_over(): lax.ppermute(total, axis, [(turned(i, k), i) for i in range(size)])  1.92 us
    ppermute x2, starting transfers between devices, next_chip(): return lax.ppermute(block, 'ctx', pairs + [(j, i) for i, j in pairs])  1.34 us
    ppermute x4, waiting for transfers between devices, other_core(): lax.ppermute(block, 'ctx', [(i, i ^ 1) for i in range(lax.axis_size('ctx'...  1.19 us
  transfers between devices with their start and end apart: 10, of which 4 were waited for; matrix products, arithmetic and copies ran while one was open for 0% of the time, Pallas kernels for 43%

profile of v17, /device:TPU:0, one launch (start us, length us, event | category | flops | bytes accessed | tf_op | source)
XLA Modules:
  0.0 37.1 jit_solution(18179926096976011503)
XLA Ops:
  0.6 1.5 %first.1 = (bf16[128,2048]{1,0:T(8,128)(2,1)S(1)}, bf16[128,2048]{1,0:T(8,128)(2,1)S(1)}, bf16[128,2048]{1,0:T(8,128)(2,1)S(1)}, bf16[128,2048]{1,0:T(8,128)(2,1...) custom-call(bf16[128,2048]{1,0:T(8,128)(2,1)} %bitcast.8, ...), custom_call_target="tpu_custom_call" | custom-call | tf_op jit(solution)/shard_map/first/pallas_call | solution.py:347
  2.2 0.5 %collective-permute-start.2 = (bf16[128,1024]{1,0:T(8,128)(2,1)S(1)}, bf16[128,1024]{1,0:T(8,128)(2,1)S(1)}, u32[]{:S(2)}, u32[]{:S(2)}) collective-permute-start(bf16[128,1024]{1,0:T(8,128)(2,1)S(1)} %get-tuple-element.49), channel_id=1, source_target_pairs={{0,4},{4,0},{8,12},{12,8},{16,20},{20,16},{24,28},{28,24},{1,5},{5... | collective-permute-start | bytes 786440 | tf_op jit(solution)/shard_map/ppermute | solution.py:403
  2.7 0.7 %collective-permute-start.1 = (bf16[128,1024]{1,0:T(8,128)(2,1)S(1)}, bf16[128,1024]{1,0:T(8,128)(2,1)S(1)}, u32[]{:S(2)}, u32[]{:S(2)}) collective-permute-start(bf16[128,1024]{1,0:T(8,128)(2,1)S(1)} %get-tuple-element.48), channel_id=1, source_target_pairs={{4,8},{12,16},{20,24},{8,4},{16,12},{24,20},{5,9},{13,17},{21,25},... | collective-permute-start | bytes 786440 | tf_op jit(solution)/shard_map/ppermute | solution.py:409
  3.4 2.0 %filter_partner.1 = (bf16[128,2048]{1,0:T(8,128)(2,1)S(1)}, bf16[128,2048]{1,0:T(8,128)(2,1)S(1)}, bf16[128,2048]{1,0:T(8,128)(2,1)S(1)}, bf16[128,2048]{1,0:T(8...) custom-call(bf16[128,2048]{1,0:T(8,128)(2,1)} %bitcast.9, ...), custom_call_target="tpu_custom_call", output_to_operand_aliasing={{0}: (4, {}), {1}: (5, {}), {2}: (6, {}), {3}: (7, {})} | custom-call | tf_op jit(solution)/shard_map/filter_partner/pallas_call | solution.py:347
  5.4 3.9 %collective-permute-start = (bf16[128,1024]{1,0:T(8,128)(2,1)S(1)}, bf16[128,1024]{1,0:T(8,128)(2,1)S(1)}, u32[]{:S(2)}, u32[]{:S(2)}) collective-permute-start(bf16[128,1024]{1,0:T(8,128)(2,1)S(1)} %get-tuple-element.47), channel_id=1, source_target_pairs={{0,4},{4,0},{8,12},{12,8},{16,20},{20,16},{24,28},{28,24},{1,5},{5... | collective-permute-start | bytes 786440 | tf_op jit(solution)/shard_map/ppermute | solution.py:403
  9.3 0.0 collective-permute-done.2.other_ref.refs_8_
  9.3 3.2 %filter_own.1.base_ref = f32[512,128]{1,0:T(8,128)S(1)} custom-call(bf16[128,2048]{1,0:T(8,128)(2,1)S(1)} %get-tuple-element.43.q_ref.c_ref.refs_2_.b_ref.refs_1_, bf16[128,2048]{1,0:T(8,128)(2,1)S(1)} %get-tuple-element.41.k_ref.a_ref.refs_0_.d_ref.refs_3_, bf16[128,2048]{1,0:T(8,128)(2,1)S(1)} %get-tuple-element.42.v_ref.b_ref.refs_1_.c_ref.refs_2_, ...), custom_call_target="tpu_custom_call" | custom-call | tf_op jit(solution)/shard_map/filter_own/pallas_call | solution.py:347
  12.5 0.7 %collective-permute-start.3 = (bf16[128,1024]{1,0:T(8,128)(2,1)S(1)}, bf16[128,1024]{1,0:T(8,128)(2,1)S(1)}, u32[]{:S(2)}, u32[]{:S(2)}) collective-permute-start(bf16[128,1024]{1,0:T(8,128)(2,1)S(1)} %get-tuple-element.51), channel_id=1, source_target_pairs={{4,8},{12,16},{20,24},{8,4},{16,12},{24,20},{5,9},{13,17},{21,25},... | collective-permute-start | bytes 786440 | tf_op jit(solution)/shard_map/ppermute | solution.py:409
  13.1 2.9 %collective-permute-start.4 = (f32[64,128]{1,0:T(8,128)S(1)}, f32[64,128]{1,0:T(8,128)S(1)}, u32[]{:S(2)}, u32[]{:S(2)}) collective-permute-start(f32[64,128]{1,0:T(8,128)S(1)} %get-tuple-element.60), channel_id=1, source_target_pairs={{0,4},{4,0},{8,12},{12,8},{16,20},{20,16},{24,28},{28,24},{1,5},{5... | collective-permute-start | bytes 98312 | tf_op jit(solution)/shard_map/ppermute | solution.py:403
  16.0 0.0 collective-permute-done.1.far_ref.refs_7_.other_ref
  16.0 1.7 %filter_far.1 = f32[64,128]{1,0:T(8,128)S(1)} custom-call(bf16[128,2048]{1,0:T(8,128)(2,1)S(1)} %get-tuple-element.43.q_ref.c_ref.refs_2_.b_ref.refs_1_, bf16[128,2048]{1,0:T(8,128)(2,1)S(1)} %get-tuple-element.41.k_ref.a_ref.refs_0_.d_ref.refs_3_, bf16[128,2048]{1,0:T(8,128)(2,1)S(1)} %get-tuple-element.42.v_ref.b_ref.refs_1_.c_ref.refs_2_, ...), custom_call_target="tpu_custom_call" | custom-call | tf_op jit(solution)/shard_map/filter_far/pallas_call | solution.py:347
  17.8 0.0 collective-permute-done.4
  17.8 1.6 %collective-permute-start.5 = (f32[64,128]{1,0:T(8,128)S(1)}, f32[64,128]{1,0:T(8,128)S(1)}, u32[]{:S(2)}, u32[]{:S(2)}) collective-permute-start(f32[64,128]{1,0:T(8,128)S(1)} %add.20), channel_id=1, source_target_pairs={{1,0},{0,1},{3,2},{2,3},{5,4},{4,5},{7,6},{6,7},{9,8},{8,9},{11,10... | collective-permute-start | bytes 98312 | tf_op jit(solution)/shard_map/ppermute | solution.py:433
  19.4 0.0 collective-permute-done.pair_ref.refs_6_
  19.4 1.5 %forward.2 = (bf16[128,2048]{1,0:T(8,128)(2,1)}, bf16[128,2048]{1,0:T(8,128)(2,1)}) custom-call(bf16[128,2048]{1,0:T(8,128)(2,1)S(1)} %get-tuple-element.41.k_ref.a_ref.refs_0_.d_ref.refs_3_, bf16[128,2048]{1,0:T(8,128)(2,1)S(1)} %get-tuple-element.42.v_ref.b_ref.refs_1_.c_ref.refs_2_, ...), custom_call_target="tpu_custom_call" | custom-call | flops 536870912 | bytes 3932160 | tf_op jit(solution)/shard_map/forward/pallas_call | solution.py:329
  20.9 0.9 %collective-permute-done.5 = f32[64,128]{1,0:T(8,128)S(1)} collective-permute-done((f32[64,128]{1,0:T(8,128)S(1)}, f32[64,128]{1,0:T(8,128)S(1)}, u32[]{:S(2)}, u32[]{:S(2)}) %collective-permute-start.5) | collective-permute-done | bytes 32800 | tf_op jit(solution)/shard_map/ppermute | solution.py:433
  21.8 2.6 %collective-permute-start.6 = (f32[64,128]{1,0:T(8,128)S(1)}, f32[64,128]{1,0:T(8,128)S(1)}, u32[]{:S(2)}, u32[]{:S(2)}) collective-permute-start(f32[64,128]{1,0:T(8,128)S(1)} %add.21), channel_id=1, source_target_pairs={{2,0},{3,1},{0,2},{1,3},{6,4},{7,5},{4,6},{5,7},{10,8},{11,9},{8,1... | collective-permute-start | bytes 98312 | tf_op jit(solution)/shard_map/ppermute | solution.py:433
  24.4 1.5 %backward.2 = (bf16[128,2048]{1,0:T(8,128)(2,1)}, bf16[128,2048]{1,0:T(8,128)(2,1)}) custom-call(bf16[128,2048]{1,0:T(8,128)(2,1)S(1)} %get-tuple-element.44.dy_ref.d_ref.refs_3_.a_ref.refs_0_, bf16[128,2048]{1,0:T(8,128)(2,1)S(1)} %get-tuple-element.43.q_ref.c_ref.refs_2_.b_ref.refs_1_, ...), custom_call_target="tpu_custom_call" | custom-call | flops 536870912 | bytes 3932160 | tf_op jit(solution)/shard_map/backward/pallas_call | solution.py:329
  25.9 0.7 %collective-permute-done.6 = f32[64,128]{1,0:T(8,128)S(1)} collective-permute-done((f32[64,128]{1,0:T(8,128)S(1)}, f32[64,128]{1,0:T(8,128)S(1)}, u32[]{:S(2)}, u32[]{:S(2)}) %collective-permute-start.6) | collective-permute-done | bytes 32800 | tf_op jit(solution)/shard_map/ppermute | solution.py:433
  26.6 0.0 collective-permute-done.3.refs_9_
  26.6 1.6 %collective-permute-start.7 = (f32[64,128]{1,0:T(8,128)S(1)}, f32[64,128]{1,0:T(8,128)S(1)}, u32[]{:S(2)}, u32[]{:S(2)}) collective-permute-start(f32[64,128]{1,0:T(8,128)S(1)} %add.22), channel_id=1, source_target_pairs={{8,0},{12,4},{0,8},{4,12},{24,16},{28,20},{16,24},{20,28},{9,1},{1... | collective-permute-start | bytes 98312 | tf_op jit(solution)/shard_map/ppermute | solution.py:433
  28.2 3.0 %forward.3 = (bf16[128,2048]{1,0:T(8,128)(2,1)}, bf16[128,2048]{1,0:T(8,128)(2,1)}) custom-call(bf16[128,2048]{1,0:T(8,128)(2,1)S(1)} %get-tuple-element.41.k_ref.a_ref.refs_0_.d_ref.refs_3_, bf16[128,2048]{1,0:T(8,128)(2,1)S(1)} %get-tuple-element.42.v_ref.b_ref.refs_1_.c_ref.refs_2_, ...), custom_call_target="tpu_custom_call", output_to_operand_aliasing={{0}: (10, {}), {1}: (11, {})} | custom-call | flops 536870912 | bytes 5505024 | tf_op jit(solution)/shard_map/forward/pallas_call | solution.py:329
  31.2 0.0 collective-permute-done.7
  31.3 0.6 %collective-permute-start.8 = (f32[64,128]{1,0:T(8,128)S(1)}, f32[64,128]{1,0:T(8,128)S(1)}, u32[]{:S(2)}, u32[]{:S(2)}) collective-permute-start(f32[64,128]{1,0:T(8,128)S(1)} %add.23), channel_id=1, source_target_pairs={{16,0},{20,4},{24,8},{28,12},{0,16},{4,20},{8,24},{12,28},{17,1},{... | collective-permute-start | bytes 98312 | tf_op jit(solution)/shard_map/ppermute | solution.py:433
  31.9 3.0 %backward.3 = (bf16[128,2048]{1,0:T(8,128)(2,1)}, bf16[128,2048]{1,0:T(8,128)(2,1)}) custom-call(bf16[128,2048]{1,0:T(8,128)(2,1)S(1)} %get-tuple-element.44.dy_ref.d_ref.refs_3_.a_ref.refs_0_, bf16[128,2048]{1,0:T(8,128)(2,1)S(1)} %get-tuple-element.43.q_ref.c_ref.refs_2_.b_ref.refs_1_, ...), custom_call_target="tpu_custom_call", output_to_operand_aliasing={{0}: (10, {}), {1}: (11, {})} | custom-call | flops 536870912 | bytes 5505024 | tf_op jit(solution)/shard_map/backward/pallas_call | solution.py:329
  34.9 0.3 collective-permute-done.8
  35.2 0.0 collective-permute-start.9
  35.3 1.2 %collective-permute-done.9 = f32[64,128]{1,0:T(8,128)S(1)} collective-permute-done((f32[64,128]{1,0:T(8,128)S(1)}, f32[64,128]{1,0:T(8,128)S(1)}, u32[]{:S(2)}, u32[]{:S(2)}) %collective-permute-start.9) | collective-permute-done | bytes 32800 | tf_op jit(solution)/shard_map/ppermute | solution.py:403
  36.4 0.6 %maximum_select_fusion = f32[128,128]{1,0:T(8,128)} fusion(f32[64,128]{1,0:T(8,128)S(1)} %collective-permute-done.9, f32[64,128]{1,0:T(8,128)S(1)} %add.24, pred[]{:T(512)S(6)} %eq.5), kind=kLoop, calls=%fused_computation | loop fusion | flops 49152 | bytes 131073 | tf_op jit(solution)/shard_map/jit(_where)/select_n | solution.py:505
  (5 shorter events, 0.0 us)
Async XLA Ops:
  2.2 7.1 %collective-permute-start.2 = (bf16[128,1024]{1,0:T(8,128)(2,1)S(1)}, bf16[128,1024]{1,0:T(8,128)(2,1)S(1)}, u32[]{:S(2)}, u32[]{:S(2)}) collective-permute-start(bf16[128,1024]{1,0:T(8,128)(2,1)S(1)} %get-tuple-element.49), channel_id=1, source_target_pairs={{0,4},{4,0},{8,12},{12,8},{16,20},{20,16},{24,28},{28,24},{1,5},{5... | collective-permute-start | bytes 786440 | tf_op jit(solution)/shard_map/ppermute | solution.py:403
  2.7 13.3 %collective-permute-start.1 = (bf16[128,1024]{1,0:T(8,128)(2,1)S(1)}, bf16[128,1024]{1,0:T(8,128)(2,1)S(1)}, u32[]{:S(2)}, u32[]{:S(2)}) collective-permute-start(bf16[128,1024]{1,0:T(8,128)(2,1)S(1)} %get-tuple-element.48), channel_id=1, source_target_pairs={{4,8},{12,16},{20,24},{8,4},{16,12},{24,20},{5,9},{13,17},{21,25},... | collective-permute-start | bytes 786440 | tf_op jit(solution)/shard_map/ppermute | solution.py:409
  5.4 14.1 %collective-permute-start = (bf16[128,1024]{1,0:T(8,128)(2,1)S(1)}, bf16[128,1024]{1,0:T(8,128)(2,1)S(1)}, u32[]{:S(2)}, u32[]{:S(2)}) collective-permute-start(bf16[128,1024]{1,0:T(8,128)(2,1)S(1)} %get-tuple-element.47), channel_id=1, source_target_pairs={{0,4},{4,0},{8,12},{12,8},{16,20},{20,16},{24,28},{28,24},{1,5},{5... | collective-permute-start | bytes 786440 | tf_op jit(solution)/shard_map/ppermute | solution.py:403
  12.5 14.2 %collective-permute-start.3 = (bf16[128,1024]{1,0:T(8,128)(2,1)S(1)}, bf16[128,1024]{1,0:T(8,128)(2,1)S(1)}, u32[]{:S(2)}, u32[]{:S(2)}) collective-permute-start(bf16[128,1024]{1,0:T(8,128)(2,1)S(1)} %get-tuple-element.51), channel_id=1, source_target_pairs={{4,8},{12,16},{20,24},{8,4},{16,12},{24,20},{5,9},{13,17},{21,25},... | collective-permute-start | bytes 786440 | tf_op jit(solution)/shard_map/ppermute | solution.py:409
  13.1 4.6 %collective-permute-start.4 = (f32[64,128]{1,0:T(8,128)S(1)}, f32[64,128]{1,0:T(8,128)S(1)}, u32[]{:S(2)}, u32[]{:S(2)}) collective-permute-start(f32[64,128]{1,0:T(8,128)S(1)} %get-tuple-element.60), channel_id=1, source_target_pairs={{0,4},{4,0},{8,12},{12,8},{16,20},{20,16},{24,28},{28,24},{1,5},{5... | collective-permute-start | bytes 98312 | tf_op jit(solution)/shard_map/ppermute | solution.py:403
  17.8 4.0 %collective-permute-start.5 = (f32[64,128]{1,0:T(8,128)S(1)}, f32[64,128]{1,0:T(8,128)S(1)}, u32[]{:S(2)}, u32[]{:S(2)}) collective-permute-start(f32[64,128]{1,0:T(8,128)S(1)} %add.20), channel_id=1, source_target_pairs={{1,0},{0,1},{3,2},{2,3},{5,4},{4,5},{7,6},{6,7},{9,8},{8,9},{11,10... | collective-permute-start | bytes 98312 | tf_op jit(solution)/shard_map/ppermute | solution.py:433
  21.8 4.8 %collective-permute-start.6 = (f32[64,128]{1,0:T(8,128)S(1)}, f32[64,128]{1,0:T(8,128)S(1)}, u32[]{:S(2)}, u32[]{:S(2)}) collective-permute-start(f32[64,128]{1,0:T(8,128)S(1)} %add.21), channel_id=1, source_target_pairs={{2,0},{3,1},{0,2},{1,3},{6,4},{7,5},{4,6},{5,7},{10,8},{11,9},{8,1... | collective-permute-start | bytes 98312 | tf_op jit(solution)/shard_map/ppermute | solution.py:433
  26.6 4.6 %collective-permute-start.7 = (f32[64,128]{1,0:T(8,128)S(1)}, f32[64,128]{1,0:T(8,128)S(1)}, u32[]{:S(2)}, u32[]{:S(2)}) collective-permute-start(f32[64,128]{1,0:T(8,128)S(1)} %add.22), channel_id=1, source_target_pairs={{8,0},{12,4},{0,8},{4,12},{24,16},{28,20},{16,24},{20,28},{9,1},{1... | collective-permute-start | bytes 98312 | tf_op jit(solution)/shard_map/ppermute | solution.py:433
  31.3 4.0 %collective-permute-start.8 = (f32[64,128]{1,0:T(8,128)S(1)}, f32[64,128]{1,0:T(8,128)S(1)}, u32[]{:S(2)}, u32[]{:S(2)}) collective-permute-start(f32[64,128]{1,0:T(8,128)S(1)} %add.23), channel_id=1, source_target_pairs={{16,0},{20,4},{24,8},{28,12},{0,16},{4,20},{8,24},{12,28},{17,1},{... | collective-permute-start | bytes 98312 | tf_op jit(solution)/shard_map/ppermute | solution.py:433
  35.2 1.2 %collective-permute-start.9 = (f32[64,128]{1,0:T(8,128)S(1)}, f32[64,128]{1,0:T(8,128)S(1)}, u32[]{:S(2)}, u32[]{:S(2)}) collective-permute-start(f32[64,128]{1,0:T(8,128)S(1)} %add.24), channel_id=1, source_target_pairs={{0,4},{4,0},{8,12},{12,8},{16,20},{20,16},{24,28},{28,24},{1,5},{5... | collective-permute-start | bytes 98312 | tf_op jit(solution)/shard_map/ppermute | solution.py:403

commit v18 on v17

--- a/solution.py
+++ b/solution.py
@@ -10,7 +10,7 @@
 
 GSIZE = 16
 LANES = 128
-BLOCK = 16
+BLOCK = 32
 STEP = 4
 VMEM = pl.BlockSpec(memory_space=pltpu.VMEM)
 
@@ -160,13 +160,13 @@
                 piece = pairs[:, column * rows : (column + 1) * rows] * for_groups(mask_ref[at : at + BLOCK, :])
                 totals[n] = piece if totals[n] is None else totals[n] + piece
     for total in totals:
-        yield jnp.concatenate(
-            [
-                total[at : at + 8] + pltpu.roll(total[at + 8 : at + 16], rows - 8, 1)
-                for at in range(0, total.shape[0], BLOCK)
-            ],
-            axis=0,
-        )
+        parts = []
+        for at in range(0, total.shape[0], BLOCK):
+            part = total[at : at + 8]
+            for row in range(8, BLOCK, 8):
+                part = part + pltpu.roll(total[at + row : at + row + 8], rows - row, 1)
+            parts.append(part)
+        yield jnp.concatenate(parts, axis=0)
 
 
 def diagonals(sums_ref, groups):

time: 37.3 us -> 35.3 us (0.946)
  Pallas kernels: 17.5 us -> 15.1 us
  starting transfers between devices: 15.1 us -> 15.6 us
    pallas_call x4, Pallas kernels: 8.43 us -> 5.83 us  [own_call(): pl.pallas_call(kernel, out_shape=out_shape, in_specs=[pl.BlockSpec(memory...]
    ppermute x4, starting transfers between devices: 6.41 us -> 6.89 us  [summed_over(): lax.ppermute(total, axis, [(turned(i, k), i) for i in range(size)])]
  transfers between devices with their start and end apart: 10 -> 10, of which waited for: 4 -> 4; matrix products, arithmetic and copies ran while one was open for 0% -> 0% of each run, Pallas kernels for 43% -> 38%
where the time goes in v18:
time: 35.3 us; the launch traced here: 35.1 us
  starting transfers between devices  15.6 us (44%)
  Pallas kernels  15.1 us (43%)
  waiting for transfers between devices  3.07 us (9%)
  between operations  0.76 us (2%)
  other arithmetic  0.67 us (2%)
    pallas_call x4, Pallas kernels, local_call(): pl.pallas_call(kernel, out_shape=out_shape, in_specs=in_specs or [VMEM] *...  9.22 us
    ppermute x4, starting transfers between devices, other_core(): lax.ppermute(block, 'ctx', [(i, i ^ 1) for i in range(lax.axis_size('ctx'...  7.35 us
    ppermute x4, starting transfers between devices, summed_over(): lax.ppermute(total, axis, [(turned(i, k), i) for i in range(size)])  6.89 us
    pallas_call x4, Pallas kernels, own_call(): pl.pallas_call(kernel, out_shape=out_shape, in_specs=[pl.BlockSpec(memory...  5.83 us
    ppermute x4, waiting for transfers between devices, summed_over(): lax.ppermute(total, axis, [(turned(i, k), i) for i in range(size)])  1.87 us
    ppermute x2, starting transfers between devices, next_chip(): return lax.ppermute(block, 'ctx', pairs + [(j, i) for i, j in pairs])  1.34 us
    ppermute x4, waiting for transfers between devices, other_core(): lax.ppermute(block, 'ctx', [(i, i ^ 1) for i in range(lax.axis_size('ctx'...  1.19 us
  transfers between devices with their start and end apart: 10, of which 4 were waited for; matrix products, arithmetic and copies ran while one was open for 0% of the time, Pallas kernels for 38%

profile of v18, /device:TPU:0, one launch (start us, length us, event | category | flops | bytes accessed | tf_op | source)
XLA Modules:
  0.0 35.1 jit_solution(6257165071029639162)
XLA Ops:
  0.6 1.5 %first.1 = (bf16[128,2048]{1,0:T(8,128)(2,1)S(1)}, bf16[128,2048]{1,0:T(8,128)(2,1)S(1)}, bf16[128,2048]{1,0:T(8,128)(2,1)S(1)}, bf16[128,2048]{1,0:T(8,128)(2,1...) custom-call(bf16[128,2048]{1,0:T(8,128)(2,1)} %bitcast.8, ...), custom_call_target="tpu_custom_call" | custom-call | tf_op jit(solution)/shard_map/first/pallas_call | solution.py:347
  2.2 0.5 %collective-permute-start.2 = (bf16[128,1024]{1,0:T(8,128)(2,1)S(1)}, bf16[128,1024]{1,0:T(8,128)(2,1)S(1)}, u32[]{:S(2)}, u32[]{:S(2)}) collective-permute-start(bf16[128,1024]{1,0:T(8,128)(2,1)S(1)} %get-tuple-element.49), channel_id=1, source_target_pairs={{0,4},{4,0},{8,12},{12,8},{16,20},{20,16},{24,28},{28,24},{1,5},{5... | collective-permute-start | bytes 786440 | tf_op jit(solution)/shard_map/ppermute | solution.py:403
  2.7 0.7 %collective-permute-start.1 = (bf16[128,1024]{1,0:T(8,128)(2,1)S(1)}, bf16[128,1024]{1,0:T(8,128)(2,1)S(1)}, u32[]{:S(2)}, u32[]{:S(2)}) collective-permute-start(bf16[128,1024]{1,0:T(8,128)(2,1)S(1)} %get-tuple-element.48), channel_id=1, source_target_pairs={{4,8},{12,16},{20,24},{8,4},{16,12},{24,20},{5,9},{13,17},{21,25},... | collective-permute-start | bytes 786440 | tf_op jit(solution)/shard_map/ppermute | solution.py:409
  3.4 1.5 %filter_partner.1 = (bf16[128,2048]{1,0:T(8,128)(2,1)S(1)}, bf16[128,2048]{1,0:T(8,128)(2,1)S(1)}, bf16[128,2048]{1,0:T(8,128)(2,1)S(1)}, bf16[128,2048]{1,0:T(8...) custom-call(bf16[128,2048]{1,0:T(8,128)(2,1)} %bitcast.9, ...), custom_call_target="tpu_custom_call", output_to_operand_aliasing={{0}: (4, {}), {1}: (5, {}), {2}: (6, {}), {3}: (7, {})} | custom-call | tf_op jit(solution)/shard_map/filter_partner/pallas_call | solution.py:347
  4.9 3.9 %collective-permute-start = (bf16[128,1024]{1,0:T(8,128)(2,1)S(1)}, bf16[128,1024]{1,0:T(8,128)(2,1)S(1)}, u32[]{:S(2)}, u32[]{:S(2)}) collective-permute-start(bf16[128,1024]{1,0:T(8,128)(2,1)S(1)} %get-tuple-element.47), channel_id=1, source_target_pairs={{0,4},{4,0},{8,12},{12,8},{16,20},{20,16},{24,28},{28,24},{1,5},{5... | collective-permute-start | bytes 786440 | tf_op jit(solution)/shard_map/ppermute | solution.py:403
  8.8 0.0 collective-permute-done.2.other_ref.refs_8_
  8.8 1.7 %filter_own.1.base_ref = f32[512,128]{1,0:T(8,128)S(1)} custom-call(bf16[128,2048]{1,0:T(8,128)(2,1)S(1)} %get-tuple-element.43.q_ref.c_ref.refs_2_.b_ref.refs_1_, bf16[128,2048]{1,0:T(8,128)(2,1)S(1)} %get-tuple-element.41.k_ref.a_ref.refs_0_.d_ref.refs_3_, bf16[128,2048]{1,0:T(8,128)(2,1)S(1)} %get-tuple-element.42.v_ref.b_ref.refs_1_.c_ref.refs_2_, ...), custom_call_target="tpu_custom_call" | custom-call | tf_op jit(solution)/shard_map/filter_own/pallas_call | solution.py:347
  10.6 0.7 %collective-permute-start.3 = (bf16[128,1024]{1,0:T(8,128)(2,1)S(1)}, bf16[128,1024]{1,0:T(8,128)(2,1)S(1)}, u32[]{:S(2)}, u32[]{:S(2)}) collective-permute-start(bf16[128,1024]{1,0:T(8,128)(2,1)S(1)} %get-tuple-element.51), channel_id=1, source_target_pairs={{4,8},{12,16},{20,24},{8,4},{16,12},{24,20},{5,9},{13,17},{21,25},... | collective-permute-start | bytes 786440 | tf_op jit(solution)/shard_map/ppermute | solution.py:409
  11.3 2.9 %collective-permute-start.4 = (f32[64,128]{1,0:T(8,128)S(1)}, f32[64,128]{1,0:T(8,128)S(1)}, u32[]{:S(2)}, u32[]{:S(2)}) collective-permute-start(f32[64,128]{1,0:T(8,128)S(1)} %get-tuple-element.60), channel_id=1, source_target_pairs={{0,4},{4,0},{8,12},{12,8},{16,20},{20,16},{24,28},{28,24},{1,5},{5... | collective-permute-start | bytes 98312 | tf_op jit(solution)/shard_map/ppermute | solution.py:403
  14.2 0.0 collective-permute-done.1.far_ref.refs_7_.other_ref
  14.2 1.0 %filter_far.1 = f32[64,128]{1,0:T(8,128)S(1)} custom-call(bf16[128,2048]{1,0:T(8,128)(2,1)S(1)} %get-tuple-element.43.q_ref.c_ref.refs_2_.b_ref.refs_1_, bf16[128,2048]{1,0:T(8,128)(2,1)S(1)} %get-tuple-element.41.k_ref.a_ref.refs_0_.d_ref.refs_3_, bf16[128,2048]{1,0:T(8,128)(2,1)S(1)} %get-tuple-element.42.v_ref.b_ref.refs_1_.c_ref.refs_2_, ...), custom_call_target="tpu_custom_call" | custom-call | tf_op jit(solution)/shard_map/filter_far/pallas_call | solution.py:347
  15.2 0.0 collective-permute-done.4
  15.2 1.6 %collective-permute-start.5 = (f32[64,128]{1,0:T(8,128)S(1)}, f32[64,128]{1,0:T(8,128)S(1)}, u32[]{:S(2)}, u32[]{:S(2)}) collective-permute-start(f32[64,128]{1,0:T(8,128)S(1)} %add.20), channel_id=1, source_target_pairs={{1,0},{0,1},{3,2},{2,3},{5,4},{4,5},{7,6},{6,7},{9,8},{8,9},{11,10... | collective-permute-start | bytes 98312 | tf_op jit(solution)/shard_map/ppermute | solution.py:433
  16.9 0.0 collective-permute-done.pair_ref.refs_6_
  16.9 1.5 %forward.2 = (bf16[128,2048]{1,0:T(8,128)(2,1)}, bf16[128,2048]{1,0:T(8,128)(2,1)}) custom-call(bf16[128,2048]{1,0:T(8,128)(2,1)S(1)} %get-tuple-element.41.k_ref.a_ref.refs_0_.d_ref.refs_3_, bf16[128,2048]{1,0:T(8,128)(2,1)S(1)} %get-tuple-element.42.v_ref.b_ref.refs_1_.c_ref.refs_2_, ...), custom_call_target="tpu_custom_call" | custom-call | flops 536870912 | bytes 3932160 | tf_op jit(solution)/shard_map/forward/pallas_call | solution.py:329
  18.4 0.8 %collective-permute-done.5 = f32[64,128]{1,0:T(8,128)S(1)} collective-permute-done((f32[64,128]{1,0:T(8,128)S(1)}, f32[64,128]{1,0:T(8,128)S(1)}, u32[]{:S(2)}, u32[]{:S(2)}) %collective-permute-start.5) | collective-permute-done | bytes 32800 | tf_op jit(solution)/shard_map/ppermute | solution.py:433
  19.2 2.6 %collective-permute-start.6 = (f32[64,128]{1,0:T(8,128)S(1)}, f32[64,128]{1,0:T(8,128)S(1)}, u32[]{:S(2)}, u32[]{:S(2)}) collective-permute-start(f32[64,128]{1,0:T(8,128)S(1)} %add.21), channel_id=1, source_target_pairs={{2,0},{3,1},{0,2},{1,3},{6,4},{7,5},{4,6},{5,7},{10,8},{11,9},{8,1... | collective-permute-start | bytes 98312 | tf_op jit(solution)/shard_map/ppermute | solution.py:433
  21.8 1.5 %backward.2 = (bf16[128,2048]{1,0:T(8,128)(2,1)}, bf16[128,2048]{1,0:T(8,128)(2,1)}) custom-call(bf16[128,2048]{1,0:T(8,128)(2,1)S(1)} %get-tuple-element.44.dy_ref.d_ref.refs_3_.a_ref.refs_0_, bf16[128,2048]{1,0:T(8,128)(2,1)S(1)} %get-tuple-element.43.q_ref.c_ref.refs_2_.b_ref.refs_1_, ...), custom_call_target="tpu_custom_call" | custom-call | flops 536870912 | bytes 3932160 | tf_op jit(solution)/shard_map/backward/pallas_call | solution.py:329
  23.3 0.7 %collective-permute-done.6 = f32[64,128]{1,0:T(8,128)S(1)} collective-permute-done((f32[64,128]{1,0:T(8,128)S(1)}, f32[64,128]{1,0:T(8,128)S(1)}, u32[]{:S(2)}, u32[]{:S(2)}) %collective-permute-start.6) | collective-permute-done | bytes 32800 | tf_op jit(solution)/shard_map/ppermute | solution.py:433
  24.0 0.0 collective-permute-done.3.refs_9_
  24.0 2.1 %collective-permute-start.7 = (f32[64,128]{1,0:T(8,128)S(1)}, f32[64,128]{1,0:T(8,128)S(1)}, u32[]{:S(2)}, u32[]{:S(2)}) collective-permute-start(f32[64,128]{1,0:T(8,128)S(1)} %add.22), channel_id=1, source_target_pairs={{8,0},{12,4},{0,8},{4,12},{24,16},{28,20},{16,24},{20,28},{9,1},{1... | collective-permute-start | bytes 98312 | tf_op jit(solution)/shard_map/ppermute | solution.py:433
  26.1 3.1 %forward.3 = (bf16[128,2048]{1,0:T(8,128)(2,1)}, bf16[128,2048]{1,0:T(8,128)(2,1)}) custom-call(bf16[128,2048]{1,0:T(8,128)(2,1)S(1)} %get-tuple-element.41.k_ref.a_ref.refs_0_.d_ref.refs_3_, bf16[128,2048]{1,0:T(8,128)(2,1)S(1)} %get-tuple-element.42.v_ref.b_ref.refs_1_.c_ref.refs_2_, ...), custom_call_target="tpu_custom_call", output_to_operand_aliasing={{0}: (10, {}), {1}: (11, {})} | custom-call | flops 536870912 | bytes 5505024 | tf_op jit(solution)/shard_map/forward/pallas_call | solution.py:329
  29.3 0.0 collective-permute-done.7
  29.3 0.6 %collective-permute-start.8 = (f32[64,128]{1,0:T(8,128)S(1)}, f32[64,128]{1,0:T(8,128)S(1)}, u32[]{:S(2)}, u32[]{:S(2)}) collective-permute-start(f32[64,128]{1,0:T(8,128)S(1)} %add.23), channel_id=1, source_target_pairs={{16,0},{20,4},{24,8},{28,12},{0,16},{4,20},{8,24},{12,28},{17,1},{... | collective-permute-start | bytes 98312 | tf_op jit(solution)/shard_map/ppermute | solution.py:433
  29.9 3.1 %backward.3 = (bf16[128,2048]{1,0:T(8,128)(2,1)}, bf16[128,2048]{1,0:T(8,128)(2,1)}) custom-call(bf16[128,2048]{1,0:T(8,128)(2,1)S(1)} %get-tuple-element.44.dy_ref.d_ref.refs_3_.a_ref.refs_0_, bf16[128,2048]{1,0:T(8,128)(2,1)S(1)} %get-tuple-element.43.q_ref.c_ref.refs_2_.b_ref.refs_1_, ...), custom_call_target="tpu_custom_call", output_to_operand_aliasing={{0}: (10, {}), {1}: (11, {})} | custom-call | flops 536870912 | bytes 5505024 | tf_op jit(solution)/shard_map/backward/pallas_call | solution.py:329
  33.0 0.3 collective-permute-done.8
  33.3 0.0 collective-permute-start.9
  33.3 1.2 %collective-permute-done.9 = f32[64,128]{1,0:T(8,128)S(1)} collective-permute-done((f32[64,128]{1,0:T(8,128)S(1)}, f32[64,128]{1,0:T(8,128)S(1)}, u32[]{:S(2)}, u32[]{:S(2)}) %collective-permute-start.9) | collective-permute-done | bytes 32800 | tf_op jit(solution)/shard_map/ppermute | solution.py:403
  34.5 0.6 %maximum_select_fusion = f32[128,128]{1,0:T(8,128)} fusion(f32[64,128]{1,0:T(8,128)S(1)} %collective-permute-done.9, f32[64,128]{1,0:T(8,128)S(1)} %add.24, pred[]{:T(512)S(6)} %eq.5), kind=kLoop, calls=%fused_computation | loop fusion | flops 49152 | bytes 131073 | tf_op jit(solution)/shard_map/jit(_where)/select_n | solution.py:505
  (5 shorter events, 0.0 us)
Async XLA Ops:
  2.2 6.6 %collective-permute-start.2 = (bf16[128,1024]{1,0:T(8,128)(2,1)S(1)}, bf16[128,1024]{1,0:T(8,128)(2,1)S(1)}, u32[]{:S(2)}, u32[]{:S(2)}) collective-permute-start(bf16[128,1024]{1,0:T(8,128)(2,1)S(1)} %get-tuple-element.49), channel_id=1, source_target_pairs={{0,4},{4,0},{8,12},{12,8},{16,20},{20,16},{24,28},{28,24},{1,5},{5... | collective-permute-start | bytes 786440 | tf_op jit(solution)/shard_map/ppermute | solution.py:403
  2.7 11.5 %collective-permute-start.1 = (bf16[128,1024]{1,0:T(8,128)(2,1)S(1)}, bf16[128,1024]{1,0:T(8,128)(2,1)S(1)}, u32[]{:S(2)}, u32[]{:S(2)}) collective-permute-start(bf16[128,1024]{1,0:T(8,128)(2,1)S(1)} %get-tuple-element.48), channel_id=1, source_target_pairs={{4,8},{12,16},{20,24},{8,4},{16,12},{24,20},{5,9},{13,17},{21,25},... | collective-permute-start | bytes 786440 | tf_op jit(solution)/shard_map/ppermute | solution.py:409
  4.9 12.0 %collective-permute-start = (bf16[128,1024]{1,0:T(8,128)(2,1)S(1)}, bf16[128,1024]{1,0:T(8,128)(2,1)S(1)}, u32[]{:S(2)}, u32[]{:S(2)}) collective-permute-start(bf16[128,1024]{1,0:T(8,128)(2,1)S(1)} %get-tuple-element.47), channel_id=1, source_target_pairs={{0,4},{4,0},{8,12},{12,8},{16,20},{20,16},{24,28},{28,24},{1,5},{5... | collective-permute-start | bytes 786440 | tf_op jit(solution)/shard_map/ppermute | solution.py:403
  10.6 13.5 %collective-permute-start.3 = (bf16[128,1024]{1,0:T(8,128)(2,1)S(1)}, bf16[128,1024]{1,0:T(8,128)(2,1)S(1)}, u32[]{:S(2)}, u32[]{:S(2)}) collective-permute-start(bf16[128,1024]{1,0:T(8,128)(2,1)S(1)} %get-tuple-element.51), channel_id=1, source_target_pairs={{4,8},{12,16},{20,24},{8,4},{16,12},{24,20},{5,9},{13,17},{21,25},... | collective-permute-start | bytes 786440 | tf_op jit(solution)/shard_map/ppermute | solution.py:409
  11.3 3.9 %collective-permute-start.4 = (f32[64,128]{1,0:T(8,128)S(1)}, f32[64,128]{1,0:T(8,128)S(1)}, u32[]{:S(2)}, u32[]{:S(2)}) collective-permute-start(f32[64,128]{1,0:T(8,128)S(1)} %get-tuple-element.60), channel_id=1, source_target_pairs={{0,4},{4,0},{8,12},{12,8},{16,20},{20,16},{24,28},{28,24},{1,5},{5... | collective-permute-start | bytes 98312 | tf_op jit(solution)/shard_map/ppermute | solution.py:403
  15.2 4.0 %collective-permute-start.5 = (f32[64,128]{1,0:T(8,128)S(1)}, f32[64,128]{1,0:T(8,128)S(1)}, u32[]{:S(2)}, u32[]{:S(2)}) collective-permute-start(f32[64,128]{1,0:T(8,128)S(1)} %add.20), channel_id=1, source_target_pairs={{1,0},{0,1},{3,2},{2,3},{5,4},{4,5},{7,6},{6,7},{9,8},{8,9},{11,10... | collective-permute-start | bytes 98312 | tf_op jit(solution)/shard_map/ppermute | solution.py:433
  19.2 4.8 %collective-permute-start.6 = (f32[64,128]{1,0:T(8,128)S(1)}, f32[64,128]{1,0:T(8,128)S(1)}, u32[]{:S(2)}, u32[]{:S(2)}) collective-permute-start(f32[64,128]{1,0:T(8,128)S(1)} %add.21), channel_id=1, source_target_pairs={{2,0},{3,1},{0,2},{1,3},{6,4},{7,5},{4,6},{5,7},{10,8},{11,9},{8,1... | collective-permute-start | bytes 98312 | tf_op jit(solution)/shard_map/ppermute | solution.py:433
  24.0 5.3 %collective-permute-start.7 = (f32[64,128]{1,0:T(8,128)S(1)}, f32[64,128]{1,0:T(8,128)S(1)}, u32[]{:S(2)}, u32[]{:S(2)}) collective-permute-start(f32[64,128]{1,0:T(8,128)S(1)} %add.22), channel_id=1, source_target_pairs={{8,0},{12,4},{0,8},{4,12},{24,16},{28,20},{16,24},{20,28},{9,1},{1... | collective-permute-start | bytes 98312 | tf_op jit(solution)/shard_map/ppermute | solution.py:433
  29.3 4.0 %collective-permute-start.8 = (f32[64,128]{1,0:T(8,128)S(1)}, f32[64,128]{1,0:T(8,128)S(1)}, u32[]{:S(2)}, u32[]{:S(2)}) collective-permute-start(f32[64,128]{1,0:T(8,128)S(1)} %add.23), channel_id=1, source_target_pairs={{16,0},{20,4},{24,8},{28,12},{0,16},{4,20},{8,24},{12,28},{17,1},{... | collective-permute-start | bytes 98312 | tf_op jit(solution)/shard_map/ppermute | solution.py:433
  33.3 1.2 %collective-permute-start.9 = (f32[64,128]{1,0:T(8,128)S(1)}, f32[64,128]{1,0:T(8,128)S(1)}, u32[]{:S(2)}, u32[]{:S(2)}) collective-permute-start(f32[64,128]{1,0:T(8,128)S(1)} %add.24), channel_id=1, source_target_pairs={{0,4},{4,0},{8,12},{12,8},{16,20},{20,16},{24,28},{28,24},{1,5},{5... | collective-permute-start | bytes 98312 | tf_op jit(solution)/shard_map/ppermute | solution.py:403

commit v19 on v18

--- a/solution.py
+++ b/solution.py
@@ -474,7 +474,6 @@
     mine = mine + other_core(theirs)
 
     half_tiles = q.shape[1] // 2 // LANES
-    few = max(half_tiles // 2, 1)
     first_others, later_others = (pair, far), (later_pair, later_far)
 
     def forward(spans, others, outs=None):
@@ -485,20 +484,16 @@
 
     for n, place in enumerate(rounds_over_chips()):
         if n == 0:
-            some_forward = forward([(0, few)], [first_others])
+            some_forward = forward([(0, half_tiles)], [first_others])
         if n == 1:
             mine = after(mine, *some_forward)
-            some_backward = backward([(half_tiles, few)], [first_others])
+            some_backward = backward([(half_tiles, half_tiles)], [first_others])
         if n == 2:
             mine = after(mine, *some_backward, later_far, later_pair)
-            mixed, grad_q = forward(
-                [(few, half_tiles - few), (half_tiles, half_tiles)], [first_others, later_others], some_forward
-            )
+            mixed, grad_q = forward([(half_tiles, half_tiles)], [later_others], some_forward)
         if n == 3:
             mine = after(mine, mixed, grad_q)
-            grad_k, grad_v = backward(
-                [(half_tiles + few, half_tiles - few), (0, half_tiles)], [first_others, later_others], some_backward
-            )
+            grad_k, grad_v = backward([(0, half_tiles)], [later_others], some_backward)
         mine = summed_over(mine, *place)
     mine = after(mine, grad_k, grad_v)
     halves = [mine, other_core(mine)]

time: 35.3 us -> 34.8 us (0.986)
  waiting for transfers between devices: 3.07 us -> 1.24 us
  starting transfers between devices: 15.6 us -> 16.9 us
    ppermute x4, waiting for transfers between devices: 1.87 us -> 0.05 us  [summed_over(): lax.ppermute(total, axis, [(turned(i, k), i) for i in range(size)])]
    ppermute x4, starting transfers between devices: 6.89 us -> 8.11 us  [summed_over(): lax.ppermute(total, axis, [(turned(i, k), i) for i in range(size)])]
  transfers between devices with their start and end apart: 10 -> 10, of which waited for: 4 -> 1; matrix products, arithmetic and copies ran while one was open for 0% -> 0% of each run, Pallas kernels for 38% -> 39%
where the time goes in v19:
time: 34.8 us; the launch traced here: 34.6 us
  starting transfers between devices  16.9 us (49%)
  Pallas kernels  15 us (43%)
  waiting for transfers between devices  1.24 us (4%)
  between operations  0.79 us (2%)
  other arithmetic  0.67 us (2%)
    pallas_call x4, Pallas kernels, local_call(): pl.pallas_call(kernel, out_shape=out_shape, in_specs=in_specs or [VMEM] *...  9.17 us
    ppermute x4, starting transfers between devices, summed_over(): lax.ppermute(total, axis, [(turned(i, k), i) for i in range(size)])  8.11 us
    ppermute x4, starting transfers between devices, other_core(): lax.ppermute(block, 'ctx', [(i, i ^ 1) for i in range(lax.axis_size('ctx'...  7.42 us
    pallas_call x4, Pallas kernels, own_call(): pl.pallas_call(kernel, out_shape=out_shape, in_specs=[pl.BlockSpec(memory...  5.83 us
    ppermute x2, starting transfers between devices, next_chip(): return lax.ppermute(block, 'ctx', pairs + [(j, i) for i, j in pairs])  1.34 us
    ppermute x4, waiting for transfers between devices, other_core(): lax.ppermute(block, 'ctx', [(i, i ^ 1) for i in range(lax.axis_size('ctx'...  1.19 us
  transfers between devices with their start and end apart: 10, of which 1 were waited for; matrix products, arithmetic and copies ran while one was open for 0% of the time, Pallas kernels for 39%

profile of v19, /device:TPU:0, one launch (start us, length us, event | category | flops | bytes accessed | tf_op | source)
XLA Modules:
  0.0 34.6 jit_solution(12134478357986932375)
XLA Ops:
  0.6 1.5 %first.1 = (bf16[128,2048]{1,0:T(8,128)(2,1)S(1)}, bf16[128,2048]{1,0:T(8,128)(2,1)S(1)}, bf16[128,2048]{1,0:T(8,128)(2,1)S(1)}, bf16[128,2048]{1,0:T(8,128)(2,1...) custom-call(bf16[128,2048]{1,0:T(8,128)(2,1)} %bitcast.8, ...), custom_call_target="tpu_custom_call" | custom-call | tf_op jit(solution)/shard_map/first/pallas_call | solution.py:347
  2.2 0.5 %collective-permute-start = (bf16[128,1024]{1,0:T(8,128)(2,1)S(1)}, bf16[128,1024]{1,0:T(8,128)(2,1)S(1)}, u32[]{:S(2)}, u32[]{:S(2)}) collective-permute-start(bf16[128,1024]{1,0:T(8,128)(2,1)S(1)} %get-tuple-element.47), channel_id=1, source_target_pairs={{0,4},{4,0},{8,12},{12,8},{16,20},{20,16},{24,28},{28,24},{1,5},{5... | collective-permute-start | bytes 786440 | tf_op jit(solution)/shard_map/ppermute | solution.py:403
  2.7 0.7 %collective-permute-start.3 = (bf16[128,1024]{1,0:T(8,128)(2,1)S(1)}, bf16[128,1024]{1,0:T(8,128)(2,1)S(1)}, u32[]{:S(2)}, u32[]{:S(2)}) collective-permute-start(bf16[128,1024]{1,0:T(8,128)(2,1)S(1)} %get-tuple-element.51), channel_id=1, source_target_pairs={{4,8},{12,16},{20,24},{8,4},{16,12},{24,20},{5,9},{13,17},{21,25},... | collective-permute-start | bytes 786440 | tf_op jit(solution)/shard_map/ppermute | solution.py:409
  3.4 1.5 %filter_partner.1 = (bf16[128,2048]{1,0:T(8,128)(2,1)S(1)}, bf16[128,2048]{1,0:T(8,128)(2,1)S(1)}, bf16[128,2048]{1,0:T(8,128)(2,1)S(1)}, bf16[128,2048]{1,0:T(8...) custom-call(bf16[128,2048]{1,0:T(8,128)(2,1)} %bitcast.9, ...), custom_call_target="tpu_custom_call", output_to_operand_aliasing={{0}: (4, {}), {1}: (5, {}), {2}: (6, {}), {3}: (7, {})} | custom-call | tf_op jit(solution)/shard_map/filter_partner/pallas_call | solution.py:347
  4.9 3.9 %collective-permute-start.2 = (bf16[128,1024]{1,0:T(8,128)(2,1)S(1)}, bf16[128,1024]{1,0:T(8,128)(2,1)S(1)}, u32[]{:S(2)}, u32[]{:S(2)}) collective-permute-start(bf16[128,1024]{1,0:T(8,128)(2,1)S(1)} %get-tuple-element.50), channel_id=1, source_target_pairs={{0,4},{4,0},{8,12},{12,8},{16,20},{20,16},{24,28},{28,24},{1,5},{5... | collective-permute-start | bytes 786440 | tf_op jit(solution)/shard_map/ppermute | solution.py:403
  8.8 0.0 collective-permute-done.other_ref.refs_6_
  8.8 1.7 %filter_own.1.base_ref = f32[512,128]{1,0:T(8,128)S(1)} custom-call(bf16[128,2048]{1,0:T(8,128)(2,1)S(1)} %get-tuple-element.43.q_ref.c_ref.refs_2_.b_ref.refs_1_, bf16[128,2048]{1,0:T(8,128)(2,1)S(1)} %get-tuple-element.41.k_ref.a_ref.refs_0_.d_ref.refs_3_, bf16[128,2048]{1,0:T(8,128)(2,1)S(1)} %get-tuple-element.42.v_ref.b_ref.refs_1_.c_ref.refs_2_, ...), custom_call_target="tpu_custom_call" | custom-call | tf_op jit(solution)/shard_map/filter_own/pallas_call | solution.py:347
  10.6 0.7 %collective-permute-start.1 = (bf16[128,1024]{1,0:T(8,128)(2,1)S(1)}, bf16[128,1024]{1,0:T(8,128)(2,1)S(1)}, u32[]{:S(2)}, u32[]{:S(2)}) collective-permute-start(bf16[128,1024]{1,0:T(8,128)(2,1)S(1)} %get-tuple-element.49), channel_id=1, source_target_pairs={{4,8},{12,16},{20,24},{8,4},{16,12},{24,20},{5,9},{13,17},{21,25},... | collective-permute-start | bytes 786440 | tf_op jit(solution)/shard_map/ppermute | solution.py:409
  11.3 2.9 %collective-permute-start.4 = (f32[64,128]{1,0:T(8,128)S(1)}, f32[64,128]{1,0:T(8,128)S(1)}, u32[]{:S(2)}, u32[]{:S(2)}) collective-permute-start(f32[64,128]{1,0:T(8,128)S(1)} %get-tuple-element.60), channel_id=1, source_target_pairs={{0,4},{4,0},{8,12},{12,8},{16,20},{20,16},{24,28},{28,24},{1,5},{5... | collective-permute-start | bytes 98312 | tf_op jit(solution)/shard_map/ppermute | solution.py:403
  14.2 0.0 collective-permute-done.3.far_ref.other_ref
  14.2 1.0 %filter_far.1 = f32[64,128]{1,0:T(8,128)S(1)} custom-call(bf16[128,2048]{1,0:T(8,128)(2,1)S(1)} %get-tuple-element.43.q_ref.c_ref.refs_2_.b_ref.refs_1_, bf16[128,2048]{1,0:T(8,128)(2,1)S(1)} %get-tuple-element.41.k_ref.a_ref.refs_0_.d_ref.refs_3_, bf16[128,2048]{1,0:T(8,128)(2,1)S(1)} %get-tuple-element.42.v_ref.b_ref.refs_1_.c_ref.refs_2_, ...), custom_call_target="tpu_custom_call" | custom-call | tf_op jit(solution)/shard_map/filter_far/pallas_call | solution.py:347
  15.2 0.0 collective-permute-done.4
  15.2 1.6 %collective-permute-start.5 = (f32[64,128]{1,0:T(8,128)S(1)}, f32[64,128]{1,0:T(8,128)S(1)}, u32[]{:S(2)}, u32[]{:S(2)}) collective-permute-start(f32[64,128]{1,0:T(8,128)S(1)} %add.20), channel_id=1, source_target_pairs={{1,0},{0,1},{3,2},{2,3},{5,4},{4,5},{7,6},{6,7},{9,8},{8,9},{11,10... | collective-permute-start | bytes 98312 | tf_op jit(solution)/shard_map/ppermute | solution.py:433
  16.9 0.0 collective-permute-done.2.pair_ref
  16.9 2.3 %forward.2 = (bf16[128,2048]{1,0:T(8,128)(2,1)}, bf16[128,2048]{1,0:T(8,128)(2,1)}) custom-call(bf16[128,2048]{1,0:T(8,128)(2,1)S(1)} %get-tuple-element.41.k_ref.a_ref.refs_0_.d_ref.refs_3_, bf16[128,2048]{1,0:T(8,128)(2,1)S(1)} %get-tuple-element.42.v_ref.b_ref.refs_1_.c_ref.refs_2_, ...), custom_call_target="tpu_custom_call" | custom-call | flops 536870912 | bytes 3932160 | tf_op jit(solution)/shard_map/forward/pallas_call | solution.py:329
  19.2 0.0 collective-permute-done.5
  19.2 2.6 %collective-permute-start.6 = (f32[64,128]{1,0:T(8,128)S(1)}, f32[64,128]{1,0:T(8,128)S(1)}, u32[]{:S(2)}, u32[]{:S(2)}) collective-permute-start(f32[64,128]{1,0:T(8,128)S(1)} %add.21), channel_id=1, source_target_pairs={{2,0},{3,1},{0,2},{1,3},{6,4},{7,5},{4,6},{5,7},{10,8},{11,9},{8,1... | collective-permute-start | bytes 98312 | tf_op jit(solution)/shard_map/ppermute | solution.py:433
  21.8 2.3 %backward.2 = (bf16[128,2048]{1,0:T(8,128)(2,1)}, bf16[128,2048]{1,0:T(8,128)(2,1)}) custom-call(bf16[128,2048]{1,0:T(8,128)(2,1)S(1)} %get-tuple-element.44.dy_ref.d_ref.refs_3_.a_ref.refs_0_, bf16[128,2048]{1,0:T(8,128)(2,1)S(1)} %get-tuple-element.43.q_ref.c_ref.refs_2_.b_ref.refs_1_, ...), custom_call_target="tpu_custom_call" | custom-call | flops 536870912 | bytes 3932160 | tf_op jit(solution)/shard_map/backward/pallas_call | solution.py:329
  24.1 0.0 collective-permute-done.6
  24.2 0.0 collective-permute-done.1.refs_7_
  24.2 2.0 %collective-permute-start.7 = (f32[64,128]{1,0:T(8,128)S(1)}, f32[64,128]{1,0:T(8,128)S(1)}, u32[]{:S(2)}, u32[]{:S(2)}) collective-permute-start(f32[64,128]{1,0:T(8,128)S(1)} %add.22), channel_id=1, source_target_pairs={{8,0},{12,4},{0,8},{4,12},{24,16},{28,20},{16,24},{20,28},{9,1},{1... | collective-permute-start | bytes 98312 | tf_op jit(solution)/shard_map/ppermute | solution.py:433
  26.1 2.3 %forward.3 = (bf16[128,2048]{1,0:T(8,128)(2,1)}, bf16[128,2048]{1,0:T(8,128)(2,1)}) custom-call(bf16[128,2048]{1,0:T(8,128)(2,1)S(1)} %get-tuple-element.41.k_ref.a_ref.refs_0_.d_ref.refs_3_, bf16[128,2048]{1,0:T(8,128)(2,1)S(1)} %get-tuple-element.42.v_ref.b_ref.refs_1_.c_ref.refs_2_, ...), custom_call_target="tpu_custom_call", output_to_operand_aliasing={{0}: (8, {}), {1}: (9, {})} | custom-call | flops 536870912 | bytes 4980736 | tf_op jit(solution)/shard_map/forward/pallas_call | solution.py:329
  28.4 0.0 collective-permute-done.7
  28.5 1.9 %collective-permute-start.8 = (f32[64,128]{1,0:T(8,128)S(1)}, f32[64,128]{1,0:T(8,128)S(1)}, u32[]{:S(2)}, u32[]{:S(2)}) collective-permute-start(f32[64,128]{1,0:T(8,128)S(1)} %add.23), channel_id=1, source_target_pairs={{16,0},{20,4},{24,8},{28,12},{0,16},{4,20},{8,24},{12,28},{17,1},{... | collective-permute-start | bytes 98312 | tf_op jit(solution)/shard_map/ppermute | solution.py:433
  30.3 2.3 %backward.3 = (bf16[128,2048]{1,0:T(8,128)(2,1)}, bf16[128,2048]{1,0:T(8,128)(2,1)}) custom-call(bf16[128,2048]{1,0:T(8,128)(2,1)S(1)} %get-tuple-element.44.dy_ref.d_ref.refs_3_.a_ref.refs_0_, bf16[128,2048]{1,0:T(8,128)(2,1)S(1)} %get-tuple-element.43.q_ref.c_ref.refs_2_.b_ref.refs_1_, ...), custom_call_target="tpu_custom_call", output_to_operand_aliasing={{0}: (8, {}), {1}: (9, {})} | custom-call | flops 536870912 | bytes 4980736 | tf_op jit(solution)/shard_map/backward/pallas_call | solution.py:329
  32.6 0.0 collective-permute-done.8
  32.7 0.1 collective-permute-start.9
  32.7 1.2 %collective-permute-done.9 = f32[64,128]{1,0:T(8,128)S(1)} collective-permute-done((f32[64,128]{1,0:T(8,128)S(1)}, f32[64,128]{1,0:T(8,128)S(1)}, u32[]{:S(2)}, u32[]{:S(2)}) %collective-permute-start.9) | collective-permute-done | bytes 32800 | tf_op jit(solution)/shard_map/ppermute | solution.py:403
  33.9 0.6 %maximum_select_fusion = f32[128,128]{1,0:T(8,128)} fusion(f32[64,128]{1,0:T(8,128)S(1)} %collective-permute-done.9, f32[64,128]{1,0:T(8,128)S(1)} %add.24, pred[]{:T(512)S(6)} %eq.5), kind=kLoop, calls=%fused_computation | loop fusion | flops 49152 | bytes 131073 | tf_op jit(solution)/shard_map/jit(_where)/select_n | solution.py:500
  (5 shorter events, 0.0 us)
Async XLA Ops:
  2.2 6.6 %collective-permute-start = (bf16[128,1024]{1,0:T(8,128)(2,1)S(1)}, bf16[128,1024]{1,0:T(8,128)(2,1)S(1)}, u32[]{:S(2)}, u32[]{:S(2)}) collective-permute-start(bf16[128,1024]{1,0:T(8,128)(2,1)S(1)} %get-tuple-element.47), channel_id=1, source_target_pairs={{0,4},{4,0},{8,12},{12,8},{16,20},{20,16},{24,28},{28,24},{1,5},{5... | collective-permute-start | bytes 786440 | tf_op jit(solution)/shard_map/ppermute | solution.py:403
  2.7 11.5 %collective-permute-start.3 = (bf16[128,1024]{1,0:T(8,128)(2,1)S(1)}, bf16[128,1024]{1,0:T(8,128)(2,1)S(1)}, u32[]{:S(2)}, u32[]{:S(2)}) collective-permute-start(bf16[128,1024]{1,0:T(8,128)(2,1)S(1)} %get-tuple-element.51), channel_id=1, source_target_pairs={{4,8},{12,16},{20,24},{8,4},{16,12},{24,20},{5,9},{13,17},{21,25},... | collective-permute-start | bytes 786440 | tf_op jit(solution)/shard_map/ppermute | solution.py:409
  4.9 12.0 %collective-permute-start.2 = (bf16[128,1024]{1,0:T(8,128)(2,1)S(1)}, bf16[128,1024]{1,0:T(8,128)(2,1)S(1)}, u32[]{:S(2)}, u32[]{:S(2)}) collective-permute-start(bf16[128,1024]{1,0:T(8,128)(2,1)S(1)} %get-tuple-element.50), channel_id=1, source_target_pairs={{0,4},{4,0},{8,12},{12,8},{16,20},{20,16},{24,28},{28,24},{1,5},{5... | collective-permute-start | bytes 786440 | tf_op jit(solution)/shard_map/ppermute | solution.py:403
  10.6 13.6 %collective-permute-start.1 = (bf16[128,1024]{1,0:T(8,128)(2,1)S(1)}, bf16[128,1024]{1,0:T(8,128)(2,1)S(1)}, u32[]{:S(2)}, u32[]{:S(2)}) collective-permute-start(bf16[128,1024]{1,0:T(8,128)(2,1)S(1)} %get-tuple-element.49), channel_id=1, source_target_pairs={{4,8},{12,16},{20,24},{8,4},{16,12},{24,20},{5,9},{13,17},{21,25},... | collective-permute-start | bytes 786440 | tf_op jit(solution)/shard_map/ppermute | solution.py:409
  11.3 3.9 %collective-permute-start.4 = (f32[64,128]{1,0:T(8,128)S(1)}, f32[64,128]{1,0:T(8,128)S(1)}, u32[]{:S(2)}, u32[]{:S(2)}) collective-permute-start(f32[64,128]{1,0:T(8,128)S(1)} %get-tuple-element.60), channel_id=1, source_target_pairs={{0,4},{4,0},{8,12},{12,8},{16,20},{20,16},{24,28},{28,24},{1,5},{5... | collective-permute-start | bytes 98312 | tf_op jit(solution)/shard_map/ppermute | solution.py:403
  15.2 4.0 %collective-permute-start.5 = (f32[64,128]{1,0:T(8,128)S(1)}, f32[64,128]{1,0:T(8,128)S(1)}, u32[]{:S(2)}, u32[]{:S(2)}) collective-permute-start(f32[64,128]{1,0:T(8,128)S(1)} %add.20), channel_id=1, source_target_pairs={{1,0},{0,1},{3,2},{2,3},{5,4},{4,5},{7,6},{6,7},{9,8},{8,9},{11,10... | collective-permute-start | bytes 98312 | tf_op jit(solution)/shard_map/ppermute | solution.py:433
  19.2 4.9 %collective-permute-start.6 = (f32[64,128]{1,0:T(8,128)S(1)}, f32[64,128]{1,0:T(8,128)S(1)}, u32[]{:S(2)}, u32[]{:S(2)}) collective-permute-start(f32[64,128]{1,0:T(8,128)S(1)} %add.21), channel_id=1, source_target_pairs={{2,0},{3,1},{0,2},{1,3},{6,4},{7,5},{4,6},{5,7},{10,8},{11,9},{8,1... | collective-permute-start | bytes 98312 | tf_op jit(solution)/shard_map/ppermute | solution.py:433
  24.2 4.3 %collective-permute-start.7 = (f32[64,128]{1,0:T(8,128)S(1)}, f32[64,128]{1,0:T(8,128)S(1)}, u32[]{:S(2)}, u32[]{:S(2)}) collective-permute-start(f32[64,128]{1,0:T(8,128)S(1)} %add.22), channel_id=1, source_target_pairs={{8,0},{12,4},{0,8},{4,12},{24,16},{28,20},{16,24},{20,28},{9,1},{1... | collective-permute-start | bytes 98312 | tf_op jit(solution)/shard_map/ppermute | solution.py:433
  28.5 4.2 %collective-permute-start.8 = (f32[64,128]{1,0:T(8,128)S(1)}, f32[64,128]{1,0:T(8,128)S(1)}, u32[]{:S(2)}, u32[]{:S(2)}) collective-permute-start(f32[64,128]{1,0:T(8,128)S(1)} %add.23), channel_id=1, source_target_pairs={{16,0},{20,4},{24,8},{28,12},{0,16},{4,20},{8,24},{12,28},{17,1},{... | collective-permute-start | bytes 98312 | tf_op jit(solution)/shard_map/ppermute | solution.py:433
  32.7 1.3 %collective-permute-start.9 = (f32[64,128]{1,0:T(8,128)S(1)}, f32[64,128]{1,0:T(8,128)S(1)}, u32[]{:S(2)}, u32[]{:S(2)}) collective-permute-start(f32[64,128]{1,0:T(8,128)S(1)} %add.24), channel_id=1, source_target_pairs={{0,4},{4,0},{8,12},{12,8},{16,20},{20,16},{24,28},{28,24},{1,5},{5... | collective-permute-start | bytes 98312 | tf_op jit(solution)/shard_map/ppermute | solution.py:403

commit v20 on v19

--- a/solution.py
+++ b/solution.py
@@ -88,45 +88,45 @@
 
 
 def first_kernel(
-    q_hbm, k_hbm, v_hbm, dy_hbm, starts_hbm, filters_hbm,
-    q_ref, k_ref, v_ref, dy_ref, far_ref, pair_ref, keep_ref, masks_ref, table_masks_ref, taps_ref,
-    starts_ref, filters_ref, sems,
+    q_hbm, k_hbm, v_hbm, dy_hbm, starts_hbm,
+    q_ref, k_ref, v_ref, dy_ref, far_ref, pair_ref, keep_ref, starts_ref, sems,
 ):
     rows = q_ref.shape[0]
     core = lax.axis_index("ctx") % 2
-    small = [
-        pltpu.make_async_copy(starts_hbm, starts_ref, sems.at[8]),
-        pltpu.make_async_copy(filters_hbm, filters_ref, sems.at[9]),
-    ]
     inputs = (q_ref, k_ref, v_ref, dy_ref)
+    flags = pltpu.make_async_copy(starts_hbm, starts_ref, sems.at[8])
     copies = half_copies((q_hbm, k_hbm, v_hbm, dy_hbm), inputs, 1 - core, sems)
-    for copy in small + copies:
+    for copy in [flags, *copies]:
         copy.start()
-
-    small[0].wait()
+    flags.wait()
+    starts = jnp.broadcast_to(starts_ref[...], (rows, rows)) > 0
+    t = lax.broadcasted_iota(jnp.int32, (rows, rows), 0)
+    s = lax.broadcasted_iota(jnp.int32, (rows, rows), 1)
+    keep_ref[0] = as_f32(t < jnp.min(jnp.where(starts, s, rows), axis=1, keepdims=True))
+    keep_ref[1] = as_f32(t >= jnp.max(jnp.where(starts, s, 0), axis=1, keepdims=True))
+    for copy in copies:
+        copy.wait()
+    sent_products(inputs, 1 - core, keep_ref, far_ref, pair_ref, core == 0)
+
+
+def as_f32(mask):
+    return jnp.where(mask, 1.0, 0.0).astype(jnp.float32)
+
+
+def make_masks(starts_ref, keep_ref, masks_ref, table_masks_ref):
+    rows = starts_ref.shape[1]
     starts = jnp.broadcast_to(starts_ref[...], (rows, rows)) > 0
     t = lax.broadcasted_iota(jnp.int32, (rows, rows), 0)
     s = lax.broadcasted_iota(jnp.int32, (rows, rows), 1)
     began = jnp.max(jnp.where(starts & (s <= t), s, 0), axis=1, keepdims=True)
-    first = jnp.min(jnp.where(starts, s, rows), axis=1, keepdims=True)
-    last = jnp.max(jnp.where(starts, s, 0), axis=1, keepdims=True)
-    as_f32 = lambda mask: jnp.where(mask, 1.0, 0.0).astype(jnp.float32)
     own = as_f32((s <= t) & (s >= began))
-    previous = as_f32((s > t) & (t < first))
-    following = as_f32((s < t) & (t >= last))
-    keep_ref[0] = as_f32(t < first)
-    keep_ref[1] = as_f32(t >= last)
+    previous = jnp.where(s > t, keep_ref[0], 0.0)
+    following = jnp.where(s < t, keep_ref[1], 0.0)
     for n, parts in enumerate(((own, previous), (own.T, following))):
         for m, mask in enumerate(parts):
             table_masks_ref[n, :, m * rows : (m + 1) * rows] = aligned(mask).astype(jnp.bfloat16)
     for n, mask in enumerate((own.T, following, previous.T)):
         masks_ref[n] = aligned(mask)
-    small[1].wait()
-    taps_ref[0] = reversed_taps(filters_ref[...])
-    taps_ref[1] = filters_ref[...].astype(jnp.float32)
-    for copy in copies:
-        copy.wait()
-    sent_products(inputs, 1 - core, keep_ref, far_ref, pair_ref, core == 0)
 
 
 def tile_products(inputs, half, index):
@@ -195,15 +195,18 @@
 
 
 def filter_partner_kernel(
-    q_hbm, k_hbm, v_hbm, dy_hbm, q_in, k_in, v_in, dy_in, keep_ref, masks_ref,
-    q_ref, k_ref, v_ref, dy_ref, out_ref, pair_ref, far_ref, sums_ref, sems, *, scale
+    q_hbm, k_hbm, v_hbm, dy_hbm, filters_hbm, q_in, k_in, v_in, dy_in, keep_ref, starts_ref,
+    q_ref, k_ref, v_ref, dy_ref, out_ref, pair_ref, far_ref, masks_ref, table_masks_ref, taps_ref,
+    sums_ref, filters_ref, sems, *, scale
 ):
     del q_in, k_in, v_in, dy_in
     core = lax.axis_index("ctx") % 2
     inputs = (q_ref, k_ref, v_ref, dy_ref)
     copies = half_copies((q_hbm, k_hbm, v_hbm, dy_hbm), inputs, core, sems)
+    copies.append(pltpu.make_async_copy(filters_hbm, filters_ref, sems.at[8]))
     for copy in copies:
         copy.start()
+    make_masks(starts_ref, keep_ref, masks_ref, table_masks_ref)
     group = lane_groups()
 
     def store(at, total):
@@ -216,6 +219,8 @@
     out_ref[...] = diagonals(sums_ref, out_ref.shape[0]) * scale
     for copy in copies:
         copy.wait()
+    taps_ref[0] = reversed_taps(filters_ref[...])
+    taps_ref[1] = filters_ref[...].astype(jnp.float32)
     sent_products(inputs, core, keep_ref, pair_ref, far_ref, core == 1)
 
 
@@ -357,23 +362,15 @@
     )(*in_hbm(*hbm_operands), *operands)
 
 
-def first(q, k, v, dy, starts, filters):
+def first(q, k, v, dy, starts):
     rows, width = q.shape
     wide = pltpu.VMEM((rows, width), jnp.bfloat16)
     sent = pltpu.VMEM((rows, width // 2), jnp.bfloat16)
     return own_call(
         first_kernel, "first",
-        [wide] * 4 + [sent] * 2 + [
-            pltpu.VMEM((2, rows, rows), jnp.float32),
-            pltpu.VMEM((3, rows, rows), jnp.float32),
-            pltpu.VMEM((2, rows, 2 * rows), jnp.bfloat16),
-            pltpu.VMEM((2, *filters.shape), jnp.float32),
-        ],
-        [
-            pltpu.VMEM(starts.shape, starts.dtype), pltpu.VMEM(filters.shape, filters.dtype),
-            pltpu.SemaphoreType.DMA((10,)),
-        ],
-        (q, k, v, dy, starts, filters), (),
+        [wide] * 4 + [sent] * 2 + [pltpu.VMEM((2, rows, rows), jnp.float32), pltpu.VMEM(starts.shape, starts.dtype)],
+        [pltpu.SemaphoreType.DMA((9,))],
+        (q, k, v, dy, starts), (),
     )
 
 
@@ -448,7 +445,7 @@
     assert rows == taps == LANES and lax.axis_size("ctx") % 2 == 0
     scale = 1.0 / math.sqrt(rows * lax.axis_size("ctx") * lax.axis_size("dp") * GSIZE)
     inputs = q, k, v, dy
-    *partly, far_out, pair_out, keep, masks, table_masks, tap_rows = first(*inputs, contig_starts, filters)
+    *partly, far_out, pair_out, keep, flags = first(*inputs, contig_starts)
     square = pltpu.VMEM((rows, rows), jnp.float32)
     part = pltpu.VMEM((groups // 2, rows), jnp.float32)
     unsummed = pltpu.VMEM((groups * 4, rows), jnp.float32)
@@ -456,10 +453,16 @@
     sent = pltpu.VMEM((rows, q.shape[1] // 2), q.dtype)
     far = next_chip(far_out)
     later_pair = other_core(pair_out)
-    q, k, v, dy, theirs, pair_out, far_out = own_call(
+    masks_made = [
+        pltpu.VMEM((3, rows, rows), jnp.float32),
+        pltpu.VMEM((2, rows, 2 * rows), jnp.bfloat16),
+        pltpu.VMEM((2, *filters.shape), jnp.float32),
+    ]
+    q, k, v, dy, theirs, pair_out, far_out, masks, table_masks, tap_rows = own_call(
         functools.partial(filter_partner_kernel, scale=scale), "filter_partner",
-        [wide] * 4 + [part, sent, sent], [unsummed, pltpu.SemaphoreType.DMA((8,))],
-        inputs, (*partly, keep, masks), {4: 0, 5: 1, 6: 2, 7: 3},
+        [wide] * 4 + [part, sent, sent] + masks_made,
+        [unsummed, pltpu.VMEM(filters.shape, filters.dtype), pltpu.SemaphoreType.DMA((9,))],
+        (*inputs, filters), (*partly, keep, flags), {5: 0, 6: 1, 7: 2, 8: 3},
     )
     pair = other_core(pair_out)
     mine = own_call(

time: 34.8 us -> 34.9 us (level)
  starting transfers between devices: 16.9 us -> 16 us
  Pallas kernels: 15 us -> 15.7 us
    ppermute x4, starting transfers between devices: 8.11 us -> 7.27 us  [summed_over(): lax.ppermute(total, axis, [(turned(i, k), i) for i in range(size)])]
    pallas_call x4, Pallas kernels: 5.83 us -> 6.54 us  [own_call(): pl.pallas_call(kernel, out_shape=out_shape, in_specs=[pl.BlockSpec(memory...]
  transfers between devices with their start and end apart: 10 -> 10, of which waited for: 1 -> 3; matrix products, arithmetic and copies ran while one was open for 0% -> 0% of each run, Pallas kernels for 39% -> 41%
where the time goes in v20:
time: 34.9 us; the launch traced here: 34.6 us
  starting transfers between devices  16 us (46%)
  Pallas kernels  15.7 us (45%)
  waiting for transfers between devices  1.53 us (4%)
  between operations  0.76 us (2%)
  other arithmetic  0.67 us (2%)
    pallas_call x4, Pallas kernels, local_call(): pl.pallas_call(kernel, out_shape=out_shape, in_specs=in_specs or [VMEM] *...  9.19 us
    ppermute x4, starting transfers between devices, other_core(): lax.ppermute(block, 'ctx', [(i, i ^ 1) for i in range(lax.axis_size('ctx'...  7.35 us
    ppermute x4, starting transfers between devices, summed_over(): lax.ppermute(total, axis, [(turned(i, k), i) for i in range(size)])  7.27 us
    pallas_call x4, Pallas kernels, own_call(): pl.pallas_call(kernel, out_shape=out_shape, in_specs=[pl.BlockSpec(memory...  6.54 us
    ppermute x2, starting transfers between devices, next_chip(): return lax.ppermute(block, 'ctx', pairs + [(j, i) for i, j in pairs])  1.34 us
    ppermute x4, waiting for transfers between devices, other_core(): lax.ppermute(block, 'ctx', [(i, i ^ 1) for i in range(lax.axis_size('ctx'...  1.19 us
  transfers between devices with their start and end apart: 10, of which 3 were waited for; matrix products, arithmetic and copies ran while one was open for 0% of the time, Pallas kernels for 41%

profile of v20, /device:TPU:0, one launch (start us, length us, event | category | flops | bytes accessed | tf_op | source)
XLA Modules:
  0.0 34.6 jit_solution(1448619479509228731)
XLA Ops:
  0.6 1.5 %first.1 = (bf16[128,2048]{1,0:T(8,128)(2,1)S(1)}, bf16[128,2048]{1,0:T(8,128)(2,1)S(1)}, bf16[128,2048]{1,0:T(8,128)(2,1)S(1)}, bf16[128,2048]{1,0:T(8,128)(2,1...) custom-call(bf16[128,2048]{1,0:T(8,128)(2,1)} %bitcast.8, ...), custom_call_target="tpu_custom_call" | custom-call | tf_op jit(solution)/shard_map/first/pallas_call | solution.py:352
  2.2 0.5 %collective-permute-start = (bf16[128,1024]{1,0:T(8,128)(2,1)S(1)}, bf16[128,1024]{1,0:T(8,128)(2,1)S(1)}, u32[]{:S(2)}, u32[]{:S(2)}) collective-permute-start(bf16[128,1024]{1,0:T(8,128)(2,1)S(1)} %get-tuple-element.48), channel_id=1, source_target_pairs={{0,4},{4,0},{8,12},{12,8},{16,20},{20,16},{24,28},{28,24},{1,5},{5... | collective-permute-start | bytes 786440 | tf_op jit(solution)/shard_map/ppermute | solution.py:400
  2.7 0.7 %collective-permute-start.3 = (bf16[128,1024]{1,0:T(8,128)(2,1)S(1)}, bf16[128,1024]{1,0:T(8,128)(2,1)S(1)}, u32[]{:S(2)}, u32[]{:S(2)}) collective-permute-start(bf16[128,1024]{1,0:T(8,128)(2,1)S(1)} %get-tuple-element.53), channel_id=1, source_target_pairs={{4,8},{12,16},{20,24},{8,4},{16,12},{24,20},{5,9},{13,17},{21,25},... | collective-permute-start | bytes 786440 | tf_op jit(solution)/shard_map/ppermute | solution.py:406
  3.4 2.3 %filter_partner.1 = (bf16[128,2048]{1,0:T(8,128)(2,1)S(1)}, bf16[128,2048]{1,0:T(8,128)(2,1)S(1)}, bf16[128,2048]{1,0:T(8,128)(2,1)S(1)}, bf16[128,2048]{1,0:T(8...) custom-call(bf16[128,2048]{1,0:T(8,128)(2,1)} %bitcast.9, ...), custom_call_target="tpu_custom_call", output_to_operand_aliasing={{0}: (5, {}), {1}: (6, {}), {2}: (7, {}), {3}: (8, {})} | custom-call | tf_op jit(solution)/shard_map/filter_partner/pallas_call | solution.py:352
  5.6 3.9 %collective-permute-start.2 = (bf16[128,1024]{1,0:T(8,128)(2,1)S(1)}, bf16[128,1024]{1,0:T(8,128)(2,1)S(1)}, u32[]{:S(2)}, u32[]{:S(2)}) collective-permute-start(bf16[128,1024]{1,0:T(8,128)(2,1)S(1)} %get-tuple-element.52), channel_id=1, source_target_pairs={{0,4},{4,0},{8,12},{12,8},{16,20},{20,16},{24,28},{28,24},{1,5},{5... | collective-permute-start | bytes 786440 | tf_op jit(solution)/shard_map/ppermute | solution.py:400
  9.5 0.0 collective-permute-done.other_ref.refs_6_
  9.5 1.7 %filter_own.1.base_ref = f32[512,128]{1,0:T(8,128)S(1)} custom-call(bf16[128,2048]{1,0:T(8,128)(2,1)S(1)} %get-tuple-element.44.q_ref.c_ref.refs_2_.b_ref.refs_1_, bf16[128,2048]{1,0:T(8,128)(2,1)S(1)} %get-tuple-element.42.k_ref.a_ref.refs_0_.d_ref.refs_3_, bf16[128,2048]{1,0:T(8,128)(2,1)S(1)} %get-tuple-element.43.v_ref.b_ref.refs_1_.c_ref.refs_2_, ...), custom_call_target="tpu_custom_call" | custom-call | tf_op jit(solution)/shard_map/filter_own/pallas_call | solution.py:352
  11.3 0.7 %collective-permute-start.1 = (bf16[128,1024]{1,0:T(8,128)(2,1)S(1)}, bf16[128,1024]{1,0:T(8,128)(2,1)S(1)}, u32[]{:S(2)}, u32[]{:S(2)}) collective-permute-start(bf16[128,1024]{1,0:T(8,128)(2,1)S(1)} %get-tuple-element.51), channel_id=1, source_target_pairs={{4,8},{12,16},{20,24},{8,4},{16,12},{24,20},{5,9},{13,17},{21,25},... | collective-permute-start | bytes 786440 | tf_op jit(solution)/shard_map/ppermute | solution.py:406
  12.0 2.9 %collective-permute-start.4 = (f32[64,128]{1,0:T(8,128)S(1)}, f32[64,128]{1,0:T(8,128)S(1)}, u32[]{:S(2)}, u32[]{:S(2)}) collective-permute-start(f32[64,128]{1,0:T(8,128)S(1)} %get-tuple-element.62), channel_id=1, source_target_pairs={{0,4},{4,0},{8,12},{12,8},{16,20},{20,16},{24,28},{28,24},{1,5},{5... | collective-permute-start | bytes 98312 | tf_op jit(solution)/shard_map/ppermute | solution.py:400
  14.9 0.0 collective-permute-done.3.far_ref.other_ref
  14.9 1.0 %filter_far.1 = f32[64,128]{1,0:T(8,128)S(1)} custom-call(bf16[128,2048]{1,0:T(8,128)(2,1)S(1)} %get-tuple-element.44.q_ref.c_ref.refs_2_.b_ref.refs_1_, bf16[128,2048]{1,0:T(8,128)(2,1)S(1)} %get-tuple-element.42.k_ref.a_ref.refs_0_.d_ref.refs_3_, bf16[128,2048]{1,0:T(8,128)(2,1)S(1)} %get-tuple-element.43.v_ref.b_ref.refs_1_.c_ref.refs_2_, ...), custom_call_target="tpu_custom_call" | custom-call | tf_op jit(solution)/shard_map/filter_far/pallas_call | solution.py:352
  15.9 0.0 collective-permute-done.4
  15.9 1.6 %collective-permute-start.5 = (f32[64,128]{1,0:T(8,128)S(1)}, f32[64,128]{1,0:T(8,128)S(1)}, u32[]{:S(2)}, u32[]{:S(2)}) collective-permute-start(f32[64,128]{1,0:T(8,128)S(1)} %add.20), channel_id=1, source_target_pairs={{1,0},{0,1},{3,2},{2,3},{5,4},{4,5},{7,6},{6,7},{9,8},{8,9},{11,10... | collective-permute-start | bytes 98312 | tf_op jit(solution)/shard_map/ppermute | solution.py:430
  17.6 0.0 collective-permute-done.2.pair_ref
  17.6 2.3 %forward.2 = (bf16[128,2048]{1,0:T(8,128)(2,1)}, bf16[128,2048]{1,0:T(8,128)(2,1)}) custom-call(bf16[128,2048]{1,0:T(8,128)(2,1)S(1)} %get-tuple-element.42.k_ref.a_ref.refs_0_.d_ref.refs_3_, bf16[128,2048]{1,0:T(8,128)(2,1)S(1)} %get-tuple-element.43.v_ref.b_ref.refs_1_.c_ref.refs_2_, ...), custom_call_target="tpu_custom_call" | custom-call | flops 536870912 | bytes 3932160 | tf_op jit(solution)/shard_map/forward/pallas_call | solution.py:334
  19.9 0.0 collective-permute-done.5
  19.9 2.6 %collective-permute-start.6 = (f32[64,128]{1,0:T(8,128)S(1)}, f32[64,128]{1,0:T(8,128)S(1)}, u32[]{:S(2)}, u32[]{:S(2)}) collective-permute-start(f32[64,128]{1,0:T(8,128)S(1)} %add.21), channel_id=1, source_target_pairs={{2,0},{3,1},{0,2},{1,3},{6,4},{7,5},{4,6},{5,7},{10,8},{11,9},{8,1... | collective-permute-start | bytes 98312 | tf_op jit(solution)/shard_map/ppermute | solution.py:430
  22.5 2.3 %backward.2 = (bf16[128,2048]{1,0:T(8,128)(2,1)}, bf16[128,2048]{1,0:T(8,128)(2,1)}) custom-call(bf16[128,2048]{1,0:T(8,128)(2,1)S(1)} %get-tuple-element.45.dy_ref.d_ref.refs_3_.a_ref.refs_0_, bf16[128,2048]{1,0:T(8,128)(2,1)S(1)} %get-tuple-element.44.q_ref.c_ref.refs_2_.b_ref.refs_1_, ...), custom_call_target="tpu_custom_call" | custom-call | flops 536870912 | bytes 3932160 | tf_op jit(solution)/shard_map/backward/pallas_call | solution.py:334
  24.9 0.0 collective-permute-done.6
  24.9 0.0 collective-permute-done.1.refs_7_
  24.9 1.6 %collective-permute-start.7 = (f32[64,128]{1,0:T(8,128)S(1)}, f32[64,128]{1,0:T(8,128)S(1)}, u32[]{:S(2)}, u32[]{:S(2)}) collective-permute-start(f32[64,128]{1,0:T(8,128)S(1)} %add.22), channel_id=1, source_target_pairs={{8,0},{12,4},{0,8},{4,12},{24,16},{28,20},{16,24},{20,28},{9,1},{1... | collective-permute-start | bytes 98312 | tf_op jit(solution)/shard_map/ppermute | solution.py:430
  26.4 2.3 %forward.3 = (bf16[128,2048]{1,0:T(8,128)(2,1)}, bf16[128,2048]{1,0:T(8,128)(2,1)}) custom-call(bf16[128,2048]{1,0:T(8,128)(2,1)S(1)} %get-tuple-element.42.k_ref.a_ref.refs_0_.d_ref.refs_3_, bf16[128,2048]{1,0:T(8,128)(2,1)S(1)} %get-tuple-element.43.v_ref.b_ref.refs_1_.c_ref.refs_2_, ...), custom_call_target="tpu_custom_call", output_to_operand_aliasing={{0}: (8, {}), {1}: (9, {})} | custom-call | flops 536870912 | bytes 4980736 | tf_op jit(solution)/shard_map/forward/pallas_call | solution.py:334
  28.8 0.1 collective-permute-done.7
  28.9 1.4 %collective-permute-start.8 = (f32[64,128]{1,0:T(8,128)S(1)}, f32[64,128]{1,0:T(8,128)S(1)}, u32[]{:S(2)}, u32[]{:S(2)}) collective-permute-start(f32[64,128]{1,0:T(8,128)S(1)} %add.23), channel_id=1, source_target_pairs={{16,0},{20,4},{24,8},{28,12},{0,16},{4,20},{8,24},{12,28},{17,1},{... | collective-permute-start | bytes 98312 | tf_op jit(solution)/shard_map/ppermute | solution.py:430
  30.3 2.3 %backward.3 = (bf16[128,2048]{1,0:T(8,128)(2,1)}, bf16[128,2048]{1,0:T(8,128)(2,1)}) custom-call(bf16[128,2048]{1,0:T(8,128)(2,1)S(1)} %get-tuple-element.45.dy_ref.d_ref.refs_3_.a_ref.refs_0_, bf16[128,2048]{1,0:T(8,128)(2,1)S(1)} %get-tuple-element.44.q_ref.c_ref.refs_2_.b_ref.refs_1_, ...), custom_call_target="tpu_custom_call", output_to_operand_aliasing={{0}: (8, {}), {1}: (9, {})} | custom-call | flops 536870912 | bytes 4980736 | tf_op jit(solution)/shard_map/backward/pallas_call | solution.py:334
  32.6 0.2 collective-permute-done.8
  32.8 0.0 collective-permute-start.9
  32.8 1.2 %collective-permute-done.9 = f32[64,128]{1,0:T(8,128)S(1)} collective-permute-done((f32[64,128]{1,0:T(8,128)S(1)}, f32[64,128]{1,0:T(8,128)S(1)}, u32[]{:S(2)}, u32[]{:S(2)}) %collective-permute-start.9) | collective-permute-done | bytes 32800 | tf_op jit(solution)/shard_map/ppermute | solution.py:400
  34.0 0.6 %maximum_select_fusion = f32[128,128]{1,0:T(8,128)} fusion(f32[64,128]{1,0:T(8,128)S(1)} %collective-permute-done.9, f32[64,128]{1,0:T(8,128)S(1)} %add.24, pred[]{:T(512)S(6)} %eq.5), kind=kLoop, calls=%fused_computation | loop fusion | flops 49152 | bytes 131073 | tf_op jit(solution)/shard_map/jit(_where)/select_n | solution.py:503
  (5 shorter events, 0.0 us)
Async XLA Ops:
  2.2 7.4 %collective-permute-start = (bf16[128,1024]{1,0:T(8,128)(2,1)S(1)}, bf16[128,1024]{1,0:T(8,128)(2,1)S(1)}, u32[]{:S(2)}, u32[]{:S(2)}) collective-permute-start(bf16[128,1024]{1,0:T(8,128)(2,1)S(1)} %get-tuple-element.48), channel_id=1, source_target_pairs={{0,4},{4,0},{8,12},{12,8},{16,20},{20,16},{24,28},{28,24},{1,5},{5... | collective-permute-start | bytes 786440 | tf_op jit(solution)/shard_map/ppermute | solution.py:400
  2.7 12.2 %collective-permute-start.3 = (bf16[128,1024]{1,0:T(8,128)(2,1)S(1)}, bf16[128,1024]{1,0:T(8,128)(2,1)S(1)}, u32[]{:S(2)}, u32[]{:S(2)}) collective-permute-start(bf16[128,1024]{1,0:T(8,128)(2,1)S(1)} %get-tuple-element.53), channel_id=1, source_target_pairs={{4,8},{12,16},{20,24},{8,4},{16,12},{24,20},{5,9},{13,17},{21,25},... | collective-permute-start | bytes 786440 | tf_op jit(solution)/shard_map/ppermute | solution.py:406
  5.6 11.9 %collective-permute-start.2 = (bf16[128,1024]{1,0:T(8,128)(2,1)S(1)}, bf16[128,1024]{1,0:T(8,128)(2,1)S(1)}, u32[]{:S(2)}, u32[]{:S(2)}) collective-permute-start(bf16[128,1024]{1,0:T(8,128)(2,1)S(1)} %get-tuple-element.52), channel_id=1, source_target_pairs={{0,4},{4,0},{8,12},{12,8},{16,20},{20,16},{24,28},{28,24},{1,5},{5... | collective-permute-start | bytes 786440 | tf_op jit(solution)/shard_map/ppermute | solution.py:400
  11.3 13.6 %collective-permute-start.1 = (bf16[128,1024]{1,0:T(8,128)(2,1)S(1)}, bf16[128,1024]{1,0:T(8,128)(2,1)S(1)}, u32[]{:S(2)}, u32[]{:S(2)}) collective-permute-start(bf16[128,1024]{1,0:T(8,128)(2,1)S(1)} %get-tuple-element.51), channel_id=1, source_target_pairs={{4,8},{12,16},{20,24},{8,4},{16,12},{24,20},{5,9},{13,17},{21,25},... | collective-permute-start | bytes 786440 | tf_op jit(solution)/shard_map/ppermute | solution.py:406
  12.0 3.9 %collective-permute-start.4 = (f32[64,128]{1,0:T(8,128)S(1)}, f32[64,128]{1,0:T(8,128)S(1)}, u32[]{:S(2)}, u32[]{:S(2)}) collective-permute-start(f32[64,128]{1,0:T(8,128)S(1)} %get-tuple-element.62), channel_id=1, source_target_pairs={{0,4},{4,0},{8,12},{12,8},{16,20},{20,16},{24,28},{28,24},{1,5},{5... | collective-permute-start | bytes 98312 | tf_op jit(solution)/shard_map/ppermute | solution.py:400
  15.9 4.0 %collective-permute-start.5 = (f32[64,128]{1,0:T(8,128)S(1)}, f32[64,128]{1,0:T(8,128)S(1)}, u32[]{:S(2)}, u32[]{:S(2)}) collective-permute-start(f32[64,128]{1,0:T(8,128)S(1)} %add.20), channel_id=1, source_target_pairs={{1,0},{0,1},{3,2},{2,3},{5,4},{4,5},{7,6},{6,7},{9,8},{8,9},{11,10... | collective-permute-start | bytes 98312 | tf_op jit(solution)/shard_map/ppermute | solution.py:430
  19.9 4.9 %collective-permute-start.6 = (f32[64,128]{1,0:T(8,128)S(1)}, f32[64,128]{1,0:T(8,128)S(1)}, u32[]{:S(2)}, u32[]{:S(2)}) collective-permute-start(f32[64,128]{1,0:T(8,128)S(1)} %add.21), channel_id=1, source_target_pairs={{2,0},{3,1},{0,2},{1,3},{6,4},{7,5},{4,6},{5,7},{10,8},{11,9},{8,1... | collective-permute-start | bytes 98312 | tf_op jit(solution)/shard_map/ppermute | solution.py:430
  24.9 4.0 %collective-permute-start.7 = (f32[64,128]{1,0:T(8,128)S(1)}, f32[64,128]{1,0:T(8,128)S(1)}, u32[]{:S(2)}, u32[]{:S(2)}) collective-permute-start(f32[64,128]{1,0:T(8,128)S(1)} %add.22), channel_id=1, source_target_pairs={{8,0},{12,4},{0,8},{4,12},{24,16},{28,20},{16,24},{20,28},{9,1},{1... | collective-permute-start | bytes 98312 | tf_op jit(solution)/shard_map/ppermute | solution.py:430
  28.9 3.9 %collective-permute-start.8 = (f32[64,128]{1,0:T(8,128)S(1)}, f32[64,128]{1,0:T(8,128)S(1)}, u32[]{:S(2)}, u32[]{:S(2)}) collective-permute-start(f32[64,128]{1,0:T(8,128)S(1)} %add.23), channel_id=1, source_target_pairs={{16,0},{20,4},{24,8},{28,12},{0,16},{4,20},{8,24},{12,28},{17,1},{... | collective-permute-start | bytes 98312 | tf_op jit(solution)/shard_map/ppermute | solution.py:430
  32.8 1.2 %collective-permute-start.9 = (f32[64,128]{1,0:T(8,128)S(1)}, f32[64,128]{1,0:T(8,128)S(1)}, u32[]{:S(2)}, u32[]{:S(2)}) collective-permute-start(f32[64,128]{1,0:T(8,128)S(1)} %add.24), channel_id=1, source_target_pairs={{0,4},{4,0},{8,12},{12,8},{16,20},{20,16},{24,28},{28,24},{1,5},{5... | collective-permute-start | bytes 98312 | tf_op jit(solution)/shard_map/ppermute | solution.py:400

commit v21 on v19

--- a/solution.py
+++ b/solution.py
@@ -315,7 +315,8 @@
                 copy.start()
             return carry
 
-        lax.fori_loop(0, count // step, body, 0)
+        for i in range(count // step):
+            body(i, 0)
         bodies += [(first + i * step, step) for i in range(count // step)]
     for n, (start, count) in enumerate(bodies):
         for copy in stored(start, count, n):

time: 34.8 us -> 34.3 us (0.986)
  Pallas kernels: 15 us -> 14.1 us
  waiting for transfers between devices: 1.24 us -> 1.72 us
    pallas_call x4, Pallas kernels: 9.17 us -> 8.23 us  [local_call(): pl.pallas_call(kernel, out_shape=out_shape, in_specs=in_specs or [VMEM] *...]
    ppermute x4, waiting for transfers between devices: 0.05 us -> 0.52 us  [summed_over(): lax.ppermute(total, axis, [(turned(i, k), i) for i in range(size)])]
  transfers between devices with their start and end apart: 10 -> 10, of which waited for: 1 -> 4; matrix products, arithmetic and copies ran while one was open for 0% -> 0% of each run, Pallas kernels for 39% -> 37%
where the time goes in v21:
time: 34.3 us; the launch traced here: 34.1 us
  starting transfers between devices  16.9 us (49%)
  Pallas kernels  14.1 us (41%)
  waiting for transfers between devices  1.72 us (5%)
  between operations  0.76 us (2%)
  other arithmetic  0.67 us (2%)
    pallas_call x4, Pallas kernels, local_call(): pl.pallas_call(kernel, out_shape=out_shape, in_specs=in_specs or [VMEM] *...  8.23 us
    ppermute x4, starting transfers between devices, summed_over(): lax.ppermute(total, axis, [(turned(i, k), i) for i in range(size)])  8.16 us
    ppermute x4, starting transfers between devices, other_core(): lax.ppermute(block, 'ctx', [(i, i ^ 1) for i in range(lax.axis_size('ctx'...  7.36 us
    pallas_call x4, Pallas kernels, own_call(): pl.pallas_call(kernel, out_shape=out_shape, in_specs=[pl.BlockSpec(memory...  5.83 us
    ppermute x2, starting transfers between devices, next_chip(): return lax.ppermute(block, 'ctx', pairs + [(j, i) for i, j in pairs])  1.34 us
    ppermute x4, waiting for transfers between devices, other_core(): lax.ppermute(block, 'ctx', [(i, i ^ 1) for i in range(lax.axis_size('ctx'...  1.19 us
  transfers between devices with their start and end apart: 10, of which 4 were waited for; matrix products, arithmetic and copies ran while one was open for 0% of the time, Pallas kernels for 37%

profile of v21, /device:TPU:0, one launch (start us, length us, event | category | flops | bytes accessed | tf_op | source)
XLA Modules:
  0.0 34.1 jit_solution(148481546143473272)
XLA Ops:
  0.6 1.5 %first.1 = (bf16[128,2048]{1,0:T(8,128)(2,1)S(1)}, bf16[128,2048]{1,0:T(8,128)(2,1)S(1)}, bf16[128,2048]{1,0:T(8,128)(2,1)S(1)}, bf16[128,2048]{1,0:T(8,128)(2,1...) custom-call(bf16[128,2048]{1,0:T(8,128)(2,1)} %bitcast.8, ...), custom_call_target="tpu_custom_call" | custom-call | tf_op jit(solution)/shard_map/first/pallas_call | solution.py:348
  2.2 0.5 %collective-permute-start = (bf16[128,1024]{1,0:T(8,128)(2,1)S(1)}, bf16[128,1024]{1,0:T(8,128)(2,1)S(1)}, u32[]{:S(2)}, u32[]{:S(2)}) collective-permute-start(bf16[128,1024]{1,0:T(8,128)(2,1)S(1)} %get-tuple-element.47), channel_id=1, source_target_pairs={{0,4},{4,0},{8,12},{12,8},{16,20},{20,16},{24,28},{28,24},{1,5},{5... | collective-permute-start | bytes 786440 | tf_op jit(solution)/shard_map/ppermute | solution.py:404
  2.7 0.7 %collective-permute-start.3 = (bf16[128,1024]{1,0:T(8,128)(2,1)S(1)}, bf16[128,1024]{1,0:T(8,128)(2,1)S(1)}, u32[]{:S(2)}, u32[]{:S(2)}) collective-permute-start(bf16[128,1024]{1,0:T(8,128)(2,1)S(1)} %get-tuple-element.51), channel_id=1, source_target_pairs={{4,8},{12,16},{20,24},{8,4},{16,12},{24,20},{5,9},{13,17},{21,25},... | collective-permute-start | bytes 786440 | tf_op jit(solution)/shard_map/ppermute | solution.py:410
  3.4 1.5 %filter_partner.1 = (bf16[128,2048]{1,0:T(8,128)(2,1)S(1)}, bf16[128,2048]{1,0:T(8,128)(2,1)S(1)}, bf16[128,2048]{1,0:T(8,128)(2,1)S(1)}, bf16[128,2048]{1,0:T(8...) custom-call(bf16[128,2048]{1,0:T(8,128)(2,1)} %bitcast.9, ...), custom_call_target="tpu_custom_call", output_to_operand_aliasing={{0}: (4, {}), {1}: (5, {}), {2}: (6, {}), {3}: (7, {})} | custom-call | tf_op jit(solution)/shard_map/filter_partner/pallas_call | solution.py:348
  4.9 3.9 %collective-permute-start.2 = (bf16[128,1024]{1,0:T(8,128)(2,1)S(1)}, bf16[128,1024]{1,0:T(8,128)(2,1)S(1)}, u32[]{:S(2)}, u32[]{:S(2)}) collective-permute-start(bf16[128,1024]{1,0:T(8,128)(2,1)S(1)} %get-tuple-element.50), channel_id=1, source_target_pairs={{0,4},{4,0},{8,12},{12,8},{16,20},{20,16},{24,28},{28,24},{1,5},{5... | collective-permute-start | bytes 786440 | tf_op jit(solution)/shard_map/ppermute | solution.py:404
  8.8 0.0 collective-permute-done.other_ref.refs_6_
  8.8 1.7 %filter_own.1.base_ref = f32[512,128]{1,0:T(8,128)S(1)} custom-call(bf16[128,2048]{1,0:T(8,128)(2,1)S(1)} %get-tuple-element.43.q_ref.c_ref.refs_2_.b_ref.refs_1_, bf16[128,2048]{1,0:T(8,128)(2,1)S(1)} %get-tuple-element.41.k_ref.a_ref.refs_0_.d_ref.refs_3_, bf16[128,2048]{1,0:T(8,128)(2,1)S(1)} %get-tuple-element.42.v_ref.b_ref.refs_1_.c_ref.refs_2_, ...), custom_call_target="tpu_custom_call" | custom-call | tf_op jit(solution)/shard_map/filter_own/pallas_call | solution.py:348
  10.6 0.7 %collective-permute-start.1 = (bf16[128,1024]{1,0:T(8,128)(2,1)S(1)}, bf16[128,1024]{1,0:T(8,128)(2,1)S(1)}, u32[]{:S(2)}, u32[]{:S(2)}) collective-permute-start(bf16[128,1024]{1,0:T(8,128)(2,1)S(1)} %get-tuple-element.49), channel_id=1, source_target_pairs={{4,8},{12,16},{20,24},{8,4},{16,12},{24,20},{5,9},{13,17},{21,25},... | collective-permute-start | bytes 786440 | tf_op jit(solution)/shard_map/ppermute | solution.py:410
  11.3 2.9 %collective-permute-start.4 = (f32[64,128]{1,0:T(8,128)S(1)}, f32[64,128]{1,0:T(8,128)S(1)}, u32[]{:S(2)}, u32[]{:S(2)}) collective-permute-start(f32[64,128]{1,0:T(8,128)S(1)} %get-tuple-element.60), channel_id=1, source_target_pairs={{0,4},{4,0},{8,12},{12,8},{16,20},{20,16},{24,28},{28,24},{1,5},{5... | collective-permute-start | bytes 98312 | tf_op jit(solution)/shard_map/ppermute | solution.py:404
  14.2 0.0 collective-permute-done.3.far_ref.other_ref
  14.2 1.0 %filter_far.1 = f32[64,128]{1,0:T(8,128)S(1)} custom-call(bf16[128,2048]{1,0:T(8,128)(2,1)S(1)} %get-tuple-element.43.q_ref.c_ref.refs_2_.b_ref.refs_1_, bf16[128,2048]{1,0:T(8,128)(2,1)S(1)} %get-tuple-element.41.k_ref.a_ref.refs_0_.d_ref.refs_3_, bf16[128,2048]{1,0:T(8,128)(2,1)S(1)} %get-tuple-element.42.v_ref.b_ref.refs_1_.c_ref.refs_2_, ...), custom_call_target="tpu_custom_call" | custom-call | tf_op jit(solution)/shard_map/filter_far/pallas_call | solution.py:348
  15.2 0.0 collective-permute-done.4
  15.2 1.6 %collective-permute-start.5 = (f32[64,128]{1,0:T(8,128)S(1)}, f32[64,128]{1,0:T(8,128)S(1)}, u32[]{:S(2)}, u32[]{:S(2)}) collective-permute-start(f32[64,128]{1,0:T(8,128)S(1)} %add.20), channel_id=1, source_target_pairs={{1,0},{0,1},{3,2},{2,3},{5,4},{4,5},{7,6},{6,7},{9,8},{8,9},{11,10... | collective-permute-start | bytes 98312 | tf_op jit(solution)/shard_map/ppermute | solution.py:434
  16.9 0.0 collective-permute-done.2.pair_ref
  16.9 2.1 %forward.2 = (bf16[128,2048]{1,0:T(8,128)(2,1)}, bf16[128,2048]{1,0:T(8,128)(2,1)}) custom-call(bf16[128,2048]{1,0:T(8,128)(2,1)S(1)} %get-tuple-element.41.k_ref.a_ref.refs_0_.d_ref.refs_3_, bf16[128,2048]{1,0:T(8,128)(2,1)S(1)} %get-tuple-element.42.v_ref.b_ref.refs_1_.c_ref.refs_2_, ...), custom_call_target="tpu_custom_call" | custom-call | flops 536870912 | bytes 3932160 | tf_op jit(solution)/shard_map/forward/pallas_call | solution.py:330
  18.9 0.3 collective-permute-done.5
  19.2 2.6 %collective-permute-start.6 = (f32[64,128]{1,0:T(8,128)S(1)}, f32[64,128]{1,0:T(8,128)S(1)}, u32[]{:S(2)}, u32[]{:S(2)}) collective-permute-start(f32[64,128]{1,0:T(8,128)S(1)} %add.21), channel_id=1, source_target_pairs={{2,0},{3,1},{0,2},{1,3},{6,4},{7,5},{4,6},{5,7},{10,8},{11,9},{8,1... | collective-permute-start | bytes 98312 | tf_op jit(solution)/shard_map/ppermute | solution.py:434
  21.8 2.1 %backward.2 = (bf16[128,2048]{1,0:T(8,128)(2,1)}, bf16[128,2048]{1,0:T(8,128)(2,1)}) custom-call(bf16[128,2048]{1,0:T(8,128)(2,1)S(1)} %get-tuple-element.44.dy_ref.d_ref.refs_3_.a_ref.refs_0_, bf16[128,2048]{1,0:T(8,128)(2,1)S(1)} %get-tuple-element.43.q_ref.c_ref.refs_2_.b_ref.refs_1_, ...), custom_call_target="tpu_custom_call" | custom-call | flops 536870912 | bytes 3932160 | tf_op jit(solution)/shard_map/backward/pallas_call | solution.py:330
  23.9 0.2 collective-permute-done.6
  24.0 0.0 collective-permute-done.1.refs_7_
  24.0 2.1 %collective-permute-start.7 = (f32[64,128]{1,0:T(8,128)S(1)}, f32[64,128]{1,0:T(8,128)S(1)}, u32[]{:S(2)}, u32[]{:S(2)}) collective-permute-start(f32[64,128]{1,0:T(8,128)S(1)} %add.22), channel_id=1, source_target_pairs={{8,0},{12,4},{0,8},{4,12},{24,16},{28,20},{16,24},{20,28},{9,1},{1... | collective-permute-start | bytes 98312 | tf_op jit(solution)/shard_map/ppermute | solution.py:434
  26.1 2.1 %forward.3 = (bf16[128,2048]{1,0:T(8,128)(2,1)}, bf16[128,2048]{1,0:T(8,128)(2,1)}) custom-call(bf16[128,2048]{1,0:T(8,128)(2,1)S(1)} %get-tuple-element.41.k_ref.a_ref.refs_0_.d_ref.refs_3_, bf16[128,2048]{1,0:T(8,128)(2,1)S(1)} %get-tuple-element.42.v_ref.b_ref.refs_1_.c_ref.refs_2_, ...), custom_call_target="tpu_custom_call", output_to_operand_aliasing={{0}: (8, {}), {1}: (9, {})} | custom-call | flops 536870912 | bytes 4980736 | tf_op jit(solution)/shard_map/forward/pallas_call | solution.py:330
  28.2 0.0 collective-permute-done.7
  28.2 1.8 %collective-permute-start.8 = (f32[64,128]{1,0:T(8,128)S(1)}, f32[64,128]{1,0:T(8,128)S(1)}, u32[]{:S(2)}, u32[]{:S(2)}) collective-permute-start(f32[64,128]{1,0:T(8,128)S(1)} %add.23), channel_id=1, source_target_pairs={{16,0},{20,4},{24,8},{28,12},{0,16},{4,20},{8,24},{12,28},{17,1},{... | collective-permute-start | bytes 98312 | tf_op jit(solution)/shard_map/ppermute | solution.py:434
  30.0 2.1 %backward.3 = (bf16[128,2048]{1,0:T(8,128)(2,1)}, bf16[128,2048]{1,0:T(8,128)(2,1)}) custom-call(bf16[128,2048]{1,0:T(8,128)(2,1)S(1)} %get-tuple-element.44.dy_ref.d_ref.refs_3_.a_ref.refs_0_, bf16[128,2048]{1,0:T(8,128)(2,1)S(1)} %get-tuple-element.43.q_ref.c_ref.refs_2_.b_ref.refs_1_, ...), custom_call_target="tpu_custom_call", output_to_operand_aliasing={{0}: (8, {}), {1}: (9, {})} | custom-call | flops 536870912 | bytes 4980736 | tf_op jit(solution)/shard_map/backward/pallas_call | solution.py:330
  32.1 0.1 collective-permute-done.8
  32.2 0.0 collective-permute-start.9
  32.2 1.2 %collective-permute-done.9 = f32[64,128]{1,0:T(8,128)S(1)} collective-permute-done((f32[64,128]{1,0:T(8,128)S(1)}, f32[64,128]{1,0:T(8,128)S(1)}, u32[]{:S(2)}, u32[]{:S(2)}) %collective-permute-start.9) | collective-permute-done | bytes 32800 | tf_op jit(solution)/shard_map/ppermute | solution.py:404
  33.4 0.6 %maximum_select_fusion = f32[128,128]{1,0:T(8,128)} fusion(f32[64,128]{1,0:T(8,128)S(1)} %collective-permute-done.9, f32[64,128]{1,0:T(8,128)S(1)} %add.24, pred[]{:T(512)S(6)} %eq.5), kind=kLoop, calls=%fused_computation | loop fusion | flops 49152 | bytes 131073 | tf_op jit(solution)/shard_map/jit(_where)/select_n | solution.py:501
  (5 shorter events, 0.0 us)
Async XLA Ops:
  2.2 6.6 %collective-permute-start = (bf16[128,1024]{1,0:T(8,128)(2,1)S(1)}, bf16[128,1024]{1,0:T(8,128)(2,1)S(1)}, u32[]{:S(2)}, u32[]{:S(2)}) collective-permute-start(bf16[128,1024]{1,0:T(8,128)(2,1)S(1)} %get-tuple-element.47), channel_id=1, source_target_pairs={{0,4},{4,0},{8,12},{12,8},{16,20},{20,16},{24,28},{28,24},{1,5},{5... | collective-permute-start | bytes 786440 | tf_op jit(solution)/shard_map/ppermute | solution.py:404
  2.7 11.5 %collective-permute-start.3 = (bf16[128,1024]{1,0:T(8,128)(2,1)S(1)}, bf16[128,1024]{1,0:T(8,128)(2,1)S(1)}, u32[]{:S(2)}, u32[]{:S(2)}) collective-permute-start(bf16[128,1024]{1,0:T(8,128)(2,1)S(1)} %get-tuple-element.51), channel_id=1, source_target_pairs={{4,8},{12,16},{20,24},{8,4},{16,12},{24,20},{5,9},{13,17},{21,25},... | collective-permute-start | bytes 786440 | tf_op jit(solution)/shard_map/ppermute | solution.py:410
  4.9 12.0 %collective-permute-start.2 = (bf16[128,1024]{1,0:T(8,128)(2,1)S(1)}, bf16[128,1024]{1,0:T(8,128)(2,1)S(1)}, u32[]{:S(2)}, u32[]{:S(2)}) collective-permute-start(bf16[128,1024]{1,0:T(8,128)(2,1)S(1)} %get-tuple-element.50), channel_id=1, source_target_pairs={{0,4},{4,0},{8,12},{12,8},{16,20},{20,16},{24,28},{28,24},{1,5},{5... | collective-permute-start | bytes 786440 | tf_op jit(solution)/shard_map/ppermute | solution.py:404
  10.6 13.5 %collective-permute-start.1 = (bf16[128,1024]{1,0:T(8,128)(2,1)S(1)}, bf16[128,1024]{1,0:T(8,128)(2,1)S(1)}, u32[]{:S(2)}, u32[]{:S(2)}) collective-permute-start(bf16[128,1024]{1,0:T(8,128)(2,1)S(1)} %get-tuple-element.49), channel_id=1, source_target_pairs={{4,8},{12,16},{20,24},{8,4},{16,12},{24,20},{5,9},{13,17},{21,25},... | collective-permute-start | bytes 786440 | tf_op jit(solution)/shard_map/ppermute | solution.py:410
  11.3 3.9 %collective-permute-start.4 = (f32[64,128]{1,0:T(8,128)S(1)}, f32[64,128]{1,0:T(8,128)S(1)}, u32[]{:S(2)}, u32[]{:S(2)}) collective-permute-start(f32[64,128]{1,0:T(8,128)S(1)} %get-tuple-element.60), channel_id=1, source_target_pairs={{0,4},{4,0},{8,12},{12,8},{16,20},{20,16},{24,28},{28,24},{1,5},{5... | collective-permute-start | bytes 98312 | tf_op jit(solution)/shard_map/ppermute | solution.py:404
  15.2 4.0 %collective-permute-start.5 = (f32[64,128]{1,0:T(8,128)S(1)}, f32[64,128]{1,0:T(8,128)S(1)}, u32[]{:S(2)}, u32[]{:S(2)}) collective-permute-start(f32[64,128]{1,0:T(8,128)S(1)} %add.20), channel_id=1, source_target_pairs={{1,0},{0,1},{3,2},{2,3},{5,4},{4,5},{7,6},{6,7},{9,8},{8,9},{11,10... | collective-permute-start | bytes 98312 | tf_op jit(solution)/shard_map/ppermute | solution.py:434
  19.2 4.8 %collective-permute-start.6 = (f32[64,128]{1,0:T(8,128)S(1)}, f32[64,128]{1,0:T(8,128)S(1)}, u32[]{:S(2)}, u32[]{:S(2)}) collective-permute-start(f32[64,128]{1,0:T(8,128)S(1)} %add.21), channel_id=1, source_target_pairs={{2,0},{3,1},{0,2},{1,3},{6,4},{7,5},{4,6},{5,7},{10,8},{11,9},{8,1... | collective-permute-start | bytes 98312 | tf_op jit(solution)/shard_map/ppermute | solution.py:434
  24.0 4.2 %collective-permute-start.7 = (f32[64,128]{1,0:T(8,128)S(1)}, f32[64,128]{1,0:T(8,128)S(1)}, u32[]{:S(2)}, u32[]{:S(2)}) collective-permute-start(f32[64,128]{1,0:T(8,128)S(1)} %add.22), channel_id=1, source_target_pairs={{8,0},{12,4},{0,8},{4,12},{24,16},{28,20},{16,24},{20,28},{9,1},{1... | collective-permute-start | bytes 98312 | tf_op jit(solution)/shard_map/ppermute | solution.py:434
  28.2 4.0 %collective-permute-start.8 = (f32[64,128]{1,0:T(8,128)S(1)}, f32[64,128]{1,0:T(8,128)S(1)}, u32[]{:S(2)}, u32[]{:S(2)}) collective-permute-start(f32[64,128]{1,0:T(8,128)S(1)} %add.23), channel_id=1, source_target_pairs={{16,0},{20,4},{24,8},{28,12},{0,16},{4,20},{8,24},{12,28},{17,1},{... | collective-permute-start | bytes 98312 | tf_op jit(solution)/shard_map/ppermute | solution.py:434
  32.2 1.2 %collective-permute-start.9 = (f32[64,128]{1,0:T(8,128)S(1)}, f32[64,128]{1,0:T(8,128)S(1)}, u32[]{:S(2)}, u32[]{:S(2)}) collective-permute-start(f32[64,128]{1,0:T(8,128)S(1)} %add.24), channel_id=1, source_target_pairs={{0,4},{4,0},{8,12},{12,8},{16,20},{20,16},{24,28},{28,24},{1,5},{5... | collective-permute-start | bytes 98312 | tf_op jit(solution)/shard_map/ppermute | solution.py:404
